TPU v7x, 32 devices: a whole 2x2x4 slice. The times are simulated.
32 devices in a mesh: seq: 8 (over z, y), kvh: 4 (over x, core).
Axes of the slice: x: 2, y: 2, z: 4, core: 2. Of those that a mesh axis runs over, the one named last changes fastest.
Arguments:
- queries: bfloat16 [1024, 2560], P('seq', 'kvh'), may hold values from -7 to 7
- keys: bfloat16 [1024, 512], P(('seq', 'kvh')), may hold values from -6 to 6
- values: bfloat16 [1024, 512], P(('seq', 'kvh')), may hold values from -6 to 6
- d_out: bfloat16 [1024, 2560], P('seq', 'kvh'), may hold values from -6 to 6
- slab_order: int32 [16], replicated, may hold values from 0 to 15, as said below
Outputs:
- query_grads: bfloat16 [1024, 2560], P('seq', 'kvh')
- key_grads: bfloat16 [1024, 512], P(('seq', 'kvh'))
- value_grads: bfloat16 [1024, 512], P(('seq', 'kvh'))
Inputs may be any that keep to these rules, and one draw needn't show every extreme that they name: `slab_order`: each number 0 to 15 appears once; slots 2 d and 2 d + 1 hold the slabs c and 15 - c for some c, in either order.
All inputs are finite; a program needn't handle non-finite values.
Results may differ from a plain program's by a relative error of at most 0.015.
Values may be sent and summed in bfloat16 or wider, within the bound.
No kernel may reach another device: no remote copies, remote signals or barrier semaphores. Data moves between devices by JAX's collectives and lax.ppermute only.
A program may use at most 64 MiB of HBM per device.

v0:
```python
import math

import jax
import jax.numpy as jnp
from jax import lax
from jax.sharding import PartitionSpec as P

HEADS = 20
KV_HEADS = 4
HEAD = 128


def per_device(queries, keys, values, d_out, slab_order):
    kv_local = KV_HEADS // lax.axis_size("kvh")
    group_size = HEADS // KV_HEADS
    softmax_scale = HEAD ** (-0.5)
    head_keys, head_values = (
        lax.all_to_all(keys, "kvh", split_axis=1, concat_axis=0, tiled=True),
        lax.all_to_all(values, "kvh", split_axis=1, concat_axis=0, tiled=True),
    )
    every_key, every_value = (
        lax.all_gather(head_keys, "seq", axis=0, tiled=True),
        lax.all_gather(head_values, "seq", axis=0, tiled=True),
    )
    local_rows = queries.shape[0]
    slab_rows = local_rows // 2
    total_rows = every_key.shape[0]
    slab_count = total_rows // slab_rows
    block_rows = math.gcd(512, total_rows)
    feature_cols = kv_local * HEAD
    slab_ids = jnp.arange(slab_count, dtype=jnp.int32)
    slot_of_slab = jnp.sum(
        jnp.where(slab_order[None, :] == slab_ids[:, None], slab_ids[None, :], 0), axis=1
    )
    positions = (
        slab_order[:, None] * slab_rows + jnp.arange(slab_rows, dtype=jnp.int32)[None, :]
    ).reshape(total_rows)
    seq_index = lax.axis_index("seq")
    query_pos = lax.dynamic_slice_in_dim(positions, seq_index * local_rows, local_rows)
    ordered_keys = jnp.take(
        every_key.reshape(slab_count, slab_rows, feature_cols), slot_of_slab, axis=0
    ).reshape(total_rows, kv_local, HEAD)
    ordered_values = jnp.take(
        every_value.reshape(slab_count, slab_rows, feature_cols), slot_of_slab, axis=0
    ).reshape(total_rows, kv_local, HEAD)
    query_row_set = queries.reshape(local_rows, kv_local, group_size, HEAD)
    gradient_row_set = d_out.reshape(local_rows, kv_local, group_size, HEAD)

    def attend(query_part, grad_part, pos_part, buffer_in):
        part_rows = query_part.shape[0]
        block_count = jnp.max(pos_part) // block_rows + 1

        def block_scores(block_index):
            first_key = block_index * block_rows
            key_block_slice = lax.dynamic_slice_in_dim(ordered_keys, first_key, block_rows, 0)
            value_block_slice = lax.dynamic_slice_in_dim(ordered_values, first_key, block_rows, 0)
            key_pos = first_key + jnp.arange(block_rows, dtype=jnp.int32)
            allowed = key_pos[None, :] <= pos_part[:, None]
            logit_scores = (
                jnp.einsum(
                    "uiyh,mih->iyum",
                    query_part,
                    key_block_slice,
                    preferred_element_type=jnp.float32,
                )
                * softmax_scale
            )
            return (
                jnp.where(allowed, logit_scores, -jnp.inf),
                key_block_slice,
                value_block_slice,
                first_key,
            )

        def stat_step(block_index, stat_pair):
            row_max, row_sum = stat_pair
            logit_scores = block_scores(block_index)[0]
            new_max = jnp.maximum(row_max, jnp.max(logit_scores, axis=-1))
            new_sum = row_sum * jnp.exp(row_max - new_max) + jnp.sum(
                jnp.exp(logit_scores - new_max[..., None]), axis=-1
            )
            return (new_max, new_sum)

        start_max = jnp.full((kv_local, group_size, part_rows), -jnp.inf, jnp.float32)
        start_sum = jnp.zeros((kv_local, group_size, part_rows), jnp.float32)
        row_max, row_sum = lax.fori_loop(0, block_count, stat_step, (start_max, start_sum))

        def weights_of(logit_scores):
            return jnp.exp(logit_scores - row_max[..., None]) / row_sum[..., None]

        def output_step(block_index, output_acc):
            logit_scores, key_block_slice, value_block_slice, first_key = block_scores(block_index)
            probability_reduced = weights_of(logit_scores).astype(jnp.bfloat16)
            return output_acc + jnp.einsum(
                "oiau,uoc->aoic",
                probability_reduced,
                value_block_slice,
                preferred_element_type=jnp.float32,
            )

        attended_output = lax.fori_loop(
            0, block_count, output_step, jnp.zeros(query_part.shape, jnp.float32)
        ).astype(jnp.bfloat16)
        delta = jnp.einsum(
            "nkgd,nkgd->kgn", grad_part, attended_output, preferred_element_type=jnp.float32
        )

        def grad_core(block_index):
            logit_scores, key_block_slice, value_block_slice, first_key = block_scores(block_index)
            probs = weights_of(logit_scores)
            probability_gradient = jnp.einsum(
                "uiyh,mih->iyum", grad_part, value_block_slice, preferred_element_type=jnp.float32
            )
            score_gradient = (probs * (probability_gradient - delta[..., None])).astype(
                jnp.bfloat16
            )
            query_term = jnp.einsum(
                "oiau,uoc->aoic",
                score_gradient,
                key_block_slice,
                preferred_element_type=jnp.float32,
            )
            return (probs, score_gradient, query_term, first_key)

        query_start = jnp.zeros(query_part.shape, jnp.float32)

        def full_step(block_index, state_pair):
            query_acc, buffer_acc = state_pair
            probs, score_gradient, query_term, first_key = grad_core(block_index)
            key_term = (
                jnp.einsum(
                    "wrci,cwrx->iwx", score_gradient, query_part, preferred_element_type=jnp.float32
                )
                * softmax_scale
            )
            value_term = jnp.einsum(
                "wrci,cwrx->iwx",
                probs.astype(jnp.bfloat16),
                grad_part,
                preferred_element_type=jnp.float32,
            )
            block_term = jnp.concatenate(
                [
                    key_term.reshape(block_rows, feature_cols),
                    value_term.reshape(block_rows, feature_cols),
                ],
                axis=1,
            )
            old_term = lax.dynamic_slice_in_dim(buffer_acc, first_key, block_rows, 0)
            buffer_acc = lax.dynamic_update_slice_in_dim(
                buffer_acc, old_term + block_term, first_key, 0
            )
            return (query_acc + query_term, buffer_acc)

        query_acc, buffer_out = lax.fori_loop(0, block_count, full_step, (query_start, buffer_in))
        return (query_acc * softmax_scale, row_max, row_sum, delta, buffer_out)

    buffer_start = jnp.zeros((total_rows, 2 * feature_cols), jnp.float32)
    first_acc, first_max, first_sum, first_delta, buffer_mid = attend(
        query_row_set[:slab_rows], gradient_row_set[:slab_rows], query_pos[:slab_rows], buffer_start
    )
    second_acc, second_max, second_sum, second_delta, buffer_done = attend(
        query_row_set[slab_rows:], gradient_row_set[slab_rows:], query_pos[slab_rows:], buffer_mid
    )
    query_acc = jnp.concatenate([first_acc, second_acc], axis=0)
    row_max = jnp.concatenate([first_max, second_max], axis=2)
    row_sum = jnp.concatenate([first_sum, second_sum], axis=2)
    delta = jnp.concatenate([first_delta, second_delta], axis=2)
    device_terms = jnp.take(
        buffer_done.reshape(slab_count, slab_rows, 2 * feature_cols), slab_order, axis=0
    ).reshape(total_rows, 2 * feature_cols)
    grad_share = lax.psum_scatter(device_terms, "seq", scatter_dimension=0, tiled=True)
    key_part_low = grad_share[:, :feature_cols].astype(jnp.bfloat16)
    value_part_low = grad_share[:, feature_cols:].astype(jnp.bfloat16)
    key_grads, value_grads = (
        lax.all_to_all(key_part_low, "kvh", split_axis=0, concat_axis=1, tiled=True),
        lax.all_to_all(value_part_low, "kvh", split_axis=0, concat_axis=1, tiled=True),
    )
    query_grads = query_acc.reshape(local_rows, kv_local * group_size * HEAD).astype(jnp.bfloat16)
    return (query_grads, key_grads, value_grads)


def solution(mesh):
    placed = (
        P("seq", "kvh"),
        P(("seq", "kvh"), None),
        P(("seq", "kvh"), None),
        P("seq", "kvh"),
        P(),
    )
    return jax.shard_map(
        per_device,
        mesh=mesh,
        in_specs=placed,
        out_specs=(P("seq", "kvh"), P(("seq", "kvh"), None), P(("seq", "kvh"), None)),
        check_vma=False,
    )
```

profile of v0, /device:TPU:0, one launch (start us, length us, event | category | flops | bytes accessed | tf_op | source)
XLA Modules:
  0.0 190.6 jit_solution(11752140999541800386)
XLA Ops:
  7.2 0.7 copy-done
  7.9 0.6 copy_bitcast_fusion.2
  8.5 4.2 %all-to-all-start.1 = ((bf16[32,4,128]{2,0,1:T(8,128)(2,1)}), bf16[32,4,128]{2,0,1:T(8,128)(2,1)S(1)}, u32[]{:S(2)}, u32[]{:S(2)}) async-start(bf16[32,4,128]{2,0,1:T(8,128)(2,1)} %copy_bitcast_fusion.2), calls=%async_computation.1 | async-start | bytes 65536 | tf_op jit(solution)/shard_map/all_to_all | solution.py:19
  12.8 0.7 compare_select_fusion.1
  13.4 0.8 select_reduce_fusion
  14.2 0.7 compare_and_fusion.1
  15.1 0.7 slice_reduce_fusion
  15.8 0.6 copy_bitcast_fusion.3
  16.5 0.9 copy-done.2
  23.1 3.3 %all-to-all-start = ((bf16[32,4,128]{2,0,1:T(8,128)(2,1)}), bf16[32,4,128]{2,0,1:T(8,128)(2,1)S(1)}, u32[]{:S(2)}, u32[]{:S(2)}) async-start(bf16[32,4,128]{2,0,1:T(8,128)(2,1)} %copy_bitcast_fusion.3), calls=%async_computation | async-start | bytes 65536 | tf_op jit(solution)/shard_map/all_to_all | solution.py:18
  26.4 31.8 %all_gather.7 = bf16[1024,128]{1,0:T(8,128)(2,1)S(1)} all-gather(bf16[128,128]{1,0:T(8,128)(2,1)S(1)} %bitcast.462), channel_id=1, replica_groups=mesh['seq'=8,'kvh'=4] {'seq'}, dimensions={0}, use_global_device_ids=true | all-gather | bytes 294912 | tf_op jit(solution)/shard_map/all_gather | solution.py:23
  58.2 30.7 %all_gather.6 = bf16[1024,128]{1,0:T(8,128)(2,1)S(1)} all-gather(bf16[128,128]{1,0:T(8,128)(2,1)S(1)} %bitcast.463), channel_id=1, replica_groups=mesh['seq'=8,'kvh'=4] {'seq'}, dimensions={0}, use_global_device_ids=true | all-gather | bytes 294912 | tf_op jit(solution)/shard_map/all_gather | solution.py:22
  88.9 0.6 gather_fusion.2
  89.5 0.6 gather_fusion.1
  90.1 0.1 broadcast_select_fusion
  90.3 1.5 while.68
  90.4 0.3 fusion.169
  90.8 0.2 exponential_reduce_fusion.4
  91.2 0.3 fusion.169
  91.5 0.2 exponential_reduce_fusion.4
  91.8 1.2 while.69
  91.9 0.4 fusion.173
  92.5 0.4 fusion.173
  93.0 0.2 multiply_reduce_fusion.1
  93.4 3.4 %while.70 = (s32[]{:T(128)}, f32[64,1,5,128]{3,0,2,1:T(8,128)S(1)}, f32[1024,256]{0,1:T(8,128)S(1)}, s32[]{:T(128)}, bf16[1024,1,128]{2,0,1:T(8,128)(2,1)S(1)}, ...) while((s32[]{:T(128)}, f32[64,1,5,128]{3,0,2,1:T(8,128)S(1)}, ...), condition=%wide.region_9.11_spmd, body=%wide.region_8.10_spmd.sunk | while | flops 211427840 | bytes 6177247 | solution.py:155
  93.5 0.3 fusion.184
  93.9 0.3 fusion.185
  94.1 0.3 fusion.186
  94.4 0.3 convolution_bitcast_fusion.12
  94.7 0.3 fusion.187
  95.0 0.1 fusion.188
  95.2 0.3 fusion.184
  95.5 0.3 fusion.185
  95.8 0.3 fusion.186
  96.1 0.3 convolution_bitcast_fusion.12
  96.4 0.3 fusion.187
  96.6 0.1 fusion.188
  96.8 0.7 while.71
  96.9 0.3 fusion.189
  97.3 0.2 exponential_reduce_fusion.5
  97.6 0.6 while.72
  97.7 0.4 fusion.193
  98.2 0.2 multiply_reduce_fusion
  98.5 1.7 while.73
  98.6 0.3 fusion.204
  98.9 0.3 fusion.205
  99.2 0.3 fusion.206
  99.5 0.3 convolution_bitcast_fusion.13
  99.7 0.3 fusion.207
  100.0 0.1 fusion.208
  100.2 0.3 copy.80
  100.5 0.6 gather_fusion
  101.1 1.2 bitcast_select_fusion
  102.4 64.9 %reduce-scatter.2.cloned.1.call-done = f32[128,256]{1,0:T(8,128)} async-done(((f32[1024,256]{1,0:T(8,128)}), f32[128,256]{1,0:T(8,128)}) %reduce-scatter.2.cloned.1.call-update) | async-done | bytes 131088 | tf_op jit(solution)/shard_map/reduce_scatter | solution.py:172
  167.2 0.9 convert.12
  168.2 0.6 fusion.120
  168.8 3.3 %all-to-all-start.2 = ((bf16[4,32,128]{2,1,0:T(8,128)(2,1)}), bf16[4,32,128]{2,1,0:T(8,128)(2,1)S(1)}, u32[]{:S(2)}, u32[]{:S(2)}) async-start(bf16[4,32,128]{2,1,0:T(8,128)(2,1)} %bitcast.99), calls=%async_computation.3 | async-start | bytes 65536 | tf_op jit(solution)/shard_map/all_to_all | solution.py:176
  172.1 0.2 copy.79
  172.3 0.8 copy.83
  173.1 2.9 %all-to-all-done.2 = bf16[4,32,128]{2,1,0:T(8,128)(2,1)S(1)} async-done(((bf16[4,32,128]{2,1,0:T(8,128)(2,1)}), bf16[4,32,128]{2,1,0:T(8,128)(2,1)S(1)}, u32[]{:S(2)}, u32[]{:S(2)}) %all-to-all-start.2) | async-done | bytes 32800 | tf_op jit(solution)/shard_map/all_to_all | solution.py:176
  176.0 3.3 %all-to-all-start.3 = ((bf16[4,32,128]{2,1,0:T(8,128)(2,1)}), bf16[4,32,128]{2,1,0:T(8,128)(2,1)S(1)}, u32[]{:S(2)}, u32[]{:S(2)}) async-start(bf16[4,32,128]{2,1,0:T(8,128)(2,1)} %bitcast.101), calls=%async_computation.4 | async-start | bytes 65536 | tf_op jit(solution)/shard_map/all_to_all | solution.py:177
  179.2 0.6 copy_bitcast_fusion.1
  179.9 3.3 %all-to-all-done.3 = bf16[4,32,128]{2,1,0:T(8,128)(2,1)S(1)} async-done(((bf16[4,32,128]{2,1,0:T(8,128)(2,1)}), bf16[4,32,128]{2,1,0:T(8,128)(2,1)S(1)}, u32[]{:S(2)}, u32[]{:S(2)}) %all-to-all-start.3) | async-done | bytes 32800 | tf_op jit(solution)/shard_map/all_to_all | solution.py:177
  183.2 0.6 copy_bitcast_fusion
  (73 shorter events, 2.5 us)
Async XLA Ops:
  7.2 0.8 copy-start
  7.2 8.6 %copy-start.3 = (bf16[32,512]{1,0:T(8,128)(2,1)S(1)}, bf16[32,512]{1,0:T(8,128)(2,1)}, u32[]{:S(2)}) copy-start(bf16[32,512]{1,0:T(8,128)(2,1)} %param.20) | copy-start | bytes 98308
  7.2 9.2 %copy-start.1 = (bf16[128,640]{1,0:T(8,128)(2,1)S(1)}, bf16[128,640]{1,0:T(8,128)(2,1)}, u32[]{:S(2)}) copy-start(bf16[128,640]{1,0:T(8,128)(2,1)} %param.19) | copy-start | bytes 491524
  8.5 14.6 %all-to-all-start.1 = ((bf16[32,4,128]{2,0,1:T(8,128)(2,1)}), bf16[32,4,128]{2,0,1:T(8,128)(2,1)S(1)}, u32[]{:S(2)}, u32[]{:S(2)}) async-start(bf16[32,4,128]{2,0,1:T(8,128)(2,1)} %copy_bitcast_fusion.2), calls=%async_computation.1 | async-start | bytes 65536 | tf_op jit(solution)/shard_map/all_to_all | solution.py:19
  16.4 0.9 copy-start.2
  23.1 35.1 %all-to-all-start = ((bf16[32,4,128]{2,0,1:T(8,128)(2,1)}), bf16[32,4,128]{2,0,1:T(8,128)(2,1)S(1)}, u32[]{:S(2)}, u32[]{:S(2)}) async-start(bf16[32,4,128]{2,0,1:T(8,128)(2,1)} %copy_bitcast_fusion.3), calls=%async_computation | async-start | bytes 65536 | tf_op jit(solution)/shard_map/all_to_all | solution.py:18
  26.4 140.8 %reduce-scatter.2.cloned.1.call-start = ((), (), s32[]{:S(2)}) async-start(), calls=%async_computation.5 | async-start | bytes 1179648 | tf_op jit(solution)/shard_map/reduce_scatter | solution.py:172
  168.8 7.2 %all-to-all-start.2 = ((bf16[4,32,128]{2,1,0:T(8,128)(2,1)}), bf16[4,32,128]{2,1,0:T(8,128)(2,1)S(1)}, u32[]{:S(2)}, u32[]{:S(2)}) async-start(bf16[4,32,128]{2,1,0:T(8,128)(2,1)} %bitcast.99), calls=%async_computation.3 | async-start | bytes 65536 | tf_op jit(solution)/shard_map/all_to_all | solution.py:176
  176.0 7.2 %all-to-all-start.3 = ((bf16[4,32,128]{2,1,0:T(8,128)(2,1)}), bf16[4,32,128]{2,1,0:T(8,128)(2,1)S(1)}, u32[]{:S(2)}, u32[]{:S(2)}) async-start(bf16[4,32,128]{2,1,0:T(8,128)(2,1)} %bitcast.101), calls=%async_computation.4 | async-start | bytes 65536 | tf_op jit(solution)/shard_map/all_to_all | solution.py:177
Sparse Core Ops, SparseCore 0:
  102.5 64.7 reduce-scatter.1
where the time goes:
time: 191 us
  waiting for transfers between devices  71.1 us (37%)
  blocking collectives  62.5 us (33%)
  between operations  19.1 us (10%)
  starting transfers between devices  14.1 us (7%)
  local copies, waits for them, and re-layouts  9.27 us (5%)
  other arithmetic  7.48 us (4%)
  matrix products  6.5 us (3%)
    reduce_scatter x1, waiting for transfers between devices, per_device(): lax.psum_scatter(device_terms, 'seq', scatter_dimension=0, tiled=True)  64.9 us
    all_gather x1, blocking collectives, per_device(): lax.all_gather(head_values, 'seq', axis=0, tiled=True)  31.8 us
    all_gather x1, blocking collectives, per_device(): lax.all_gather(head_keys, 'seq', axis=0, tiled=True)  30.7 us
    all_to_all x1, starting transfers between devices, per_device(): lax.all_to_all(values, 'kvh', split_axis=1, concat_axis=0, tiled=True)  4.21 us
  transfers between devices with their start and end apart: 5, of which 3 were waited for; matrix products, arithmetic and copies ran while one was open for 3% of the time, Pallas kernels for 0%

commit v1 on v0

v1 whole, which is shorter than its diff:
```python
import functools
import math

import jax
import jax.numpy as jnp
from jax import lax
from jax.experimental import pallas as pl
from jax.experimental.pallas import tpu as pltpu
from jax.sharding import PartitionSpec as P

HEADS = 20
KV_HEADS = 4
HEAD = 128
VMEM_LIMIT = 56 * 1024 * 1024


def repeat(count, body):
    if count <= 8:
        for step in range(count):
            body(step)
    else:
        pl.loop(0, count)(body)


def pack_kernel(kvh, keys_ref, values_ref, out_ref):
    width = out_ref.shape[2] // 2
    for k in range(kvh):
        cols = slice(k * width, (k + 1) * width)
        key_part = keys_ref[:, cols]
        value_part = values_ref[:, cols]
        for s in range(out_ref.shape[0] // kvh):
            out_ref[s * kvh + k, :, :width] = key_part
            out_ref[s * kvh + k, :, width:] = value_part


def combine_kernel(kvh, terms_ref, key_ref, value_ref):
    width = terms_ref.shape[2] // 2
    seq = terms_ref.shape[0] // kvh
    for k in range(kvh):
        total = terms_ref[k].astype(jnp.float32)
        for s in range(1, seq):
            total = total + terms_ref[s * kvh + k].astype(jnp.float32)
        total = total.astype(jnp.bfloat16)
        key_ref[:, k * width : (k + 1) * width] = total[:, :width]
        value_ref[:, k * width : (k + 1) * width] = total[:, width:]


def attend_kernel(
    group,
    order_ref,
    me_ref,
    q_ref,
    do_ref,
    kv_ref,
    dq_ref,
    dkv_ref,
    slot_ref,
    qs_ref,
    ds_ref,
    kvs_ref,
    s_ref,
    dp_ref,
    m_ref,
    l_ref,
    d_ref,
    acc_ref,
    dq_acc_ref,
):
    slabs = order_ref.shape[0]
    total = kv_ref.shape[0]
    slab_rows = total // slabs
    heads = q_ref.shape[1] // HEAD
    kv_local = heads // group
    chunk_slabs = math.gcd(4, slabs)
    chunk = chunk_slabs * slab_rows
    chunks = slabs // chunk_slabs
    steps = chunks + 1
    columns = group * slab_rows
    width = kv_local * HEAD
    scale = HEAD ** (-0.5)
    exponent_scale = scale * math.log2(math.e)

    for slot in range(slabs):
        slot_ref[order_ref[slot]] = slot
    me = me_ref[0]
    first, second = order_ref[2 * me], order_ref[2 * me + 1]
    low_half = jnp.where(first < second, 0, 1)
    low_slab = jnp.minimum(first, second)
    high_slab = jnp.maximum(first, second)
    low_steps = low_slab // chunk_slabs + 1

    def sort_slab(slab):
        rows = pl.ds(pl.multiple_of(slot_ref[slab] * slab_rows, slab_rows), slab_rows)
        kvs_ref[pl.ds(pl.multiple_of(slab * slab_rows, slab_rows), slab_rows), :] = kv_ref[rows, :]

    for slab in range(slabs):
        sort_slab(slab)

    for g in range(kv_local):
        key_cols = slice(g * HEAD, (g + 1) * HEAD)
        value_cols = slice(width + g * HEAD, width + (g + 1) * HEAD)
        for half in range(2):
            side = low_half if half == 0 else 1 - low_half
            rows = pl.ds(pl.multiple_of(side * slab_rows, slab_rows), slab_rows)
            for h in range(group):
                cols = slice((g * group + h) * HEAD, (g * group + h + 1) * HEAD)
                qs_ref[half, h * slab_rows : (h + 1) * slab_rows, :] = q_ref[rows, cols]
                ds_ref[half, h * slab_rows : (h + 1) * slab_rows, :] = do_ref[rows, cols]
        m_ref[...] = jnp.full(m_ref.shape, -jnp.inf, jnp.float32)
        l_ref[...] = jnp.zeros(l_ref.shape, jnp.float32)
        d_ref[...] = jnp.zeros(d_ref.shape, jnp.float32)
        acc_ref[...] = jnp.zeros(acc_ref.shape, jnp.float32)
        dq_acc_ref[...] = jnp.zeros(dq_acc_ref.shape, jnp.float32)

        def place(step):
            is_high = jnp.where(step >= low_steps, 1, 0)
            at = jnp.where(step >= low_steps, step - low_steps, step)
            return is_high, at, pl.ds(pl.multiple_of(at * chunk, chunk), chunk)

        def score_step(step):
            half, at, rows = place(step)
            slab = jnp.where(half == 1, high_slab, low_slab)
            scores = lax.dot_general(
                kvs_ref[rows, key_cols],
                qs_ref[half],
                (((1,), (1,)), ((), ())),
                preferred_element_type=jnp.float32,
            )
            key_pos = at * chunk + lax.broadcasted_iota(jnp.int32, scores.shape, 0)
            query_pos = slab * slab_rows + lax.rem(
                lax.broadcasted_iota(jnp.int32, (1, columns), 1), slab_rows
            )
            scores = jnp.where(key_pos <= query_pos, scores, -jnp.inf)
            s_ref[step] = scores
            m_ref[half] = jnp.maximum(m_ref[half], jnp.max(scores, axis=0, keepdims=True))
            dp_ref[step] = lax.dot_general(
                kvs_ref[rows, value_cols],
                ds_ref[half],
                (((1,), (1,)), ((), ())),
                preferred_element_type=jnp.float32,
            )

        repeat(steps, score_step)

        def sum_step(step):
            half, at, rows = place(step)
            expon = jnp.exp2((s_ref[step] - m_ref[half]) * exponent_scale)
            s_ref[step] = expon
            l_ref[half] = l_ref[half] + jnp.sum(expon, axis=0, keepdims=True)
            d_ref[half] = d_ref[half] + jnp.sum(expon * dp_ref[step], axis=0, keepdims=True)

        repeat(steps, sum_step)
        inverse = 1.0 / l_ref[...]
        l_ref[...] = inverse
        d_ref[...] = d_ref[...] * inverse

        def grad_step(step):
            half, at, rows = place(step)
            probs = s_ref[step] * l_ref[half]
            score_grads = (probs * (dp_ref[step] - d_ref[half])).astype(jnp.bfloat16)
            acc_ref[rows, HEAD:] = acc_ref[rows, HEAD:] + jnp.dot(
                probs.astype(jnp.bfloat16), ds_ref[half], preferred_element_type=jnp.float32
            )
            acc_ref[rows, :HEAD] = acc_ref[rows, :HEAD] + jnp.dot(
                score_grads, qs_ref[half], preferred_element_type=jnp.float32
            )
            dq_acc_ref[half] = dq_acc_ref[half] + lax.dot_general(
                kvs_ref[rows, key_cols],
                score_grads,
                (((0,), (0,)), ((), ())),
                preferred_element_type=jnp.float32,
            )

        repeat(steps, grad_step)

        for half in range(2):
            side = low_half if half == 0 else 1 - low_half
            rows = pl.ds(pl.multiple_of(side * slab_rows, slab_rows), slab_rows)
            grads = (jnp.transpose(dq_acc_ref[half]) * scale).astype(jnp.bfloat16)
            for h in range(group):
                cols = slice((g * group + h) * HEAD, (g * group + h + 1) * HEAD)
                dq_ref[rows, cols] = grads[h * slab_rows : (h + 1) * slab_rows, :]

        def place_slab(slab):
            rows = pl.ds(pl.multiple_of(slot_ref[slab] * slab_rows, slab_rows), slab_rows)
            terms = acc_ref[pl.ds(pl.multiple_of(slab * slab_rows, slab_rows), slab_rows), :]
            dkv_ref[rows, key_cols] = (terms[:, :HEAD] * scale).astype(jnp.bfloat16)
            dkv_ref[rows, value_cols] = terms[:, HEAD:].astype(jnp.bfloat16)

        for slab in range(slabs):
            place_slab(slab)


def per_device(queries, keys, values, d_out, slab_order):
    axes = ("seq", "kvh")
    kvh = lax.axis_size("kvh")
    seq = lax.axis_size("seq")
    devices = seq * kvh
    kv_local = KV_HEADS // kvh
    group = HEADS // KV_HEADS
    local_rows, query_width = queries.shape
    cache_rows = keys.shape[0]
    slabs = slab_order.shape[0]
    slab_rows = local_rows // 2
    total = slab_rows * slabs
    width = kv_local * HEAD
    chunk_slabs = math.gcd(4, slabs)
    chunk = chunk_slabs * slab_rows
    steps = slabs // chunk_slabs + 1
    columns = group * slab_rows
    params = pltpu.CompilerParams(vmem_limit_bytes=VMEM_LIMIT)
    vmem = pl.BlockSpec(memory_space=pltpu.VMEM)
    smem = pl.BlockSpec(memory_space=pltpu.SMEM)

    packed = pl.pallas_call(
        functools.partial(pack_kernel, kvh),
        out_shape=jax.ShapeDtypeStruct((devices, cache_rows, 2 * width), keys.dtype),
        in_specs=[vmem, vmem],
        out_specs=vmem,
        compiler_params=params,
        name="pack",
    )(keys, values)
    gathered = lax.all_to_all(packed, axes, split_axis=0, concat_axis=0, tiled=True)
    gathered = gathered.reshape(total, 2 * width)

    me = lax.axis_index("seq").astype(jnp.int32).reshape(1)
    query_grads, terms = pl.pallas_call(
        functools.partial(attend_kernel, group),
        out_shape=(
            jax.ShapeDtypeStruct(queries.shape, jnp.bfloat16),
            jax.ShapeDtypeStruct((total, 2 * width), jnp.bfloat16),
        ),
        in_specs=[smem, smem, vmem, vmem, vmem],
        out_specs=(vmem, vmem),
        scratch_shapes=[
            pltpu.SMEM((slabs,), jnp.int32),
            pltpu.VMEM((2, columns, HEAD), jnp.bfloat16),
            pltpu.VMEM((2, columns, HEAD), jnp.bfloat16),
            pltpu.VMEM((total, 2 * width), jnp.bfloat16),
            pltpu.VMEM((steps, chunk, columns), jnp.float32),
            pltpu.VMEM((steps, chunk, columns), jnp.float32),
            pltpu.VMEM((2, 1, columns), jnp.float32),
            pltpu.VMEM((2, 1, columns), jnp.float32),
            pltpu.VMEM((2, 1, columns), jnp.float32),
            pltpu.VMEM((total, 2 * HEAD), jnp.float32),
            pltpu.VMEM((2, HEAD, columns), jnp.float32),
        ],
        compiler_params=params,
        name="attend",
    )(slab_order, me, queries, d_out, gathered)

    owned = lax.all_to_all(
        terms.reshape(devices, cache_rows, 2 * width), axes, split_axis=0, concat_axis=0, tiled=True
    )
    key_grads, value_grads = pl.pallas_call(
        functools.partial(combine_kernel, kvh),
        out_shape=(
            jax.ShapeDtypeStruct(keys.shape, jnp.bfloat16),
            jax.ShapeDtypeStruct(values.shape, jnp.bfloat16),
        ),
        in_specs=[vmem],
        out_specs=(vmem, vmem),
        compiler_params=params,
        name="combine",
    )(owned)
    return (query_grads, key_grads, value_grads)


def solution(mesh):
    placed = (
        P("seq", "kvh"),
        P(("seq", "kvh"), None),
        P(("seq", "kvh"), None),
        P("seq", "kvh"),
        P(),
    )
    return jax.shard_map(
        per_device,
        mesh=mesh,
        in_specs=placed,
        out_specs=(P("seq", "kvh"), P(("seq", "kvh"), None), P(("seq", "kvh"), None)),
        check_vma=False,
    )
```

time: 191 us -> 51.5 us (0.27)
  waiting for transfers between devices: 71.1 us -> 15.5 us
  blocking collectives: 62.5 us -> 18.9 us
  between operations: 19.1 us -> 0.65 us
  local copies, waits for them, and re-layouts: 9.27 us -> 0.8 us
  Pallas kernels: 0 us -> 7.97 us
  other arithmetic: 7.48 us -> 0 us
  starting transfers between devices: 14.1 us -> 7.3 us
  matrix products: 6.5 us -> 0 us
    reduce_scatter x1 -> x0, waiting for transfers between devices: 64.9 us -> none  [per_device(): lax.psum_scatter(device_terms, 'seq', scatter_dimension=0, tiled=True)]
    all_gather x2 -> x0, blocking collectives: 62.5 us -> none  [the longest x1 31.8 us: per_device(): lax.all_gather(head_values, 'seq', axis=0, tiled=True)]
    all_to_all x0 -> x1, blocking collectives: none -> 18.9 us  [per_device(): lax.all_to_all(terms.reshape(devices, cache_rows, 2 * width), axes, split...]
    all_to_all x4 -> x1, waiting for transfers between devices: 6.2 us -> 15.5 us  [per_device(): lax.all_to_all(packed, axes, split_axis=0, concat_axis=0, tiled=True)]
    pallas_call x0 -> x3, Pallas kernels: none -> 7.97 us  [the longest x1 4.59 us: per_device(): pl.pallas_call(functools.partial(attend_kernel, group), out_shape=(jax.Sh...]
    all_to_all x4 -> x1, starting transfers between devices: 14 us -> 7.3 us  [per_device(): lax.all_to_all(packed, axes, split_axis=0, concat_axis=0, tiled=True)]
    dot_general x21 -> x0, matrix products: 6.5 us -> none  [the longest x6 1.97 us: block_scores(): jnp.einsum('uiyh,mih->iyum', query_part, key_block_slice, preferred_eleme...]
    all_to_all x4 -> x0, local copies, waits for them, and re-layouts: 2.48 us -> none  [the longest x1 0.62 us: per_device(): lax.all_to_all(keys, 'kvh', split_axis=1, concat_axis=0, tiled=True)]
  transfers between devices with their start and end apart: 5 -> 1, of which waited for: 3 -> 1; matrix products, arithmetic and copies ran while one was open for 3% -> 0% of each run, Pallas kernels for 0% -> 0%
where the time goes in v1:
time: 51.5 us; the launch traced here: 51.1 us
  blocking collectives  18.9 us (37%)
  waiting for transfers between devices  15.5 us (30%)
  Pallas kernels  7.97 us (15%)
  starting transfers between devices  7.3 us (14%)
  local copies, waits for them, and re-layouts  0.8 us (2%)
  between operations  0.65 us (1%)
    all_to_all x1, blocking collectives, per_device(): lax.all_to_all(terms.reshape(devices, cache_rows, 2 * width), axes, split...  18.9 us
    all_to_all x1, waiting for transfers between devices, per_device(): lax.all_to_all(packed, axes, split_axis=0, concat_axis=0, tiled=True)  15.5 us
    all_to_all x1, starting transfers between devices, per_device(): lax.all_to_all(packed, axes, split_axis=0, concat_axis=0, tiled=True)  7.3 us
    pallas_call x1, Pallas kernels, per_device(): pl.pallas_call(functools.partial(attend_kernel, group), out_shape=(jax.Sh...  4.59 us
    pallas_call x1, Pallas kernels, per_device(): pl.pallas_call(functools.partial(combine_kernel, kvh), out_shape=(jax.Sha...  1.73 us
    pallas_call x1, Pallas kernels, per_device(): pl.pallas_call(functools.partial(pack_kernel, kvh), out_shape=jax.ShapeDt...  1.64 us
  transfers between devices with their start and end apart: 1, of which 1 were waited for; matrix products, arithmetic and copies ran while one was open for 0% of the time, Pallas kernels for 0%

profile of v1, /device:TPU:0, one launch (start us, length us, event | category | flops | bytes accessed | tf_op | source)
XLA Modules:
  0.0 51.1 jit_solution(9456450586106286373)
XLA Ops:
  0.6 1.6 %pack.1 = bf16[32,32,256]{2,1,0:T(8,128)(2,1)} custom-call(bf16[32,512]{1,0:T(8,128)(2,1)} %keys_ref.1, bf16[32,512]{1,0:T(8,128)(2,1)} %values_ref.1), custom_call_target="tpu_custom_call" | custom-call | tf_op jit(solution)/shard_map/pack/pallas_call | solution.py:215
  2.3 7.3 %all-to-all-start = ((bf16[32,32,256]{2,1,0:T(8,128)(2,1)}), bf16[32,32,256]{2,1,0:T(8,128)(2,1)S(1)}, u32[]{:S(2)}, u32[]{:S(2)}) async-start(bf16[32,32,256]{2,1,0:T(8,128)(2,1)} %pack.1), calls=%async_computation | async-start | bytes 1048576 | tf_op jit(solution)/shard_map/all_to_all | solution.py:223
  9.6 15.5 %all-to-all-done = bf16[32,32,256]{2,1,0:T(8,128)(2,1)S(1)} async-done(((bf16[32,32,256]{2,1,0:T(8,128)(2,1)}), bf16[32,32,256]{2,1,0:T(8,128)(2,1)S(1)}, u32[]{:S(2)}, u32[]{:S(2)}) %all-to-all-start) | async-done | bytes 524320 | tf_op jit(solution)/shard_map/all_to_all | solution.py:223
  25.1 0.0 copy-start
  25.1 0.8 %copy-done = bf16[32,32,256]{2,1,0:T(8,128)(2,1)} copy-done((bf16[32,32,256]{2,1,0:T(8,128)(2,1)}, bf16[32,32,256]{2,1,0:T(8,128)(2,1)S(1)}, u32[]{:S(2)}) %copy-start) | copy-done | bytes 524312
  25.9 4.6 %attend.1 = (bf16[128,640]{1,0:T(8,128)(2,1)}, bf16[1024,256]{1,0:T(8,128)(2,1)}) custom-call(s32[16]{0:T(128)} %order_ref.1, s32[1]{0:T(128)} %bitcast.me_ref, bf16[128,640]{1,0:T(8,128)(2,1)} %q_ref.1, bf16[128,640]{1,0:T(8,128)(2,1)} %do_ref.1, bf16[1024,256]{1,0:T(8,128)(2,1)} %bitcast.3), custom_call_target="tpu_custom_call" | custom-call | tf_op jit(solution)/shard_map/attend/pallas_call | solution.py:227
  30.5 18.9 %all_to_all.10.terms_ref = bf16[32,32,256]{2,1,0:T(8,128)(2,1)} all-to-all(bf16[32,32,256]{2,1,0:T(8,128)(2,1)} %bitcast.4), channel_id=1, replica_groups=mesh['seq'=8,'kvh'=4] {'seq','kvh'}, dimensions={0} | all-to-all | bytes 1048576 | tf_op jit(solution)/shard_map/all_to_all | solution.py:252
  49.4 1.7 %combine.1 = (bf16[32,512]{1,0:T(8,128)(2,1)}, bf16[32,512]{1,0:T(8,128)(2,1)}) custom-call(bf16[32,32,256]{2,1,0:T(8,128)(2,1)} %all_to_all.10.terms_ref), custom_call_target="tpu_custom_call" | custom-call | tf_op jit(solution)/shard_map/combine/pallas_call | solution.py:255
Async XLA Ops:
  2.3 22.9 %all-to-all-start = ((bf16[32,32,256]{2,1,0:T(8,128)(2,1)}), bf16[32,32,256]{2,1,0:T(8,128)(2,1)S(1)}, u32[]{:S(2)}, u32[]{:S(2)}) async-start(bf16[32,32,256]{2,1,0:T(8,128)(2,1)} %pack.1), calls=%async_computation | async-start | bytes 1048576 | tf_op jit(solution)/shard_map/all_to_all | solution.py:223
  25.1 0.8 %copy-start = (bf16[32,32,256]{2,1,0:T(8,128)(2,1)}, bf16[32,32,256]{2,1,0:T(8,128)(2,1)S(1)}, u32[]{:S(2)}) copy-start(bf16[32,32,256]{2,1,0:T(8,128)(2,1)S(1)} %all-to-all-done) | copy-start | bytes 1572868

commit v2 on v1

v2 whole, which is shorter than its diff:
```python
import functools
import math

import jax
import jax.numpy as jnp
from jax import lax
from jax.experimental import pallas as pl
from jax.experimental.pallas import tpu as pltpu
from jax.sharding import Mesh
from jax.sharding import PartitionSpec as P

HEADS = 20
KV_HEADS = 4
HEAD = 128
GROUP = HEADS // KV_HEADS
SCALE = HEAD ** (-0.5)
EXPONENT_SCALE = SCALE * math.log2(math.e)
LOWEST = -1e30
VMEM_LIMIT = 56 * 1024 * 1024
ROWS_DOT_ROWS = (((1,), (1,)), ((), ()))
COLS_DOT_COLS = (((0,), (0,)), ((), ()))


def repeat(count, body):
    if count <= 8:
        for step in range(count):
            body(step)
    else:
        pl.loop(0, count)(body)


def at_rows(start, size):
    return pl.ds(pl.multiple_of(start, size), size)


def pair_of(order_ref, index):
    first, second = order_ref[2 * index], order_ref[2 * index + 1]
    return jnp.minimum(first, second), jnp.where(first < second, 0, 1)


class Work:
    def __init__(self, order_ref, me_ref, kv_ref, ks_ref, q_refs, d_refs, qs_ref, ds_ref):
        self.slab_rows = q_refs[0].shape[0] // 2
        self.outer = kv_ref.shape[0] // (2 * self.slab_rows)
        self.order_ref = order_ref
        me = me_ref[0]
        self.at, self.side = me // 2, me % 2
        self.low = [pair_of(order_ref, me), pair_of(order_ref, me + 1 - 2 * self.side)]
        self.half_rows = self.outer * self.slab_rows
        self.chunk = math.gcd(256, self.half_rows)
        rows = self.slab_rows

        def stack_keys(j):
            _, place = pair_of(order_ref, 2 * j + self.side)
            for half in range(2):
                here = place if half == 0 else 1 - place
                ks_ref[half, at_rows(j * rows, rows), :] = kv_ref[at_rows((2 * j + here) * rows, rows), :]

        repeat(self.outer, stack_keys)
        for owner in range(2):
            for half in range(2):
                place = self.low[owner][1]
                source = at_rows((place if half == 0 else 1 - place) * rows, rows)
                for h in range(GROUP):
                    cols = slice(h * HEAD, (h + 1) * HEAD)
                    qs_ref[owner, half, h * rows : (h + 1) * rows, :] = q_refs[owner][source, cols]
                    ds_ref[owner, half, h * rows : (h + 1) * rows, :] = d_refs[owner][source, cols]

    def blocks(self, body):
        rows = self.slab_rows
        for owner in range(2):
            repeat(
                self.half_rows // self.chunk,
                lambda n: body(owner, 1, 0, n * self.chunk, self.chunk, n * self.chunk, None),
            )

            def pick(j):
                low, _ = pair_of(self.order_ref, 2 * j + self.side)
                half = jnp.where(self.low[owner][0] >= low, 0, 1)
                mask = None if owner == 1 else j == self.at
                body(owner, half, half, j * rows, rows, self.half_rows + j * rows, mask)

            repeat(self.outer, pick)
            if owner == 0:
                body(owner, 1, 1, self.at * rows, rows, 2 * self.half_rows, True)

    def scores(self, ks_ref, qs_ref, owner, q_half, k_half, first, size, mask):
        scores = lax.dot_general(
            ks_ref[k_half, at_rows(first, size), :HEAD],
            qs_ref[owner, q_half],
            ROWS_DOT_ROWS,
            preferred_element_type=jnp.float32,
        )
        if mask is not None:
            key = lax.broadcasted_iota(jnp.int32, scores.shape, 0)
            query = lax.rem(lax.broadcasted_iota(jnp.int32, (1, scores.shape[1]), 1), self.slab_rows)
            if mask is not True:
                query = query + jnp.where(mask, 0, self.slab_rows)
            scores = jnp.where(key <= query, scores, LOWEST)
        return scores

    def grads(self, ks_ref, ds_ref, owner, q_half, k_half, first, size):
        return lax.dot_general(
            ks_ref[k_half, at_rows(first, size), HEAD:],
            ds_ref[owner, q_half],
            ROWS_DOT_ROWS,
            preferred_element_type=jnp.float32,
        )


def pack_kernel(kvh, keys_ref, values_ref, out_ref):
    for k in range(kvh):
        cols = slice(k * HEAD, (k + 1) * HEAD)
        key_part = keys_ref[:, cols]
        value_part = values_ref[:, cols]
        for s in range(out_ref.shape[0] // kvh):
            out_ref[s * kvh + k, :, :HEAD] = key_part
            out_ref[s * kvh + k, :, HEAD:] = value_part


def stats_kernel(
    order_ref, me_ref, q_ref, do_ref, q2_ref, do2_ref, kv_ref, out_ref,
    ks_ref, qs_ref, ds_ref, s_ref, m_ref, l_ref, d_ref,
):
    work = Work(order_ref, me_ref, kv_ref, ks_ref, (q_ref, q2_ref), (do_ref, do2_ref), qs_ref, ds_ref)
    m_ref[...] = jnp.full(m_ref.shape, LOWEST, jnp.float32)
    l_ref[...] = jnp.zeros(l_ref.shape, jnp.float32)
    d_ref[...] = jnp.zeros(d_ref.shape, jnp.float32)

    def maximum(owner, q_half, k_half, first, size, place, mask):
        scores = work.scores(ks_ref, qs_ref, owner, q_half, k_half, first, size, mask)
        s_ref[owner, at_rows(place, size), :] = scores
        m_ref[owner, q_half] = jnp.maximum(
            m_ref[owner, q_half], jnp.max(scores, axis=0, keepdims=True)
        )

    work.blocks(maximum)

    def sums(owner, q_half, k_half, first, size, place, mask):
        grads = work.grads(ks_ref, ds_ref, owner, q_half, k_half, first, size)
        scores = s_ref[owner, at_rows(place, size), :]
        expon = jnp.exp2((scores - m_ref[owner, q_half]) * EXPONENT_SCALE)
        l_ref[owner, q_half] = l_ref[owner, q_half] + jnp.sum(expon, axis=0, keepdims=True)
        d_ref[owner, q_half] = d_ref[owner, q_half] + jnp.sum(expon * grads, axis=0, keepdims=True)

    work.blocks(sums)
    for owner in range(2):
        for half in range(2):
            base = (2 * owner + half) * 3
            out_ref[base : base + 1, :] = m_ref[owner, half]
            out_ref[base + 1 : base + 2, :] = l_ref[owner, half]
            out_ref[base + 2 : base + 3, :] = d_ref[owner, half]


def grads_kernel(
    order_ref, me_ref, q_ref, do_ref, q2_ref, do2_ref, kv_ref, mine_ref, theirs_ref,
    dq_ref, dq2_ref, dkv_ref,
    ks_ref, qs_ref, ds_ref, m_ref, d_ref, acc_ref, dq_acc_ref,
):
    work = Work(order_ref, me_ref, kv_ref, ks_ref, (q_ref, q2_ref), (do_ref, do2_ref), qs_ref, ds_ref)
    acc_ref[...] = jnp.zeros(acc_ref.shape, jnp.float32)
    dq_acc_ref[...] = jnp.zeros(dq_acc_ref.shape, jnp.float32)
    for owner in range(2):
        for half in range(2):
            base = (2 * owner + half) * 3
            base2 = (2 * (1 - owner) + half) * 3
            m1, m2 = mine_ref[base : base + 1, :], theirs_ref[base2 : base2 + 1, :]
            top = jnp.maximum(m1, m2)
            w1 = jnp.exp2((m1 - top) * EXPONENT_SCALE)
            w2 = jnp.exp2((m2 - top) * EXPONENT_SCALE)
            total = w1 * mine_ref[base + 1 : base + 2, :] + w2 * theirs_ref[base2 + 1 : base2 + 2, :]
            delta = w1 * mine_ref[base + 2 : base + 3, :] + w2 * theirs_ref[base2 + 2 : base2 + 3, :]
            m_ref[owner, half] = top * EXPONENT_SCALE + jnp.log2(total)
            d_ref[owner, half] = delta / total

    def gradients(owner, q_half, k_half, first, size, place, mask):
        scores = work.scores(ks_ref, qs_ref, owner, q_half, k_half, first, size, mask)
        grads = work.grads(ks_ref, ds_ref, owner, q_half, k_half, first, size)
        probs = jnp.exp2(scores * EXPONENT_SCALE - m_ref[owner, q_half])
        score_grads = (probs * (grads - d_ref[owner, q_half])).astype(jnp.bfloat16)
        rows = at_rows(first, size)
        acc_ref[k_half, rows, HEAD:] = acc_ref[k_half, rows, HEAD:] + jnp.dot(
            probs.astype(jnp.bfloat16), ds_ref[owner, q_half], preferred_element_type=jnp.float32
        )
        acc_ref[k_half, rows, :HEAD] = acc_ref[k_half, rows, :HEAD] + jnp.dot(
            score_grads, qs_ref[owner, q_half], preferred_element_type=jnp.float32
        )
        dq_acc_ref[owner, q_half] = dq_acc_ref[owner, q_half] + lax.dot_general(
            ks_ref[k_half, rows, :HEAD], score_grads, COLS_DOT_COLS, preferred_element_type=jnp.float32
        )

    work.blocks(gradients)
    rows = work.slab_rows
    for owner, target in ((0, dq_ref), (1, dq2_ref)):
        for half in range(2):
            place = work.low[owner][1]
            source = at_rows((place if half == 0 else 1 - place) * rows, rows)
            grads = (jnp.transpose(dq_acc_ref[owner, half]) * SCALE).astype(target.dtype)
            for h in range(GROUP):
                target[source, h * HEAD : (h + 1) * HEAD] = grads[h * rows : (h + 1) * rows, :]

    def write_terms(j):
        _, place = pair_of(order_ref, 2 * j + work.side)
        for half in range(2):
            here = place if half == 0 else 1 - place
            target = at_rows((2 * j + here) * rows, rows)
            source = at_rows(j * rows, rows)
            dkv_ref[target, :HEAD] = (acc_ref[half, source, :HEAD] * SCALE).astype(jnp.bfloat16)
            dkv_ref[target, HEAD:] = acc_ref[half, source, HEAD:].astype(jnp.bfloat16)

    repeat(work.outer, write_terms)


def combine_kernel(kvh, terms_ref, key_ref, value_ref):
    seq = terms_ref.shape[0] // kvh
    for k in range(kvh):
        total = terms_ref[k].astype(jnp.float32)
        for s in range(1, seq):
            total = total + terms_ref[s * kvh + k].astype(jnp.float32)
        total = total.astype(jnp.bfloat16)
        key_ref[:, k * HEAD : (k + 1) * HEAD] = total[:, :HEAD]
        value_ref[:, k * HEAD : (k + 1) * HEAD] = total[:, HEAD:]


def per_device(queries, keys, values, d_out, slab_order):
    axes = ("outer", "kvh")
    kvh = lax.axis_size("kvh")
    outer = lax.axis_size("outer")
    peers = outer * kvh
    local_rows, query_width = queries.shape
    cache_rows = keys.shape[0]
    slab_rows = local_rows // 2
    column_rows = outer * local_rows
    half_rows = outer * slab_rows
    columns = GROUP * slab_rows
    swap = [(0, 1), (1, 0)]
    params = pltpu.CompilerParams(vmem_limit_bytes=VMEM_LIMIT)
    vmem = pl.BlockSpec(memory_space=pltpu.VMEM)
    smem = pl.BlockSpec(memory_space=pltpu.SMEM)
    shape = jax.ShapeDtypeStruct

    queries2 = lax.ppermute(queries, "pair", swap)
    d_out2 = lax.ppermute(d_out, "pair", swap)
    packed = pl.pallas_call(
        functools.partial(pack_kernel, kvh),
        out_shape=shape((peers, cache_rows, 2 * HEAD), keys.dtype),
        in_specs=[vmem, vmem],
        out_specs=vmem,
        compiler_params=params,
        name="pack",
    )(keys, values)
    gathered = lax.all_to_all(packed, axes, split_axis=0, concat_axis=0, tiled=True)
    gathered = gathered.reshape(column_rows, 2 * HEAD)

    me = (lax.axis_index("outer") * 2 + lax.axis_index("pair")).astype(jnp.int32).reshape(1)
    stacks = [
        pltpu.VMEM((2, half_rows, 2 * HEAD), jnp.bfloat16),
        pltpu.VMEM((2, 2, columns, HEAD), jnp.bfloat16),
        pltpu.VMEM((2, 2, columns, HEAD), jnp.bfloat16),
    ]
    row_stat = pltpu.VMEM((2, 2, 1, columns), jnp.float32)
    operands = (slab_order, me, queries, d_out, queries2, d_out2, gathered)
    stats = pl.pallas_call(
        stats_kernel,
        out_shape=shape((12, columns), jnp.float32),
        in_specs=[smem, smem] + [vmem] * 5,
        out_specs=vmem,
        scratch_shapes=stacks
        + [pltpu.VMEM((2, 2 * half_rows + slab_rows, columns), jnp.float32), row_stat, row_stat, row_stat],
        compiler_params=params,
        name="stats",
    )(*operands)
    stats2 = lax.ppermute(stats, "pair", swap)
    own_grads, other_grads, terms = pl.pallas_call(
        grads_kernel,
        out_shape=(
            shape(queries.shape, jnp.float32),
            shape(queries.shape, jnp.bfloat16),
            shape((column_rows, 2 * HEAD), jnp.bfloat16),
        ),
        in_specs=[smem, smem] + [vmem] * 7,
        out_specs=(vmem, vmem, vmem),
        scratch_shapes=stacks
        + [
            row_stat,
            row_stat,
            pltpu.VMEM((2, half_rows, 2 * HEAD), jnp.float32),
            pltpu.VMEM((2, 2, HEAD, columns), jnp.float32),
        ],
        compiler_params=params,
        name="grads",
    )(*operands, stats, stats2)
    received_grads = lax.ppermute(other_grads, "pair", swap)
    owned = lax.all_to_all(
        terms.reshape(peers, cache_rows, 2 * HEAD), axes, split_axis=0, concat_axis=0, tiled=True
    )
    query_grads = (own_grads + received_grads.astype(jnp.float32)).astype(jnp.bfloat16)
    key_grads, value_grads = pl.pallas_call(
        functools.partial(combine_kernel, kvh),
        out_shape=(shape(keys.shape, jnp.bfloat16), shape(values.shape, jnp.bfloat16)),
        in_specs=[vmem],
        out_specs=(vmem, vmem),
        compiler_params=params,
        name="combine",
    )(owned)
    return (query_grads, key_grads, value_grads)


def solution(mesh):
    kvh = mesh.shape["kvh"]
    pairs = mesh.shape["seq"] // 2
    paired = Mesh(mesh.devices.reshape(pairs, 2, kvh), ("outer", "pair", "kvh"))
    seq = ("outer", "pair")
    cache = P(("outer", "pair", "kvh"), None)
    placed = (P(seq, "kvh"), cache, cache, P(seq, "kvh"), P())
    return jax.shard_map(
        per_device,
        mesh=paired,
        in_specs=placed,
        out_specs=(P(seq, "kvh"), cache, cache),
        check_vma=False,
    )
```

time: 51.5 us -> 51.7 us (level)
  blocking collectives: 18.9 us -> 0 us
  starting transfers between devices: 7.3 us -> 18.5 us
  Pallas kernels: 7.97 us -> 11 us
  waiting for transfers between devices: 15.5 us -> 18.3 us
  local copies, waits for them, and re-layouts: 0.8 us -> 2.09 us
  other arithmetic: 0 us -> 0.71 us
    all_to_all x1 -> x0, blocking collectives: 18.9 us -> none  [per_device(): lax.all_to_all(terms.reshape(devices, cache_rows, 2 * width), axes, split...]
    ppermute x0 -> x4, waiting for transfers between devices: none -> 15.6 us  [the longest x1 5.02 us: per_device(): received_grads = lax.ppermute(other_grads, 'pair', swap)]
    all_to_all x1, waiting for transfers between devices: 15.5 us -> 0.01 us  [per_device(): lax.all_to_all(packed, axes, split_axis=0, concat_axis=0, tiled=True)]
    all_to_all x0 -> x1, starting transfers between devices: none -> 5.86 us  [per_device(): lax.all_to_all(terms.reshape(peers, cache_rows, 2 * HEAD), axes, split_ax...]
    ppermute x0 -> x4, starting transfers between devices: none -> 5.18 us  [the longest x1 1.58 us: per_device(): queries2 = lax.ppermute(queries, 'pair', swap)]
    pallas_call x3 -> x4, Pallas kernels: 7.97 us -> 11 us  [the longest x1 4.96 us: per_device(): pl.pallas_call(grads_kernel, out_shape=(shape(queries.shape, jnp.float32)...]
    all_to_all x0 -> x1, waiting for transfers between devices: none -> 2.73 us  [per_device(): lax.all_to_all(terms.reshape(peers, cache_rows, 2 * HEAD), axes, split_ax...]
    unnamed x2 -> x18, local copies, waits for them, and re-layouts: 0.8 us -> 2.09 us
  transfers between devices with their start and end apart: 1 -> 6, of which waited for: 1 -> 5; matrix products, arithmetic and copies ran while one was open for 0% -> 1% of each run, Pallas kernels for 0% -> 0%
where the time goes in v2:
time: 51.7 us; the launch traced here: 51.3 us
  starting transfers between devices  18.5 us (36%)
  waiting for transfers between devices  18.3 us (35%)
  Pallas kernels  11 us (21%)
  local copies, waits for them, and re-layouts  2.09 us (4%)
  other arithmetic  0.71 us (1%)
  between operations  0.68 us (1%)
    all_to_all x1, starting transfers between devices, per_device(): lax.all_to_all(packed, axes, split_axis=0, concat_axis=0, tiled=True)  7.49 us
    all_to_all x1, starting transfers between devices, per_device(): lax.all_to_all(terms.reshape(peers, cache_rows, 2 * HEAD), axes, split_ax...  5.86 us
    ppermute x1, waiting for transfers between devices, per_device(): received_grads = lax.ppermute(other_grads, 'pair', swap)  5.02 us
    ppermute x1, waiting for transfers between devices, per_device(): queries2 = lax.ppermute(queries, 'pair', swap)  4.98 us
    pallas_call x1, Pallas kernels, per_device(): pl.pallas_call(grads_kernel, out_shape=(shape(queries.shape, jnp.float32)...  4.96 us
    ppermute x1, waiting for transfers between devices, per_device(): d_out2 = lax.ppermute(d_out, 'pair', swap)  3.04 us
    pallas_call x1, Pallas kernels, per_device(): pl.pallas_call(stats_kernel, out_shape=shape((12, columns), jnp.float32),...  2.89 us
    all_to_all x1, waiting for transfers between devices, per_device(): lax.all_to_all(terms.reshape(peers, cache_rows, 2 * HEAD), axes, split_ax...  2.73 us
  transfers between devices with their start and end apart: 6, of which 5 were waited for; matrix products, arithmetic and copies ran while one was open for 1% of the time, Pallas kernels for 0%

profile of v2, /device:TPU:0, one launch (start us, length us, event | category | flops | bytes accessed | tf_op | source)
XLA Modules:
  0.0 51.3 jit_solution(11672798346862579372)
XLA Ops:
  0.6 1.5 %pack.1 = bf16[16,32,256]{2,1,0:T(8,128)(2,1)} custom-call(bf16[32,512]{1,0:T(8,128)(2,1)} %keys_ref.1, bf16[32,512]{1,0:T(8,128)(2,1)} %values_ref.1), custom_call_target="tpu_custom_call" | custom-call | tf_op jit(solution)/shard_map/pack/pallas_call | solution.py:244
  2.1 0.0 copy-start.2
  2.1 0.0 copy-start.3
  2.2 7.5 %all-to-all-start = ((bf16[16,32,256]{2,1,0:T(8,128)(2,1)}), bf16[16,32,256]{2,1,0:T(8,128)(2,1)S(1)}, u32[]{:S(2)}, u32[]{:S(2)}) async-start(bf16[16,32,256]{2,1,0:T(8,128)(2,1)} %pack.1), calls=%async_computation | async-start | bytes 524288 | tf_op jit(solution)/shard_map/all_to_all | solution.py:252
  9.6 0.0 copy-done.2
  9.7 1.6 %collective-permute-start = (bf16[128,640]{1,0:T(8,128)(2,1)S(1)}, bf16[128,640]{1,0:T(8,128)(2,1)S(1)}, u32[]{:S(2)}, u32[]{:S(2)}) collective-permute-start(bf16[128,640]{1,0:T(8,128)(2,1)S(1)} %copy-done.2), channel_id=1, source_target_pairs={{0,4},{4,0},{1,5},{5,1},{2,6},{6,2},{3,7},{7,3},{8,12},{12,8},{9,1... | collective-permute-start | bytes 491528 | tf_op jit(solution)/shard_map/ppermute | solution.py:242
  11.2 0.0 copy-done.3
  11.2 0.5 collective-permute-start.1
  11.8 5.0 %collective-permute-done.q2_ref = bf16[128,640]{1,0:T(8,128)(2,1)S(1)} collective-permute-done((bf16[128,640]{1,0:T(8,128)(2,1)S(1)}, bf16[128,640]{1,0:T(8,128)(2,1)S(1)}, u32[]{:S(2)}, u32[]{:S(2)}) %collective-permute-start) | collective-permute-done | bytes 163872 | tf_op jit(solution)/shard_map/ppermute | solution.py:242
  16.7 0.0 copy-start.4
  16.7 3.0 %collective-permute-done.1.do2_ref = bf16[128,640]{1,0:T(8,128)(2,1)S(1)} collective-permute-done((bf16[128,640]{1,0:T(8,128)(2,1)S(1)}, bf16[128,640]{1,0:T(8,128)(2,1)S(1)}, u32[]{:S(2)}, u32[]{:S(2)}) %collective-permute-start.1) | collective-permute-done | bytes 163872 | tf_op jit(solution)/shard_map/ppermute | solution.py:243
  19.8 0.0 copy-start.5
  19.8 0.0 all-to-all-done
  19.8 0.0 copy-start
  19.8 0.0 copy-done.4
  19.8 0.7 %copy-done.5 = bf16[128,640]{1,0:T(8,128)(2,1)} copy-done((bf16[128,640]{1,0:T(8,128)(2,1)}, bf16[128,640]{1,0:T(8,128)(2,1)S(1)}, u32[]{:S(2)}) %copy-start.5) | copy-done | bytes 163864
  20.4 0.1 copy-done
  20.5 2.9 %stats.1.mine_ref = f32[12,320]{1,0:T(8,128)} custom-call(s32[16]{0:T(128)} %order_ref.3, s32[1]{0:T(128)} %bitcast.me_ref, bf16[128,640]{1,0:T(8,128)(2,1)} %q_ref.3, bf16[128,640]{1,0:T(8,128)(2,1)} %do_ref.3, bf16[128,640]{1,0:T(8,128)(2,1)} %copy-done.4, bf16[128,640]{1,0:T(8,128)(2,1)} %copy-done.5, bf16[512,256]{1,0:T(8,128)(2,1)} %bitcast.3), custom_call_target="tpu_custom_call" | custom-call | tf_op jit(solution)/shard_map/stats/pallas_call | solution.py:263
  23.4 1.5 %collective-permute-start.2 = (f32[12,320]{1,0:T(8,128)}, f32[12,320]{1,0:T(8,128)S(1)}, u32[]{:S(2)}, u32[]{:S(2)}) collective-permute-start(f32[12,320]{1,0:T(8,128)} %stats.1.mine_ref), channel_id=1, source_target_pairs={{0,4},{4,0},{1,5},{5,1},{2,6},{6,2},{3,7},{7,3},{8,12},{12,8},{9,1... | collective-permute-start | bytes 46088 | tf_op jit(solution)/shard_map/ppermute | solution.py:273
  24.9 2.5 %collective-permute-done.2.theirs_ref = f32[12,320]{1,0:T(8,128)S(1)} collective-permute-done((f32[12,320]{1,0:T(8,128)}, f32[12,320]{1,0:T(8,128)S(1)}, u32[]{:S(2)}, u32[]{:S(2)}) %collective-permute-start.2) | collective-permute-done | bytes 15392 | tf_op jit(solution)/shard_map/ppermute | solution.py:273
  27.5 0.0 copy-start.7
  27.5 0.6 %copy-done.7 = f32[12,320]{1,0:T(8,128)} copy-done((f32[12,320]{1,0:T(8,128)}, f32[12,320]{1,0:T(8,128)S(1)}, u32[]{:S(2)}) %copy-start.7) | copy-done | bytes 15384
  28.1 5.0 %grads.1 = (f32[128,640]{1,0:T(8,128)}, bf16[128,640]{1,0:T(8,128)(2,1)}, bf16[512,256]{1,0:T(8,128)(2,1)}) custom-call(s32[16]{0:T(128)} %order_ref.3, s32[1]{0:T(128)} %bitcast.me_ref, bf16[128,640]{1,0:T(8,128)(2,1)} %q_ref.3, bf16[128,640]{1,0:T(8,128)(2,1)} %do_ref.3, bf16[128,640]{1,0:T(8,128)(2,1)} %copy-done.4, bf16[128,640]{1,0:T(8,128)(2,1)} %copy-done.5, ...), custom_call_target="tpu_custom_call" | custom-call | tf_op jit(solution)/shard_map/grads/pallas_call | solution.py:274
  33.0 0.0 copy-start.6
  33.0 0.0 copy-start.8
  33.0 5.9 %all-to-all-start.1 = ((bf16[16,32,256]{2,1,0:T(8,128)(2,1)}), bf16[16,32,256]{2,1,0:T(8,128)(2,1)S(1)}, u32[]{:S(2)}, u32[]{:S(2)}) async-start(bf16[16,32,256]{2,1,0:T(8,128)(2,1)} %bitcast.5), calls=%async_computation.1 | async-start | bytes 524288 | tf_op jit(solution)/shard_map/all_to_all | solution.py:294
  38.9 0.0 copy-done.8
  38.9 1.6 %collective-permute-start.3 = (bf16[128,640]{1,0:T(8,128)(2,1)S(1)}, bf16[128,640]{1,0:T(8,128)(2,1)S(1)}, u32[]{:S(2)}, u32[]{:S(2)}) collective-permute-start(bf16[128,640]{1,0:T(8,128)(2,1)S(1)} %copy-done.8), channel_id=1, source_target_pairs={{0,4},{4,0},{1,5},{5,1},{2,6},{6,2},{3,7},{7,3},{8,12},{12,8},{9,1... | collective-permute-start | bytes 491528 | tf_op jit(solution)/shard_map/ppermute | solution.py:293
  40.5 5.0 %collective-permute-done.3 = bf16[128,640]{1,0:T(8,128)(2,1)S(1)} collective-permute-done((bf16[128,640]{1,0:T(8,128)(2,1)S(1)}, bf16[128,640]{1,0:T(8,128)(2,1)S(1)}, u32[]{:S(2)}, u32[]{:S(2)}) %collective-permute-start.3) | collective-permute-done | bytes 163872 | tf_op jit(solution)/shard_map/ppermute | solution.py:293
  45.5 0.0 copy-done.6
  45.5 0.7 %add_convert_fusion = bf16[128,640]{1,0:T(8,128)(2,1)} fusion(f32[128,640]{1,0:T(8,128)S(1)} %copy-done.6, bf16[128,640]{1,0:T(8,128)(2,1)S(1)} %collective-permute-done.3), kind=kLoop, calls=%fused_computation | loop fusion | flops 245760 | bytes 655360 | tf_op jit(solution)/shard_map/convert_element_type | solution.py:297
  46.2 2.7 %all-to-all-done.1.terms_ref = bf16[16,32,256]{2,1,0:T(8,128)(2,1)S(1)} async-done(((bf16[16,32,256]{2,1,0:T(8,128)(2,1)}), bf16[16,32,256]{2,1,0:T(8,128)(2,1)S(1)}, u32[]{:S(2)}, u32[]{:S(2)}) %all-to-all-start.1) | async-done | bytes 262176 | tf_op jit(solution)/shard_map/all_to_all | solution.py:294
  48.9 0.0 copy-start.1
  48.9 0.7 %copy-done.1 = bf16[16,32,256]{2,1,0:T(8,128)(2,1)} copy-done((bf16[16,32,256]{2,1,0:T(8,128)(2,1)}, bf16[16,32,256]{2,1,0:T(8,128)(2,1)S(1)}, u32[]{:S(2)}) %copy-start.1) | copy-done | bytes 262168
  49.7 1.6 %combine.1 = (bf16[32,512]{1,0:T(8,128)(2,1)}, bf16[32,512]{1,0:T(8,128)(2,1)}) custom-call(bf16[16,32,256]{2,1,0:T(8,128)(2,1)} %copy-done.1), custom_call_target="tpu_custom_call" | custom-call | tf_op jit(solution)/shard_map/combine/pallas_call | solution.py:298
Async XLA Ops:
  2.1 7.5 %copy-start.2 = (bf16[128,640]{1,0:T(8,128)(2,1)S(1)}, bf16[128,640]{1,0:T(8,128)(2,1)}, u32[]{:S(2)}) copy-start(bf16[128,640]{1,0:T(8,128)(2,1)} %q_ref.3) | copy-start | bytes 491524
  2.1 9.1 %copy-start.3 = (bf16[128,640]{1,0:T(8,128)(2,1)S(1)}, bf16[128,640]{1,0:T(8,128)(2,1)}, u32[]{:S(2)}) copy-start(bf16[128,640]{1,0:T(8,128)(2,1)} %do_ref.3) | copy-start | bytes 491524
  2.2 17.6 %all-to-all-start = ((bf16[16,32,256]{2,1,0:T(8,128)(2,1)}), bf16[16,32,256]{2,1,0:T(8,128)(2,1)S(1)}, u32[]{:S(2)}, u32[]{:S(2)}) async-start(bf16[16,32,256]{2,1,0:T(8,128)(2,1)} %pack.1), calls=%async_computation | async-start | bytes 524288 | tf_op jit(solution)/shard_map/all_to_all | solution.py:252
  9.7 7.1 %collective-permute-start = (bf16[128,640]{1,0:T(8,128)(2,1)S(1)}, bf16[128,640]{1,0:T(8,128)(2,1)S(1)}, u32[]{:S(2)}, u32[]{:S(2)}) collective-permute-start(bf16[128,640]{1,0:T(8,128)(2,1)S(1)} %copy-done.2), channel_id=1, source_target_pairs={{0,4},{4,0},{1,5},{5,1},{2,6},{6,2},{3,7},{7,3},{8,12},{12,8},{9,1... | collective-permute-start | bytes 491528 | tf_op jit(solution)/shard_map/ppermute | solution.py:242
  11.2 8.5 %collective-permute-start.1 = (bf16[128,640]{1,0:T(8,128)(2,1)S(1)}, bf16[128,640]{1,0:T(8,128)(2,1)S(1)}, u32[]{:S(2)}, u32[]{:S(2)}) collective-permute-start(bf16[128,640]{1,0:T(8,128)(2,1)S(1)} %copy-done.3), channel_id=1, source_target_pairs={{0,4},{4,0},{1,5},{5,1},{2,6},{6,2},{3,7},{7,3},{8,12},{12,8},{9,1... | collective-permute-start | bytes 491528 | tf_op jit(solution)/shard_map/ppermute | solution.py:243
  16.7 3.0 %copy-start.4 = (bf16[128,640]{1,0:T(8,128)(2,1)}, bf16[128,640]{1,0:T(8,128)(2,1)S(1)}, u32[]{:S(2)}) copy-start(bf16[128,640]{1,0:T(8,128)(2,1)S(1)} %collective-permute-done.q2_ref) | copy-start | bytes 491524
  19.8 0.7 %copy-start.5 = (bf16[128,640]{1,0:T(8,128)(2,1)}, bf16[128,640]{1,0:T(8,128)(2,1)S(1)}, u32[]{:S(2)}) copy-start(bf16[128,640]{1,0:T(8,128)(2,1)S(1)} %collective-permute-done.1.do2_ref) | copy-start | bytes 491524
  19.8 0.8 %copy-start = (bf16[16,32,256]{2,1,0:T(8,128)(2,1)}, bf16[16,32,256]{2,1,0:T(8,128)(2,1)S(1)}, u32[]{:S(2)}) copy-start(bf16[16,32,256]{2,1,0:T(8,128)(2,1)S(1)} %all-to-all-done) | copy-start | bytes 786436
  23.4 4.0 %collective-permute-start.2 = (f32[12,320]{1,0:T(8,128)}, f32[12,320]{1,0:T(8,128)S(1)}, u32[]{:S(2)}, u32[]{:S(2)}) collective-permute-start(f32[12,320]{1,0:T(8,128)} %stats.1.mine_ref), channel_id=1, source_target_pairs={{0,4},{4,0},{1,5},{5,1},{2,6},{6,2},{3,7},{7,3},{8,12},{12,8},{9,1... | collective-permute-start | bytes 46088 | tf_op jit(solution)/shard_map/ppermute | solution.py:273
  27.5 0.6 %copy-start.7 = (f32[12,320]{1,0:T(8,128)}, f32[12,320]{1,0:T(8,128)S(1)}, u32[]{:S(2)}) copy-start(f32[12,320]{1,0:T(8,128)S(1)} %collective-permute-done.2.theirs_ref) | copy-start | bytes 46084
  33.0 12.5 %copy-start.6 = (f32[128,640]{1,0:T(8,128)S(1)}, f32[128,640]{1,0:T(8,128)}, u32[]{:S(2)}) copy-start(f32[128,640]{1,0:T(8,128)} %get-tuple-element.8) | copy-start | bytes 983044
  33.0 5.9 %copy-start.8 = (bf16[128,640]{1,0:T(8,128)(2,1)S(1)}, bf16[128,640]{1,0:T(8,128)(2,1)}, u32[]{:S(2)}) copy-start(bf16[128,640]{1,0:T(8,128)(2,1)} %get-tuple-element.9) | copy-start | bytes 491524
  33.0 15.9 %all-to-all-start.1 = ((bf16[16,32,256]{2,1,0:T(8,128)(2,1)}), bf16[16,32,256]{2,1,0:T(8,128)(2,1)S(1)}, u32[]{:S(2)}, u32[]{:S(2)}) async-start(bf16[16,32,256]{2,1,0:T(8,128)(2,1)} %bitcast.5), calls=%async_computation.1 | async-start | bytes 524288 | tf_op jit(solution)/shard_map/all_to_all | solution.py:294
  38.9 6.6 %collective-permute-start.3 = (bf16[128,640]{1,0:T(8,128)(2,1)S(1)}, bf16[128,640]{1,0:T(8,128)(2,1)S(1)}, u32[]{:S(2)}, u32[]{:S(2)}) collective-permute-start(bf16[128,640]{1,0:T(8,128)(2,1)S(1)} %copy-done.8), channel_id=1, source_target_pairs={{0,4},{4,0},{1,5},{5,1},{2,6},{6,2},{3,7},{7,3},{8,12},{12,8},{9,1... | collective-permute-start | bytes 491528 | tf_op jit(solution)/shard_map/ppermute | solution.py:293
  48.9 0.7 %copy-start.1 = (bf16[16,32,256]{2,1,0:T(8,128)(2,1)}, bf16[16,32,256]{2,1,0:T(8,128)(2,1)S(1)}, u32[]{:S(2)}) copy-start(bf16[16,32,256]{2,1,0:T(8,128)(2,1)S(1)} %all-to-all-done.1.terms_ref) | copy-start | bytes 786436

commit v3 on v2

--- a/solution.py
+++ b/solution.py
@@ -16,7 +16,6 @@
 SCALE = HEAD ** (-0.5)
 EXPONENT_SCALE = SCALE * math.log2(math.e)
 LOWEST = -1e30
-VMEM_LIMIT = 56 * 1024 * 1024
 ROWS_DOT_ROWS = (((1,), (1,)), ((), ()))
 COLS_DOT_COLS = (((0,), (0,)), ((), ()))
 
@@ -38,33 +37,44 @@
     return jnp.minimum(first, second), jnp.where(first < second, 0, 1)
 
 
+def load(source_ref, target_ref, sem):
+    copy = pltpu.make_async_copy(source_ref, target_ref, sem)
+    copy.start()
+    return copy
+
+
 class Work:
-    def __init__(self, order_ref, me_ref, kv_ref, ks_ref, q_refs, d_refs, qs_ref, ds_ref):
-        self.slab_rows = q_refs[0].shape[0] // 2
-        self.outer = kv_ref.shape[0] // (2 * self.slab_rows)
+    def __init__(self, order_ref, me_ref, kv_ref, ks_ref, sems):
+        self.half_rows = ks_ref.shape[1]
+        self.outer = order_ref.shape[0] // 4
+        self.slab_rows = self.half_rows // self.outer
         self.order_ref = order_ref
         me = me_ref[0]
         self.at, self.side = me // 2, me % 2
-        self.low = [pair_of(order_ref, me), pair_of(order_ref, me + 1 - 2 * self.side)]
-        self.half_rows = self.outer * self.slab_rows
+        self.low = [pair_of(order_ref, me)[0], pair_of(order_ref, me + 1 - 2 * self.side)[0]]
         self.chunk = math.gcd(256, self.half_rows)
         rows = self.slab_rows
 
-        def stack_keys(j):
+        def copies(j):
             _, place = pair_of(order_ref, 2 * j + self.side)
             for half in range(2):
                 here = place if half == 0 else 1 - place
-                ks_ref[half, at_rows(j * rows, rows), :] = kv_ref[at_rows((2 * j + here) * rows, rows), :]
-
-        repeat(self.outer, stack_keys)
-        for owner in range(2):
-            for half in range(2):
-                place = self.low[owner][1]
-                source = at_rows((place if half == 0 else 1 - place) * rows, rows)
-                for h in range(GROUP):
-                    cols = slice(h * HEAD, (h + 1) * HEAD)
-                    qs_ref[owner, half, h * rows : (h + 1) * rows, :] = q_refs[owner][source, cols]
-                    ds_ref[owner, half, h * rows : (h + 1) * rows, :] = d_refs[owner][source, cols]
+                yield pltpu.make_async_copy(
+                    kv_ref.at[at_rows((2 * j + here) * rows, rows)],
+                    ks_ref.at[half, at_rows(j * rows, rows)],
+                    sems.at[2 * j + half],
+                )
+
+        def start(j):
+            for copy in copies(j):
+                copy.start()
+
+        def wait(j):
+            for copy in copies(j):
+                copy.wait()
+
+        repeat(self.outer, start)
+        self.wait = lambda: repeat(self.outer, wait)
 
     def blocks(self, body):
         rows = self.slab_rows
@@ -76,7 +86,7 @@
 
             def pick(j):
                 low, _ = pair_of(self.order_ref, 2 * j + self.side)
-                half = jnp.where(self.low[owner][0] >= low, 0, 1)
+                half = jnp.where(self.low[owner] >= low, 0, 1)
                 mask = None if owner == 1 else j == self.at
                 body(owner, half, half, j * rows, rows, self.half_rows + j * rows, mask)
 
@@ -118,14 +128,26 @@
             out_ref[s * kvh + k, :, HEAD:] = value_part
 
 
-def stats_kernel(
-    order_ref, me_ref, q_ref, do_ref, q2_ref, do2_ref, kv_ref, out_ref,
-    ks_ref, qs_ref, ds_ref, s_ref, m_ref, l_ref, d_ref,
-):
-    work = Work(order_ref, me_ref, kv_ref, ks_ref, (q_ref, q2_ref), (do_ref, do2_ref), qs_ref, ds_ref)
+def stack_kernel(order_ref, me_ref, q_ref, do_ref, q2_ref, do2_ref, qs_ref, ds_ref):
+    rows = q_ref.shape[0] // 2
+    me = me_ref[0]
+    for owner, index in ((0, me), (1, me + 1 - 2 * (me % 2))):
+        _, place = pair_of(order_ref, index)
+        for half in range(2):
+            source = at_rows((place if half == 0 else 1 - place) * rows, rows)
+            for target, parts in ((qs_ref, (q_ref, q2_ref)), (ds_ref, (do_ref, do2_ref))):
+                for h in range(GROUP):
+                    target[owner, half, h * rows : (h + 1) * rows, :] = parts[owner][
+                        source, h * HEAD : (h + 1) * HEAD
+                    ]
+
+
+def stats_kernel(order_ref, me_ref, qs_ref, ds_ref, kv_ref, out_ref, ks_ref, s_ref, m_ref, l_ref, d_ref, sems):
+    work = Work(order_ref, me_ref, kv_ref, ks_ref, sems)
     m_ref[...] = jnp.full(m_ref.shape, LOWEST, jnp.float32)
     l_ref[...] = jnp.zeros(l_ref.shape, jnp.float32)
     d_ref[...] = jnp.zeros(d_ref.shape, jnp.float32)
+    work.wait()
 
     def maximum(owner, q_half, k_half, first, size, place, mask):
         scores = work.scores(ks_ref, qs_ref, owner, q_half, k_half, first, size, mask)
@@ -153,13 +175,19 @@
 
 
 def grads_kernel(
-    order_ref, me_ref, q_ref, do_ref, q2_ref, do2_ref, kv_ref, mine_ref, theirs_ref,
+    order_ref, me_ref, qs_ref, ds_ref, kv_ref, mine_any, theirs_any,
     dq_ref, dq2_ref, dkv_ref,
-    ks_ref, qs_ref, ds_ref, m_ref, d_ref, acc_ref, dq_acc_ref,
+    ks_ref, mine_ref, theirs_ref, m_ref, d_ref, acc_ref, dq_acc_ref, sems, stat_sems,
 ):
-    work = Work(order_ref, me_ref, kv_ref, ks_ref, (q_ref, q2_ref), (do_ref, do2_ref), qs_ref, ds_ref)
+    work = Work(order_ref, me_ref, kv_ref, ks_ref, sems)
+    stat_copies = [
+        load(mine_any, mine_ref, stat_sems.at[0]),
+        load(theirs_any, theirs_ref, stat_sems.at[1]),
+    ]
     acc_ref[...] = jnp.zeros(acc_ref.shape, jnp.float32)
     dq_acc_ref[...] = jnp.zeros(dq_acc_ref.shape, jnp.float32)
+    for copy in stat_copies:
+        copy.wait()
     for owner in range(2):
         for half in range(2):
             base = (2 * owner + half) * 3
@@ -172,6 +200,7 @@
             delta = w1 * mine_ref[base + 2 : base + 3, :] + w2 * theirs_ref[base2 + 2 : base2 + 3, :]
             m_ref[owner, half] = top * EXPONENT_SCALE + jnp.log2(total)
             d_ref[owner, half] = delta / total
+    work.wait()
 
     def gradients(owner, q_half, k_half, first, size, place, mask):
         scores = work.scores(ks_ref, qs_ref, owner, q_half, k_half, first, size, mask)
@@ -191,9 +220,10 @@
 
     work.blocks(gradients)
     rows = work.slab_rows
-    for owner, target in ((0, dq_ref), (1, dq2_ref)):
-        for half in range(2):
-            place = work.low[owner][1]
+    me = me_ref[0]
+    for owner, index, target in ((0, me, dq_ref), (1, me + 1 - 2 * work.side, dq2_ref)):
+        _, place = pair_of(order_ref, index)
+        for half in range(2):
             source = at_rows((place if half == 0 else 1 - place) * rows, rows)
             grads = (jnp.transpose(dq_acc_ref[owner, half]) * SCALE).astype(target.dtype)
             for h in range(GROUP):
@@ -211,7 +241,8 @@
     repeat(work.outer, write_terms)
 
 
-def combine_kernel(kvh, terms_ref, key_ref, value_ref):
+def combine_kernel(kvh, terms_any, key_ref, value_ref, terms_ref, sem):
+    load(terms_any, terms_ref, sem).wait()
     seq = terms_ref.shape[0] // kvh
     for k in range(kvh):
         total = terms_ref[k].astype(jnp.float32)
@@ -220,6 +251,10 @@
         total = total.astype(jnp.bfloat16)
         key_ref[:, k * HEAD : (k + 1) * HEAD] = total[:, :HEAD]
         value_ref[:, k * HEAD : (k + 1) * HEAD] = total[:, HEAD:]
+
+
+def finish_kernel(own_ref, received_ref, out_ref):
+    out_ref[...] = (own_ref[...] + received_ref[...].astype(jnp.float32)).astype(jnp.bfloat16)
 
 
 def per_device(queries, keys, values, d_out, slab_order):
@@ -234,9 +269,11 @@
     half_rows = outer * slab_rows
     columns = GROUP * slab_rows
     swap = [(0, 1), (1, 0)]
-    params = pltpu.CompilerParams(vmem_limit_bytes=VMEM_LIMIT)
+    params = pltpu.CompilerParams(vmem_limit_bytes=(8 << 20) + (6 << 10) * column_rows)
+    beside = pl.CostEstimate(flops=2 * 10**10, bytes_accessed=10**6, transcendentals=0)
     vmem = pl.BlockSpec(memory_space=pltpu.VMEM)
     smem = pl.BlockSpec(memory_space=pltpu.SMEM)
+    anywhere = pl.BlockSpec(memory_space=pl.ANY)
     shape = jax.ShapeDtypeStruct
 
     queries2 = lax.ppermute(queries, "pair", swap)
@@ -253,23 +290,35 @@
     gathered = gathered.reshape(column_rows, 2 * HEAD)
 
     me = (lax.axis_index("outer") * 2 + lax.axis_index("pair")).astype(jnp.int32).reshape(1)
-    stacks = [
-        pltpu.VMEM((2, half_rows, 2 * HEAD), jnp.bfloat16),
-        pltpu.VMEM((2, 2, columns, HEAD), jnp.bfloat16),
-        pltpu.VMEM((2, 2, columns, HEAD), jnp.bfloat16),
-    ]
+    stack = shape((2, 2, columns, HEAD), jnp.bfloat16)
+    stacks = pl.pallas_call(
+        stack_kernel,
+        out_shape=(stack, stack),
+        in_specs=[smem, smem] + [vmem] * 4,
+        out_specs=(vmem, vmem),
+        compiler_params=params,
+        cost_estimate=beside,
+        name="stack",
+    )(slab_order, me, queries, d_out, queries2, d_out2)
+    sorted_keys = pltpu.VMEM((2, half_rows, 2 * HEAD), jnp.bfloat16)
+    key_sems = pltpu.SemaphoreType.DMA((2 * outer,))
     row_stat = pltpu.VMEM((2, 2, 1, columns), jnp.float32)
-    operands = (slab_order, me, queries, d_out, queries2, d_out2, gathered)
     stats = pl.pallas_call(
         stats_kernel,
         out_shape=shape((12, columns), jnp.float32),
-        in_specs=[smem, smem] + [vmem] * 5,
+        in_specs=[smem, smem, vmem, vmem, anywhere],
         out_specs=vmem,
-        scratch_shapes=stacks
-        + [pltpu.VMEM((2, 2 * half_rows + slab_rows, columns), jnp.float32), row_stat, row_stat, row_stat],
+        scratch_shapes=[
+            sorted_keys,
+            pltpu.VMEM((2, 2 * half_rows + slab_rows, columns), jnp.float32),
+            row_stat,
+            row_stat,
+            row_stat,
+            key_sems,
+        ],
         compiler_params=params,
         name="stats",
-    )(*operands)
+    )(slab_order, me, *stacks, gathered)
     stats2 = lax.ppermute(stats, "pair", swap)
     own_grads, other_grads, terms = pl.pallas_call(
         grads_kernel,
@@ -278,28 +327,41 @@
             shape(queries.shape, jnp.bfloat16),
             shape((column_rows, 2 * HEAD), jnp.bfloat16),
         ),
-        in_specs=[smem, smem] + [vmem] * 7,
+        in_specs=[smem, smem, vmem, vmem] + [anywhere] * 3,
         out_specs=(vmem, vmem, vmem),
-        scratch_shapes=stacks
-        + [
+        scratch_shapes=[
+            sorted_keys,
+            pltpu.VMEM((12, columns), jnp.float32),
+            pltpu.VMEM((12, columns), jnp.float32),
             row_stat,
             row_stat,
             pltpu.VMEM((2, half_rows, 2 * HEAD), jnp.float32),
             pltpu.VMEM((2, 2, HEAD, columns), jnp.float32),
+            key_sems,
+            pltpu.SemaphoreType.DMA((2,)),
         ],
         compiler_params=params,
         name="grads",
-    )(*operands, stats, stats2)
+    )(slab_order, me, *stacks, gathered, stats, stats2)
     received_grads = lax.ppermute(other_grads, "pair", swap)
     owned = lax.all_to_all(
         terms.reshape(peers, cache_rows, 2 * HEAD), axes, split_axis=0, concat_axis=0, tiled=True
     )
-    query_grads = (own_grads + received_grads.astype(jnp.float32)).astype(jnp.bfloat16)
+    query_grads = pl.pallas_call(
+        finish_kernel,
+        out_shape=shape(queries.shape, jnp.bfloat16),
+        in_specs=[vmem, vmem],
+        out_specs=vmem,
+        compiler_params=params,
+        cost_estimate=beside,
+        name="finish",
+    )(own_grads, received_grads)
     key_grads, value_grads = pl.pallas_call(
         functools.partial(combine_kernel, kvh),
         out_shape=(shape(keys.shape, jnp.bfloat16), shape(values.shape, jnp.bfloat16)),
-        in_specs=[vmem],
+        in_specs=[anywhere],
         out_specs=(vmem, vmem),
+        scratch_shapes=[pltpu.VMEM((peers, cache_rows, 2 * HEAD), jnp.bfloat16), pltpu.SemaphoreType.DMA],
         compiler_params=params,
         name="combine",
     )(owned)

time: 51.7 us -> 49.1 us (0.950)
  starting transfers between devices: 18.5 us -> 16.3 us
  waiting for transfers between devices: 18.3 us -> 20.3 us
  Pallas kernels: 11 us -> 9.18 us
  other arithmetic: 0.71 us -> 0 us
    all_to_all x1, waiting for transfers between devices: 0.01 us -> 8.7 us  [per_device(): lax.all_to_all(packed, axes, split_axis=0, concat_axis=0, tiled=True)]
    all_to_all x1, waiting for transfers between devices: 2.73 us -> 9.04 us  [per_device(): lax.all_to_all(terms.reshape(peers, cache_rows, 2 * HEAD), axes, split_ax...]
    ppermute x1, waiting for transfers between devices: 4.98 us -> 0.01 us  [per_device(): queries2 = lax.ppermute(queries, 'pair', swap)]
    ppermute x1, waiting for transfers between devices: 5.02 us -> 0.26 us  [per_device(): received_grads = lax.ppermute(other_grads, 'pair', swap)]
    ppermute x1, waiting for transfers between devices: 3.04 us -> 0.01 us  [per_device(): d_out2 = lax.ppermute(d_out, 'pair', swap)]
    all_to_all x1, starting transfers between devices: 5.86 us -> 3.53 us  [per_device(): lax.all_to_all(terms.reshape(peers, cache_rows, 2 * HEAD), axes, split_ax...]
    ppermute x1, starting transfers between devices: 1.58 us -> 3.03 us  [per_device(): queries2 = lax.ppermute(queries, 'pair', swap)]
    pallas_call x0 -> x2, Pallas kernels: none -> 1.38 us  [the longest x1 0.71 us: per_device(): pl.pallas_call(finish_kernel, out_shape=shape(queries.shape, jnp.bfloat16...]
  transfers between devices with their start and end apart: 6 -> 6, of which waited for: 5 -> 4; matrix products, arithmetic and copies ran while one was open for 1% -> 0% of each run, Pallas kernels for 0% -> 4%
where the time goes in v3:
time: 49.1 us; the launch traced here: 48.6 us
  waiting for transfers between devices  20.3 us (41%)
  starting transfers between devices  16.3 us (33%)
  Pallas kernels  9.18 us (19%)
  local copies, waits for them, and re-layouts  2.13 us (4%)
  between operations  0.73 us (1%)
    all_to_all x1, waiting for transfers between devices, per_device(): lax.all_to_all(terms.reshape(peers, cache_rows, 2 * HEAD), axes, split_ax...  9.04 us
    all_to_all x1, waiting for transfers between devices, per_device(): lax.all_to_all(packed, axes, split_axis=0, concat_axis=0, tiled=True)  8.7 us
    all_to_all x1, starting transfers between devices, per_device(): lax.all_to_all(packed, axes, split_axis=0, concat_axis=0, tiled=True)  6.47 us
    pallas_call x1, Pallas kernels, per_device(): pl.pallas_call(grads_kernel, out_shape=(shape(queries.shape, jnp.float32)...  4.49 us
    all_to_all x1, starting transfers between devices, per_device(): lax.all_to_all(terms.reshape(peers, cache_rows, 2 * HEAD), axes, split_ax...  3.53 us
    ppermute x1, starting transfers between devices, per_device(): queries2 = lax.ppermute(queries, 'pair', swap)  3.03 us
    ppermute x1, waiting for transfers between devices, per_device(): stats2 = lax.ppermute(stats, 'pair', swap)  2.31 us
    unnamed x10, local copies, waits for them, and re-layouts  2.13 us
  transfers between devices with their start and end apart: 6, of which 4 were waited for; matrix products, arithmetic and copies ran while one was open for 0% of the time, Pallas kernels for 4%

profile of v3, /device:TPU:0, one launch (start us, length us, event | category | flops | bytes accessed | tf_op | source)
XLA Modules:
  0.0 48.6 jit_solution(10069137028798602122)
XLA Ops:
  0.6 3.0 %collective-permute-start = (bf16[128,640]{1,0:T(8,128)(2,1)}, bf16[128,640]{1,0:T(8,128)(2,1)S(1)}, u32[]{:S(2)}, u32[]{:S(2)}) collective-permute-start(bf16[128,640]{1,0:T(8,128)(2,1)} %q_ref.1), channel_id=1, source_target_pairs={{0,4},{4,0},{1,5},{5,1},{2,6},{6,2},{3,7},{7,3},{8,12},{12,8},{9,1... | collective-permute-start | bytes 491528 | tf_op jit(solution)/shard_map/ppermute | solution.py:279
  3.7 0.1 collective-permute-start.1
  3.7 0.0 copy-start
  3.7 0.8 %copy-done = bf16[32,512]{1,0:T(8,128)(2,1)S(1)} copy-done((bf16[32,512]{1,0:T(8,128)(2,1)S(1)}, bf16[32,512]{1,0:T(8,128)(2,1)}, u32[]{:S(2)}) %copy-start) | copy-done | bytes 32792
  4.5 0.0 copy-start.1
  4.5 0.8 %copy-done.1 = bf16[32,512]{1,0:T(8,128)(2,1)S(1)} copy-done((bf16[32,512]{1,0:T(8,128)(2,1)S(1)}, bf16[32,512]{1,0:T(8,128)(2,1)}, u32[]{:S(2)}) %copy-start.1) | copy-done | bytes 32792
  5.3 0.7 %pack.1 = bf16[16,32,256]{2,1,0:T(8,128)(2,1)} custom-call(bf16[32,512]{1,0:T(8,128)(2,1)S(1)} %copy-done, bf16[32,512]{1,0:T(8,128)(2,1)S(1)} %copy-done.1), custom_call_target="tpu_custom_call" | custom-call | tf_op jit(solution)/shard_map/pack/pallas_call | solution.py:281
  6.0 0.0 copy-start.3
  6.0 0.0 copy-start.4
  6.0 6.5 %all-to-all-start = ((bf16[16,32,256]{2,1,0:T(8,128)(2,1)}), bf16[16,32,256]{2,1,0:T(8,128)(2,1)S(1)}, u32[]{:S(2)}, u32[]{:S(2)}) async-start(bf16[16,32,256]{2,1,0:T(8,128)(2,1)} %pack.1), calls=%async_computation | async-start | bytes 524288 | tf_op jit(solution)/shard_map/all_to_all | solution.py:289
  12.5 0.0 copy-start.2
  12.5 0.0 collective-permute-done.q2_ref
  12.5 0.0 collective-permute-done.1.do2_ref
  12.5 0.0 copy-done.3
  12.5 0.0 copy-done.4
  12.5 0.6 %copy-done.2 = s32[16]{0:T(128)S(1)} copy-done((s32[16]{0:T(128)S(1)}, s32[16]{0:T(128)}, u32[]{:S(2)}) %copy-start.2) | copy-done | bytes 88
  13.1 0.7 %stack.1 = (bf16[2,2,320,128]{3,2,1,0:T(8,128)(2,1)S(1)}, bf16[2,2,320,128]{3,2,1,0:T(8,128)(2,1)S(1)}) custom-call(s32[16]{0:T(128)S(1)} %copy-done.2, s32[1]{0:T(128)} %bitcast.me_ref, bf16[128,640]{1,0:T(8,128)(2,1)S(1)} %copy-done.3, bf16[128,640]{1,0:T(8,128)(2,1)S(1)} %copy-done.4, bf16[128,640]{1,0:T(8,128)(2,1)S(1)} %collective-permute-done.q2_ref, ...), custom_call_target="tpu_custom_call" | custom-call | flops 20000000000 | bytes 1000000 | tf_op jit(solution)/shard_map/stack/pallas_call | solution.py:294
  13.8 8.7 %all-to-all-done = bf16[16,32,256]{2,1,0:T(8,128)(2,1)S(1)} async-done(((bf16[16,32,256]{2,1,0:T(8,128)(2,1)}), bf16[16,32,256]{2,1,0:T(8,128)(2,1)S(1)}, u32[]{:S(2)}, u32[]{:S(2)}) %all-to-all-start) | async-done | bytes 262176 | tf_op jit(solution)/shard_map/all_to_all | solution.py:289
  22.5 1.9 %stats.1.mine_any = f32[12,320]{1,0:T(8,128)S(1)} custom-call(s32[16]{0:T(128)S(1)} %copy-done.2, s32[1]{0:T(128)} %bitcast.me_ref, bf16[2,2,320,128]{3,2,1,0:T(8,128)(2,1)S(1)} %get-tuple-element.10.qs_ref, bf16[2,2,320,128]{3,2,1,0:T(8,128)(2,1)S(1)} %get-tuple-element.11.ds_ref, bf16[512,256]{1,0:T(8,128)(2,1)S(1)} %bitcast.3), custom_call_target="tpu_custom_call" | custom-call | tf_op jit(solution)/shard_map/stats/pallas_call | solution.py:306
  24.4 1.6 %collective-permute-start.2 = (f32[12,320]{1,0:T(8,128)S(1)}, f32[12,320]{1,0:T(8,128)S(1)}, u32[]{:S(2)}, u32[]{:S(2)}) collective-permute-start(f32[12,320]{1,0:T(8,128)S(1)} %stats.1.mine_any), channel_id=1, source_target_pairs={{0,4},{4,0},{1,5},{5,1},{2,6},{6,2},{3,7},{7,3},{8,12},{12,8},{9,1... | collective-permute-start | bytes 46088 | tf_op jit(solution)/shard_map/ppermute | solution.py:322
  26.0 2.3 %collective-permute-done.2.theirs_any = f32[12,320]{1,0:T(8,128)S(1)} collective-permute-done((f32[12,320]{1,0:T(8,128)S(1)}, f32[12,320]{1,0:T(8,128)S(1)}, u32[]{:S(2)}, u32[]{:S(2)}) %collective-permute-start.2) | collective-permute-done | bytes 15392 | tf_op jit(solution)/shard_map/ppermute | solution.py:322
  28.3 4.5 %grads.1 = (f32[128,640]{1,0:T(8,128)S(1)}, bf16[128,640]{1,0:T(8,128)(2,1)S(1)}, bf16[512,256]{1,0:T(8,128)(2,1)}) custom-call(s32[16]{0:T(128)S(1)} %copy-done.2, s32[1]{0:T(128)} %bitcast.me_ref, bf16[2,2,320,128]{3,2,1,0:T(8,128)(2,1)S(1)} %get-tuple-element.10.qs_ref, bf16[2,2,320,128]{3,2,1,0:T(8,128)(2,1)S(1)} %get-tuple-element.11.ds_ref, ...), custom_call_target="tpu_custom_call" | custom-call | tf_op jit(solution)/shard_map/grads/pallas_call | solution.py:323
  32.8 1.6 %collective-permute-start.3 = (bf16[128,640]{1,0:T(8,128)(2,1)S(1)}, bf16[128,640]{1,0:T(8,128)(2,1)S(1)}, u32[]{:S(2)}, u32[]{:S(2)}) collective-permute-start(bf16[128,640]{1,0:T(8,128)(2,1)S(1)} %get-tuple-element.13), channel_id=1, source_target_pairs={{0,4},{4,0},{1,5},{5,1},{2,6},{6,2},{3,7},{7,3},{8,12},{12,8},{9,1... | collective-permute-start | bytes 491528 | tf_op jit(solution)/shard_map/ppermute | solution.py:346
  34.4 3.5 %all-to-all-start.1 = ((bf16[16,32,256]{2,1,0:T(8,128)(2,1)}), bf16[16,32,256]{2,1,0:T(8,128)(2,1)S(1)}, u32[]{:S(2)}, u32[]{:S(2)}) async-start(bf16[16,32,256]{2,1,0:T(8,128)(2,1)} %bitcast.2), calls=%async_computation.1 | async-start | bytes 524288 | tf_op jit(solution)/shard_map/all_to_all | solution.py:347
  37.9 0.3 collective-permute-done.3.received_ref
  38.2 0.7 %finish.1 = bf16[128,640]{1,0:T(8,128)(2,1)} custom-call(f32[128,640]{1,0:T(8,128)S(1)} %get-tuple-element.12.own_ref, bf16[128,640]{1,0:T(8,128)(2,1)S(1)} %collective-permute-done.3.received_ref), custom_call_target="tpu_custom_call" | custom-call | flops 20000000000 | bytes 1000000 | tf_op jit(solution)/shard_map/finish/pallas_call | solution.py:350
  38.9 9.0 %all-to-all-done.1.terms_any = bf16[16,32,256]{2,1,0:T(8,128)(2,1)S(1)} async-done(((bf16[16,32,256]{2,1,0:T(8,128)(2,1)}), bf16[16,32,256]{2,1,0:T(8,128)(2,1)S(1)}, u32[]{:S(2)}, u32[]{:S(2)}) %all-to-all-start.1) | async-done | bytes 262176 | tf_op jit(solution)/shard_map/all_to_all | solution.py:347
  47.9 0.7 %combine.1 = (bf16[32,512]{1,0:T(8,128)(2,1)}, bf16[32,512]{1,0:T(8,128)(2,1)}) custom-call(bf16[16,32,256]{2,1,0:T(8,128)(2,1)S(1)} %all-to-all-done.1.terms_any), custom_call_target="tpu_custom_call" | custom-call | tf_op jit(solution)/shard_map/combine/pallas_call | solution.py:359
Async XLA Ops:
  0.6 11.9 %collective-permute-start = (bf16[128,640]{1,0:T(8,128)(2,1)}, bf16[128,640]{1,0:T(8,128)(2,1)S(1)}, u32[]{:S(2)}, u32[]{:S(2)}) collective-permute-start(bf16[128,640]{1,0:T(8,128)(2,1)} %q_ref.1), channel_id=1, source_target_pairs={{0,4},{4,0},{1,5},{5,1},{2,6},{6,2},{3,7},{7,3},{8,12},{12,8},{9,1... | collective-permute-start | bytes 491528 | tf_op jit(solution)/shard_map/ppermute | solution.py:279
  3.7 8.8 %collective-permute-start.1 = (bf16[128,640]{1,0:T(8,128)(2,1)}, bf16[128,640]{1,0:T(8,128)(2,1)S(1)}, u32[]{:S(2)}, u32[]{:S(2)}) collective-permute-start(bf16[128,640]{1,0:T(8,128)(2,1)} %do_ref.1), channel_id=1, source_target_pairs={{0,4},{4,0},{1,5},{5,1},{2,6},{6,2},{3,7},{7,3},{8,12},{12,8},{9,1... | collective-permute-start | bytes 491528 | tf_op jit(solution)/shard_map/ppermute | solution.py:280
  3.7 0.8 %copy-start = (bf16[32,512]{1,0:T(8,128)(2,1)S(1)}, bf16[32,512]{1,0:T(8,128)(2,1)}, u32[]{:S(2)}) copy-start(bf16[32,512]{1,0:T(8,128)(2,1)} %keys_ref.1) | copy-start | bytes 98308
  4.5 0.8 %copy-start.1 = (bf16[32,512]{1,0:T(8,128)(2,1)S(1)}, bf16[32,512]{1,0:T(8,128)(2,1)}, u32[]{:S(2)}) copy-start(bf16[32,512]{1,0:T(8,128)(2,1)} %values_ref.1) | copy-start | bytes 98308
  6.0 6.5 %copy-start.3 = (bf16[128,640]{1,0:T(8,128)(2,1)S(1)}, bf16[128,640]{1,0:T(8,128)(2,1)}, u32[]{:S(2)}) copy-start(bf16[128,640]{1,0:T(8,128)(2,1)} %q_ref.1) | copy-start | bytes 491524
  6.0 6.5 %copy-start.4 = (bf16[128,640]{1,0:T(8,128)(2,1)S(1)}, bf16[128,640]{1,0:T(8,128)(2,1)}, u32[]{:S(2)}) copy-start(bf16[128,640]{1,0:T(8,128)(2,1)} %do_ref.1) | copy-start | bytes 491524
  6.0 16.5 %all-to-all-start = ((bf16[16,32,256]{2,1,0:T(8,128)(2,1)}), bf16[16,32,256]{2,1,0:T(8,128)(2,1)S(1)}, u32[]{:S(2)}, u32[]{:S(2)}) async-start(bf16[16,32,256]{2,1,0:T(8,128)(2,1)} %pack.1), calls=%async_computation | async-start | bytes 524288 | tf_op jit(solution)/shard_map/all_to_all | solution.py:289
  12.5 0.7 %copy-start.2 = (s32[16]{0:T(128)S(1)}, s32[16]{0:T(128)}, u32[]{:S(2)}) copy-start(s32[16]{0:T(128)} %order_ref.5) | copy-start | bytes 196
  24.4 3.9 %collective-permute-start.2 = (f32[12,320]{1,0:T(8,128)S(1)}, f32[12,320]{1,0:T(8,128)S(1)}, u32[]{:S(2)}, u32[]{:S(2)}) collective-permute-start(f32[12,320]{1,0:T(8,128)S(1)} %stats.1.mine_any), channel_id=1, source_target_pairs={{0,4},{4,0},{1,5},{5,1},{2,6},{6,2},{3,7},{7,3},{8,12},{12,8},{9,1... | collective-permute-start | bytes 46088 | tf_op jit(solution)/shard_map/ppermute | solution.py:322
  32.8 5.4 %collective-permute-start.3 = (bf16[128,640]{1,0:T(8,128)(2,1)S(1)}, bf16[128,640]{1,0:T(8,128)(2,1)S(1)}, u32[]{:S(2)}, u32[]{:S(2)}) collective-permute-start(bf16[128,640]{1,0:T(8,128)(2,1)S(1)} %get-tuple-element.13), channel_id=1, source_target_pairs={{0,4},{4,0},{1,5},{5,1},{2,6},{6,2},{3,7},{7,3},{8,12},{12,8},{9,1... | collective-permute-start | bytes 491528 | tf_op jit(solution)/shard_map/ppermute | solution.py:346
  34.4 13.5 %all-to-all-start.1 = ((bf16[16,32,256]{2,1,0:T(8,128)(2,1)}), bf16[16,32,256]{2,1,0:T(8,128)(2,1)S(1)}, u32[]{:S(2)}, u32[]{:S(2)}) async-start(bf16[16,32,256]{2,1,0:T(8,128)(2,1)} %bitcast.2), calls=%async_computation.1 | async-start | bytes 524288 | tf_op jit(solution)/shard_map/all_to_all | solution.py:347

commit v4 on v3

v4 whole, which is shorter than its diff:
```python
import functools
import math

import jax
import jax.numpy as jnp
from jax import lax
from jax.experimental import pallas as pl
from jax.experimental.pallas import tpu as pltpu
from jax.sharding import Mesh
from jax.sharding import PartitionSpec as P

HEADS = 20
KV_HEADS = 4
HEAD = 128
GROUP = HEADS // KV_HEADS
SCALE = HEAD ** (-0.5)
EXPONENT_SCALE = SCALE * math.log2(math.e)
LOWEST = -1e30
ROWS_DOT_ROWS = (((1,), (1,)), ((), ()))
COLS_DOT_COLS = (((0,), (0,)), ((), ()))


def repeat(count, body):
    if count <= 8:
        for step in range(count):
            body(step)
    else:
        pl.loop(0, count)(body)


def at_rows(start, size):
    return pl.ds(pl.multiple_of(start, size), size)


def pair_of(order_ref, index):
    first, second = order_ref[2 * index], order_ref[2 * index + 1]
    return jnp.minimum(first, second), jnp.where(first < second, 0, 1)


def load(source_ref, target_ref, sem):
    copy = pltpu.make_async_copy(source_ref, target_ref, sem)
    copy.start()
    return copy


class Work:
    def __init__(self, order_ref, kv_refs, ks_ref, sems):
        self.half_rows = ks_ref.shape[1]
        self.outer = len(kv_refs)
        self.slab_rows = self.half_rows // self.outer
        self.chunk = math.gcd(256, self.half_rows)
        rows = self.slab_rows
        at, side = lax.axis_index("outer"), lax.axis_index("pair")
        self.low = [pair_of(order_ref, 2 * at + side)[0], pair_of(order_ref, 2 * at + 1 - side)[0]]
        self.pairs = [
            pair_of(order_ref, 2 * lax.rem(at + self.outer - d, self.outer) + side)
            for d in range(self.outer)
        ]
        self.copies = []
        for d, kv_ref in enumerate(kv_refs):
            for half in range(2):
                source = at_rows(self.here(d, half) * rows, rows)
                self.copies.append(
                    load(kv_ref.at[source], ks_ref.at[half, pl.ds(d * rows, rows)], sems.at[2 * d + half])
                )

    def here(self, d, half):
        place = self.pairs[d][1]
        return place if half == 0 else 1 - place

    def wait(self):
        for copy in self.copies:
            copy.wait()

    def blocks(self, body):
        rows = self.slab_rows
        for owner in range(2):
            repeat(
                self.half_rows // self.chunk,
                lambda n: body(owner, 1, 0, n * self.chunk, self.chunk, n * self.chunk, False),
            )
            for d in range(self.outer):
                if owner == 0 and d == 0:
                    body(owner, 0, 0, 0, rows, self.half_rows, True)
                    body(owner, 1, 1, 0, rows, 2 * self.half_rows, True)
                else:
                    half = jnp.where(self.low[owner] >= self.pairs[d][0], 0, 1)
                    body(owner, half, half, d * rows, rows, self.half_rows + d * rows, False)

    def scores(self, ks_ref, qs_ref, owner, q_half, k_half, first, size, mask):
        scores = lax.dot_general(
            ks_ref[k_half, at_rows(first, size), :HEAD],
            qs_ref[owner, q_half],
            ROWS_DOT_ROWS,
            preferred_element_type=jnp.float32,
        )
        if mask:
            key = lax.broadcasted_iota(jnp.int32, scores.shape, 0)
            query = lax.rem(lax.broadcasted_iota(jnp.int32, (1, scores.shape[1]), 1), self.slab_rows)
            scores = jnp.where(key <= query, scores, LOWEST)
        return scores

    def grads(self, ks_ref, ds_ref, owner, q_half, k_half, first, size):
        return lax.dot_general(
            ks_ref[k_half, at_rows(first, size), HEAD:],
            ds_ref[owner, q_half],
            ROWS_DOT_ROWS,
            preferred_element_type=jnp.float32,
        )


def split_kernel(keys_ref, values_ref, *refs):
    outs, sems = refs[:-1], refs[-1]
    kvh = len(outs)
    copies = []
    for e, out_ref in enumerate(outs):
        head = lax.rem(lax.axis_index("kvh") + e, kvh)
        cols = at_rows(head * HEAD, HEAD)
        copies.append(load(keys_ref.at[:, cols], out_ref.at[:, pl.ds(0, HEAD)], sems.at[2 * e]))
        copies.append(load(values_ref.at[:, cols], out_ref.at[:, pl.ds(HEAD, HEAD)], sems.at[2 * e + 1]))
    for copy in copies:
        copy.wait()


def join_kernel(*refs):
    parts, out_ref, sems = refs[:-2], refs[-2], refs[-1]
    kvh = len(parts)
    rows = parts[0].shape[0]
    copies = []
    for e, part_ref in enumerate(parts):
        source = lax.rem(lax.axis_index("kvh") + kvh - e, kvh)
        copies.append(load(part_ref, out_ref.at[at_rows(source * rows, rows)], sems.at[e]))
    for copy in copies:
        copy.wait()


def stack_kernel(order_ref, q_ref, do_ref, q2_ref, do2_ref, qs_ref, ds_ref):
    rows = q_ref.shape[0] // 2
    at, side = lax.axis_index("outer"), lax.axis_index("pair")
    for owner, index in ((0, 2 * at + side), (1, 2 * at + 1 - side)):
        _, place = pair_of(order_ref, index)
        for half in range(2):
            source = at_rows((place if half == 0 else 1 - place) * rows, rows)
            for target, parts in ((qs_ref, (q_ref, q2_ref)), (ds_ref, (do_ref, do2_ref))):
                for h in range(GROUP):
                    target[owner, half, h * rows : (h + 1) * rows, :] = parts[owner][
                        source, h * HEAD : (h + 1) * HEAD
                    ]


def stats_kernel(order_ref, qs_ref, ds_ref, *refs):
    kv_refs, (out_ref, ks_ref, s_ref, m_ref, l_ref, d_ref, sems) = refs[:-7], refs[-7:]
    work = Work(order_ref, kv_refs, ks_ref, sems)
    m_ref[...] = jnp.full(m_ref.shape, LOWEST, jnp.float32)
    l_ref[...] = jnp.zeros(l_ref.shape, jnp.float32)
    d_ref[...] = jnp.zeros(d_ref.shape, jnp.float32)
    work.wait()

    def maximum(owner, q_half, k_half, first, size, place, mask):
        scores = work.scores(ks_ref, qs_ref, owner, q_half, k_half, first, size, mask)
        s_ref[owner, at_rows(place, size), :] = scores
        m_ref[owner, q_half] = jnp.maximum(
            m_ref[owner, q_half], jnp.max(scores, axis=0, keepdims=True)
        )

    work.blocks(maximum)

    def sums(owner, q_half, k_half, first, size, place, mask):
        grads = work.grads(ks_ref, ds_ref, owner, q_half, k_half, first, size)
        scores = s_ref[owner, at_rows(place, size), :]
        expon = jnp.exp2((scores - m_ref[owner, q_half]) * EXPONENT_SCALE)
        l_ref[owner, q_half] = l_ref[owner, q_half] + jnp.sum(expon, axis=0, keepdims=True)
        d_ref[owner, q_half] = d_ref[owner, q_half] + jnp.sum(expon * grads, axis=0, keepdims=True)

    work.blocks(sums)
    for owner in range(2):
        for half in range(2):
            base = (2 * owner + half) * 3
            out_ref[base : base + 1, :] = m_ref[owner, half]
            out_ref[base + 1 : base + 2, :] = l_ref[owner, half]
            out_ref[base + 2 : base + 3, :] = d_ref[owner, half]


def grads_kernel(outer, order_ref, qs_ref, ds_ref, *refs):
    kv_refs, (mine_any, theirs_any, dq_ref, dq2_ref) = refs[:outer], refs[outer : outer + 4]
    term_refs = refs[outer + 4 : 2 * outer + 4]
    ks_ref, mine_ref, theirs_ref, m_ref, d_ref, acc_ref, dq_acc_ref, sems, stat_sems = refs[2 * outer + 4 :]
    work = Work(order_ref, kv_refs, ks_ref, sems)
    stat_copies = [
        load(mine_any, mine_ref, stat_sems.at[0]),
        load(theirs_any, theirs_ref, stat_sems.at[1]),
    ]
    acc_ref[...] = jnp.zeros(acc_ref.shape, jnp.float32)
    dq_acc_ref[...] = jnp.zeros(dq_acc_ref.shape, jnp.float32)
    for copy in stat_copies:
        copy.wait()
    for owner in range(2):
        for half in range(2):
            base = (2 * owner + half) * 3
            base2 = (2 * (1 - owner) + half) * 3
            m1, m2 = mine_ref[base : base + 1, :], theirs_ref[base2 : base2 + 1, :]
            top = jnp.maximum(m1, m2)
            w1 = jnp.exp2((m1 - top) * EXPONENT_SCALE)
            w2 = jnp.exp2((m2 - top) * EXPONENT_SCALE)
            total = w1 * mine_ref[base + 1 : base + 2, :] + w2 * theirs_ref[base2 + 1 : base2 + 2, :]
            delta = w1 * mine_ref[base + 2 : base + 3, :] + w2 * theirs_ref[base2 + 2 : base2 + 3, :]
            m_ref[owner, half] = top * EXPONENT_SCALE + jnp.log2(total)
            d_ref[owner, half] = delta / total
    work.wait()

    def gradients(owner, q_half, k_half, first, size, place, mask):
        scores = work.scores(ks_ref, qs_ref, owner, q_half, k_half, first, size, mask)
        grads = work.grads(ks_ref, ds_ref, owner, q_half, k_half, first, size)
        probs = jnp.exp2(scores * EXPONENT_SCALE - m_ref[owner, q_half])
        score_grads = (probs * (grads - d_ref[owner, q_half])).astype(jnp.bfloat16)
        rows = at_rows(first, size)
        acc_ref[k_half, rows, HEAD:] = acc_ref[k_half, rows, HEAD:] + jnp.dot(
            probs.astype(jnp.bfloat16), ds_ref[owner, q_half], preferred_element_type=jnp.float32
        )
        acc_ref[k_half, rows, :HEAD] = acc_ref[k_half, rows, :HEAD] + jnp.dot(
            score_grads, qs_ref[owner, q_half], preferred_element_type=jnp.float32
        )
        dq_acc_ref[owner, q_half] = dq_acc_ref[owner, q_half] + lax.dot_general(
            ks_ref[k_half, rows, :HEAD], score_grads, COLS_DOT_COLS, preferred_element_type=jnp.float32
        )

    work.blocks(gradients)
    rows = work.slab_rows
    at, side = lax.axis_index("outer"), lax.axis_index("pair")
    for owner, index, target in ((0, 2 * at + side, dq_ref), (1, 2 * at + 1 - side, dq2_ref)):
        _, place = pair_of(order_ref, index)
        for half in range(2):
            source = at_rows((place if half == 0 else 1 - place) * rows, rows)
            grads = (jnp.transpose(dq_acc_ref[owner, half]) * SCALE).astype(target.dtype)
            for h in range(GROUP):
                target[source, h * HEAD : (h + 1) * HEAD] = grads[h * rows : (h + 1) * rows, :]

    for d, term_ref in enumerate(term_refs):
        for half in range(2):
            target = at_rows(work.here(d, half) * rows, rows)
            source = slice(d * rows, (d + 1) * rows)
            term_ref[target, :HEAD] = (acc_ref[half, source, :HEAD] * SCALE).astype(term_ref.dtype)
            term_ref[target, HEAD:] = acc_ref[half, source, HEAD:].astype(term_ref.dtype)


def sum_kernel(outer, *refs):
    terms, outs, (total_ref,) = refs[:outer], refs[outer:-1], refs[-1:]
    total = terms[0][...]
    for term_ref in terms[1:]:
        total = total + term_ref[...].astype(jnp.float32)
    total_ref[...] = total
    kvh = len(outs)
    rows = outs[0].shape[0]
    for e, out_ref in enumerate(outs):
        target = lax.rem(lax.axis_index("kvh") + e, kvh)
        out_ref[...] = total_ref[at_rows(target * rows, rows), :].astype(jnp.bfloat16)


def place_kernel(*refs):
    parts, (key_ref, value_ref, sems) = refs[:-3], refs[-3:]
    kvh = len(parts)
    copies = []
    for e, part_ref in enumerate(parts):
        head = lax.rem(lax.axis_index("kvh") + kvh - e, kvh)
        cols = at_rows(head * HEAD, HEAD)
        copies.append(load(part_ref.at[:, pl.ds(0, HEAD)], key_ref.at[:, cols], sems.at[2 * e]))
        copies.append(load(part_ref.at[:, pl.ds(HEAD, HEAD)], value_ref.at[:, cols], sems.at[2 * e + 1]))
    for copy in copies:
        copy.wait()


def finish_kernel(own_ref, received_ref, out_ref):
    out_ref[...] = (own_ref[...] + received_ref[...].astype(jnp.float32)).astype(jnp.bfloat16)


def per_device(queries, keys, values, d_out, slab_order):
    kvh = lax.axis_size("kvh")
    outer = lax.axis_size("outer")
    local_rows, query_width = queries.shape
    cache_rows = keys.shape[0]
    slab_rows = local_rows // 2
    half_rows = outer * slab_rows
    columns = GROUP * slab_rows
    params = pltpu.CompilerParams(vmem_limit_bytes=(8 << 20) + (6 << 10) * 2 * half_rows)
    beside = pl.CostEstimate(flops=2 * 10**10, bytes_accessed=10**6, transcendentals=0)
    vmem = pl.BlockSpec(memory_space=pltpu.VMEM)
    smem = pl.BlockSpec(memory_space=pltpu.SMEM)
    anywhere = pl.BlockSpec(memory_space=pl.ANY)
    shape = jax.ShapeDtypeStruct
    dma = pltpu.SemaphoreType.DMA

    def shift(array, axis, by):
        size = lax.axis_size(axis)
        return lax.ppermute(array, axis, [(n, (n + by) % size) for n in range(size)])

    part = shape((cache_rows, 2 * HEAD), jnp.bfloat16)
    block = shape((local_rows, 2 * HEAD), jnp.bfloat16)
    parts = pl.pallas_call(
        split_kernel,
        out_shape=(part,) * kvh,
        in_specs=[anywhere, anywhere],
        out_specs=(vmem,) * kvh,
        scratch_shapes=[dma((2 * kvh,))],
        compiler_params=params,
        name="split",
    )(keys, values)
    parts = [parts[0]] + [shift(parts[e], "kvh", e) for e in range(1, kvh)]
    queries2 = shift(queries, "pair", 1)
    d_out2 = shift(d_out, "pair", 1)
    own_block = pl.pallas_call(
        join_kernel,
        out_shape=block,
        in_specs=[anywhere] * kvh,
        out_specs=vmem,
        scratch_shapes=[dma((kvh,))],
        compiler_params=params,
        name="join",
    )(*parts)
    blocks = [own_block] + [shift(own_block, "outer", d) for d in range(1, outer)]

    stack = shape((2, 2, columns, HEAD), jnp.bfloat16)
    stacks = pl.pallas_call(
        stack_kernel,
        out_shape=(stack, stack),
        in_specs=[smem] + [vmem] * 4,
        out_specs=(vmem, vmem),
        compiler_params=params,
        cost_estimate=beside,
        name="stack",
    )(slab_order, queries, d_out, queries2, d_out2)
    sorted_keys = pltpu.VMEM((2, half_rows, 2 * HEAD), jnp.bfloat16)
    key_sems = dma((2 * outer,))
    row_stat = pltpu.VMEM((2, 2, 1, columns), jnp.float32)
    all_stats = (12, columns)
    stats = pl.pallas_call(
        stats_kernel,
        out_shape=shape(all_stats, jnp.float32),
        in_specs=[smem, vmem, vmem] + [anywhere] * outer,
        out_specs=vmem,
        scratch_shapes=[
            sorted_keys,
            pltpu.VMEM((2, 2 * half_rows + slab_rows, columns), jnp.float32),
            row_stat,
            row_stat,
            row_stat,
            key_sems,
        ],
        compiler_params=params,
        name="stats",
    )(slab_order, *stacks, *blocks)
    stats2 = shift(stats, "pair", 1)
    own_grads, other_grads, *terms = pl.pallas_call(
        functools.partial(grads_kernel, outer),
        out_shape=(
            shape(queries.shape, jnp.float32),
            shape(queries.shape, jnp.bfloat16),
            shape(block.shape, jnp.float32),
        )
        + (block,) * (outer - 1),
        in_specs=[smem, vmem, vmem] + [anywhere] * (outer + 2),
        out_specs=(vmem,) * (outer + 2),
        scratch_shapes=[
            sorted_keys,
            pltpu.VMEM(all_stats, jnp.float32),
            pltpu.VMEM(all_stats, jnp.float32),
            row_stat,
            row_stat,
            pltpu.VMEM((2, half_rows, 2 * HEAD), jnp.float32),
            pltpu.VMEM((2, 2, HEAD, columns), jnp.float32),
            key_sems,
            dma((2,)),
        ],
        compiler_params=params,
        name="grads",
    )(slab_order, *stacks, *blocks, stats, stats2)
    terms = [terms[0]] + [shift(terms[d], "outer", -d) for d in range(1, outer)]
    received_grads = shift(other_grads, "pair", 1)
    query_grads = pl.pallas_call(
        finish_kernel,
        out_shape=shape(queries.shape, jnp.bfloat16),
        in_specs=[vmem, vmem],
        out_specs=vmem,
        compiler_params=params,
        cost_estimate=beside,
        name="finish",
    )(own_grads, received_grads)
    owned = pl.pallas_call(
        functools.partial(sum_kernel, outer),
        out_shape=(part,) * kvh,
        in_specs=[vmem] * outer,
        out_specs=(vmem,) * kvh,
        scratch_shapes=[pltpu.VMEM(block.shape, jnp.float32)],
        compiler_params=params,
        name="sum",
    )(*terms)
    owned = [owned[0]] + [shift(owned[e], "kvh", e) for e in range(1, kvh)]
    key_grads, value_grads = pl.pallas_call(
        place_kernel,
        out_shape=(shape(keys.shape, jnp.bfloat16), shape(values.shape, jnp.bfloat16)),
        in_specs=[anywhere] * kvh,
        out_specs=(anywhere, anywhere),
        scratch_shapes=[dma((2 * kvh,))],
        compiler_params=params,
        name="place",
    )(*owned)
    return (query_grads, key_grads, value_grads)


def solution(mesh):
    kvh = mesh.shape["kvh"]
    pairs = mesh.shape["seq"] // 2
    paired = Mesh(mesh.devices.reshape(pairs, 2, kvh), ("outer", "pair", "kvh"))
    seq = ("outer", "pair")
    cache = P(("outer", "pair", "kvh"), None)
    placed = (P(seq, "kvh"), cache, cache, P(seq, "kvh"), P())
    return jax.shard_map(
        per_device,
        mesh=paired,
        in_specs=placed,
        out_specs=(P(seq, "kvh"), cache, cache),
        check_vma=False,
    )
```

time: 49.1 us -> 47.4 us (0.965)
  waiting for transfers between devices: 20.3 us -> 14.4 us
  starting transfers between devices: 16.3 us -> 20.9 us
  Pallas kernels: 9.18 us -> 8.22 us
    all_to_all x2 -> x0, waiting for transfers between devices: 17.7 us -> none  [the longest x1 9.04 us: per_device(): lax.all_to_all(terms.reshape(peers, cache_rows, 2 * HEAD), axes, split_ax...]
    ppermute x4 -> x16, starting transfers between devices: 6.28 us -> 20.9 us  [shift(): lax.ppermute(array, axis, [(n, (n + by) % size) for n in range(size)])]
    ppermute x4 -> x16, waiting for transfers between devices: 2.57 us -> 14.4 us  [shift(): lax.ppermute(array, axis, [(n, (n + by) % size) for n in range(size)])]
    all_to_all x2 -> x0, starting transfers between devices: 10 us -> none  [the longest x1 6.47 us: per_device(): lax.all_to_all(packed, axes, split_axis=0, concat_axis=0, tiled=True)]
    pallas_call x5 -> x7, Pallas kernels: 8.47 us -> 7.52 us  [the longest x1 3.99 us: per_device(): pl.pallas_call(functools.partial(grads_kernel, outer), out_shape=(shape(q...]
  transfers between devices with their start and end apart: 6 -> 16, of which waited for: 4 -> 9; matrix products, arithmetic and copies ran while one was open for 0% -> 0% of each run, Pallas kernels for 4% -> 3%
where the time goes in v4:
time: 47.4 us; the launch traced here: 46.6 us
  starting transfers between devices  20.9 us (44%)
  waiting for transfers between devices  14.4 us (30%)
  Pallas kernels  8.22 us (17%)
  local copies, waits for them, and re-layouts  2.43 us (5%)
  between operations  0.75 us (2%)
    ppermute x16, starting transfers between devices, shift(): lax.ppermute(array, axis, [(n, (n + by) % size) for n in range(size)])  20.9 us
    ppermute x16, waiting for transfers between devices, shift(): lax.ppermute(array, axis, [(n, (n + by) % size) for n in range(size)])  14.4 us
    pallas_call x1, Pallas kernels, per_device(): pl.pallas_call(functools.partial(grads_kernel, outer), out_shape=(shape(q...  3.99 us
    unnamed x10, local copies, waits for them, and re-layouts  2.43 us
    pallas_call x1, Pallas kernels, per_device(): pl.pallas_call(stats_kernel, out_shape=shape(all_stats, jnp.float32), in_...  1.9 us
  transfers between devices with their start and end apart: 16, of which 9 were waited for; matrix products, arithmetic and copies ran while one was open for 0% of the time, Pallas kernels for 3%

profile of v4, /device:TPU:0, one launch (start us, length us, event | category | flops | bytes accessed | tf_op | source)
XLA Modules:
  0.0 46.6 jit_solution(9317121206427214041)
XLA Ops:
  0.6 3.0 %collective-permute-start = (bf16[128,640]{1,0:T(8,128)(2,1)}, bf16[128,640]{1,0:T(8,128)(2,1)S(1)}, u32[]{:S(2)}, u32[]{:S(2)}) collective-permute-start(bf16[128,640]{1,0:T(8,128)(2,1)} %q_ref.1), channel_id=1, source_target_pairs={{0,4},{4,0},{1,5},{5,1},{2,6},{6,2},{3,7},{7,3},{8,12},{12,8},{9,1... | collective-permute-start | bytes 491528 | tf_op jit(solution)/shard_map/ppermute | solution.py:294
  3.7 0.1 collective-permute-start.1
  3.7 0.0 copy-start
  3.7 0.8 %copy-done = bf16[32,512]{1,0:T(8,128)(2,1)S(1)} copy-done((bf16[32,512]{1,0:T(8,128)(2,1)S(1)}, bf16[32,512]{1,0:T(8,128)(2,1)}, u32[]{:S(2)}) %copy-start) | copy-done | bytes 32792
  4.5 0.0 copy-start.1
  4.5 0.8 %copy-done.1 = bf16[32,512]{1,0:T(8,128)(2,1)S(1)} copy-done((bf16[32,512]{1,0:T(8,128)(2,1)S(1)}, bf16[32,512]{1,0:T(8,128)(2,1)}, u32[]{:S(2)}) %copy-start.1) | copy-done | bytes 32792
  5.3 0.0 copy-start.3
  5.3 0.1 split.1
  5.4 0.1 collective-permute-start.2
  5.4 2.0 %collective-permute-start.3 = (bf16[32,256]{1,0:T(8,128)(2,1)S(1)}, bf16[32,256]{1,0:T(8,128)(2,1)S(1)}, u32[]{:S(2)}, u32[]{:S(2)}) collective-permute-start(bf16[32,256]{1,0:T(8,128)(2,1)S(1)} %get-tuple-element.25), channel_id=1, source_target_pairs={{0,2},{1,3},{2,0},{3,1},{4,6},{5,7},{6,4},{7,5},{8,10},{9,11},{10,... | collective-permute-start | bytes 49160 | tf_op jit(solution)/shard_map/ppermute | solution.py:294
  7.4 1.4 %collective-permute-start.4 = (bf16[32,256]{1,0:T(8,128)(2,1)S(1)}, bf16[32,256]{1,0:T(8,128)(2,1)S(1)}, u32[]{:S(2)}, u32[]{:S(2)}) collective-permute-start(bf16[32,256]{1,0:T(8,128)(2,1)S(1)} %get-tuple-element.26), channel_id=1, source_target_pairs={{0,3},{1,0},{2,1},{3,2},{4,7},{5,4},{6,5},{7,6},{8,11},{9,8},{10,9... | collective-permute-start | bytes 49160 | tf_op jit(solution)/shard_map/ppermute | solution.py:294
  8.8 0.0 collective-permute-done.2.refs_1_
  8.8 0.4 collective-permute-done.3.refs_2_
  9.2 1.0 %collective-permute-done.4.refs_3_ = bf16[32,256]{1,0:T(8,128)(2,1)S(1)} collective-permute-done((bf16[32,256]{1,0:T(8,128)(2,1)S(1)}, bf16[32,256]{1,0:T(8,128)(2,1)S(1)}, u32[]{:S(2)}, u32[]{:S(2)}) %collective-permute-start.4) | collective-permute-done | bytes 16416 | tf_op jit(solution)/shard_map/ppermute | solution.py:294
  10.3 0.0 copy-start.2
  10.3 0.1 join.1.refs_0_
  10.4 3.7 %collective-permute-start.7 = (bf16[128,256]{1,0:T(8,128)(2,1)S(1)}, bf16[128,256]{1,0:T(8,128)(2,1)S(1)}, u32[]{:S(2)}, u32[]{:S(2)}) collective-permute-start(bf16[128,256]{1,0:T(8,128)(2,1)S(1)} %join.1.refs_0_), channel_id=1, source_target_pairs={{0,24},{8,0},{16,8},{24,16},{1,25},{9,1},{17,9},{25,17},{2,26},{10... | collective-permute-start | bytes 196616 | tf_op jit(solution)/shard_map/ppermute | solution.py:294
  14.0 0.0 collective-permute-start.6
  14.0 1.0 %collective-permute-start.5 = (bf16[128,256]{1,0:T(8,128)(2,1)S(1)}, bf16[128,256]{1,0:T(8,128)(2,1)S(1)}, u32[]{:S(2)}, u32[]{:S(2)}) collective-permute-start(bf16[128,256]{1,0:T(8,128)(2,1)S(1)} %join.1.refs_0_), channel_id=1, source_target_pairs={{0,8},{8,16},{16,24},{24,0},{1,9},{9,17},{17,25},{25,1},{2,10},{10... | collective-permute-start | bytes 196616 | tf_op jit(solution)/shard_map/ppermute | solution.py:294
  15.1 0.0 collective-permute-done.q2_ref
  15.1 0.0 collective-permute-done.1.do2_ref
  15.1 0.0 copy-done.3
  15.1 0.0 copy-done.2
  15.1 0.0 copy-start.4
  15.1 0.9 %copy-done.4 = bf16[128,640]{1,0:T(8,128)(2,1)S(1)} copy-done((bf16[128,640]{1,0:T(8,128)(2,1)S(1)}, bf16[128,640]{1,0:T(8,128)(2,1)}, u32[]{:S(2)}) %copy-start.4) | copy-done | bytes 163864
  16.0 0.7 %stack.1 = (bf16[2,2,320,128]{3,2,1,0:T(8,128)(2,1)S(1)}, bf16[2,2,320,128]{3,2,1,0:T(8,128)(2,1)S(1)}) custom-call(s32[16]{0:T(128)S(1)} %copy-done.2, bf16[128,640]{1,0:T(8,128)(2,1)S(1)} %copy-done.3, bf16[128,640]{1,0:T(8,128)(2,1)S(1)} %copy-done.4, bf16[128,640]{1,0:T(8,128)(2,1)S(1)} %collective-permute-done.q2_ref, ...), custom_call_target="tpu_custom_call" | custom-call | flops 20000000000 | bytes 1000000 | tf_op jit(solution)/shard_map/stack/pallas_call | solution.py:322
  16.7 0.0 collective-permute-done.7.refs_3_
  16.7 4.9 %collective-permute-done.6.refs_2_ = bf16[128,256]{1,0:T(8,128)(2,1)S(1)} collective-permute-done((bf16[128,256]{1,0:T(8,128)(2,1)S(1)}, bf16[128,256]{1,0:T(8,128)(2,1)S(1)}, u32[]{:S(2)}, u32[]{:S(2)}) %collective-permute-start.6) | collective-permute-done | bytes 65568 | tf_op jit(solution)/shard_map/ppermute | solution.py:294
  21.6 0.0 collective-permute-done.5.refs_1_
  21.6 1.9 %stats.1.refs_4_ = f32[12,320]{1,0:T(8,128)S(1)} custom-call(s32[16]{0:T(128)S(1)} %copy-done.2, bf16[2,2,320,128]{3,2,1,0:T(8,128)(2,1)S(1)} %get-tuple-element.21.qs_ref, bf16[2,2,320,128]{3,2,1,0:T(8,128)(2,1)S(1)} %get-tuple-element.22.ds_ref, bf16[128,256]{1,0:T(8,128)(2,1)S(1)} %join.1.refs_0_, bf16[128,256]{1,0:T(8,128)(2,1)S(1)} %collective-permute-done.5.refs_1_, ...), custom_call_target="tpu_custom_call" | custom-call | tf_op jit(solution)/shard_map/stats/pallas_call | solution.py:335
  23.5 1.6 %collective-permute-start.8 = (f32[12,320]{1,0:T(8,128)S(1)}, f32[12,320]{1,0:T(8,128)S(1)}, u32[]{:S(2)}, u32[]{:S(2)}) collective-permute-start(f32[12,320]{1,0:T(8,128)S(1)} %stats.1.refs_4_), channel_id=1, source_target_pairs={{0,4},{4,0},{1,5},{5,1},{2,6},{6,2},{3,7},{7,3},{8,12},{12,8},{9,1... | collective-permute-start | bytes 46088 | tf_op jit(solution)/shard_map/ppermute | solution.py:294
  25.1 2.3 %collective-permute-done.8.refs_5_ = f32[12,320]{1,0:T(8,128)S(1)} collective-permute-done((f32[12,320]{1,0:T(8,128)S(1)}, f32[12,320]{1,0:T(8,128)S(1)}, u32[]{:S(2)}, u32[]{:S(2)}) %collective-permute-start.8) | collective-permute-done | bytes 15392 | tf_op jit(solution)/shard_map/ppermute | solution.py:294
  27.4 4.0 %grads.1 = (f32[128,640]{1,0:T(8,128)S(1)}, bf16[128,640]{1,0:T(8,128)(2,1)S(1)}, f32[128,256]{1,0:T(8,128)S(1)}, bf16[128,256]{1,0:T(8,128)(2,1)S(1)}, bf16[128...) custom-call(s32[16]{0:T(128)S(1)} %copy-done.2, bf16[2,2,320,128]{3,2,1,0:T(8,128)(2,1)S(1)} %get-tuple-element.21.qs_ref, ...), custom_call_target="tpu_custom_call" | custom-call | tf_op jit(solution)/shard_map/grads/pallas_call | solution.py:352
  31.4 1.6 %collective-permute-start.9 = (bf16[128,640]{1,0:T(8,128)(2,1)S(1)}, bf16[128,640]{1,0:T(8,128)(2,1)S(1)}, u32[]{:S(2)}, u32[]{:S(2)}) collective-permute-start(bf16[128,640]{1,0:T(8,128)(2,1)S(1)} %get-tuple-element.28), channel_id=1, source_target_pairs={{0,4},{4,0},{1,5},{5,1},{2,6},{6,2},{3,7},{7,3},{8,12},{12,8},{9,1... | collective-permute-start | bytes 491528 | tf_op jit(solution)/shard_map/ppermute | solution.py:294
  33.0 1.6 %collective-permute-start.10 = (bf16[128,256]{1,0:T(8,128)(2,1)S(1)}, bf16[128,256]{1,0:T(8,128)(2,1)S(1)}, u32[]{:S(2)}, u32[]{:S(2)}) collective-permute-start(bf16[128,256]{1,0:T(8,128)(2,1)S(1)} %get-tuple-element.30), channel_id=1, source_target_pairs={{0,24},{8,0},{16,8},{24,16},{1,25},{9,1},{17,9},{25,17},{2,26},{10... | collective-permute-start | bytes 196616 | tf_op jit(solution)/shard_map/ppermute | solution.py:294
  34.6 0.2 collective-permute-start.11
  34.7 2.0 %collective-permute-start.12 = (bf16[128,256]{1,0:T(8,128)(2,1)S(1)}, bf16[128,256]{1,0:T(8,128)(2,1)S(1)}, u32[]{:S(2)}, u32[]{:S(2)}) collective-permute-start(bf16[128,256]{1,0:T(8,128)(2,1)S(1)} %get-tuple-element.32), channel_id=1, source_target_pairs={{0,8},{8,16},{16,24},{24,0},{1,9},{9,17},{17,25},{25,1},{2,10},{10... | collective-permute-start | bytes 196616 | tf_op jit(solution)/shard_map/ppermute | solution.py:294
  36.8 0.5 %collective-permute-done.10.refs_1_ = bf16[128,256]{1,0:T(8,128)(2,1)S(1)} collective-permute-done((bf16[128,256]{1,0:T(8,128)(2,1)S(1)}, bf16[128,256]{1,0:T(8,128)(2,1)S(1)}, u32[]{:S(2)}, u32[]{:S(2)}) %collective-permute-start.10) | collective-permute-done | bytes 65568 | tf_op jit(solution)/shard_map/ppermute | solution.py:294
  37.3 3.7 %collective-permute-done.11.refs_2_ = bf16[128,256]{1,0:T(8,128)(2,1)S(1)} collective-permute-done((bf16[128,256]{1,0:T(8,128)(2,1)S(1)}, bf16[128,256]{1,0:T(8,128)(2,1)S(1)}, u32[]{:S(2)}, u32[]{:S(2)}) %collective-permute-start.11) | collective-permute-done | bytes 65568 | tf_op jit(solution)/shard_map/ppermute | solution.py:294
  41.0 0.0 collective-permute-done.12.refs_3_
  41.1 0.1 collective-permute-start.13
  41.1 1.3 %collective-permute-start.14 = (bf16[32,256]{1,0:T(8,128)(2,1)S(1)}, bf16[32,256]{1,0:T(8,128)(2,1)S(1)}, u32[]{:S(2)}, u32[]{:S(2)}) collective-permute-start(bf16[32,256]{1,0:T(8,128)(2,1)S(1)} %get-tuple-element.35), channel_id=1, source_target_pairs={{0,2},{1,3},{2,0},{3,1},{4,6},{5,7},{6,4},{7,5},{8,10},{9,11},{10,... | collective-permute-start | bytes 49160 | tf_op jit(solution)/shard_map/ppermute | solution.py:294
  42.4 1.4 %collective-permute-start.15 = (bf16[32,256]{1,0:T(8,128)(2,1)S(1)}, bf16[32,256]{1,0:T(8,128)(2,1)S(1)}, u32[]{:S(2)}, u32[]{:S(2)}) collective-permute-start(bf16[32,256]{1,0:T(8,128)(2,1)S(1)} %get-tuple-element.36), channel_id=1, source_target_pairs={{0,3},{1,0},{2,1},{3,2},{4,7},{5,4},{6,5},{7,6},{8,11},{9,8},{10,9... | collective-permute-start | bytes 49160 | tf_op jit(solution)/shard_map/ppermute | solution.py:294
  43.8 0.5 %collective-permute-done.13.refs_1_ = bf16[32,256]{1,0:T(8,128)(2,1)S(1)} collective-permute-done((bf16[32,256]{1,0:T(8,128)(2,1)S(1)}, bf16[32,256]{1,0:T(8,128)(2,1)S(1)}, u32[]{:S(2)}, u32[]{:S(2)}) %collective-permute-start.13) | collective-permute-done | bytes 16416 | tf_op jit(solution)/shard_map/ppermute | solution.py:294
  44.3 0.7 %collective-permute-done.14.refs_2_ = bf16[32,256]{1,0:T(8,128)(2,1)S(1)} collective-permute-done((bf16[32,256]{1,0:T(8,128)(2,1)S(1)}, bf16[32,256]{1,0:T(8,128)(2,1)S(1)}, u32[]{:S(2)}, u32[]{:S(2)}) %collective-permute-start.14) | collective-permute-done | bytes 16416 | tf_op jit(solution)/shard_map/ppermute | solution.py:294
  44.9 0.3 collective-permute-done.15.refs_3_
  45.2 0.7 %place.1 = (bf16[32,512]{1,0:T(8,128)(2,1)}, bf16[32,512]{1,0:T(8,128)(2,1)}) custom-call(bf16[32,256]{1,0:T(8,128)(2,1)S(1)} %get-tuple-element.33.refs_0_, bf16[32,256]{1,0:T(8,128)(2,1)S(1)} %collective-permute-done.13.refs_1_, bf16[32,256]{1,0:T(8,128)(2,1)S(1)} %collective-permute-done.14.refs_2_, bf16[32,256]{1,0:T(8,128)(2,1)S(1)} %collective-permute-done.15.refs_3_), custom_call_target="tpu_custom_call" | custom-call | tf_op jit(solution)/shard_map/place/pallas_call | solution.py:397
  45.9 0.0 collective-permute-done.9.received_ref
  45.9 0.7 %finish.1 = bf16[128,640]{1,0:T(8,128)(2,1)} custom-call(f32[128,640]{1,0:T(8,128)S(1)} %get-tuple-element.27.own_ref, bf16[128,640]{1,0:T(8,128)(2,1)S(1)} %collective-permute-done.9.received_ref), custom_call_target="tpu_custom_call" | custom-call | flops 20000000000 | bytes 1000000 | tf_op jit(solution)/shard_map/finish/pallas_call | solution.py:378
  (1 shorter events, 0.0 us)
Async XLA Ops:
  0.6 14.4 %collective-permute-start = (bf16[128,640]{1,0:T(8,128)(2,1)}, bf16[128,640]{1,0:T(8,128)(2,1)S(1)}, u32[]{:S(2)}, u32[]{:S(2)}) collective-permute-start(bf16[128,640]{1,0:T(8,128)(2,1)} %q_ref.1), channel_id=1, source_target_pairs={{0,4},{4,0},{1,5},{5,1},{2,6},{6,2},{3,7},{7,3},{8,12},{12,8},{9,1... | collective-permute-start | bytes 491528 | tf_op jit(solution)/shard_map/ppermute | solution.py:294
  3.7 11.4 %collective-permute-start.1 = (bf16[128,640]{1,0:T(8,128)(2,1)}, bf16[128,640]{1,0:T(8,128)(2,1)S(1)}, u32[]{:S(2)}, u32[]{:S(2)}) collective-permute-start(bf16[128,640]{1,0:T(8,128)(2,1)} %do_ref.1), channel_id=1, source_target_pairs={{0,4},{4,0},{1,5},{5,1},{2,6},{6,2},{3,7},{7,3},{8,12},{12,8},{9,1... | collective-permute-start | bytes 491528 | tf_op jit(solution)/shard_map/ppermute | solution.py:294
  3.7 0.8 %copy-start = (bf16[32,512]{1,0:T(8,128)(2,1)S(1)}, bf16[32,512]{1,0:T(8,128)(2,1)}, u32[]{:S(2)}) copy-start(bf16[32,512]{1,0:T(8,128)(2,1)} %keys_ref.1) | copy-start | bytes 98308
  4.5 0.8 %copy-start.1 = (bf16[32,512]{1,0:T(8,128)(2,1)S(1)}, bf16[32,512]{1,0:T(8,128)(2,1)}, u32[]{:S(2)}) copy-start(bf16[32,512]{1,0:T(8,128)(2,1)} %values_ref.1) | copy-start | bytes 98308
  5.3 9.8 %copy-start.3 = (bf16[128,640]{1,0:T(8,128)(2,1)S(1)}, bf16[128,640]{1,0:T(8,128)(2,1)}, u32[]{:S(2)}) copy-start(bf16[128,640]{1,0:T(8,128)(2,1)} %q_ref.1) | copy-start | bytes 491524
  5.4 3.4 %collective-permute-start.2 = (bf16[32,256]{1,0:T(8,128)(2,1)S(1)}, bf16[32,256]{1,0:T(8,128)(2,1)S(1)}, u32[]{:S(2)}, u32[]{:S(2)}) collective-permute-start(bf16[32,256]{1,0:T(8,128)(2,1)S(1)} %get-tuple-element.24), channel_id=1, source_target_pairs={{0,1},{1,2},{2,3},{3,0},{4,5},{5,6},{6,7},{7,4},{8,9},{9,10},{10,1... | collective-permute-start | bytes 49160 | tf_op jit(solution)/shard_map/ppermute | solution.py:294
  5.4 3.8 %collective-permute-start.3 = (bf16[32,256]{1,0:T(8,128)(2,1)S(1)}, bf16[32,256]{1,0:T(8,128)(2,1)S(1)}, u32[]{:S(2)}, u32[]{:S(2)}) collective-permute-start(bf16[32,256]{1,0:T(8,128)(2,1)S(1)} %get-tuple-element.25), channel_id=1, source_target_pairs={{0,2},{1,3},{2,0},{3,1},{4,6},{5,7},{6,4},{7,5},{8,10},{9,11},{10,... | collective-permute-start | bytes 49160 | tf_op jit(solution)/shard_map/ppermute | solution.py:294
  7.4 2.8 %collective-permute-start.4 = (bf16[32,256]{1,0:T(8,128)(2,1)S(1)}, bf16[32,256]{1,0:T(8,128)(2,1)S(1)}, u32[]{:S(2)}, u32[]{:S(2)}) collective-permute-start(bf16[32,256]{1,0:T(8,128)(2,1)S(1)} %get-tuple-element.26), channel_id=1, source_target_pairs={{0,3},{1,0},{2,1},{3,2},{4,7},{5,4},{6,5},{7,6},{8,11},{9,8},{10,9... | collective-permute-start | bytes 49160 | tf_op jit(solution)/shard_map/ppermute | solution.py:294
  10.3 4.8 %copy-start.2 = (s32[16]{0:T(128)S(1)}, s32[16]{0:T(128)}, u32[]{:S(2)}) copy-start(s32[16]{0:T(128)} %order_ref.5) | copy-start | bytes 196
  10.4 6.3 %collective-permute-start.7 = (bf16[128,256]{1,0:T(8,128)(2,1)S(1)}, bf16[128,256]{1,0:T(8,128)(2,1)S(1)}, u32[]{:S(2)}, u32[]{:S(2)}) collective-permute-start(bf16[128,256]{1,0:T(8,128)(2,1)S(1)} %join.1.refs_0_), channel_id=1, source_target_pairs={{0,24},{8,0},{16,8},{24,16},{1,25},{9,1},{17,9},{25,17},{2,26},{10... | collective-permute-start | bytes 196616 | tf_op jit(solution)/shard_map/ppermute | solution.py:294
  14.0 7.6 %collective-permute-start.6 = (bf16[128,256]{1,0:T(8,128)(2,1)S(1)}, bf16[128,256]{1,0:T(8,128)(2,1)S(1)}, u32[]{:S(2)}, u32[]{:S(2)}) collective-permute-start(bf16[128,256]{1,0:T(8,128)(2,1)S(1)} %join.1.refs_0_), channel_id=1, source_target_pairs={{0,16},{8,24},{16,0},{24,8},{1,17},{9,25},{17,1},{25,9},{2,18},{10... | collective-permute-start | bytes 196616 | tf_op jit(solution)/shard_map/ppermute | solution.py:294
  14.0 7.6 %collective-permute-start.5 = (bf16[128,256]{1,0:T(8,128)(2,1)S(1)}, bf16[128,256]{1,0:T(8,128)(2,1)S(1)}, u32[]{:S(2)}, u32[]{:S(2)}) collective-permute-start(bf16[128,256]{1,0:T(8,128)(2,1)S(1)} %join.1.refs_0_), channel_id=1, source_target_pairs={{0,8},{8,16},{16,24},{24,0},{1,9},{9,17},{17,25},{25,1},{2,10},{10... | collective-permute-start | bytes 196616 | tf_op jit(solution)/shard_map/ppermute | solution.py:294
  15.1 0.9 %copy-start.4 = (bf16[128,640]{1,0:T(8,128)(2,1)S(1)}, bf16[128,640]{1,0:T(8,128)(2,1)}, u32[]{:S(2)}) copy-start(bf16[128,640]{1,0:T(8,128)(2,1)} %do_ref.1) | copy-start | bytes 491524
  23.5 3.9 %collective-permute-start.8 = (f32[12,320]{1,0:T(8,128)S(1)}, f32[12,320]{1,0:T(8,128)S(1)}, u32[]{:S(2)}, u32[]{:S(2)}) collective-permute-start(f32[12,320]{1,0:T(8,128)S(1)} %stats.1.refs_4_), channel_id=1, source_target_pairs={{0,4},{4,0},{1,5},{5,1},{2,6},{6,2},{3,7},{7,3},{8,12},{12,8},{9,1... | collective-permute-start | bytes 46088 | tf_op jit(solution)/shard_map/ppermute | solution.py:294
  31.4 14.5 %collective-permute-start.9 = (bf16[128,640]{1,0:T(8,128)(2,1)S(1)}, bf16[128,640]{1,0:T(8,128)(2,1)S(1)}, u32[]{:S(2)}, u32[]{:S(2)}) collective-permute-start(bf16[128,640]{1,0:T(8,128)(2,1)S(1)} %get-tuple-element.28), channel_id=1, source_target_pairs={{0,4},{4,0},{1,5},{5,1},{2,6},{6,2},{3,7},{7,3},{8,12},{12,8},{9,1... | collective-permute-start | bytes 491528 | tf_op jit(solution)/shard_map/ppermute | solution.py:294
  33.0 4.3 %collective-permute-start.10 = (bf16[128,256]{1,0:T(8,128)(2,1)S(1)}, bf16[128,256]{1,0:T(8,128)(2,1)S(1)}, u32[]{:S(2)}, u32[]{:S(2)}) collective-permute-start(bf16[128,256]{1,0:T(8,128)(2,1)S(1)} %get-tuple-element.30), channel_id=1, source_target_pairs={{0,24},{8,0},{16,8},{24,16},{1,25},{9,1},{17,9},{25,17},{2,26},{10... | collective-permute-start | bytes 196616 | tf_op jit(solution)/shard_map/ppermute | solution.py:294
  34.6 6.5 %collective-permute-start.11 = (bf16[128,256]{1,0:T(8,128)(2,1)S(1)}, bf16[128,256]{1,0:T(8,128)(2,1)S(1)}, u32[]{:S(2)}, u32[]{:S(2)}) collective-permute-start(bf16[128,256]{1,0:T(8,128)(2,1)S(1)} %get-tuple-element.31), channel_id=1, source_target_pairs={{0,16},{8,24},{16,0},{24,8},{1,17},{9,25},{17,1},{25,9},{2,18},{10... | collective-permute-start | bytes 196616 | tf_op jit(solution)/shard_map/ppermute | solution.py:294
  34.7 6.3 %collective-permute-start.12 = (bf16[128,256]{1,0:T(8,128)(2,1)S(1)}, bf16[128,256]{1,0:T(8,128)(2,1)S(1)}, u32[]{:S(2)}, u32[]{:S(2)}) collective-permute-start(bf16[128,256]{1,0:T(8,128)(2,1)S(1)} %get-tuple-element.32), channel_id=1, source_target_pairs={{0,8},{8,16},{16,24},{24,0},{1,9},{9,17},{17,25},{25,1},{2,10},{10... | collective-permute-start | bytes 196616 | tf_op jit(solution)/shard_map/ppermute | solution.py:294
  41.1 3.2 %collective-permute-start.13 = (bf16[32,256]{1,0:T(8,128)(2,1)S(1)}, bf16[32,256]{1,0:T(8,128)(2,1)S(1)}, u32[]{:S(2)}, u32[]{:S(2)}) collective-permute-start(bf16[32,256]{1,0:T(8,128)(2,1)S(1)} %get-tuple-element.34), channel_id=1, source_target_pairs={{0,1},{1,2},{2,3},{3,0},{4,5},{5,6},{6,7},{7,4},{8,9},{9,10},{10,1... | collective-permute-start | bytes 49160 | tf_op jit(solution)/shard_map/ppermute | solution.py:294
  41.1 3.8 %collective-permute-start.14 = (bf16[32,256]{1,0:T(8,128)(2,1)S(1)}, bf16[32,256]{1,0:T(8,128)(2,1)S(1)}, u32[]{:S(2)}, u32[]{:S(2)}) collective-permute-start(bf16[32,256]{1,0:T(8,128)(2,1)S(1)} %get-tuple-element.35), channel_id=1, source_target_pairs={{0,2},{1,3},{2,0},{3,1},{4,6},{5,7},{6,4},{7,5},{8,10},{9,11},{10,... | collective-permute-start | bytes 49160 | tf_op jit(solution)/shard_map/ppermute | solution.py:294
  42.4 2.8 %collective-permute-start.15 = (bf16[32,256]{1,0:T(8,128)(2,1)S(1)}, bf16[32,256]{1,0:T(8,128)(2,1)S(1)}, u32[]{:S(2)}, u32[]{:S(2)}) collective-permute-start(bf16[32,256]{1,0:T(8,128)(2,1)S(1)} %get-tuple-element.36), channel_id=1, source_target_pairs={{0,3},{1,0},{2,1},{3,2},{4,7},{5,4},{6,5},{7,6},{8,11},{9,8},{10,9... | collective-permute-start | bytes 49160 | tf_op jit(solution)/shard_map/ppermute | solution.py:294

commit v5 on v4

v5 whole, which is shorter than its diff:
```python
import functools
import math

import jax
import jax.numpy as jnp
from jax import lax
from jax.experimental import pallas as pl
from jax.experimental.pallas import tpu as pltpu
from jax.sharding import Mesh
from jax.sharding import PartitionSpec as P

HEADS = 20
KV_HEADS = 4
HEAD = 128
GROUP = HEADS // KV_HEADS
SCALE = HEAD ** (-0.5)
EXPONENT_SCALE = SCALE * math.log2(math.e)
LOWEST = -1e30
ROWS_DOT_ROWS = (((1,), (1,)), ((), ()))
COLS_DOT_COLS = (((0,), (0,)), ((), ()))


def at_rows(start, size):
    return pl.ds(pl.multiple_of(start, size), size)


def load(source_ref, target_ref, sem):
    copy = pltpu.make_async_copy(source_ref, target_ref, sem)
    copy.start()
    return copy


def wait_all(copies):
    for copy in copies:
        copy.wait()


class Work:
    def __init__(self, order_ref, half_rows, outer):
        self.half_rows, self.outer = half_rows, outer
        self.slab_rows = half_rows // outer
        self.chunk = math.gcd(256, half_rows)
        at, side = lax.axis_index("outer"), lax.axis_index("pair")

        def pair_of(index):
            first, second = order_ref[2 * index], order_ref[2 * index + 1]
            return jnp.minimum(first, second), jnp.where(first < second, 0, 1)

        self.owners = [pair_of(2 * at + side), pair_of(2 * at + 1 - side)]
        self.pairs = [pair_of(2 * lax.rem(at + outer - d, outer) + side) for d in range(outer)]

    def query_slot(self, owner, half):
        place = self.owners[owner][1]
        return jnp.where(half == 0, place, 1 - place)

    def key_slot(self, d, half):
        place = self.pairs[d][1]
        return place if half == 0 else 1 - place

    def blocks(self, body):
        rows = self.slab_rows
        for owner in range(2):
            for first in range(0, self.half_rows, self.chunk):
                body(owner, 1, 0, first, self.chunk, first, False)
            for d in range(self.outer):
                if owner == 0 and d == 0:
                    body(owner, 0, 0, 0, rows, self.half_rows, True)
                    body(owner, 1, 1, 0, rows, 2 * self.half_rows, True)
                else:
                    half = jnp.where(self.owners[owner][0] >= self.pairs[d][0], 0, 1)
                    body(owner, half, half, d * rows, rows, self.half_rows + d * rows, False)


def split_kernel(keys_ref, values_ref, q_ref, do_ref, *refs):
    parts, (qd_ref, sems) = refs[:-2], refs[-2:]
    kvh = len(parts)
    copies = []
    for e, part_ref in enumerate(parts):
        head = lax.rem(lax.axis_index("kvh") + e, kvh)
        cols = at_rows(head * HEAD, HEAD)
        for n, source_ref in enumerate((keys_ref, values_ref)):
            copies.append((source_ref.at[:, cols], part_ref.at[:, pl.ds(n * HEAD, HEAD)]))
    rows = q_ref.shape[0] // 2
    for n, source_ref in enumerate((q_ref, do_ref)):
        for slot in range(2):
            for h in range(GROUP):
                copies.append((
                    source_ref.at[pl.ds(slot * rows, rows), pl.ds(h * HEAD, HEAD)],
                    qd_ref.at[n, slot, pl.ds(h * rows, rows)],
                ))
    wait_all([load(*copy, sems.at[n]) for n, copy in enumerate(copies)])


def join_kernel(*refs):
    parts, (out_ref, sems) = refs[:-2], refs[-2:]
    kvh = len(parts)
    rows = parts[0].shape[0]
    copies = []
    for e, part_ref in enumerate(parts):
        source = lax.rem(lax.axis_index("kvh") + kvh - e, kvh)
        copies.append(load(part_ref, out_ref.at[at_rows(source * rows, rows)], sems.at[e]))
    wait_all(copies)


def stats_kernel(order_ref, own_ref, other_ref, *refs):
    kv_refs, (out_ref, e_ref, dp_ref, ks_ref, m_ref, l_ref, d_ref, sems) = refs[:-8], refs[-8:]
    work = Work(order_ref, ks_ref.shape[1], len(kv_refs))
    rows = work.slab_rows
    copies = []
    for d, kv_ref in enumerate(kv_refs):
        for half in range(2):
            source = at_rows(work.key_slot(d, half) * rows, rows)
            copies.append(
                load(kv_ref.at[source], ks_ref.at[half, pl.ds(d * rows, rows)], sems.at[2 * d + half])
            )
    m_ref[...] = jnp.full(m_ref.shape, LOWEST, jnp.float32)
    l_ref[...] = jnp.zeros(l_ref.shape, jnp.float32)
    d_ref[...] = jnp.zeros(d_ref.shape, jnp.float32)
    wait_all(copies)
    qd_refs = (own_ref, other_ref)

    def maximum(owner, q_half, k_half, first, size, place, masked):
        slot = work.query_slot(owner, q_half)
        scores = lax.dot_general(
            ks_ref[k_half, pl.ds(first, size), :HEAD],
            qd_refs[owner][0, slot],
            ROWS_DOT_ROWS,
            preferred_element_type=jnp.float32,
        )
        if masked:
            key = lax.broadcasted_iota(jnp.int32, scores.shape, 0)
            query = lax.rem(lax.broadcasted_iota(jnp.int32, (1, scores.shape[1]), 1), rows)
            scores = jnp.where(key <= query, scores, LOWEST)
        e_ref[owner, pl.ds(place, size), :] = scores
        m_ref[owner, q_half] = jnp.maximum(
            m_ref[owner, q_half], jnp.max(scores, axis=0, keepdims=True)
        )
        dp_ref[owner, pl.ds(place, size), :] = lax.dot_general(
            ks_ref[k_half, pl.ds(first, size), HEAD:],
            qd_refs[owner][1, slot],
            ROWS_DOT_ROWS,
            preferred_element_type=jnp.float32,
        )

    work.blocks(maximum)

    def sums(owner, q_half, k_half, first, size, place, masked):
        scores = e_ref[owner, pl.ds(place, size), :]
        grads = dp_ref[owner, pl.ds(place, size), :]
        expon = jnp.exp2((scores - m_ref[owner, q_half]) * EXPONENT_SCALE)
        e_ref[owner, pl.ds(place, size), :] = expon
        l_ref[owner, q_half] = l_ref[owner, q_half] + jnp.sum(expon, axis=0, keepdims=True)
        d_ref[owner, q_half] = d_ref[owner, q_half] + jnp.sum(expon * grads, axis=0, keepdims=True)

    work.blocks(sums)
    for owner in range(2):
        for half in range(2):
            base = (2 * owner + half) * 3
            out_ref[base : base + 1, :] = m_ref[owner, half]
            out_ref[base + 1 : base + 2, :] = l_ref[owner, half]
            out_ref[base + 2 : base + 3, :] = d_ref[owner, half]


def grads_kernel(outer, order_ref, own_ref, other_ref, mine_ref, theirs_ref, e_ref, dp_ref, *refs):
    term_refs, (gs_ref, w_ref, d_ref, acc_ref) = refs[:outer], refs[outer:]
    work = Work(order_ref, acc_ref.shape[1], outer)
    rows = work.slab_rows
    acc_ref[...] = jnp.zeros(acc_ref.shape, jnp.float32)
    for owner in range(2):
        for half in range(2):
            base = (2 * owner + half) * 3
            base2 = (2 * (1 - owner) + half) * 3
            m1, m2 = mine_ref[base : base + 1, :], theirs_ref[base2 : base2 + 1, :]
            top = jnp.maximum(m1, m2)
            w1 = jnp.exp2((m1 - top) * EXPONENT_SCALE)
            w2 = jnp.exp2((m2 - top) * EXPONENT_SCALE)
            total = w1 * mine_ref[base + 1 : base + 2, :] + w2 * theirs_ref[base2 + 1 : base2 + 2, :]
            delta = w1 * mine_ref[base + 2 : base + 3, :] + w2 * theirs_ref[base2 + 2 : base2 + 3, :]
            w_ref[owner, half] = w1 / total
            d_ref[owner, half] = delta / total
    qd_refs = (own_ref, other_ref)

    def gradients(owner, q_half, k_half, first, size, place, masked):
        slot = work.query_slot(owner, q_half)
        here = pl.ds(place, size)
        probs = e_ref[owner, here, :] * w_ref[owner, q_half]
        score_grads = (probs * (dp_ref[owner, here, :] - d_ref[owner, q_half])).astype(jnp.bfloat16)
        gs_ref[owner, here, :] = score_grads
        keys = pl.ds(first, size)
        acc_ref[k_half, keys, HEAD:] = acc_ref[k_half, keys, HEAD:] + jnp.dot(
            probs.astype(jnp.bfloat16), qd_refs[owner][1, slot], preferred_element_type=jnp.float32
        )
        acc_ref[k_half, keys, :HEAD] = acc_ref[k_half, keys, :HEAD] + jnp.dot(
            score_grads, qd_refs[owner][0, slot], preferred_element_type=jnp.float32
        )

    work.blocks(gradients)
    for d, term_ref in enumerate(term_refs):
        for half in range(2):
            target = at_rows(work.key_slot(d, half) * rows, rows)
            source = slice(d * rows, (d + 1) * rows)
            term_ref[target, :HEAD] = (acc_ref[half, source, :HEAD] * SCALE).astype(term_ref.dtype)
            term_ref[target, HEAD:] = acc_ref[half, source, HEAD:].astype(term_ref.dtype)


def query_kernel(outer, order_ref, gs_ref, ks_ref, own_ref, other_ref, acc_ref):
    work = Work(order_ref, ks_ref.shape[1], outer)
    rows = work.slab_rows
    acc_ref[...] = jnp.zeros(acc_ref.shape, jnp.float32)

    def terms(owner, q_half, k_half, first, size, place, masked):
        acc_ref[owner, q_half] = acc_ref[owner, q_half] + lax.dot_general(
            ks_ref[k_half, pl.ds(first, size), :HEAD],
            gs_ref[owner, pl.ds(place, size), :],
            COLS_DOT_COLS,
            preferred_element_type=jnp.float32,
        )

    work.blocks(terms)
    for owner, target in ((0, own_ref), (1, other_ref)):
        for half in range(2):
            place = at_rows(work.query_slot(owner, half) * rows, rows)
            grads = (jnp.transpose(acc_ref[owner, half]) * SCALE).astype(target.dtype)
            for h in range(GROUP):
                target[place, h * HEAD : (h + 1) * HEAD] = grads[h * rows : (h + 1) * rows, :]


def sum_kernel(outer, *refs):
    terms, outs, total_ref = refs[:outer], refs[outer:-1], refs[-1]
    total = terms[0][...]
    for term_ref in terms[1:]:
        total = total + term_ref[...].astype(jnp.float32)
    total_ref[...] = total
    kvh = len(outs)
    rows = outs[0].shape[0]
    for e, out_ref in enumerate(outs):
        target = lax.rem(lax.axis_index("kvh") + e, kvh)
        out_ref[...] = total_ref[at_rows(target * rows, rows), :].astype(jnp.bfloat16)


def place_kernel(own_ref, received_ref, *refs):
    parts, (dq_out, key_out, value_out, dq_ref, sems) = refs[:-5], refs[-5:]
    kvh = len(parts)
    copies = []
    for e, part_ref in enumerate(parts):
        head = lax.rem(lax.axis_index("kvh") + kvh - e, kvh)
        cols = at_rows(head * HEAD, HEAD)
        copies.append(load(part_ref.at[:, pl.ds(0, HEAD)], key_out.at[:, cols], sems.at[2 * e]))
        copies.append(load(part_ref.at[:, pl.ds(HEAD, HEAD)], value_out.at[:, cols], sems.at[2 * e + 1]))
    dq_ref[...] = (own_ref[...] + received_ref[...].astype(jnp.float32)).astype(jnp.bfloat16)
    copies.append(load(dq_ref, dq_out, sems.at[2 * kvh]))
    wait_all(copies)


def per_device(queries, keys, values, d_out, slab_order):
    kvh = lax.axis_size("kvh")
    outer = lax.axis_size("outer")
    local_rows, query_width = queries.shape
    cache_rows = keys.shape[0]
    slab_rows = local_rows // 2
    half_rows = outer * slab_rows
    columns = GROUP * slab_rows
    params = pltpu.CompilerParams(vmem_limit_bytes=(8 << 20) + (10 << 10) * 2 * half_rows)
    beside = pl.CostEstimate(flops=2 * 10**10, bytes_accessed=10**6, transcendentals=0)
    vmem = pl.BlockSpec(memory_space=pltpu.VMEM)
    smem = pl.BlockSpec(memory_space=pltpu.SMEM)
    anywhere = pl.BlockSpec(memory_space=pl.ANY)
    shape = jax.ShapeDtypeStruct
    dma = pltpu.SemaphoreType.DMA
    low, full = jnp.bfloat16, jnp.float32

    def call(kernel, name, limit=params, **arguments):
        return pl.pallas_call(kernel, compiler_params=limit, name=name, **arguments)

    def shift(array, axis, by):
        size = lax.axis_size(axis)
        return lax.ppermute(array, axis, [(n, (n + by) % size) for n in range(size)])

    part = shape((cache_rows, 2 * HEAD), low)
    block = shape((local_rows, 2 * HEAD), low)
    *parts, own_qd = call(
        split_kernel,
        "split",
        out_shape=(part,) * kvh + (shape((2, 2, columns, HEAD), low),),
        limit=pltpu.CompilerParams(vmem_limit_bytes=56 << 20),
        in_specs=[anywhere] * 4,
        out_specs=(anywhere,) * (kvh + 1),
        scratch_shapes=[dma((2 * kvh + 4 * GROUP,))],
    )(keys, values, queries, d_out)
    parts = [parts[0]] + [shift(parts[e], "kvh", e) for e in range(1, kvh)]
    other_qd = shift(own_qd, "pair", 1)
    own_block = call(
        join_kernel,
        "join",
        out_shape=block,
        in_specs=[anywhere] * kvh,
        out_specs=vmem,
        scratch_shapes=[dma((kvh,))],
    )(*parts)
    blocks = [own_block] + [shift(own_block, "outer", d) for d in range(1, outer)]

    all_stats = shape((12, columns), full)
    score_rows = (2, 2 * half_rows + slab_rows, columns)
    row_stat = pltpu.VMEM((2, 2, 1, columns), full)
    stats, expon, grad_probs, sorted_keys = call(
        stats_kernel,
        "stats",
        out_shape=(
            all_stats,
            shape(score_rows, full),
            shape(score_rows, full),
            shape((2, half_rows, 2 * HEAD), low),
        ),
        in_specs=[smem, vmem, vmem] + [anywhere] * outer,
        out_specs=(vmem,) * 4,
        scratch_shapes=[row_stat, row_stat, row_stat, dma((2 * outer,))],
    )(slab_order, own_qd, other_qd, *blocks)
    stats2 = shift(stats, "pair", 1)
    *terms, score_grads = call(
        functools.partial(grads_kernel, outer),
        "grads",
        out_shape=(shape(block.shape, full),) + (block,) * (outer - 1) + (shape(score_rows, low),),
        in_specs=[smem] + [vmem] * 6,
        out_specs=(vmem,) * (outer + 1),
        scratch_shapes=[row_stat, row_stat, pltpu.VMEM((2, half_rows, 2 * HEAD), full)],
    )(slab_order, own_qd, other_qd, stats, stats2, expon, grad_probs)
    terms = [terms[0]] + [shift(terms[d], "outer", -d) for d in range(1, outer)]
    own_grads, other_grads = call(
        functools.partial(query_kernel, outer),
        "query_terms",
        out_shape=(shape(queries.shape, full), shape(queries.shape, low)),
        in_specs=[smem, vmem, vmem],
        out_specs=(vmem, vmem),
        scratch_shapes=[pltpu.VMEM((2, 2, HEAD, columns), full)],
        cost_estimate=beside,
    )(slab_order, score_grads, sorted_keys)
    received_grads = shift(other_grads, "pair", 1)
    owned = call(
        functools.partial(sum_kernel, outer),
        "sum",
        out_shape=(part,) * kvh,
        in_specs=[vmem] * outer,
        out_specs=(vmem,) * kvh,
        scratch_shapes=[pltpu.VMEM(block.shape, full)],
    )(*terms)
    owned = [owned[0]] + [shift(owned[e], "kvh", e) for e in range(1, kvh)]
    return call(
        place_kernel,
        "place",
        out_shape=(shape(queries.shape, low), shape(keys.shape, low), shape(values.shape, low)),
        in_specs=[vmem, vmem] + [anywhere] * kvh,
        out_specs=(anywhere,) * 3,
        scratch_shapes=[pltpu.VMEM(queries.shape, low), dma((2 * kvh + 1,))],
    )(own_grads, received_grads, *owned)


def solution(mesh):
    kvh = mesh.shape["kvh"]
    pairs = mesh.shape["seq"] // 2
    paired = Mesh(mesh.devices.reshape(pairs, 2, kvh), ("outer", "pair", "kvh"))
    seq = ("outer", "pair")
    cache = P(("outer", "pair", "kvh"), None)
    placed = (P(seq, "kvh"), cache, cache, P(seq, "kvh"), P())
    return jax.shard_map(
        per_device,
        mesh=paired,
        in_specs=placed,
        out_specs=(P(seq, "kvh"), cache, cache),
        check_vma=False,
    )
```

time: 47.4 us -> 58.6 us (1.24)
  Pallas kernels: 8.22 us -> 19.3 us
  waiting for transfers between devices: 14.4 us -> 17.2 us
  starting transfers between devices: 20.9 us -> 18.1 us
    pallas_call x8 -> x7, Pallas kernels: 8.22 us -> 19.3 us  [the longest x1 13.3 us: per_device(): call(split_kernel, 'split', out_shape=(part,) * kvh + (shape((2, 2, colum...]
    ppermute x16 -> x15, waiting for transfers between devices: 14.4 us -> 17.2 us  [shift(): lax.ppermute(array, axis, [(n, (n + by) % size) for n in range(size)])]
    ppermute x16 -> x15, starting transfers between devices: 20.9 us -> 18.1 us  [shift(): lax.ppermute(array, axis, [(n, (n + by) % size) for n in range(size)])]
    unnamed x10 -> x8, local copies, waits for them, and re-layouts: 2.43 us -> 2.35 us
  transfers between devices with their start and end apart: 16 -> 15, of which waited for: 9 -> 11; matrix products, arithmetic and copies ran while one was open for 0% -> 0% of each run, Pallas kernels for 3% -> 0%
where the time goes in v5:
time: 58.6 us; the launch traced here: 57.7 us
  Pallas kernels  19.3 us (33%)
  starting transfers between devices  18.1 us (31%)
  waiting for transfers between devices  17.2 us (29%)
  local copies, waits for them, and re-layouts  2.35 us (4%)
  between operations  0.71 us (1%)
    ppermute x15, starting transfers between devices, shift(): lax.ppermute(array, axis, [(n, (n + by) % size) for n in range(size)])  18.1 us
    ppermute x15, waiting for transfers between devices, shift(): lax.ppermute(array, axis, [(n, (n + by) % size) for n in range(size)])  17.2 us
    pallas_call x1, Pallas kernels, per_device(): call(split_kernel, 'split', out_shape=(part,) * kvh + (shape((2, 2, colum...  13.3 us
    unnamed x8, local copies, waits for them, and re-layouts  2.35 us
    pallas_call x1, Pallas kernels, per_device(): call(stats_kernel, 'stats', out_shape=(all_stats, shape(score_rows, full)...  2.33 us
    pallas_call x1, Pallas kernels, per_device(): call(functools.partial(grads_kernel, outer), 'grads', out_shape=(shape(bl...  1.46 us
    pallas_call x1, Pallas kernels, per_device(): call(functools.partial(query_kernel, outer), 'query_terms', out_shape=(sh...  1.3 us
  transfers between devices with their start and end apart: 15, of which 11 were waited for; matrix products, arithmetic and copies ran while one was open for 0% of the time, Pallas kernels for 0%

profile of v5, /device:TPU:0, one launch (start us, length us, event | category | flops | bytes accessed | tf_op | source)
XLA Modules:
  0.0 57.7 jit_solution(16636832010619076362)
XLA Ops:
  0.6 13.3 %split.1 = (bf16[32,256]{1,0:T(8,128)(2,1)}, bf16[32,256]{1,0:T(8,128)(2,1)}, bf16[32,256]{1,0:T(8,128)(2,1)}, bf16[32,256]{1,0:T(8,128)(2,1)}, bf16[2,2,320,128]{3,2,1,0:T(8,128)(2,1)}) custom-call(bf16[32,512]{1,0:T(8,128)(2,1)} %keys_ref.1, bf16[32,512]{1,0:T(8,128)(2,1)} %values_ref.1, bf16[128,640]{1,0:T(8,128)(2,1)} %q_ref.1, bf16[128,640]{1,0:T(8,128)(2,1)} %do_ref.1), custom_call_target="tpu_custom_call" | custom-call | tf_op jit(solution)/shard_map/split/pallas_call | solution.py:281
  13.9 3.0 %collective-permute-start = (bf16[2,2,320,128]{3,2,1,0:T(8,128)(2,1)}, bf16[2,2,320,128]{3,2,1,0:T(8,128)(2,1)S(1)}, u32[]{:S(2)}, u32[]{:S(2)}) collective-permute-start(bf16[2,2,320,128]{3,2,1,0:T(8,128)(2,1)} %get-tuple-element.23.own_ref), channel_id=1, source_target_pairs={{0,4},{4,0},{1,5},{5,1},{2,6},{6,2},{3,7},{7,3},{8,12},{12,8},{9,1... | collective-permute-start | bytes 983048 | tf_op jit(solution)/shard_map/ppermute | solution.py:277
  16.9 0.0 collective-permute-start.1
  17.0 1.5 %collective-permute-start.2 = (bf16[32,256]{1,0:T(8,128)(2,1)}, bf16[32,256]{1,0:T(8,128)(2,1)S(1)}, u32[]{:S(2)}, u32[]{:S(2)}) collective-permute-start(bf16[32,256]{1,0:T(8,128)(2,1)} %get-tuple-element.26), channel_id=1, source_target_pairs={{0,2},{1,3},{2,0},{3,1},{4,6},{5,7},{6,4},{7,5},{8,10},{9,11},{10,... | collective-permute-start | bytes 49160 | tf_op jit(solution)/shard_map/ppermute | solution.py:277
  18.5 1.4 %collective-permute-start.3 = (bf16[32,256]{1,0:T(8,128)(2,1)}, bf16[32,256]{1,0:T(8,128)(2,1)S(1)}, u32[]{:S(2)}, u32[]{:S(2)}) collective-permute-start(bf16[32,256]{1,0:T(8,128)(2,1)} %get-tuple-element.27), channel_id=1, source_target_pairs={{0,3},{1,0},{2,1},{3,2},{4,7},{5,4},{6,5},{7,6},{8,11},{9,8},{10,9... | collective-permute-start | bytes 49160 | tf_op jit(solution)/shard_map/ppermute | solution.py:277
  19.9 0.4 collective-permute-done.1.refs_1_
  20.3 0.6 %collective-permute-done.2.refs_2_ = bf16[32,256]{1,0:T(8,128)(2,1)S(1)} collective-permute-done((bf16[32,256]{1,0:T(8,128)(2,1)}, bf16[32,256]{1,0:T(8,128)(2,1)S(1)}, u32[]{:S(2)}, u32[]{:S(2)}) %collective-permute-start.2) | collective-permute-done | bytes 16416 | tf_op jit(solution)/shard_map/ppermute | solution.py:277
  20.9 0.6 %collective-permute-done.3.refs_3_ = bf16[32,256]{1,0:T(8,128)(2,1)S(1)} collective-permute-done((bf16[32,256]{1,0:T(8,128)(2,1)}, bf16[32,256]{1,0:T(8,128)(2,1)S(1)}, u32[]{:S(2)}, u32[]{:S(2)}) %collective-permute-start.3) | collective-permute-done | bytes 16416 | tf_op jit(solution)/shard_map/ppermute | solution.py:277
  21.6 0.0 copy-start.1
  21.6 0.7 %copy-done.1 = bf16[32,256]{1,0:T(8,128)(2,1)S(1)} copy-done((bf16[32,256]{1,0:T(8,128)(2,1)S(1)}, bf16[32,256]{1,0:T(8,128)(2,1)}, u32[]{:S(2)}) %copy-start.1) | copy-done | bytes 16408
  22.3 0.1 join.1.refs_0_
  22.4 3.7 %collective-permute-start.6 = (bf16[128,256]{1,0:T(8,128)(2,1)S(1)}, bf16[128,256]{1,0:T(8,128)(2,1)S(1)}, u32[]{:S(2)}, u32[]{:S(2)}) collective-permute-start(bf16[128,256]{1,0:T(8,128)(2,1)S(1)} %join.1.refs_0_), channel_id=1, source_target_pairs={{0,24},{8,0},{16,8},{24,16},{1,25},{9,1},{17,9},{25,17},{2,26},{10... | collective-permute-start | bytes 196616 | tf_op jit(solution)/shard_map/ppermute | solution.py:277
  26.0 0.0 collective-permute-start.5
  26.0 1.0 %collective-permute-start.4 = (bf16[128,256]{1,0:T(8,128)(2,1)S(1)}, bf16[128,256]{1,0:T(8,128)(2,1)S(1)}, u32[]{:S(2)}, u32[]{:S(2)}) collective-permute-start(bf16[128,256]{1,0:T(8,128)(2,1)S(1)} %join.1.refs_0_), channel_id=1, source_target_pairs={{0,8},{8,16},{16,24},{24,0},{1,9},{9,17},{17,25},{25,1},{2,10},{10... | collective-permute-start | bytes 196616 | tf_op jit(solution)/shard_map/ppermute | solution.py:277
  27.1 1.5 %collective-permute-done.6.refs_3_ = bf16[128,256]{1,0:T(8,128)(2,1)S(1)} collective-permute-done((bf16[128,256]{1,0:T(8,128)(2,1)S(1)}, bf16[128,256]{1,0:T(8,128)(2,1)S(1)}, u32[]{:S(2)}, u32[]{:S(2)}) %collective-permute-start.6) | collective-permute-done | bytes 65568 | tf_op jit(solution)/shard_map/ppermute | solution.py:277
  28.6 5.0 %collective-permute-done.5.refs_2_ = bf16[128,256]{1,0:T(8,128)(2,1)S(1)} collective-permute-done((bf16[128,256]{1,0:T(8,128)(2,1)S(1)}, bf16[128,256]{1,0:T(8,128)(2,1)S(1)}, u32[]{:S(2)}, u32[]{:S(2)}) %collective-permute-start.5) | collective-permute-done | bytes 65568 | tf_op jit(solution)/shard_map/ppermute | solution.py:277
  33.6 0.0 collective-permute-done.4.refs_1_
  33.6 0.0 collective-permute-done.other_ref
  33.6 0.0 copy-start
  33.6 1.0 %copy-done = bf16[2,2,320,128]{3,2,1,0:T(8,128)(2,1)S(1)} copy-done((bf16[2,2,320,128]{3,2,1,0:T(8,128)(2,1)S(1)}, bf16[2,2,320,128]{3,2,1,0:T(8,128)(2,1)}, u32[]{:S(2)}) %copy-start) | copy-done | bytes 327704
  34.6 0.0 copy-start.2
  34.6 0.7 %copy-done.2 = s32[16]{0:T(128)S(1)} copy-done((s32[16]{0:T(128)S(1)}, s32[16]{0:T(128)}, u32[]{:S(2)}) %copy-start.2) | copy-done | bytes 88
  35.2 2.3 %stats.1 = (f32[12,320]{1,0:T(8,128)S(1)}, f32[2,576,320]{2,1,0:T(8,128)S(1)}, f32[2,576,320]{2,1,0:T(8,128)S(1)}, bf16[2,256,256]{2,1,0:T(8,128)(2,1)S(1)}) custom-call(s32[16]{0:T(128)S(1)} %copy-done.2, bf16[2,2,320,128]{3,2,1,0:T(8,128)(2,1)S(1)} %copy-done, bf16[2,2,320,128]{3,2,1,0:T(8,128)(2,1)S(1)} %collective-permute-done.other_ref, ...), custom_call_target="tpu_custom_call" | custom-call | tf_op jit(solution)/shard_map/stats/pallas_call | solution.py:305
  37.6 0.6 collective-permute-start.7
  38.1 3.3 %collective-permute-done.7.theirs_ref = f32[12,320]{1,0:T(8,128)S(1)} collective-permute-done((f32[12,320]{1,0:T(8,128)S(1)}, f32[12,320]{1,0:T(8,128)S(1)}, u32[]{:S(2)}, u32[]{:S(2)}) %collective-permute-start.7) | collective-permute-done | bytes 15392 | tf_op jit(solution)/shard_map/ppermute | solution.py:277
  41.5 0.0 copy-start.3
  41.5 1.5 %grads.1 = (f32[128,256]{1,0:T(8,128)S(1)}, bf16[128,256]{1,0:T(8,128)(2,1)S(1)}, bf16[128,256]{1,0:T(8,128)(2,1)S(1)}, bf16[128,256]{1,0:T(8,128)(2,1)S(1)}, bf16[2,576,320]{2,1,0:T(8,128)(2,1)S(1)}) custom-call(s32[16]{0:T(128)S(1)} %copy-done.2, bf16[2,2,320,128]{3,2,1,0:T(8,128)(2,1)S(1)} %copy-done, ...), custom_call_target="tpu_custom_call" | custom-call | tf_op jit(solution)/shard_map/grads/pallas_call | solution.py:319
  42.9 0.0 copy-done.3
  42.9 1.3 %query_terms.1 = (f32[128,640]{1,0:T(8,128)S(1)}, bf16[128,640]{1,0:T(8,128)(2,1)S(1)}) custom-call(s32[16]{0:T(128)S(1)} %copy-done.3, bf16[2,576,320]{2,1,0:T(8,128)(2,1)S(1)} %get-tuple-element.31.gs_ref, bf16[2,256,256]{2,1,0:T(8,128)(2,1)S(1)} %get-tuple-element.32.ks_ref), custom_call_target="tpu_custom_call" | custom-call | flops 20000000000 | bytes 1000000 | tf_op jit(solution)/shard_map/query_terms/pallas_call | solution.py:328
  44.2 0.6 collective-permute-start.8
  44.8 1.6 %collective-permute-start.9 = (bf16[128,256]{1,0:T(8,128)(2,1)S(1)}, bf16[128,256]{1,0:T(8,128)(2,1)S(1)}, u32[]{:S(2)}, u32[]{:S(2)}) collective-permute-start(bf16[128,256]{1,0:T(8,128)(2,1)S(1)} %get-tuple-element.36), channel_id=1, source_target_pairs={{0,24},{8,0},{16,8},{24,16},{1,25},{9,1},{17,9},{25,17},{2,26},{10... | collective-permute-start | bytes 196616 | tf_op jit(solution)/shard_map/ppermute | solution.py:277
  46.4 0.2 collective-permute-start.10
  46.6 2.0 %collective-permute-start.11 = (bf16[128,256]{1,0:T(8,128)(2,1)S(1)}, bf16[128,256]{1,0:T(8,128)(2,1)S(1)}, u32[]{:S(2)}, u32[]{:S(2)}) collective-permute-start(bf16[128,256]{1,0:T(8,128)(2,1)S(1)} %get-tuple-element.38), channel_id=1, source_target_pairs={{0,8},{8,16},{16,24},{24,0},{1,9},{9,17},{17,25},{25,1},{2,10},{10... | collective-permute-start | bytes 196616 | tf_op jit(solution)/shard_map/ppermute | solution.py:277
  48.6 0.6 collective-permute-done.9.refs_1_
  49.1 3.7 %collective-permute-done.10.refs_2_ = bf16[128,256]{1,0:T(8,128)(2,1)S(1)} collective-permute-done((bf16[128,256]{1,0:T(8,128)(2,1)S(1)}, bf16[128,256]{1,0:T(8,128)(2,1)S(1)}, u32[]{:S(2)}, u32[]{:S(2)}) %collective-permute-start.10) | collective-permute-done | bytes 65568 | tf_op jit(solution)/shard_map/ppermute | solution.py:277
  52.8 0.0 collective-permute-done.11.refs_3_
  52.9 0.1 collective-permute-start.12
  53.0 1.1 %collective-permute-start.13 = (bf16[32,256]{1,0:T(8,128)(2,1)S(1)}, bf16[32,256]{1,0:T(8,128)(2,1)S(1)}, u32[]{:S(2)}, u32[]{:S(2)}) collective-permute-start(bf16[32,256]{1,0:T(8,128)(2,1)S(1)} %get-tuple-element.41), channel_id=1, source_target_pairs={{0,2},{1,3},{2,0},{3,1},{4,6},{5,7},{6,4},{7,5},{8,10},{9,11},{10,... | collective-permute-start | bytes 49160 | tf_op jit(solution)/shard_map/ppermute | solution.py:277
  54.1 1.4 %collective-permute-start.14 = (bf16[32,256]{1,0:T(8,128)(2,1)S(1)}, bf16[32,256]{1,0:T(8,128)(2,1)S(1)}, u32[]{:S(2)}, u32[]{:S(2)}) collective-permute-start(bf16[32,256]{1,0:T(8,128)(2,1)S(1)} %get-tuple-element.42), channel_id=1, source_target_pairs={{0,3},{1,0},{2,1},{3,2},{4,7},{5,4},{6,5},{7,6},{8,11},{9,8},{10,9... | collective-permute-start | bytes 49160 | tf_op jit(solution)/shard_map/ppermute | solution.py:277
  55.5 0.6 %collective-permute-done.12.refs_1_ = bf16[32,256]{1,0:T(8,128)(2,1)S(1)} collective-permute-done((bf16[32,256]{1,0:T(8,128)(2,1)S(1)}, bf16[32,256]{1,0:T(8,128)(2,1)S(1)}, u32[]{:S(2)}, u32[]{:S(2)}) %collective-permute-start.12) | collective-permute-done | bytes 16416 | tf_op jit(solution)/shard_map/ppermute | solution.py:277
  56.1 0.7 %collective-permute-done.13.refs_2_ = bf16[32,256]{1,0:T(8,128)(2,1)S(1)} collective-permute-done((bf16[32,256]{1,0:T(8,128)(2,1)S(1)}, bf16[32,256]{1,0:T(8,128)(2,1)S(1)}, u32[]{:S(2)}, u32[]{:S(2)}) %collective-permute-start.13) | collective-permute-done | bytes 16416 | tf_op jit(solution)/shard_map/ppermute | solution.py:277
  56.8 0.1 collective-permute-done.14.refs_3_
  56.9 0.0 collective-permute-done.8.received_ref
  56.9 0.8 %place.1 = (bf16[128,640]{1,0:T(8,128)(2,1)}, bf16[32,512]{1,0:T(8,128)(2,1)}, bf16[32,512]{1,0:T(8,128)(2,1)}) custom-call(f32[128,640]{1,0:T(8,128)S(1)} %get-tuple-element.33.own_ref, bf16[128,640]{1,0:T(8,128)(2,1)S(1)} %collective-permute-done.8.received_ref, bf16[32,256]{1,0:T(8,128)(2,1)S(1)} %get-tuple-element.39.refs_0_, ...), custom_call_target="tpu_custom_call" | custom-call | tf_op jit(solution)/shard_map/place/pallas_call | solution.py:347
  (1 shorter events, 0.0 us)
Async XLA Ops:
  13.9 19.7 %collective-permute-start = (bf16[2,2,320,128]{3,2,1,0:T(8,128)(2,1)}, bf16[2,2,320,128]{3,2,1,0:T(8,128)(2,1)S(1)}, u32[]{:S(2)}, u32[]{:S(2)}) collective-permute-start(bf16[2,2,320,128]{3,2,1,0:T(8,128)(2,1)} %get-tuple-element.23.own_ref), channel_id=1, source_target_pairs={{0,4},{4,0},{1,5},{5,1},{2,6},{6,2},{3,7},{7,3},{8,12},{12,8},{9,1... | collective-permute-start | bytes 983048 | tf_op jit(solution)/shard_map/ppermute | solution.py:277
  16.9 3.4 %collective-permute-start.1 = (bf16[32,256]{1,0:T(8,128)(2,1)}, bf16[32,256]{1,0:T(8,128)(2,1)S(1)}, u32[]{:S(2)}, u32[]{:S(2)}) collective-permute-start(bf16[32,256]{1,0:T(8,128)(2,1)} %get-tuple-element.25), channel_id=1, source_target_pairs={{0,1},{1,2},{2,3},{3,0},{4,5},{5,6},{6,7},{7,4},{8,9},{9,10},{10,1... | collective-permute-start | bytes 49160 | tf_op jit(solution)/shard_map/ppermute | solution.py:277
  17.0 4.0 %collective-permute-start.2 = (bf16[32,256]{1,0:T(8,128)(2,1)}, bf16[32,256]{1,0:T(8,128)(2,1)S(1)}, u32[]{:S(2)}, u32[]{:S(2)}) collective-permute-start(bf16[32,256]{1,0:T(8,128)(2,1)} %get-tuple-element.26), channel_id=1, source_target_pairs={{0,2},{1,3},{2,0},{3,1},{4,6},{5,7},{6,4},{7,5},{8,10},{9,11},{10,... | collective-permute-start | bytes 49160 | tf_op jit(solution)/shard_map/ppermute | solution.py:277
  18.5 3.1 %collective-permute-start.3 = (bf16[32,256]{1,0:T(8,128)(2,1)}, bf16[32,256]{1,0:T(8,128)(2,1)S(1)}, u32[]{:S(2)}, u32[]{:S(2)}) collective-permute-start(bf16[32,256]{1,0:T(8,128)(2,1)} %get-tuple-element.27), channel_id=1, source_target_pairs={{0,3},{1,0},{2,1},{3,2},{4,7},{5,4},{6,5},{7,6},{8,11},{9,8},{10,9... | collective-permute-start | bytes 49160 | tf_op jit(solution)/shard_map/ppermute | solution.py:277
  21.6 0.7 %copy-start.1 = (bf16[32,256]{1,0:T(8,128)(2,1)S(1)}, bf16[32,256]{1,0:T(8,128)(2,1)}, u32[]{:S(2)}) copy-start(bf16[32,256]{1,0:T(8,128)(2,1)} %get-tuple-element.24.refs_0_) | copy-start | bytes 49156
  22.4 6.2 %collective-permute-start.6 = (bf16[128,256]{1,0:T(8,128)(2,1)S(1)}, bf16[128,256]{1,0:T(8,128)(2,1)S(1)}, u32[]{:S(2)}, u32[]{:S(2)}) collective-permute-start(bf16[128,256]{1,0:T(8,128)(2,1)S(1)} %join.1.refs_0_), channel_id=1, source_target_pairs={{0,24},{8,0},{16,8},{24,16},{1,25},{9,1},{17,9},{25,17},{2,26},{10... | collective-permute-start | bytes 196616 | tf_op jit(solution)/shard_map/ppermute | solution.py:277
  26.0 7.6 %collective-permute-start.5 = (bf16[128,256]{1,0:T(8,128)(2,1)S(1)}, bf16[128,256]{1,0:T(8,128)(2,1)S(1)}, u32[]{:S(2)}, u32[]{:S(2)}) collective-permute-start(bf16[128,256]{1,0:T(8,128)(2,1)S(1)} %join.1.refs_0_), channel_id=1, source_target_pairs={{0,16},{8,24},{16,0},{24,8},{1,17},{9,25},{17,1},{25,9},{2,18},{10... | collective-permute-start | bytes 196616 | tf_op jit(solution)/shard_map/ppermute | solution.py:277
  26.0 7.6 %collective-permute-start.4 = (bf16[128,256]{1,0:T(8,128)(2,1)S(1)}, bf16[128,256]{1,0:T(8,128)(2,1)S(1)}, u32[]{:S(2)}, u32[]{:S(2)}) collective-permute-start(bf16[128,256]{1,0:T(8,128)(2,1)S(1)} %join.1.refs_0_), channel_id=1, source_target_pairs={{0,8},{8,16},{16,24},{24,0},{1,9},{9,17},{17,25},{25,1},{2,10},{10... | collective-permute-start | bytes 196616 | tf_op jit(solution)/shard_map/ppermute | solution.py:277
  33.6 1.0 %copy-start = (bf16[2,2,320,128]{3,2,1,0:T(8,128)(2,1)S(1)}, bf16[2,2,320,128]{3,2,1,0:T(8,128)(2,1)}, u32[]{:S(2)}) copy-start(bf16[2,2,320,128]{3,2,1,0:T(8,128)(2,1)} %get-tuple-element.23.own_ref) | copy-start | bytes 983044
  34.6 0.7 %copy-start.2 = (s32[16]{0:T(128)S(1)}, s32[16]{0:T(128)}, u32[]{:S(2)}) copy-start(s32[16]{0:T(128)} %order_ref.5) | copy-start | bytes 196
  37.6 3.9 %collective-permute-start.7 = (f32[12,320]{1,0:T(8,128)S(1)}, f32[12,320]{1,0:T(8,128)S(1)}, u32[]{:S(2)}, u32[]{:S(2)}) collective-permute-start(f32[12,320]{1,0:T(8,128)S(1)} %get-tuple-element.28.mine_ref), channel_id=1, source_target_pairs={{0,4},{4,0},{1,5},{5,1},{2,6},{6,2},{3,7},{7,3},{8,12},{12,8},{9,1... | collective-permute-start | bytes 46088 | tf_op jit(solution)/shard_map/ppermute | solution.py:277
  41.5 1.5 %copy-start.3 = (s32[16]{0:T(128)S(1)}, s32[16]{0:T(128)}, u32[]{:S(2)}) copy-start(s32[16]{0:T(128)} %order_ref.5) | copy-start | bytes 196
  44.2 12.7 %collective-permute-start.8 = (bf16[128,640]{1,0:T(8,128)(2,1)S(1)}, bf16[128,640]{1,0:T(8,128)(2,1)S(1)}, u32[]{:S(2)}, u32[]{:S(2)}) collective-permute-start(bf16[128,640]{1,0:T(8,128)(2,1)S(1)} %get-tuple-element.34), channel_id=1, source_target_pairs={{0,4},{4,0},{1,5},{5,1},{2,6},{6,2},{3,7},{7,3},{8,12},{12,8},{9,1... | collective-permute-start | bytes 491528 | tf_op jit(solution)/shard_map/ppermute | solution.py:277
  44.8 4.3 %collective-permute-start.9 = (bf16[128,256]{1,0:T(8,128)(2,1)S(1)}, bf16[128,256]{1,0:T(8,128)(2,1)S(1)}, u32[]{:S(2)}, u32[]{:S(2)}) collective-permute-start(bf16[128,256]{1,0:T(8,128)(2,1)S(1)} %get-tuple-element.36), channel_id=1, source_target_pairs={{0,24},{8,0},{16,8},{24,16},{1,25},{9,1},{17,9},{25,17},{2,26},{10... | collective-permute-start | bytes 196616 | tf_op jit(solution)/shard_map/ppermute | solution.py:277
  46.4 6.5 %collective-permute-start.10 = (bf16[128,256]{1,0:T(8,128)(2,1)S(1)}, bf16[128,256]{1,0:T(8,128)(2,1)S(1)}, u32[]{:S(2)}, u32[]{:S(2)}) collective-permute-start(bf16[128,256]{1,0:T(8,128)(2,1)S(1)} %get-tuple-element.37), channel_id=1, source_target_pairs={{0,16},{8,24},{16,0},{24,8},{1,17},{9,25},{17,1},{25,9},{2,18},{10... | collective-permute-start | bytes 196616 | tf_op jit(solution)/shard_map/ppermute | solution.py:277
  46.6 6.3 %collective-permute-start.11 = (bf16[128,256]{1,0:T(8,128)(2,1)S(1)}, bf16[128,256]{1,0:T(8,128)(2,1)S(1)}, u32[]{:S(2)}, u32[]{:S(2)}) collective-permute-start(bf16[128,256]{1,0:T(8,128)(2,1)S(1)} %get-tuple-element.38), channel_id=1, source_target_pairs={{0,8},{8,16},{16,24},{24,0},{1,9},{9,17},{17,25},{25,1},{2,10},{10... | collective-permute-start | bytes 196616 | tf_op jit(solution)/shard_map/ppermute | solution.py:277
  52.9 3.2 %collective-permute-start.12 = (bf16[32,256]{1,0:T(8,128)(2,1)S(1)}, bf16[32,256]{1,0:T(8,128)(2,1)S(1)}, u32[]{:S(2)}, u32[]{:S(2)}) collective-permute-start(bf16[32,256]{1,0:T(8,128)(2,1)S(1)} %get-tuple-element.40), channel_id=1, source_target_pairs={{0,1},{1,2},{2,3},{3,0},{4,5},{5,6},{6,7},{7,4},{8,9},{9,10},{10,1... | collective-permute-start | bytes 49160 | tf_op jit(solution)/shard_map/ppermute | solution.py:277
  53.0 3.8 %collective-permute-start.13 = (bf16[32,256]{1,0:T(8,128)(2,1)S(1)}, bf16[32,256]{1,0:T(8,128)(2,1)S(1)}, u32[]{:S(2)}, u32[]{:S(2)}) collective-permute-start(bf16[32,256]{1,0:T(8,128)(2,1)S(1)} %get-tuple-element.41), channel_id=1, source_target_pairs={{0,2},{1,3},{2,0},{3,1},{4,6},{5,7},{6,4},{7,5},{8,10},{9,11},{10,... | collective-permute-start | bytes 49160 | tf_op jit(solution)/shard_map/ppermute | solution.py:277
  54.1 2.8 %collective-permute-start.14 = (bf16[32,256]{1,0:T(8,128)(2,1)S(1)}, bf16[32,256]{1,0:T(8,128)(2,1)S(1)}, u32[]{:S(2)}, u32[]{:S(2)}) collective-permute-start(bf16[32,256]{1,0:T(8,128)(2,1)S(1)} %get-tuple-element.42), channel_id=1, source_target_pairs={{0,3},{1,0},{2,1},{3,2},{4,7},{5,4},{6,5},{7,6},{8,11},{9,8},{10,9... | collective-permute-start | bytes 49160 | tf_op jit(solution)/shard_map/ppermute | solution.py:277

commit v6 on v5

v6 whole, which is shorter than its diff:
```python
import functools
import math

import jax
import jax.numpy as jnp
from jax import lax
from jax.experimental import pallas as pl
from jax.experimental.pallas import tpu as pltpu
from jax.sharding import Mesh
from jax.sharding import PartitionSpec as P

HEADS = 20
KV_HEADS = 4
HEAD = 128
GROUP = HEADS // KV_HEADS
SCALE = HEAD ** (-0.5)
EXPONENT_SCALE = SCALE * math.log2(math.e)
LOWEST = -1e30
ROWS_DOT_ROWS = (((1,), (1,)), ((), ()))
COLS_DOT_COLS = (((0,), (0,)), ((), ()))


def at_rows(start, size):
    return pl.ds(pl.multiple_of(start, size), size)


def load(source_ref, target_ref, sem):
    copy = pltpu.make_async_copy(source_ref, target_ref, sem)
    copy.start()
    return copy


def wait_all(copies):
    for copy in copies:
        copy.wait()


class Work:
    def __init__(self, order_ref, slab_rows, outer):
        self.slab_rows = slab_rows
        at, side = lax.axis_index("outer"), lax.axis_index("pair")

        def pair_of(index):
            first, second = order_ref[2 * index], order_ref[2 * index + 1]
            return jnp.minimum(first, second), jnp.where(first < second, 0, 1)

        self.owners = [pair_of(2 * at + side), pair_of(2 * at + 1 - side)]
        self.pairs = [pair_of(2 * lax.rem(at + outer - d, outer) + side) for d in range(outer)]

    def query_slot(self, owner, half):
        place = self.owners[owner][1]
        return jnp.where(half == 0, place, 1 - place)

    def key_slot(self, d, half):
        place = self.pairs[d][1]
        return place if half == 0 else 1 - place

    def blocks(self, members, body):
        rows = self.slab_rows
        half_rows = len(members) * rows
        chunk = math.gcd(256, half_rows)
        for owner in range(2):
            for first in range(0, half_rows, chunk):
                body(owner, 1, 0, first, chunk, first, False)
            for n, d in enumerate(members):
                if owner == 0 and d == 0:
                    body(owner, 0, 0, n * rows, rows, half_rows + n * rows, True)
                    body(owner, 1, 1, n * rows, rows, 2 * half_rows, True)
                else:
                    half = jnp.where(self.owners[owner][0] >= self.pairs[d][0], 0, 1)
                    body(owner, half, half, n * rows, rows, half_rows + n * rows, False)


def split_kernel(cache_ref, *refs):
    parts, sems = refs[:-1], refs[-1]
    kvh = len(parts)
    rows = parts[0].shape[0]
    copies = []
    for e, part_ref in enumerate(parts):
        head = lax.rem(lax.axis_index("kvh") + e, kvh)
        cols = at_rows(head * HEAD, HEAD)
        for n in range(2):
            source = cache_ref.at[pl.ds(n * rows, rows), cols]
            copies.append(load(source, part_ref.at[:, pl.ds(n * HEAD, HEAD)], sems.at[2 * e + n]))
    wait_all(copies)


def stack_kernel(q_ref, do_ref, after_ref, out_ref):
    rows = q_ref.shape[0] // 2
    for n, source_ref in enumerate((q_ref, do_ref)):
        for slot in range(2):
            for h in range(GROUP):
                out_ref[n, slot, h * rows : (h + 1) * rows, :] = source_ref[
                    slot * rows : (slot + 1) * rows, h * HEAD : (h + 1) * HEAD
                ]


def join_kernel(*refs):
    parts, (out_ref, sems) = refs[:-2], refs[-2:]
    kvh = len(parts)
    rows = parts[0].shape[0]
    copies = []
    for e, part_ref in enumerate(parts):
        source = lax.rem(lax.axis_index("kvh") + kvh - e, kvh)
        copies.append(load(part_ref, out_ref.at[at_rows(source * rows, rows)], sems.at[e]))
    wait_all(copies)


def stats_kernel(outer, members, order_ref, own_ref, other_ref, *refs):
    kv_refs, (out_ref, e_ref, dp_ref, ks_ref, m_ref, l_ref, d_ref, sems) = refs[:-8], refs[-8:]
    rows = ks_ref.shape[1] // len(members)
    work = Work(order_ref, rows, outer)
    copies = []
    for n, (d, kv_ref) in enumerate(zip(members, kv_refs)):
        for half in range(2):
            source = at_rows(work.key_slot(d, half) * rows, rows)
            copies.append(
                load(kv_ref.at[source], ks_ref.at[half, pl.ds(n * rows, rows)], sems.at[2 * n + half])
            )
    m_ref[...] = jnp.full(m_ref.shape, LOWEST, jnp.float32)
    l_ref[...] = jnp.zeros(l_ref.shape, jnp.float32)
    d_ref[...] = jnp.zeros(d_ref.shape, jnp.float32)
    wait_all(copies)
    qd_refs = (own_ref, other_ref)

    def maximum(owner, q_half, k_half, first, size, place, masked):
        slot = work.query_slot(owner, q_half)
        scores = lax.dot_general(
            ks_ref[k_half, pl.ds(first, size), :HEAD],
            qd_refs[owner][0, slot],
            ROWS_DOT_ROWS,
            preferred_element_type=jnp.float32,
        )
        if masked:
            key = lax.broadcasted_iota(jnp.int32, scores.shape, 0)
            query = lax.rem(lax.broadcasted_iota(jnp.int32, (1, scores.shape[1]), 1), rows)
            scores = jnp.where(key <= query, scores, LOWEST)
        e_ref[owner, pl.ds(place, size), :] = scores
        m_ref[owner, q_half] = jnp.maximum(
            m_ref[owner, q_half], jnp.max(scores, axis=0, keepdims=True)
        )
        dp_ref[owner, pl.ds(place, size), :] = lax.dot_general(
            ks_ref[k_half, pl.ds(first, size), HEAD:],
            qd_refs[owner][1, slot],
            ROWS_DOT_ROWS,
            preferred_element_type=jnp.float32,
        )

    work.blocks(members, maximum)

    def sums(owner, q_half, k_half, first, size, place, masked):
        scores = e_ref[owner, pl.ds(place, size), :]
        grads = dp_ref[owner, pl.ds(place, size), :]
        expon = jnp.exp2((scores - m_ref[owner, q_half]) * EXPONENT_SCALE)
        e_ref[owner, pl.ds(place, size), :] = expon
        l_ref[owner, q_half] = l_ref[owner, q_half] + jnp.sum(expon, axis=0, keepdims=True)
        d_ref[owner, q_half] = d_ref[owner, q_half] + jnp.sum(expon * grads, axis=0, keepdims=True)

    work.blocks(members, sums)
    for owner in range(2):
        for half in range(2):
            base = (2 * owner + half) * 3
            out_ref[base : base + 1, :] = m_ref[owner, half]
            out_ref[base + 1 : base + 2, :] = l_ref[owner, half]
            out_ref[base + 2 : base + 3, :] = d_ref[owner, half]


def merged(stats_refs, base):
    rows = [ref[base : base + 3, :] for ref in stats_refs]
    top = functools.reduce(jnp.maximum, [part[:1] for part in rows])
    weights = [jnp.exp2((part[:1] - top) * EXPONENT_SCALE) for part in rows]
    total = sum(weight * part[1:2] for weight, part in zip(weights, rows))
    delta = sum(weight * part[2:3] for weight, part in zip(weights, rows))
    return top, total, delta


def merge_kernel(first_ref, second_ref, out_ref):
    for base in range(0, 12, 3):
        for n, row in enumerate(merged((first_ref, second_ref), base)):
            out_ref[base + n : base + n + 1, :] = row


def grads_kernel(outer, groups, order_ref, own_ref, other_ref, *refs):
    count = len(groups)
    stats_refs, theirs_ref, refs = refs[:count], refs[count], refs[count + 1 :]
    e_refs, dp_refs, refs = refs[:count], refs[count : 2 * count], refs[2 * count :]
    term_refs, gs_refs, refs = refs[:outer], refs[outer : outer + count], refs[outer + count :]
    acc_refs, (w_ref, d_ref) = refs[:count], refs[count:]
    rows = term_refs[0].shape[0] // 2
    work = Work(order_ref, rows, outer)
    for owner in range(2):
        for half in range(2):
            base = (2 * owner + half) * 3
            base2 = (2 * (1 - owner) + half) * 3
            mine = merged(stats_refs, base)
            theirs = [theirs_ref[base2 + n : base2 + n + 1, :] for n in range(3)]
            top = jnp.maximum(mine[0], theirs[0])
            w1 = jnp.exp2((mine[0] - top) * EXPONENT_SCALE)
            w2 = jnp.exp2((theirs[0] - top) * EXPONENT_SCALE)
            total = w1 * mine[1] + w2 * theirs[1]
            d_ref[owner, half] = (w1 * mine[2] + w2 * theirs[2]) / total
            for n, stats_ref in enumerate(stats_refs):
                weight = jnp.exp2((stats_ref[base : base + 1, :] - top) * EXPONENT_SCALE)
                w_ref[n, owner, half] = weight / total
    qd_refs = (own_ref, other_ref)

    for n, members in enumerate(groups):
        acc_ref = acc_refs[n]
        acc_ref[...] = jnp.zeros(acc_ref.shape, jnp.float32)

        def gradients(owner, q_half, k_half, first, size, place, masked):
            slot = work.query_slot(owner, q_half)
            here = pl.ds(place, size)
            probs = e_refs[n][owner, here, :] * w_ref[n, owner, q_half]
            grads = (probs * (dp_refs[n][owner, here, :] - d_ref[owner, q_half])).astype(jnp.bfloat16)
            gs_refs[n][owner, here, :] = grads
            keys = pl.ds(first, size)
            acc_ref[k_half, keys, HEAD:] = acc_ref[k_half, keys, HEAD:] + jnp.dot(
                probs.astype(jnp.bfloat16), qd_refs[owner][1, slot], preferred_element_type=jnp.float32
            )
            acc_ref[k_half, keys, :HEAD] = acc_ref[k_half, keys, :HEAD] + jnp.dot(
                grads, qd_refs[owner][0, slot], preferred_element_type=jnp.float32
            )

        work.blocks(members, gradients)
        for at, d in enumerate(members):
            term_ref = term_refs[d]
            for half in range(2):
                target = at_rows(work.key_slot(d, half) * rows, rows)
                source = slice(at * rows, (at + 1) * rows)
                term_ref[target, :HEAD] = (acc_ref[half, source, :HEAD] * SCALE).astype(term_ref.dtype)
                term_ref[target, HEAD:] = acc_ref[half, source, HEAD:].astype(term_ref.dtype)


def query_kernel(outer, groups, order_ref, after_ref, *refs):
    count = len(groups)
    gs_refs, ks_refs, (own_ref, other_ref, acc_ref) = refs[:count], refs[count : 2 * count], refs[2 * count :]
    rows = own_ref.shape[0] // 2
    work = Work(order_ref, rows, outer)
    acc_ref[...] = jnp.zeros(acc_ref.shape, jnp.float32)

    for n, members in enumerate(groups):

        def terms(owner, q_half, k_half, first, size, place, masked):
            acc_ref[owner, q_half] = acc_ref[owner, q_half] + lax.dot_general(
                ks_refs[n][k_half, pl.ds(first, size), :HEAD],
                gs_refs[n][owner, pl.ds(place, size), :],
                COLS_DOT_COLS,
                preferred_element_type=jnp.float32,
            )

        work.blocks(members, terms)
    for owner, target in ((0, own_ref), (1, other_ref)):
        for half in range(2):
            place = at_rows(work.query_slot(owner, half) * rows, rows)
            grads = (jnp.transpose(acc_ref[owner, half]) * SCALE).astype(target.dtype)
            for h in range(GROUP):
                target[place, h * HEAD : (h + 1) * HEAD] = grads[h * rows : (h + 1) * rows, :]


def sum_kernel(outer, *refs):
    terms, outs, total_ref = refs[:outer], refs[outer:-1], refs[-1]
    total = terms[0][...]
    for term_ref in terms[1:]:
        total = total + term_ref[...].astype(jnp.float32)
    total_ref[...] = total
    kvh = len(outs)
    rows = outs[0].shape[0]
    for e, out_ref in enumerate(outs):
        target = lax.rem(lax.axis_index("kvh") + e, kvh)
        out_ref[...] = total_ref[at_rows(target * rows, rows), :].astype(jnp.bfloat16)


def place_kernel(own_ref, received_ref, *refs):
    parts, (dq_out, key_out, value_out, dq_ref, sems) = refs[:-5], refs[-5:]
    kvh = len(parts)
    copies = []
    for e, part_ref in enumerate(parts):
        head = lax.rem(lax.axis_index("kvh") + kvh - e, kvh)
        cols = at_rows(head * HEAD, HEAD)
        copies.append(load(part_ref.at[:, pl.ds(0, HEAD)], key_out.at[:, cols], sems.at[2 * e]))
        copies.append(load(part_ref.at[:, pl.ds(HEAD, HEAD)], value_out.at[:, cols], sems.at[2 * e + 1]))
    dq_ref[...] = (own_ref[...] + received_ref[...].astype(jnp.float32)).astype(jnp.bfloat16)
    copies.append(load(dq_ref, dq_out, sems.at[2 * kvh]))
    wait_all(copies)


def per_device(queries, keys, values, d_out, slab_order):
    kvh = lax.axis_size("kvh")
    outer = lax.axis_size("outer")
    local_rows, query_width = queries.shape
    cache_rows = keys.shape[0]
    slab_rows = local_rows // 2
    columns = GROUP * slab_rows
    params = pltpu.CompilerParams(vmem_limit_bytes=(8 << 20) + (10 << 10) * outer * local_rows)
    beside = pl.CostEstimate(flops=2 * 10**10, bytes_accessed=10**6, transcendentals=0)
    vmem = pl.BlockSpec(memory_space=pltpu.VMEM)
    smem = pl.BlockSpec(memory_space=pltpu.SMEM)
    anywhere = pl.BlockSpec(memory_space=pl.ANY)
    shape = jax.ShapeDtypeStruct
    dma = pltpu.SemaphoreType.DMA
    low, full = jnp.bfloat16, jnp.float32

    def call(kernel, name, **arguments):
        return pl.pallas_call(kernel, compiler_params=params, name=name, **arguments)

    def shift(array, axis, by):
        size = lax.axis_size(axis)
        return lax.ppermute(array, axis, [(n, (n + by) % size) for n in range(size)])

    part = shape((cache_rows, 2 * HEAD), low)
    block = shape((local_rows, 2 * HEAD), low)
    parts = call(
        split_kernel,
        "split",
        out_shape=(part,) * kvh,
        in_specs=[vmem],
        out_specs=(vmem,) * kvh,
        scratch_shapes=[dma((2 * kvh,))],
    )(jnp.concatenate([keys, values], axis=0))
    own_qd = call(
        stack_kernel,
        "stack",
        out_shape=shape((2, 2, columns, HEAD), low),
        in_specs=[vmem, vmem, anywhere],
        out_specs=vmem,
        cost_estimate=beside,
    )(queries, d_out, parts[0])
    parts = [parts[0]] + [shift(parts[e], "kvh", e) for e in range(1, kvh)]
    other_qd = shift(own_qd, "pair", 1)
    own_block = call(
        join_kernel,
        "join",
        out_shape=block,
        in_specs=[anywhere] * kvh,
        out_specs=vmem,
        scratch_shapes=[dma((kvh,))],
    )(*parts)
    blocks = [own_block] + [shift(own_block, "outer", d) for d in range(1, outer)]

    far = outer // 2 + 1
    groups = [[0, *range(far, outer)], list(range(1, far))]
    all_stats = shape((12, columns), full)
    row_stat = pltpu.VMEM((2, 2, 1, columns), full)
    results = []
    for n, members in enumerate(groups):
        half_rows = len(members) * slab_rows
        score_rows = (2, 2 * half_rows + slab_rows, columns)
        results.append(
            call(
                functools.partial(stats_kernel, outer, members),
                "stats",
                out_shape=(
                    all_stats,
                    shape(score_rows, full),
                    shape(score_rows, full),
                    shape((2, half_rows, 2 * HEAD), low),
                ),
                in_specs=[smem, vmem, vmem] + [anywhere] * len(members),
                out_specs=(vmem,) * 4,
                scratch_shapes=[row_stat, row_stat, row_stat, dma((2 * len(members),))],
                cost_estimate=beside if n == 0 else None,
            )(slab_order, own_qd, other_qd, *[blocks[d] for d in members])
        )
    stats, expon, grad_probs, sorted_keys = zip(*results)
    mine = call(
        merge_kernel, "merge", out_shape=all_stats, in_specs=[vmem, vmem], out_specs=vmem
    )(*stats)
    theirs = shift(mine, "pair", 1)
    count = len(groups)
    grads = call(
        functools.partial(grads_kernel, outer, groups),
        "grads",
        out_shape=(shape(block.shape, full),)
        + (block,) * (outer - 1)
        + tuple(shape(scores.shape, low) for scores in expon),
        in_specs=[smem] + [vmem] * (3 + 3 * count),
        out_specs=(vmem,) * (outer + count),
        scratch_shapes=[pltpu.VMEM(keys_low.shape, full) for keys_low in sorted_keys]
        + [pltpu.VMEM((count, 2, 2, 1, columns), full), row_stat],
    )(slab_order, own_qd, other_qd, *stats, theirs, *expon, *grad_probs)
    terms, score_grads = grads[:outer], grads[outer:]
    terms = [terms[0]] + [shift(terms[d], "outer", -d) for d in range(1, outer)]
    own_grads, other_grads = call(
        functools.partial(query_kernel, outer, groups),
        "query_terms",
        out_shape=(shape(queries.shape, full), shape(queries.shape, low)),
        in_specs=[smem, anywhere] + [vmem] * (2 * count),
        out_specs=(vmem, vmem),
        scratch_shapes=[pltpu.VMEM((2, 2, HEAD, columns), full)],
        cost_estimate=beside,
    )(slab_order, terms[1], *score_grads, *sorted_keys)
    received_grads = shift(other_grads, "pair", 1)
    owned = call(
        functools.partial(sum_kernel, outer),
        "sum",
        out_shape=(part,) * kvh,
        in_specs=[vmem] * outer,
        out_specs=(vmem,) * kvh,
        scratch_shapes=[pltpu.VMEM(block.shape, full)],
    )(*terms)
    owned = [owned[0]] + [shift(owned[e], "kvh", e) for e in range(1, kvh)]
    return call(
        place_kernel,
        "place",
        out_shape=(shape(queries.shape, low), shape(keys.shape, low), shape(values.shape, low)),
        in_specs=[vmem, vmem] + [anywhere] * kvh,
        out_specs=(anywhere,) * 3,
        scratch_shapes=[pltpu.VMEM(queries.shape, low), dma((2 * kvh + 1,))],
    )(own_grads, received_grads, *owned)


def solution(mesh):
    kvh = mesh.shape["kvh"]
    pairs = mesh.shape["seq"] // 2
    paired = Mesh(mesh.devices.reshape(pairs, 2, kvh), ("outer", "pair", "kvh"))
    seq = ("outer", "pair")
    cache = P(("outer", "pair", "kvh"), None)
    placed = (P(seq, "kvh"), cache, cache, P(seq, "kvh"), P())
    return jax.shard_map(
        per_device,
        mesh=paired,
        in_specs=placed,
        out_specs=(P(seq, "kvh"), cache, cache),
        check_vma=False,
    )
```

time: 58.6 us -> 47.9 us (0.82)
  Pallas kernels: 19.3 us -> 6.99 us
  starting transfers between devices: 18.1 us -> 19.8 us
  local copies, waits for them, and re-layouts: 2.35 us -> 0.92 us
  other arithmetic: 0 us -> 0.82 us
  waiting for transfers between devices: 17.2 us -> 18 us
    pallas_call x4 -> x7, Pallas kernels: 18.4 us -> 6.05 us  [the longest x2 2.92 us: per_device(): call(functools.partial(stats_kernel, outer, members), 'stats', out_shape=...]
    ppermute x15, starting transfers between devices: 18.1 us -> 19.8 us  [shift(): lax.ppermute(array, axis, [(n, (n + by) % size) for n in range(size)])]
    unnamed x8 -> x6, local copies, waits for them, and re-layouts: 2.35 us -> 0.92 us
    concatenate x0 -> x1, other arithmetic: none -> 0.82 us  [per_device(): jnp.concatenate([keys, values], axis=0)]
    ppermute x15, waiting for transfers between devices: 17.2 us -> 18 us  [shift(): lax.ppermute(array, axis, [(n, (n + by) % size) for n in range(size)])]
  transfers between devices with their start and end apart: 15 -> 15, of which waited for: 11 -> 11; matrix products, arithmetic and copies ran while one was open for 0% -> 0% of each run, Pallas kernels for 0% -> 3%
where the time goes in v6:
time: 47.9 us; the launch traced here: 47.2 us
  starting transfers between devices  19.8 us (41%)
  waiting for transfers between devices  18 us (38%)
  Pallas kernels  6.99 us (15%)
  local copies, waits for them, and re-layouts  0.92 us (2%)
  other arithmetic  0.82 us (2%)
  between operations  0.73 us (2%)
    ppermute x15, starting transfers between devices, shift(): lax.ppermute(array, axis, [(n, (n + by) % size) for n in range(size)])  19.8 us
    ppermute x15, waiting for transfers between devices, shift(): lax.ppermute(array, axis, [(n, (n + by) % size) for n in range(size)])  18 us
    pallas_call x2, Pallas kernels, per_device(): call(functools.partial(stats_kernel, outer, members), 'stats', out_shape=...  2.92 us
    pallas_call x1, Pallas kernels, per_device(): call(functools.partial(query_kernel, outer, groups), 'query_terms', out_s...  1.46 us
    pallas_call x1, Pallas kernels, per_device(): call(functools.partial(grads_kernel, outer, groups), 'grads', out_shape=(...  1.45 us
  transfers between devices with their start and end apart: 15, of which 11 were waited for; matrix products, arithmetic and copies ran while one was open for 0% of the time, Pallas kernels for 3%

profile of v6, /device:TPU:0, one launch (start us, length us, event | category | flops | bytes accessed | tf_op | source)
XLA Modules:
  0.0 47.2 jit_solution(10461876786816430058)
XLA Ops:
  0.6 0.0 copy-start.1
  0.6 0.8 %pad_maximum_fusion.cache_ref = bf16[64,512]{1,0:T(8,128)(2,1)S(1)} fusion(bf16[32,512]{1,0:T(8,128)(2,1)} %param.7, bf16[32,512]{1,0:T(8,128)(2,1)} %param.6), kind=kLoop, calls=%fused_computation | loop fusion | flops 131072 | bytes 131072 | tf_op jit(solution)/shard_map/concatenate | solution.py:320
  1.5 0.1 split.1
  1.6 0.0 copy-done.1
  1.6 0.0 copy-start.2
  1.6 0.9 %copy-done.2 = bf16[128,640]{1,0:T(8,128)(2,1)S(1)} copy-done((bf16[128,640]{1,0:T(8,128)(2,1)S(1)}, bf16[128,640]{1,0:T(8,128)(2,1)}, u32[]{:S(2)}) %copy-start.2) | copy-done | bytes 163864
  2.5 0.1 stack.1.own_ref
  2.6 3.0 %collective-permute-start = (bf16[2,2,320,128]{3,2,1,0:T(8,128)(2,1)S(1)}, bf16[2,2,320,128]{3,2,1,0:T(8,128)(2,1)S(1)}, u32[]{:S(2)}, u32[]{:S(2)}) collective-permute-start(bf16[2,2,320,128]{3,2,1,0:T(8,128)(2,1)S(1)} %stack.1.own_ref), channel_id=1, source_target_pairs={{0,4},{4,0},{1,5},{5,1},{2,6},{6,2},{3,7},{7,3},{8,12},{12,8},{9,1... | collective-permute-start | bytes 983048 | tf_op jit(solution)/shard_map/ppermute | solution.py:309
  5.6 0.0 collective-permute-start.1
  5.6 1.5 %collective-permute-start.2 = (bf16[32,256]{1,0:T(8,128)(2,1)S(1)}, bf16[32,256]{1,0:T(8,128)(2,1)S(1)}, u32[]{:S(2)}, u32[]{:S(2)}) collective-permute-start(bf16[32,256]{1,0:T(8,128)(2,1)S(1)} %get-tuple-element.29), channel_id=1, source_target_pairs={{0,2},{1,3},{2,0},{3,1},{4,6},{5,7},{6,4},{7,5},{8,10},{9,11},{10,... | collective-permute-start | bytes 49160 | tf_op jit(solution)/shard_map/ppermute | solution.py:309
  7.1 0.0 copy-start
  7.1 1.4 %collective-permute-start.3 = (bf16[32,256]{1,0:T(8,128)(2,1)S(1)}, bf16[32,256]{1,0:T(8,128)(2,1)S(1)}, u32[]{:S(2)}, u32[]{:S(2)}) collective-permute-start(bf16[32,256]{1,0:T(8,128)(2,1)S(1)} %get-tuple-element.30), channel_id=1, source_target_pairs={{0,3},{1,0},{2,1},{3,2},{4,7},{5,4},{6,5},{7,6},{8,11},{9,8},{10,9... | collective-permute-start | bytes 49160 | tf_op jit(solution)/shard_map/ppermute | solution.py:309
  8.6 0.2 collective-permute-done.1.refs_1_
  8.8 0.6 %collective-permute-done.2.refs_2_ = bf16[32,256]{1,0:T(8,128)(2,1)S(1)} collective-permute-done((bf16[32,256]{1,0:T(8,128)(2,1)S(1)}, bf16[32,256]{1,0:T(8,128)(2,1)S(1)}, u32[]{:S(2)}, u32[]{:S(2)}) %collective-permute-start.2) | collective-permute-done | bytes 16416 | tf_op jit(solution)/shard_map/ppermute | solution.py:309
  9.4 0.6 %collective-permute-done.3.refs_3_ = bf16[32,256]{1,0:T(8,128)(2,1)S(1)} collective-permute-done((bf16[32,256]{1,0:T(8,128)(2,1)S(1)}, bf16[32,256]{1,0:T(8,128)(2,1)S(1)}, u32[]{:S(2)}, u32[]{:S(2)}) %collective-permute-start.3) | collective-permute-done | bytes 16416 | tf_op jit(solution)/shard_map/ppermute | solution.py:309
  10.0 0.1 join.1.refs_0_
  10.1 3.7 %collective-permute-start.4 = (bf16[128,256]{1,0:T(8,128)(2,1)S(1)}, bf16[128,256]{1,0:T(8,128)(2,1)S(1)}, u32[]{:S(2)}, u32[]{:S(2)}) collective-permute-start(bf16[128,256]{1,0:T(8,128)(2,1)S(1)} %join.1.refs_0_), channel_id=1, source_target_pairs={{0,24},{8,0},{16,8},{24,16},{1,25},{9,1},{17,9},{25,17},{2,26},{10... | collective-permute-start | bytes 196616 | tf_op jit(solution)/shard_map/ppermute | solution.py:309
  13.8 0.0 collective-permute-start.6
  13.8 1.0 %collective-permute-start.5 = (bf16[128,256]{1,0:T(8,128)(2,1)S(1)}, bf16[128,256]{1,0:T(8,128)(2,1)S(1)}, u32[]{:S(2)}, u32[]{:S(2)}) collective-permute-start(bf16[128,256]{1,0:T(8,128)(2,1)S(1)} %join.1.refs_0_), channel_id=1, source_target_pairs={{0,8},{8,16},{16,24},{24,0},{1,9},{9,17},{17,25},{25,1},{2,10},{10... | collective-permute-start | bytes 196616 | tf_op jit(solution)/shard_map/ppermute | solution.py:309
  14.8 1.5 %collective-permute-done.4.refs_1_ = bf16[128,256]{1,0:T(8,128)(2,1)S(1)} collective-permute-done((bf16[128,256]{1,0:T(8,128)(2,1)S(1)}, bf16[128,256]{1,0:T(8,128)(2,1)S(1)}, u32[]{:S(2)}, u32[]{:S(2)}) %collective-permute-start.4) | collective-permute-done | bytes 65568 | tf_op jit(solution)/shard_map/ppermute | solution.py:309
  16.3 0.0 collective-permute-done.other_ref
  16.3 0.0 copy-done
  16.3 1.5 %stats.2 = (f32[12,320]{1,0:T(8,128)S(1)}, f32[2,320,320]{2,1,0:T(8,128)S(1)}, f32[2,320,320]{2,1,0:T(8,128)S(1)}, bf16[2,128,256]{2,1,0:T(8,128)(2,1)S(1)}) custom-call(s32[16]{0:T(128)S(1)} %copy-done, bf16[2,2,320,128]{3,2,1,0:T(8,128)(2,1)S(1)} %stack.1.own_ref, bf16[2,2,320,128]{3,2,1,0:T(8,128)(2,1)S(1)} %collective-permute-done.other_ref, ...), custom_call_target="tpu_custom_call" | custom-call | flops 20000000000 | bytes 1000000 | tf_op jit(solution)/shard_map/stats/pallas_call | solution.py:350
  17.8 3.5 %collective-permute-done.6.refs_1_ = bf16[128,256]{1,0:T(8,128)(2,1)S(1)} collective-permute-done((bf16[128,256]{1,0:T(8,128)(2,1)S(1)}, bf16[128,256]{1,0:T(8,128)(2,1)S(1)}, u32[]{:S(2)}, u32[]{:S(2)}) %collective-permute-start.6) | collective-permute-done | bytes 65568 | tf_op jit(solution)/shard_map/ppermute | solution.py:309
  21.3 0.0 collective-permute-done.5.refs_0_
  21.3 1.4 %stats.3 = (f32[12,320]{1,0:T(8,128)S(1)}, f32[2,320,320]{2,1,0:T(8,128)S(1)}, f32[2,320,320]{2,1,0:T(8,128)S(1)}, bf16[2,128,256]{2,1,0:T(8,128)(2,1)S(1)}) custom-call(s32[16]{0:T(128)S(1)} %copy-done, bf16[2,2,320,128]{3,2,1,0:T(8,128)(2,1)S(1)} %stack.1.own_ref, bf16[2,2,320,128]{3,2,1,0:T(8,128)(2,1)S(1)} %collective-permute-done.other_ref, ...), custom_call_target="tpu_custom_call" | custom-call | tf_op jit(solution)/shard_map/stats/pallas_call | solution.py:350
  22.8 0.6 %collective-permute-start.7 = (f32[12,320]{1,0:T(8,128)S(1)}, f32[12,320]{1,0:T(8,128)S(1)}, u32[]{:S(2)}, u32[]{:S(2)}) collective-permute-start(f32[12,320]{1,0:T(8,128)S(1)} %merge.1), channel_id=1, source_target_pairs={{0,4},{4,0},{1,5},{5,1},{2,6},{6,2},{3,7},{7,3},{8,12},{12,8},{9,1... | collective-permute-start | bytes 46088 | tf_op jit(solution)/shard_map/ppermute | solution.py:309
  23.4 3.3 %collective-permute-done.7.refs_2_ = f32[12,320]{1,0:T(8,128)S(1)} collective-permute-done((f32[12,320]{1,0:T(8,128)S(1)}, f32[12,320]{1,0:T(8,128)S(1)}, u32[]{:S(2)}, u32[]{:S(2)}) %collective-permute-start.7) | collective-permute-done | bytes 15392 | tf_op jit(solution)/shard_map/ppermute | solution.py:309
  26.7 1.4 %grads.1 = (f32[128,256]{1,0:T(8,128)S(1)}, bf16[128,256]{1,0:T(8,128)(2,1)S(1)}, bf16[128,256]{1,0:T(8,128)(2,1)S(1)}, bf16[128,256]{1,0:T(8,128)(2,1)S(1)}, bf...) custom-call(s32[16]{0:T(128)S(1)} %copy-done, bf16[2,2,320,128]{3,2,1,0:T(8,128)(2,1)S(1)} %stack.1.own_ref, ...), custom_call_target="tpu_custom_call" | custom-call | tf_op jit(solution)/shard_map/grads/pallas_call | solution.py:371
  28.2 1.6 %collective-permute-start.8 = (bf16[128,256]{1,0:T(8,128)(2,1)S(1)}, bf16[128,256]{1,0:T(8,128)(2,1)S(1)}, u32[]{:S(2)}, u32[]{:S(2)}) collective-permute-start(bf16[128,256]{1,0:T(8,128)(2,1)S(1)} %get-tuple-element.37), channel_id=1, source_target_pairs={{0,24},{8,0},{16,8},{24,16},{1,25},{9,1},{17,9},{25,17},{2,26},{10... | collective-permute-start | bytes 196616 | tf_op jit(solution)/shard_map/ppermute | solution.py:309
  29.8 2.7 %collective-permute-done.8.after_ref.refs_1_ = bf16[128,256]{1,0:T(8,128)(2,1)S(1)} collective-permute-done((bf16[128,256]{1,0:T(8,128)(2,1)S(1)}, bf16[128,256]{1,0:T(8,128)(2,1)S(1)}, u32[]{:S(2)}, u32[]{:S(2)}) %collective-permute-start.8) | collective-permute-done | bytes 65568 | tf_op jit(solution)/shard_map/ppermute | solution.py:309
  32.5 1.5 %query_terms.1 = (f32[128,640]{1,0:T(8,128)S(1)}, bf16[128,640]{1,0:T(8,128)(2,1)S(1)}) custom-call(s32[16]{0:T(128)S(1)} %copy-done, bf16[128,256]{1,0:T(8,128)(2,1)S(1)} %collective-permute-done.8.after_ref.refs_1_, bf16[2,320,320]{2,1,0:T(8,128)(2,1)S(1)} %get-tuple-element.38.refs_0_, bf16[2,320,320]{2,1,0:T(8,128)(2,1)S(1)} %get-tuple-element.39.refs_1_, ...), custom_call_target="tpu_custom_call" | custom-call | flops 20000000000 | bytes 1000000 | tf_op jit(solution)/shard_map/query_terms/pallas_call | solution.py:384
  33.9 0.6 %collective-permute-start.9 = (bf16[128,640]{1,0:T(8,128)(2,1)S(1)}, bf16[128,640]{1,0:T(8,128)(2,1)S(1)}, u32[]{:S(2)}, u32[]{:S(2)}) collective-permute-start(bf16[128,640]{1,0:T(8,128)(2,1)S(1)} %get-tuple-element.43), channel_id=1, source_target_pairs={{0,4},{4,0},{1,5},{5,1},{2,6},{6,2},{3,7},{7,3},{8,12},{12,8},{9,1... | collective-permute-start | bytes 491528 | tf_op jit(solution)/shard_map/ppermute | solution.py:309
  34.5 1.7 %collective-permute-start.10 = (bf16[128,256]{1,0:T(8,128)(2,1)S(1)}, bf16[128,256]{1,0:T(8,128)(2,1)S(1)}, u32[]{:S(2)}, u32[]{:S(2)}) collective-permute-start(bf16[128,256]{1,0:T(8,128)(2,1)S(1)} %get-tuple-element.45), channel_id=1, source_target_pairs={{0,16},{8,24},{16,0},{24,8},{1,17},{9,25},{17,1},{25,9},{2,18},{10... | collective-permute-start | bytes 196616 | tf_op jit(solution)/shard_map/ppermute | solution.py:309
  36.3 2.2 %collective-permute-start.11 = (bf16[128,256]{1,0:T(8,128)(2,1)S(1)}, bf16[128,256]{1,0:T(8,128)(2,1)S(1)}, u32[]{:S(2)}, u32[]{:S(2)}) collective-permute-start(bf16[128,256]{1,0:T(8,128)(2,1)S(1)} %get-tuple-element.46), channel_id=1, source_target_pairs={{0,8},{8,16},{16,24},{24,0},{1,9},{9,17},{17,25},{25,1},{2,10},{10... | collective-permute-start | bytes 196616 | tf_op jit(solution)/shard_map/ppermute | solution.py:309
  38.4 1.9 %collective-permute-done.10.refs_2_ = bf16[128,256]{1,0:T(8,128)(2,1)S(1)} collective-permute-done((bf16[128,256]{1,0:T(8,128)(2,1)S(1)}, bf16[128,256]{1,0:T(8,128)(2,1)S(1)}, u32[]{:S(2)}, u32[]{:S(2)}) %collective-permute-start.10) | collective-permute-done | bytes 65568 | tf_op jit(solution)/shard_map/ppermute | solution.py:309
  40.4 1.9 %collective-permute-done.11.refs_3_ = bf16[128,256]{1,0:T(8,128)(2,1)S(1)} collective-permute-done((bf16[128,256]{1,0:T(8,128)(2,1)S(1)}, bf16[128,256]{1,0:T(8,128)(2,1)S(1)}, u32[]{:S(2)}, u32[]{:S(2)}) %collective-permute-start.11) | collective-permute-done | bytes 65568 | tf_op jit(solution)/shard_map/ppermute | solution.py:309
  42.4 0.1 collective-permute-start.12
  42.4 1.0 %collective-permute-start.13 = (bf16[32,256]{1,0:T(8,128)(2,1)S(1)}, bf16[32,256]{1,0:T(8,128)(2,1)S(1)}, u32[]{:S(2)}, u32[]{:S(2)}) collective-permute-start(bf16[32,256]{1,0:T(8,128)(2,1)S(1)} %get-tuple-element.49), channel_id=1, source_target_pairs={{0,2},{1,3},{2,0},{3,1},{4,6},{5,7},{6,4},{7,5},{8,10},{9,11},{10,... | collective-permute-start | bytes 49160 | tf_op jit(solution)/shard_map/ppermute | solution.py:309
  43.4 1.4 %collective-permute-start.14 = (bf16[32,256]{1,0:T(8,128)(2,1)S(1)}, bf16[32,256]{1,0:T(8,128)(2,1)S(1)}, u32[]{:S(2)}, u32[]{:S(2)}) collective-permute-start(bf16[32,256]{1,0:T(8,128)(2,1)S(1)} %get-tuple-element.50), channel_id=1, source_target_pairs={{0,3},{1,0},{2,1},{3,2},{4,7},{5,4},{6,5},{7,6},{8,11},{9,8},{10,9... | collective-permute-start | bytes 49160 | tf_op jit(solution)/shard_map/ppermute | solution.py:309
  44.8 0.8 %collective-permute-done.12.refs_1_ = bf16[32,256]{1,0:T(8,128)(2,1)S(1)} collective-permute-done((bf16[32,256]{1,0:T(8,128)(2,1)S(1)}, bf16[32,256]{1,0:T(8,128)(2,1)S(1)}, u32[]{:S(2)}, u32[]{:S(2)}) %collective-permute-start.12) | collective-permute-done | bytes 16416 | tf_op jit(solution)/shard_map/ppermute | solution.py:309
  45.6 0.8 %collective-permute-done.13.refs_2_ = bf16[32,256]{1,0:T(8,128)(2,1)S(1)} collective-permute-done((bf16[32,256]{1,0:T(8,128)(2,1)S(1)}, bf16[32,256]{1,0:T(8,128)(2,1)S(1)}, u32[]{:S(2)}, u32[]{:S(2)}) %collective-permute-start.13) | collective-permute-done | bytes 16416 | tf_op jit(solution)/shard_map/ppermute | solution.py:309
  46.4 0.0 collective-permute-done.14.refs_3_
  46.4 0.0 collective-permute-done.9.received_ref
  46.4 0.8 %place.1 = (bf16[128,640]{1,0:T(8,128)(2,1)}, bf16[32,512]{1,0:T(8,128)(2,1)}, bf16[32,512]{1,0:T(8,128)(2,1)}) custom-call(f32[128,640]{1,0:T(8,128)S(1)} %get-tuple-element.42.own_ref, bf16[128,640]{1,0:T(8,128)(2,1)S(1)} %collective-permute-done.9.received_ref, bf16[32,256]{1,0:T(8,128)(2,1)S(1)} %get-tuple-element.47.refs_0_, ...), custom_call_target="tpu_custom_call" | custom-call | tf_op jit(solution)/shard_map/place/pallas_call | solution.py:403
  (2 shorter events, 0.1 us)
Async XLA Ops:
  0.6 1.0 %copy-start.1 = (bf16[128,640]{1,0:T(8,128)(2,1)S(1)}, bf16[128,640]{1,0:T(8,128)(2,1)}, u32[]{:S(2)}) copy-start(bf16[128,640]{1,0:T(8,128)(2,1)} %q_ref.1) | copy-start | bytes 491524
  1.6 0.9 %copy-start.2 = (bf16[128,640]{1,0:T(8,128)(2,1)S(1)}, bf16[128,640]{1,0:T(8,128)(2,1)}, u32[]{:S(2)}) copy-start(bf16[128,640]{1,0:T(8,128)(2,1)} %do_ref.1) | copy-start | bytes 491524
  2.6 13.7 %collective-permute-start = (bf16[2,2,320,128]{3,2,1,0:T(8,128)(2,1)S(1)}, bf16[2,2,320,128]{3,2,1,0:T(8,128)(2,1)S(1)}, u32[]{:S(2)}, u32[]{:S(2)}) collective-permute-start(bf16[2,2,320,128]{3,2,1,0:T(8,128)(2,1)S(1)} %stack.1.own_ref), channel_id=1, source_target_pairs={{0,4},{4,0},{1,5},{5,1},{2,6},{6,2},{3,7},{7,3},{8,12},{12,8},{9,1... | collective-permute-start | bytes 983048 | tf_op jit(solution)/shard_map/ppermute | solution.py:309
  5.6 3.2 %collective-permute-start.1 = (bf16[32,256]{1,0:T(8,128)(2,1)S(1)}, bf16[32,256]{1,0:T(8,128)(2,1)S(1)}, u32[]{:S(2)}, u32[]{:S(2)}) collective-permute-start(bf16[32,256]{1,0:T(8,128)(2,1)S(1)} %get-tuple-element.28), channel_id=1, source_target_pairs={{0,1},{1,2},{2,3},{3,0},{4,5},{5,6},{6,7},{7,4},{8,9},{9,10},{10,1... | collective-permute-start | bytes 49160 | tf_op jit(solution)/shard_map/ppermute | solution.py:309
  5.6 3.8 %collective-permute-start.2 = (bf16[32,256]{1,0:T(8,128)(2,1)S(1)}, bf16[32,256]{1,0:T(8,128)(2,1)S(1)}, u32[]{:S(2)}, u32[]{:S(2)}) collective-permute-start(bf16[32,256]{1,0:T(8,128)(2,1)S(1)} %get-tuple-element.29), channel_id=1, source_target_pairs={{0,2},{1,3},{2,0},{3,1},{4,6},{5,7},{6,4},{7,5},{8,10},{9,11},{10,... | collective-permute-start | bytes 49160 | tf_op jit(solution)/shard_map/ppermute | solution.py:309
  7.1 9.2 %copy-start = (s32[16]{0:T(128)S(1)}, s32[16]{0:T(128)}, u32[]{:S(2)}) copy-start(s32[16]{0:T(128)} %order_ref.7) | copy-start | bytes 196
  7.1 2.9 %collective-permute-start.3 = (bf16[32,256]{1,0:T(8,128)(2,1)S(1)}, bf16[32,256]{1,0:T(8,128)(2,1)S(1)}, u32[]{:S(2)}, u32[]{:S(2)}) collective-permute-start(bf16[32,256]{1,0:T(8,128)(2,1)S(1)} %get-tuple-element.30), channel_id=1, source_target_pairs={{0,3},{1,0},{2,1},{3,2},{4,7},{5,4},{6,5},{7,6},{8,11},{9,8},{10,9... | collective-permute-start | bytes 49160 | tf_op jit(solution)/shard_map/ppermute | solution.py:309
  10.1 6.2 %collective-permute-start.4 = (bf16[128,256]{1,0:T(8,128)(2,1)S(1)}, bf16[128,256]{1,0:T(8,128)(2,1)S(1)}, u32[]{:S(2)}, u32[]{:S(2)}) collective-permute-start(bf16[128,256]{1,0:T(8,128)(2,1)S(1)} %join.1.refs_0_), channel_id=1, source_target_pairs={{0,24},{8,0},{16,8},{24,16},{1,25},{9,1},{17,9},{25,17},{2,26},{10... | collective-permute-start | bytes 196616 | tf_op jit(solution)/shard_map/ppermute | solution.py:309
  13.8 7.6 %collective-permute-start.6 = (bf16[128,256]{1,0:T(8,128)(2,1)S(1)}, bf16[128,256]{1,0:T(8,128)(2,1)S(1)}, u32[]{:S(2)}, u32[]{:S(2)}) collective-permute-start(bf16[128,256]{1,0:T(8,128)(2,1)S(1)} %join.1.refs_0_), channel_id=1, source_target_pairs={{0,16},{8,24},{16,0},{24,8},{1,17},{9,25},{17,1},{25,9},{2,18},{10... | collective-permute-start | bytes 196616 | tf_op jit(solution)/shard_map/ppermute | solution.py:309
  13.8 7.6 %collective-permute-start.5 = (bf16[128,256]{1,0:T(8,128)(2,1)S(1)}, bf16[128,256]{1,0:T(8,128)(2,1)S(1)}, u32[]{:S(2)}, u32[]{:S(2)}) collective-permute-start(bf16[128,256]{1,0:T(8,128)(2,1)S(1)} %join.1.refs_0_), channel_id=1, source_target_pairs={{0,8},{8,16},{16,24},{24,0},{1,9},{9,17},{17,25},{25,1},{2,10},{10... | collective-permute-start | bytes 196616 | tf_op jit(solution)/shard_map/ppermute | solution.py:309
  22.8 3.9 %collective-permute-start.7 = (f32[12,320]{1,0:T(8,128)S(1)}, f32[12,320]{1,0:T(8,128)S(1)}, u32[]{:S(2)}, u32[]{:S(2)}) collective-permute-start(f32[12,320]{1,0:T(8,128)S(1)} %merge.1), channel_id=1, source_target_pairs={{0,4},{4,0},{1,5},{5,1},{2,6},{6,2},{3,7},{7,3},{8,12},{12,8},{9,1... | collective-permute-start | bytes 46088 | tf_op jit(solution)/shard_map/ppermute | solution.py:309
  28.2 4.3 %collective-permute-start.8 = (bf16[128,256]{1,0:T(8,128)(2,1)S(1)}, bf16[128,256]{1,0:T(8,128)(2,1)S(1)}, u32[]{:S(2)}, u32[]{:S(2)}) collective-permute-start(bf16[128,256]{1,0:T(8,128)(2,1)S(1)} %get-tuple-element.37), channel_id=1, source_target_pairs={{0,24},{8,0},{16,8},{24,16},{1,25},{9,1},{17,9},{25,17},{2,26},{10... | collective-permute-start | bytes 196616 | tf_op jit(solution)/shard_map/ppermute | solution.py:309
  33.9 12.5 %collective-permute-start.9 = (bf16[128,640]{1,0:T(8,128)(2,1)S(1)}, bf16[128,640]{1,0:T(8,128)(2,1)S(1)}, u32[]{:S(2)}, u32[]{:S(2)}) collective-permute-start(bf16[128,640]{1,0:T(8,128)(2,1)S(1)} %get-tuple-element.43), channel_id=1, source_target_pairs={{0,4},{4,0},{1,5},{5,1},{2,6},{6,2},{3,7},{7,3},{8,12},{12,8},{9,1... | collective-permute-start | bytes 491528 | tf_op jit(solution)/shard_map/ppermute | solution.py:309
  34.5 5.9 %collective-permute-start.10 = (bf16[128,256]{1,0:T(8,128)(2,1)S(1)}, bf16[128,256]{1,0:T(8,128)(2,1)S(1)}, u32[]{:S(2)}, u32[]{:S(2)}) collective-permute-start(bf16[128,256]{1,0:T(8,128)(2,1)S(1)} %get-tuple-element.45), channel_id=1, source_target_pairs={{0,16},{8,24},{16,0},{24,8},{1,17},{9,25},{17,1},{25,9},{2,18},{10... | collective-permute-start | bytes 196616 | tf_op jit(solution)/shard_map/ppermute | solution.py:309
  36.3 6.1 %collective-permute-start.11 = (bf16[128,256]{1,0:T(8,128)(2,1)S(1)}, bf16[128,256]{1,0:T(8,128)(2,1)S(1)}, u32[]{:S(2)}, u32[]{:S(2)}) collective-permute-start(bf16[128,256]{1,0:T(8,128)(2,1)S(1)} %get-tuple-element.46), channel_id=1, source_target_pairs={{0,8},{8,16},{16,24},{24,0},{1,9},{9,17},{17,25},{25,1},{2,10},{10... | collective-permute-start | bytes 196616 | tf_op jit(solution)/shard_map/ppermute | solution.py:309
  42.4 3.2 %collective-permute-start.12 = (bf16[32,256]{1,0:T(8,128)(2,1)S(1)}, bf16[32,256]{1,0:T(8,128)(2,1)S(1)}, u32[]{:S(2)}, u32[]{:S(2)}) collective-permute-start(bf16[32,256]{1,0:T(8,128)(2,1)S(1)} %get-tuple-element.48), channel_id=1, source_target_pairs={{0,1},{1,2},{2,3},{3,0},{4,5},{5,6},{6,7},{7,4},{8,9},{9,10},{10,1... | collective-permute-start | bytes 49160 | tf_op jit(solution)/shard_map/ppermute | solution.py:309
  42.4 4.0 %collective-permute-start.13 = (bf16[32,256]{1,0:T(8,128)(2,1)S(1)}, bf16[32,256]{1,0:T(8,128)(2,1)S(1)}, u32[]{:S(2)}, u32[]{:S(2)}) collective-permute-start(bf16[32,256]{1,0:T(8,128)(2,1)S(1)} %get-tuple-element.49), channel_id=1, source_target_pairs={{0,2},{1,3},{2,0},{3,1},{4,6},{5,7},{6,4},{7,5},{8,10},{9,11},{10,... | collective-permute-start | bytes 49160 | tf_op jit(solution)/shard_map/ppermute | solution.py:309
  43.4 3.0 %collective-permute-start.14 = (bf16[32,256]{1,0:T(8,128)(2,1)S(1)}, bf16[32,256]{1,0:T(8,128)(2,1)S(1)}, u32[]{:S(2)}, u32[]{:S(2)}) collective-permute-start(bf16[32,256]{1,0:T(8,128)(2,1)S(1)} %get-tuple-element.50), channel_id=1, source_target_pairs={{0,3},{1,0},{2,1},{3,2},{4,7},{5,4},{6,5},{7,6},{8,11},{9,8},{10,9... | collective-permute-start | bytes 49160 | tf_op jit(solution)/shard_map/ppermute | solution.py:309

commit v7 on v6

--- a/solution.py
+++ b/solution.py
@@ -107,6 +107,7 @@
 
 
 def stats_kernel(outer, members, order_ref, own_ref, other_ref, *refs):
+    refs = refs[:len(members)] + refs[-8:]
     kv_refs, (out_ref, e_ref, dp_ref, ks_ref, m_ref, l_ref, d_ref, sems) = refs[:-8], refs[-8:]
     rows = ks_ref.shape[1] // len(members)
     work = Work(order_ref, rows, outer)
@@ -174,9 +175,10 @@
     return top, total, delta
 
 
-def merge_kernel(first_ref, second_ref, out_ref):
+def merge_kernel(*refs):
+    stats_refs, out_ref = refs[:-1], refs[-1]
     for base in range(0, 12, 3):
-        for n, row in enumerate(merged((first_ref, second_ref), base)):
+        for n, row in enumerate(merged(stats_refs, base)):
             out_ref[base + n : base + n + 1, :] = row
 
 
@@ -232,7 +234,7 @@
                 term_ref[target, HEAD:] = acc_ref[half, source, HEAD:].astype(term_ref.dtype)
 
 
-def query_kernel(outer, groups, order_ref, after_ref, *refs):
+def query_kernel(outer, groups, order_ref, *refs):
     count = len(groups)
     gs_refs, ks_refs, (own_ref, other_ref, acc_ref) = refs[:count], refs[count : 2 * count], refs[2 * count :]
     rows = own_ref.shape[0] // 2
@@ -335,11 +337,13 @@
         in_specs=[anywhere] * kvh,
         out_specs=vmem,
         scratch_shapes=[dma((kvh,))],
+        cost_estimate=beside,
     )(*parts)
     blocks = [own_block] + [shift(own_block, "outer", d) for d in range(1, outer)]
 
     far = outer // 2 + 1
-    groups = [[0, *range(far, outer)], list(range(1, far))]
+    groups = [[0, *range(far, outer)], list(range(2, far)), [1]]
+    groups = [members for members in groups if members]
     all_stats = shape((12, columns), full)
     row_stat = pltpu.VMEM((2, 2, 1, columns), full)
     results = []
@@ -356,15 +360,15 @@
                     shape(score_rows, full),
                     shape((2, half_rows, 2 * HEAD), low),
                 ),
-                in_specs=[smem, vmem, vmem] + [anywhere] * len(members),
+                in_specs=[smem, vmem, vmem] + [anywhere] * (len(members) + min(n, 1)),
                 out_specs=(vmem,) * 4,
                 scratch_shapes=[row_stat, row_stat, row_stat, dma((2 * len(members),))],
-                cost_estimate=beside if n == 0 else None,
-            )(slab_order, own_qd, other_qd, *[blocks[d] for d in members])
+                cost_estimate=beside if n + 1 < len(groups) else None,
+            )(slab_order, own_qd, other_qd, *[blocks[d] for d in members], *[done[0] for done in results[-1:]])
         )
     stats, expon, grad_probs, sorted_keys = zip(*results)
     mine = call(
-        merge_kernel, "merge", out_shape=all_stats, in_specs=[vmem, vmem], out_specs=vmem
+        merge_kernel, "merge", out_shape=all_stats, in_specs=[vmem] * len(stats), out_specs=vmem
     )(*stats)
     theirs = shift(mine, "pair", 1)
     count = len(groups)
@@ -385,11 +389,11 @@
         functools.partial(query_kernel, outer, groups),
         "query_terms",
         out_shape=(shape(queries.shape, full), shape(queries.shape, low)),
-        in_specs=[smem, anywhere] + [vmem] * (2 * count),
+        in_specs=[smem] + [vmem] * (2 * count),
         out_specs=(vmem, vmem),
         scratch_shapes=[pltpu.VMEM((2, 2, HEAD, columns), full)],
         cost_estimate=beside,
-    )(slab_order, terms[1], *score_grads, *sorted_keys)
+    )(slab_order, *score_grads, *sorted_keys)
     received_grads = shift(other_grads, "pair", 1)
     owned = call(
         functools.partial(sum_kernel, outer),
@@ -398,6 +402,7 @@
         in_specs=[vmem] * outer,
         out_specs=(vmem,) * kvh,
         scratch_shapes=[pltpu.VMEM(block.shape, full)],
+        cost_estimate=beside,
     )(*terms)
     owned = [owned[0]] + [shift(owned[e], "kvh", e) for e in range(1, kvh)]
     return call(

time: 47.9 us -> 40.8 us (0.85)
  waiting for transfers between devices: 18 us -> 10.7 us
  Pallas kernels: 6.99 us -> 7.9 us
    ppermute x15, waiting for transfers between devices: 18 us -> 10.7 us  [shift(): lax.ppermute(array, axis, [(n, (n + by) % size) for n in range(size)])]
    pallas_call x2 -> x3, Pallas kernels: 2.92 us -> 3.68 us  [per_device(): call(functools.partial(stats_kernel, outer, members), 'stats', out_shape=...]
  transfers between devices with their start and end apart: 15 -> 15, of which waited for: 11 -> 9; matrix products, arithmetic and copies ran while one was open for 0% -> 0% of each run, Pallas kernels for 3% -> 11%
where the time goes in v7:
time: 40.8 us; the launch traced here: 40.5 us
  starting transfers between devices  19.4 us (48%)
  waiting for transfers between devices  10.7 us (26%)
  Pallas kernels  7.9 us (19%)
  local copies, waits for them, and re-layouts  0.93 us (2%)
  other arithmetic  0.82 us (2%)
  between operations  0.74 us (2%)
    ppermute x15, starting transfers between devices, shift(): lax.ppermute(array, axis, [(n, (n + by) % size) for n in range(size)])  19.4 us
    ppermute x15, waiting for transfers between devices, shift(): lax.ppermute(array, axis, [(n, (n + by) % size) for n in range(size)])  10.7 us
    pallas_call x3, Pallas kernels, per_device(): call(functools.partial(stats_kernel, outer, members), 'stats', out_shape=...  3.68 us
    pallas_call x1, Pallas kernels, per_device(): call(functools.partial(query_kernel, outer, groups), 'query_terms', out_s...  1.54 us
    pallas_call x1, Pallas kernels, per_device(): call(functools.partial(grads_kernel, outer, groups), 'grads', out_shape=(...  1.47 us
    unnamed x6, local copies, waits for them, and re-layouts  0.93 us
    concatenate x1, other arithmetic, per_device(): jnp.concatenate([keys, values], axis=0)  0.82 us
  transfers between devices with their start and end apart: 15, of which 9 were waited for; matrix products, arithmetic and copies ran while one was open for 0% of the time, Pallas kernels for 11%

profile of v7, /device:TPU:0, one launch (start us, length us, event | category | flops | bytes accessed | tf_op | source)
XLA Modules:
  0.0 40.5 jit_solution(17673367163506655916)
XLA Ops:
  0.6 0.0 copy-start.1
  0.6 0.8 %pad_maximum_fusion.cache_ref = bf16[64,512]{1,0:T(8,128)(2,1)S(1)} fusion(bf16[32,512]{1,0:T(8,128)(2,1)} %param.7, bf16[32,512]{1,0:T(8,128)(2,1)} %param.6), kind=kLoop, calls=%fused_computation | loop fusion | flops 131072 | bytes 131072 | tf_op jit(solution)/shard_map/concatenate | solution.py:322
  1.5 0.1 split.1
  1.6 0.5 %collective-permute-start.1 = (bf16[32,256]{1,0:T(8,128)(2,1)S(1)}, bf16[32,256]{1,0:T(8,128)(2,1)S(1)}, u32[]{:S(2)}, u32[]{:S(2)}) collective-permute-start(bf16[32,256]{1,0:T(8,128)(2,1)S(1)} %get-tuple-element.33), channel_id=1, source_target_pairs={{0,1},{1,2},{2,3},{3,0},{4,5},{5,6},{6,7},{7,4},{8,9},{9,10},{10,1... | collective-permute-start | bytes 49160 | tf_op jit(solution)/shard_map/ppermute | solution.py:311
  2.1 2.6 %collective-permute-start.2 = (bf16[32,256]{1,0:T(8,128)(2,1)S(1)}, bf16[32,256]{1,0:T(8,128)(2,1)S(1)}, u32[]{:S(2)}, u32[]{:S(2)}) collective-permute-start(bf16[32,256]{1,0:T(8,128)(2,1)S(1)} %get-tuple-element.34), channel_id=1, source_target_pairs={{0,2},{1,3},{2,0},{3,1},{4,6},{5,7},{6,4},{7,5},{8,10},{9,11},{10,... | collective-permute-start | bytes 49160 | tf_op jit(solution)/shard_map/ppermute | solution.py:311
  4.6 1.4 %collective-permute-start.3 = (bf16[32,256]{1,0:T(8,128)(2,1)S(1)}, bf16[32,256]{1,0:T(8,128)(2,1)S(1)}, u32[]{:S(2)}, u32[]{:S(2)}) collective-permute-start(bf16[32,256]{1,0:T(8,128)(2,1)S(1)} %get-tuple-element.35), channel_id=1, source_target_pairs={{0,3},{1,0},{2,1},{3,2},{4,7},{5,4},{6,5},{7,6},{8,11},{9,8},{10,9... | collective-permute-start | bytes 49160 | tf_op jit(solution)/shard_map/ppermute | solution.py:311
  6.0 0.0 copy-done.1
  6.0 0.0 copy-start.2
  6.0 0.9 %copy-done.2 = bf16[128,640]{1,0:T(8,128)(2,1)S(1)} copy-done((bf16[128,640]{1,0:T(8,128)(2,1)S(1)}, bf16[128,640]{1,0:T(8,128)(2,1)}, u32[]{:S(2)}) %copy-start.2) | copy-done | bytes 163864
  7.0 0.1 stack.1.own_ref
  7.0 0.0 copy-start
  7.0 1.6 %collective-permute-start = (bf16[2,2,320,128]{3,2,1,0:T(8,128)(2,1)S(1)}, bf16[2,2,320,128]{3,2,1,0:T(8,128)(2,1)S(1)}, u32[]{:S(2)}, u32[]{:S(2)}) collective-permute-start(bf16[2,2,320,128]{3,2,1,0:T(8,128)(2,1)S(1)} %stack.1.own_ref), channel_id=1, source_target_pairs={{0,4},{4,0},{1,5},{5,1},{2,6},{6,2},{3,7},{7,3},{8,12},{12,8},{9,1... | collective-permute-start | bytes 983048 | tf_op jit(solution)/shard_map/ppermute | solution.py:311
  8.6 0.0 collective-permute-done.1.refs_1_
  8.6 0.0 collective-permute-done.2.refs_2_
  8.6 0.0 collective-permute-done.3.refs_3_
  8.6 0.1 join.1.refs_0_
  8.8 3.7 %collective-permute-start.4 = (bf16[128,256]{1,0:T(8,128)(2,1)S(1)}, bf16[128,256]{1,0:T(8,128)(2,1)S(1)}, u32[]{:S(2)}, u32[]{:S(2)}) collective-permute-start(bf16[128,256]{1,0:T(8,128)(2,1)S(1)} %join.1.refs_0_), channel_id=1, source_target_pairs={{0,24},{8,0},{16,8},{24,16},{1,25},{9,1},{17,9},{25,17},{2,26},{10... | collective-permute-start | bytes 196616 | tf_op jit(solution)/shard_map/ppermute | solution.py:311
  12.4 0.0 collective-permute-start.6
  12.4 1.0 %collective-permute-start.5 = (bf16[128,256]{1,0:T(8,128)(2,1)S(1)}, bf16[128,256]{1,0:T(8,128)(2,1)S(1)}, u32[]{:S(2)}, u32[]{:S(2)}) collective-permute-start(bf16[128,256]{1,0:T(8,128)(2,1)S(1)} %join.1.refs_0_), channel_id=1, source_target_pairs={{0,16},{8,24},{16,0},{24,8},{1,17},{9,25},{17,1},{25,9},{2,18},{10... | collective-permute-start | bytes 196616 | tf_op jit(solution)/shard_map/ppermute | solution.py:311
  13.4 1.3 %collective-permute-done.4.refs_1_ = bf16[128,256]{1,0:T(8,128)(2,1)S(1)} collective-permute-done((bf16[128,256]{1,0:T(8,128)(2,1)S(1)}, bf16[128,256]{1,0:T(8,128)(2,1)S(1)}, u32[]{:S(2)}, u32[]{:S(2)}) %collective-permute-start.4) | collective-permute-done | bytes 65568 | tf_op jit(solution)/shard_map/ppermute | solution.py:311
  14.8 1.0 %collective-permute-done.other_ref = bf16[2,2,320,128]{3,2,1,0:T(8,128)(2,1)S(1)} collective-permute-done((bf16[2,2,320,128]{3,2,1,0:T(8,128)(2,1)S(1)}, bf16[2,2,320,128]{3,2,1,0:T(8,128)(2,1)S(1)}, u32[]{:S(2)}, u32[]{:S(2)}) %collective-permute-start) | collective-permute-done | bytes 327712 | tf_op jit(solution)/shard_map/ppermute | solution.py:311
  15.8 0.0 copy-done
  15.8 1.5 %stats.3 = (f32[12,320]{1,0:T(8,128)S(1)}, f32[2,320,320]{2,1,0:T(8,128)S(1)}, f32[2,320,320]{2,1,0:T(8,128)S(1)}, bf16[2,128,256]{2,1,0:T(8,128)(2,1)S(1)}) custom-call(s32[16]{0:T(128)S(1)} %copy-done, bf16[2,2,320,128]{3,2,1,0:T(8,128)(2,1)S(1)} %stack.1.own_ref, bf16[2,2,320,128]{3,2,1,0:T(8,128)(2,1)S(1)} %collective-permute-done.other_ref, ...), custom_call_target="tpu_custom_call" | custom-call | flops 20000000000 | bytes 1000000 | tf_op jit(solution)/shard_map/stats/pallas_call | solution.py:354
  17.3 2.2 %collective-permute-done.5.refs_0_ = bf16[128,256]{1,0:T(8,128)(2,1)S(1)} collective-permute-done((bf16[128,256]{1,0:T(8,128)(2,1)S(1)}, bf16[128,256]{1,0:T(8,128)(2,1)S(1)}, u32[]{:S(2)}, u32[]{:S(2)}) %collective-permute-start.5) | collective-permute-done | bytes 65568 | tf_op jit(solution)/shard_map/ppermute | solution.py:311
  19.5 1.1 %stats.4 = (f32[12,320]{1,0:T(8,128)S(1)}, f32[2,192,320]{2,1,0:T(8,128)S(1)}, f32[2,192,320]{2,1,0:T(8,128)S(1)}, bf16[2,64,256]{2,1,0:T(8,128)(2,1)S(1)}) custom-call(s32[16]{0:T(128)S(1)} %copy-done, bf16[2,2,320,128]{3,2,1,0:T(8,128)(2,1)S(1)} %stack.1.own_ref, bf16[2,2,320,128]{3,2,1,0:T(8,128)(2,1)S(1)} %collective-permute-done.other_ref, ...), custom_call_target="tpu_custom_call" | custom-call | flops 20000000000 | bytes 1000000 | tf_op jit(solution)/shard_map/stats/pallas_call | solution.py:354
  20.6 0.0 collective-permute-done.6.refs_0_
  20.6 1.1 %stats.5 = (f32[12,320]{1,0:T(8,128)S(1)}, f32[2,192,320]{2,1,0:T(8,128)S(1)}, f32[2,192,320]{2,1,0:T(8,128)S(1)}, bf16[2,64,256]{2,1,0:T(8,128)(2,1)S(1)}) custom-call(s32[16]{0:T(128)S(1)} %copy-done, bf16[2,2,320,128]{3,2,1,0:T(8,128)(2,1)S(1)} %stack.1.own_ref, bf16[2,2,320,128]{3,2,1,0:T(8,128)(2,1)S(1)} %collective-permute-done.other_ref, ...), custom_call_target="tpu_custom_call" | custom-call | tf_op jit(solution)/shard_map/stats/pallas_call | solution.py:354
  21.7 0.1 merge.1
  21.8 1.5 %collective-permute-start.7 = (f32[12,320]{1,0:T(8,128)S(1)}, f32[12,320]{1,0:T(8,128)S(1)}, u32[]{:S(2)}, u32[]{:S(2)}) collective-permute-start(f32[12,320]{1,0:T(8,128)S(1)} %merge.1), channel_id=1, source_target_pairs={{0,4},{4,0},{1,5},{5,1},{2,6},{6,2},{3,7},{7,3},{8,12},{12,8},{9,1... | collective-permute-start | bytes 46088 | tf_op jit(solution)/shard_map/ppermute | solution.py:311
  23.3 2.4 %collective-permute-done.7.refs_3_ = f32[12,320]{1,0:T(8,128)S(1)} collective-permute-done((f32[12,320]{1,0:T(8,128)S(1)}, f32[12,320]{1,0:T(8,128)S(1)}, u32[]{:S(2)}, u32[]{:S(2)}) %collective-permute-start.7) | collective-permute-done | bytes 15392 | tf_op jit(solution)/shard_map/ppermute | solution.py:311
  25.7 1.5 %grads.1 = (f32[128,256]{1,0:T(8,128)S(1)}, bf16[128,256]{1,0:T(8,128)(2,1)S(1)}, bf16[128,256]{1,0:T(8,128)(2,1)S(1)}, bf16[128,256]{1,0:T(8,128)(2,1)S(1)}, bf...) custom-call(s32[16]{0:T(128)S(1)} %copy-done, ...), custom_call_target="tpu_custom_call" | custom-call | tf_op jit(solution)/shard_map/grads/pallas_call | solution.py:375
  27.1 2.0 %collective-permute-start.9 = (bf16[128,256]{1,0:T(8,128)(2,1)S(1)}, bf16[128,256]{1,0:T(8,128)(2,1)S(1)}, u32[]{:S(2)}, u32[]{:S(2)}) collective-permute-start(bf16[128,256]{1,0:T(8,128)(2,1)S(1)} %get-tuple-element.54), channel_id=1, source_target_pairs={{0,24},{8,0},{16,8},{24,16},{1,25},{9,1},{17,9},{25,17},{2,26},{10... | collective-permute-start | bytes 196616 | tf_op jit(solution)/shard_map/ppermute | solution.py:311
  29.1 0.0 collective-permute-start.10
  29.1 0.6 %collective-permute-start.11 = (bf16[128,256]{1,0:T(8,128)(2,1)S(1)}, bf16[128,256]{1,0:T(8,128)(2,1)S(1)}, u32[]{:S(2)}, u32[]{:S(2)}) collective-permute-start(bf16[128,256]{1,0:T(8,128)(2,1)S(1)} %get-tuple-element.56), channel_id=1, source_target_pairs={{0,8},{8,16},{16,24},{24,0},{1,9},{9,17},{17,25},{25,1},{2,10},{10... | collective-permute-start | bytes 196616 | tf_op jit(solution)/shard_map/ppermute | solution.py:311
  29.8 1.5 %query_terms.1 = (f32[128,640]{1,0:T(8,128)S(1)}, bf16[128,640]{1,0:T(8,128)(2,1)S(1)}) custom-call(s32[16]{0:T(128)S(1)} %copy-done, bf16[2,320,320]{2,1,0:T(8,128)(2,1)S(1)} %get-tuple-element.45.refs_0_, bf16[2,192,320]{2,1,0:T(8,128)(2,1)S(1)} %get-tuple-element.46.refs_1_, bf16[2,192,320]{2,1,0:T(8,128)(2,1)S(1)} %get-tuple-element.47.refs_2_, ...), custom_call_target="tpu_custom_call" | custom-call | flops 20000000000 | bytes 1000000 | tf_op jit(solution)/shard_map/query_terms/pallas_call | solution.py:388
  31.3 1.6 %collective-permute-start.8 = (bf16[128,640]{1,0:T(8,128)(2,1)S(1)}, bf16[128,640]{1,0:T(8,128)(2,1)S(1)}, u32[]{:S(2)}, u32[]{:S(2)}) collective-permute-start(bf16[128,640]{1,0:T(8,128)(2,1)S(1)} %get-tuple-element.52), channel_id=1, source_target_pairs={{0,4},{4,0},{1,5},{5,1},{2,6},{6,2},{3,7},{7,3},{8,12},{12,8},{9,1... | collective-permute-start | bytes 491528 | tf_op jit(solution)/shard_map/ppermute | solution.py:311
  32.9 0.0 collective-permute-done.9.refs_1_
  32.9 1.6 %collective-permute-done.10.refs_2_ = bf16[128,256]{1,0:T(8,128)(2,1)S(1)} collective-permute-done((bf16[128,256]{1,0:T(8,128)(2,1)S(1)}, bf16[128,256]{1,0:T(8,128)(2,1)S(1)}, u32[]{:S(2)}, u32[]{:S(2)}) %collective-permute-start.10) | collective-permute-done | bytes 65568 | tf_op jit(solution)/shard_map/ppermute | solution.py:311
  34.5 0.7 %collective-permute-done.11.refs_3_ = bf16[128,256]{1,0:T(8,128)(2,1)S(1)} collective-permute-done((bf16[128,256]{1,0:T(8,128)(2,1)S(1)}, bf16[128,256]{1,0:T(8,128)(2,1)S(1)}, u32[]{:S(2)}, u32[]{:S(2)}) %collective-permute-start.11) | collective-permute-done | bytes 65568 | tf_op jit(solution)/shard_map/ppermute | solution.py:311
  35.3 0.1 collective-permute-start.12
  35.3 1.5 %collective-permute-start.13 = (bf16[32,256]{1,0:T(8,128)(2,1)S(1)}, bf16[32,256]{1,0:T(8,128)(2,1)S(1)}, u32[]{:S(2)}, u32[]{:S(2)}) collective-permute-start(bf16[32,256]{1,0:T(8,128)(2,1)S(1)} %get-tuple-element.59), channel_id=1, source_target_pairs={{0,2},{1,3},{2,0},{3,1},{4,6},{5,7},{6,4},{7,5},{8,10},{9,11},{10,... | collective-permute-start | bytes 49160 | tf_op jit(solution)/shard_map/ppermute | solution.py:311
  36.9 1.4 %collective-permute-start.14 = (bf16[32,256]{1,0:T(8,128)(2,1)S(1)}, bf16[32,256]{1,0:T(8,128)(2,1)S(1)}, u32[]{:S(2)}, u32[]{:S(2)}) collective-permute-start(bf16[32,256]{1,0:T(8,128)(2,1)S(1)} %get-tuple-element.60), channel_id=1, source_target_pairs={{0,3},{1,0},{2,1},{3,2},{4,7},{5,4},{6,5},{7,6},{8,11},{9,8},{10,9... | collective-permute-start | bytes 49160 | tf_op jit(solution)/shard_map/ppermute | solution.py:311
  38.3 0.2 collective-permute-done.12.refs_1_
  38.5 0.7 %collective-permute-done.13.refs_2_ = bf16[32,256]{1,0:T(8,128)(2,1)S(1)} collective-permute-done((bf16[32,256]{1,0:T(8,128)(2,1)S(1)}, bf16[32,256]{1,0:T(8,128)(2,1)S(1)}, u32[]{:S(2)}, u32[]{:S(2)}) %collective-permute-start.13) | collective-permute-done | bytes 16416 | tf_op jit(solution)/shard_map/ppermute | solution.py:311
  39.1 0.6 %collective-permute-done.14.refs_3_ = bf16[32,256]{1,0:T(8,128)(2,1)S(1)} collective-permute-done((bf16[32,256]{1,0:T(8,128)(2,1)S(1)}, bf16[32,256]{1,0:T(8,128)(2,1)S(1)}, u32[]{:S(2)}, u32[]{:S(2)}) %collective-permute-start.14) | collective-permute-done | bytes 16416 | tf_op jit(solution)/shard_map/ppermute | solution.py:311
  39.7 0.0 collective-permute-done.8.received_ref
  39.7 0.8 %place.1 = (bf16[128,640]{1,0:T(8,128)(2,1)}, bf16[32,512]{1,0:T(8,128)(2,1)}, bf16[32,512]{1,0:T(8,128)(2,1)}) custom-call(f32[128,640]{1,0:T(8,128)S(1)} %get-tuple-element.51.own_ref, bf16[128,640]{1,0:T(8,128)(2,1)S(1)} %collective-permute-done.8.received_ref, bf16[32,256]{1,0:T(8,128)(2,1)S(1)} %get-tuple-element.57.refs_0_, ...), custom_call_target="tpu_custom_call" | custom-call | tf_op jit(solution)/shard_map/place/pallas_call | solution.py:408
  (1 shorter events, 0.0 us)
Async XLA Ops:
  0.6 5.4 %copy-start.1 = (bf16[128,640]{1,0:T(8,128)(2,1)S(1)}, bf16[128,640]{1,0:T(8,128)(2,1)}, u32[]{:S(2)}) copy-start(bf16[128,640]{1,0:T(8,128)(2,1)} %q_ref.1) | copy-start | bytes 491524
  1.6 7.0 %collective-permute-start.1 = (bf16[32,256]{1,0:T(8,128)(2,1)S(1)}, bf16[32,256]{1,0:T(8,128)(2,1)S(1)}, u32[]{:S(2)}, u32[]{:S(2)}) collective-permute-start(bf16[32,256]{1,0:T(8,128)(2,1)S(1)} %get-tuple-element.33), channel_id=1, source_target_pairs={{0,1},{1,2},{2,3},{3,0},{4,5},{5,6},{6,7},{7,4},{8,9},{9,10},{10,1... | collective-permute-start | bytes 49160 | tf_op jit(solution)/shard_map/ppermute | solution.py:311
  2.1 6.5 %collective-permute-start.2 = (bf16[32,256]{1,0:T(8,128)(2,1)S(1)}, bf16[32,256]{1,0:T(8,128)(2,1)S(1)}, u32[]{:S(2)}, u32[]{:S(2)}) collective-permute-start(bf16[32,256]{1,0:T(8,128)(2,1)S(1)} %get-tuple-element.34), channel_id=1, source_target_pairs={{0,2},{1,3},{2,0},{3,1},{4,6},{5,7},{6,4},{7,5},{8,10},{9,11},{10,... | collective-permute-start | bytes 49160 | tf_op jit(solution)/shard_map/ppermute | solution.py:311
  4.6 4.0 %collective-permute-start.3 = (bf16[32,256]{1,0:T(8,128)(2,1)S(1)}, bf16[32,256]{1,0:T(8,128)(2,1)S(1)}, u32[]{:S(2)}, u32[]{:S(2)}) collective-permute-start(bf16[32,256]{1,0:T(8,128)(2,1)S(1)} %get-tuple-element.35), channel_id=1, source_target_pairs={{0,3},{1,0},{2,1},{3,2},{4,7},{5,4},{6,5},{7,6},{8,11},{9,8},{10,9... | collective-permute-start | bytes 49160 | tf_op jit(solution)/shard_map/ppermute | solution.py:311
  6.0 0.9 %copy-start.2 = (bf16[128,640]{1,0:T(8,128)(2,1)S(1)}, bf16[128,640]{1,0:T(8,128)(2,1)}, u32[]{:S(2)}) copy-start(bf16[128,640]{1,0:T(8,128)(2,1)} %do_ref.1) | copy-start | bytes 491524
  7.0 8.8 %copy-start = (s32[16]{0:T(128)S(1)}, s32[16]{0:T(128)}, u32[]{:S(2)}) copy-start(s32[16]{0:T(128)} %order_ref.9) | copy-start | bytes 196
  7.0 8.8 %collective-permute-start = (bf16[2,2,320,128]{3,2,1,0:T(8,128)(2,1)S(1)}, bf16[2,2,320,128]{3,2,1,0:T(8,128)(2,1)S(1)}, u32[]{:S(2)}, u32[]{:S(2)}) collective-permute-start(bf16[2,2,320,128]{3,2,1,0:T(8,128)(2,1)S(1)} %stack.1.own_ref), channel_id=1, source_target_pairs={{0,4},{4,0},{1,5},{5,1},{2,6},{6,2},{3,7},{7,3},{8,12},{12,8},{9,1... | collective-permute-start | bytes 983048 | tf_op jit(solution)/shard_map/ppermute | solution.py:311
  8.8 6.0 %collective-permute-start.4 = (bf16[128,256]{1,0:T(8,128)(2,1)S(1)}, bf16[128,256]{1,0:T(8,128)(2,1)S(1)}, u32[]{:S(2)}, u32[]{:S(2)}) collective-permute-start(bf16[128,256]{1,0:T(8,128)(2,1)S(1)} %join.1.refs_0_), channel_id=1, source_target_pairs={{0,24},{8,0},{16,8},{24,16},{1,25},{9,1},{17,9},{25,17},{2,26},{10... | collective-permute-start | bytes 196616 | tf_op jit(solution)/shard_map/ppermute | solution.py:311
  12.4 8.2 %collective-permute-start.6 = (bf16[128,256]{1,0:T(8,128)(2,1)S(1)}, bf16[128,256]{1,0:T(8,128)(2,1)S(1)}, u32[]{:S(2)}, u32[]{:S(2)}) collective-permute-start(bf16[128,256]{1,0:T(8,128)(2,1)S(1)} %join.1.refs_0_), channel_id=1, source_target_pairs={{0,8},{8,16},{16,24},{24,0},{1,9},{9,17},{17,25},{25,1},{2,10},{10... | collective-permute-start | bytes 196616 | tf_op jit(solution)/shard_map/ppermute | solution.py:311
  12.4 7.1 %collective-permute-start.5 = (bf16[128,256]{1,0:T(8,128)(2,1)S(1)}, bf16[128,256]{1,0:T(8,128)(2,1)S(1)}, u32[]{:S(2)}, u32[]{:S(2)}) collective-permute-start(bf16[128,256]{1,0:T(8,128)(2,1)S(1)} %join.1.refs_0_), channel_id=1, source_target_pairs={{0,16},{8,24},{16,0},{24,8},{1,17},{9,25},{17,1},{25,9},{2,18},{10... | collective-permute-start | bytes 196616 | tf_op jit(solution)/shard_map/ppermute | solution.py:311
  21.8 3.9 %collective-permute-start.7 = (f32[12,320]{1,0:T(8,128)S(1)}, f32[12,320]{1,0:T(8,128)S(1)}, u32[]{:S(2)}, u32[]{:S(2)}) collective-permute-start(f32[12,320]{1,0:T(8,128)S(1)} %merge.1), channel_id=1, source_target_pairs={{0,4},{4,0},{1,5},{5,1},{2,6},{6,2},{3,7},{7,3},{8,12},{12,8},{9,1... | collective-permute-start | bytes 46088 | tf_op jit(solution)/shard_map/ppermute | solution.py:311
  27.1 5.8 %collective-permute-start.9 = (bf16[128,256]{1,0:T(8,128)(2,1)S(1)}, bf16[128,256]{1,0:T(8,128)(2,1)S(1)}, u32[]{:S(2)}, u32[]{:S(2)}) collective-permute-start(bf16[128,256]{1,0:T(8,128)(2,1)S(1)} %get-tuple-element.54), channel_id=1, source_target_pairs={{0,24},{8,0},{16,8},{24,16},{1,25},{9,1},{17,9},{25,17},{2,26},{10... | collective-permute-start | bytes 196616 | tf_op jit(solution)/shard_map/ppermute | solution.py:311
  29.1 5.4 %collective-permute-start.10 = (bf16[128,256]{1,0:T(8,128)(2,1)S(1)}, bf16[128,256]{1,0:T(8,128)(2,1)S(1)}, u32[]{:S(2)}, u32[]{:S(2)}) collective-permute-start(bf16[128,256]{1,0:T(8,128)(2,1)S(1)} %get-tuple-element.55), channel_id=1, source_target_pairs={{0,16},{8,24},{16,0},{24,8},{1,17},{9,25},{17,1},{25,9},{2,18},{10... | collective-permute-start | bytes 196616 | tf_op jit(solution)/shard_map/ppermute | solution.py:311
  29.1 6.1 %collective-permute-start.11 = (bf16[128,256]{1,0:T(8,128)(2,1)S(1)}, bf16[128,256]{1,0:T(8,128)(2,1)S(1)}, u32[]{:S(2)}, u32[]{:S(2)}) collective-permute-start(bf16[128,256]{1,0:T(8,128)(2,1)S(1)} %get-tuple-element.56), channel_id=1, source_target_pairs={{0,8},{8,16},{16,24},{24,0},{1,9},{9,17},{17,25},{25,1},{2,10},{10... | collective-permute-start | bytes 196616 | tf_op jit(solution)/shard_map/ppermute | solution.py:311
  31.3 8.4 %collective-permute-start.8 = (bf16[128,640]{1,0:T(8,128)(2,1)S(1)}, bf16[128,640]{1,0:T(8,128)(2,1)S(1)}, u32[]{:S(2)}, u32[]{:S(2)}) collective-permute-start(bf16[128,640]{1,0:T(8,128)(2,1)S(1)} %get-tuple-element.52), channel_id=1, source_target_pairs={{0,4},{4,0},{1,5},{5,1},{2,6},{6,2},{3,7},{7,3},{8,12},{12,8},{9,1... | collective-permute-start | bytes 491528 | tf_op jit(solution)/shard_map/ppermute | solution.py:311
  35.3 3.2 %collective-permute-start.12 = (bf16[32,256]{1,0:T(8,128)(2,1)S(1)}, bf16[32,256]{1,0:T(8,128)(2,1)S(1)}, u32[]{:S(2)}, u32[]{:S(2)}) collective-permute-start(bf16[32,256]{1,0:T(8,128)(2,1)S(1)} %get-tuple-element.58), channel_id=1, source_target_pairs={{0,1},{1,2},{2,3},{3,0},{4,5},{5,6},{6,7},{7,4},{8,9},{9,10},{10,1... | collective-permute-start | bytes 49160 | tf_op jit(solution)/shard_map/ppermute | solution.py:311
  35.3 3.8 %collective-permute-start.13 = (bf16[32,256]{1,0:T(8,128)(2,1)S(1)}, bf16[32,256]{1,0:T(8,128)(2,1)S(1)}, u32[]{:S(2)}, u32[]{:S(2)}) collective-permute-start(bf16[32,256]{1,0:T(8,128)(2,1)S(1)} %get-tuple-element.59), channel_id=1, source_target_pairs={{0,2},{1,3},{2,0},{3,1},{4,6},{5,7},{6,4},{7,5},{8,10},{9,11},{10,... | collective-permute-start | bytes 49160 | tf_op jit(solution)/shard_map/ppermute | solution.py:311
  36.9 2.8 %collective-permute-start.14 = (bf16[32,256]{1,0:T(8,128)(2,1)S(1)}, bf16[32,256]{1,0:T(8,128)(2,1)S(1)}, u32[]{:S(2)}, u32[]{:S(2)}) collective-permute-start(bf16[32,256]{1,0:T(8,128)(2,1)S(1)} %get-tuple-element.60), channel_id=1, source_target_pairs={{0,3},{1,0},{2,1},{3,2},{4,7},{5,4},{6,5},{7,6},{8,11},{9,8},{10,9... | collective-permute-start | bytes 49160 | tf_op jit(solution)/shard_map/ppermute | solution.py:311

commit v8 on v7

v8 whole, which is shorter than its diff:
```python
import functools
import math

import jax
import jax.numpy as jnp
from jax import lax
from jax.experimental import pallas as pl
from jax.experimental.pallas import tpu as pltpu
from jax.sharding import Mesh
from jax.sharding import PartitionSpec as P

HEADS = 20
KV_HEADS = 4
HEAD = 128
GROUP = HEADS // KV_HEADS
SCALE = HEAD ** (-0.5)
EXPONENT_SCALE = SCALE * math.log2(math.e)
LOWEST = -1e30
ROWS_DOT_ROWS = (((1,), (1,)), ((), ()))
COLS_DOT_COLS = (((0,), (0,)), ((), ()))


def at_rows(start, size):
    return pl.ds(pl.multiple_of(start, size), size)


def load(source_ref, target_ref, sem):
    copy = pltpu.make_async_copy(source_ref, target_ref, sem)
    copy.start()
    return copy


def wait_all(copies):
    for copy in copies:
        copy.wait()


def partner(index, distance, size):
    if size & (size - 1) == 0:
        return index ^ distance
    return (index + size - distance) % size


def target_of(index, distance, size):
    if size & (size - 1) == 0:
        return index ^ distance
    return (index + distance) % size


def pick(condition, chosen, other):
    return lax.select(condition, chosen, jnp.full_like(chosen, other))


class Work:
    def __init__(self, order_ref, rows, outer, members, block_refs):
        self.rows, self.members, self.block_refs = rows, members, block_refs
        self.low_rows = len(members) * rows
        at, side = lax.axis_index("outer"), lax.axis_index("pair")

        def pair_of(index):
            first, second = order_ref[2 * index], order_ref[2 * index + 1]
            return jnp.minimum(first, second), jnp.where(first < second, 0, 1)

        self.owners = [pair_of(2 * at + side), pair_of(2 * at + 1 - side)]
        self.pairs = [pair_of(2 * partner(at, d, outer) + side) for d in members]

    @staticmethod
    def slot(place, half):
        return jnp.where(half == 0, place, 1 - place)

    def query_slot(self, owner, half):
        return self.slot(self.owners[owner][1], half)

    def key_rows(self, n, half):
        return at_rows(self.slot(self.pairs[n][1], half) * self.rows, self.rows)

    def keys(self, n, half, cols):
        return self.block_refs[n][self.key_rows(n, half), cols]

    def low_keys(self, cols):
        return jnp.concatenate([self.keys(n, 0, cols) for n in range(len(self.members))], axis=0)

    def tiles(self, owner):
        found = []
        for n, d in enumerate(self.members):
            here = pl.ds(self.low_rows + n * self.rows, self.rows)
            if owner == 0 and d == 0:
                found.append((n, 0, here, True))
                found.append((n, 1, pl.ds(2 * self.low_rows, self.rows), True))
            else:
                half = jnp.where(self.owners[owner][0] >= self.pairs[n][0], 0, 1)
                found.append((n, half, here, False))
        return found


def split_kernel(cache_ref, *refs):
    parts, sems = refs[:-1], refs[-1]
    kvh = len(parts)
    rows = parts[0].shape[0]
    copies = []
    for e, part_ref in enumerate(parts):
        cols = at_rows(target_of(lax.axis_index("kvh"), e, kvh) * HEAD, HEAD)
        for n in range(2):
            source = cache_ref.at[pl.ds(n * rows, rows), cols]
            copies.append(load(source, part_ref.at[:, pl.ds(n * HEAD, HEAD)], sems.at[2 * e + n]))
    wait_all(copies)


def stack_kernel(q_ref, do_ref, after_ref, out_ref):
    rows = q_ref.shape[0] // 2
    for n, source_ref in enumerate((q_ref, do_ref)):
        for slot in range(2):
            for h in range(GROUP):
                out_ref[n, slot, h * rows : (h + 1) * rows, :] = source_ref[
                    slot * rows : (slot + 1) * rows, h * HEAD : (h + 1) * HEAD
                ]


def join_kernel(*refs):
    parts, (out_ref, sems) = refs[:-2], refs[-2:]
    kvh = len(parts)
    rows = parts[0].shape[0]
    copies = []
    for e, part_ref in enumerate(parts):
        source = partner(lax.axis_index("kvh"), e, kvh)
        copies.append(load(part_ref, out_ref.at[at_rows(source * rows, rows)], sems.at[e]))
    wait_all(copies)


def stats_kernel(outer, members, order_ref, own_ref, other_ref, *refs):
    block_refs, (out_ref, e_ref, dp_ref) = refs[: len(members)], refs[-3:]
    rows = block_refs[0].shape[0] // 2
    work = Work(order_ref, rows, outer, members, block_refs)
    low_part = pl.ds(0, work.low_rows)
    key_cols, value_cols = slice(0, HEAD), slice(HEAD, 2 * HEAD)

    def products(keys, queries):
        return lax.dot_general(keys, queries, ROWS_DOT_ROWS, preferred_element_type=jnp.float32)

    tops = []
    for owner, qd_ref in enumerate((own_ref, other_ref)):
        high = work.query_slot(owner, 1)
        scores = products(work.low_keys(key_cols), qd_ref[0, high])
        e_ref[owner, low_part, :] = scores
        dp_ref[owner, low_part, :] = products(work.low_keys(value_cols), qd_ref[1, high])
        top = [jnp.full((1, scores.shape[1]), LOWEST, jnp.float32), jnp.max(scores, axis=0, keepdims=True)]
        for n, half, here, masked in work.tiles(owner):
            slot = work.query_slot(owner, half)
            scores = products(work.keys(n, half, key_cols), qd_ref[0, slot])
            if masked:
                key = lax.broadcasted_iota(jnp.int32, scores.shape, 0)
                query = lax.rem(lax.broadcasted_iota(jnp.int32, (1, scores.shape[1]), 1), rows)
                scores = jnp.where(key <= query, scores, LOWEST)
            e_ref[owner, here, :] = scores
            dp_ref[owner, here, :] = products(work.keys(n, half, value_cols), qd_ref[1, slot])
            most = jnp.max(scores, axis=0, keepdims=True)
            for side in range(2):
                seen = most if masked else pick(half == side, most, LOWEST)
                if not masked or half == side:
                    top[side] = jnp.maximum(top[side], seen)
        tops.append(top)

    for owner, top in enumerate(tops):

        def sums(here, most):
            expon = jnp.exp2((e_ref[owner, here, :] - most) * EXPONENT_SCALE)
            e_ref[owner, here, :] = expon
            return [
                jnp.sum(expon, axis=0, keepdims=True),
                jnp.sum(expon * dp_ref[owner, here, :], axis=0, keepdims=True),
            ]

        zero = jnp.zeros_like(top[0])
        totals = [[zero, zero], sums(low_part, top[1])]
        for n, half, here, masked in work.tiles(owner):
            part = sums(here, top[half] if masked else lax.select(half == 0, top[0], top[1]))
            for side in range(2):
                if not masked or half == side:
                    seen = part if masked else [pick(half == side, one, 0) for one in part]
                    totals[side] = [total + one for total, one in zip(totals[side], seen)]
        for half in range(2):
            base = (2 * owner + half) * 3
            for n, row in enumerate((top[half], *totals[half])):
                out_ref[base + n : base + n + 1, :] = row


def merged(stats_refs, base):
    rows = [ref[base : base + 3, :] for ref in stats_refs]
    top = functools.reduce(jnp.maximum, [part[:1] for part in rows])
    weights = [jnp.exp2((part[:1] - top) * EXPONENT_SCALE) for part in rows]
    total = sum(weight * part[1:2] for weight, part in zip(weights, rows))
    delta = sum(weight * part[2:3] for weight, part in zip(weights, rows))
    return top, total, delta


def merge_kernel(*refs):
    stats_refs, out_ref = refs[:-1], refs[-1]
    for base in range(0, 12, 3):
        for n, row in enumerate(merged(stats_refs, base)):
            out_ref[base + n : base + n + 1, :] = row


def grads_kernel(outer, groups, order_ref, own_ref, other_ref, *refs):
    count = len(groups)
    stats_refs, theirs_ref, refs = refs[:count], refs[count], refs[count + 1 :]
    e_refs, dp_refs, refs = refs[:count], refs[count : 2 * count], refs[2 * count :]
    term_refs, gs_refs = refs[:outer], refs[outer:]
    rows = term_refs[0].shape[0] // 2
    weights, deltas = [[] for _ in groups], []
    for owner in range(2):
        delta = []
        group_weights = [[] for _ in groups]
        for half in range(2):
            base = (2 * owner + half) * 3
            base2 = (2 * (1 - owner) + half) * 3
            mine = merged(stats_refs, base)
            theirs = [theirs_ref[base2 + n : base2 + n + 1, :] for n in range(3)]
            top = jnp.maximum(mine[0], theirs[0])
            w1 = jnp.exp2((mine[0] - top) * EXPONENT_SCALE)
            w2 = jnp.exp2((theirs[0] - top) * EXPONENT_SCALE)
            total = w1 * mine[1] + w2 * theirs[1]
            delta.append((w1 * mine[2] + w2 * theirs[2]) / total)
            for n, stats_ref in enumerate(stats_refs):
                weight = jnp.exp2((stats_ref[base : base + 1, :] - top) * EXPONENT_SCALE)
                group_weights[n].append(weight / total)
        deltas.append(delta)
        for n in range(count):
            weights[n].append(group_weights[n])

    for n, members in enumerate(groups):
        work = Work(order_ref, rows, outer, members, None)
        terms = [[None] * len(members), [None] * len(members)]

        def add(half, at, pair):
            old = terms[half][at]
            terms[half][at] = pair if old is None else [one + more for one, more in zip(old, pair)]

        for owner, qd_ref in enumerate((own_ref, other_ref)):

            def gradients(here, slot, weight, delta):
                probs = e_refs[n][owner, here, :] * weight
                grads = (probs * (dp_refs[n][owner, here, :] - delta)).astype(jnp.bfloat16)
                gs_refs[n][owner, here, :] = grads
                return [
                    jnp.dot(grads, qd_ref[0, slot], preferred_element_type=jnp.float32),
                    jnp.dot(probs.astype(jnp.bfloat16), qd_ref[1, slot], preferred_element_type=jnp.float32),
                ]

            weight, delta = weights[n][owner], deltas[owner]
            low_part = pl.ds(0, work.low_rows)
            part = gradients(low_part, work.query_slot(owner, 1), weight[1], delta[1])
            for at in range(len(members)):
                add(0, at, [one[at * rows : (at + 1) * rows] for one in part])
            for at, half, here, masked in work.tiles(owner):
                slot = work.query_slot(owner, half)
                if masked:
                    add(half, at, gradients(here, slot, weight[half], delta[half]))
                else:
                    is_low = half == 0
                    part = gradients(here, slot, lax.select(is_low, *weight), lax.select(is_low, *delta))
                    for side in range(2):
                        add(side, at, [pick(half == side, one, 0) for one in part])
        for at, d in enumerate(members):
            term_ref = term_refs[d]
            for half in range(2):
                target = work.key_rows(at, half)
                of_keys, of_values = terms[half][at]
                term_ref[target, :HEAD] = (of_keys * SCALE).astype(term_ref.dtype)
                term_ref[target, HEAD:] = of_values.astype(term_ref.dtype)


def query_kernel(outer, groups, order_ref, *refs):
    count = len(groups)
    block_refs, gs_refs, (own_ref, other_ref) = refs[:outer], refs[outer : outer + count], refs[outer + count :]
    rows = own_ref.shape[0] // 2
    works = [
        Work(order_ref, rows, outer, members, [block_refs[d] for d in members]) for members in groups
    ]
    cols = slice(0, HEAD)
    for owner, target in ((0, own_ref), (1, other_ref)):
        totals = [None, None]

        def add(half, part):
            totals[half] = part if totals[half] is None else totals[half] + part

        for gs_ref, work in zip(gs_refs, works):

            def terms(keys, here):
                return lax.dot_general(
                    keys, gs_ref[owner, here, :], COLS_DOT_COLS, preferred_element_type=jnp.float32
                )

            add(1, terms(work.low_keys(cols), pl.ds(0, work.low_rows)))
            for n, half, here, masked in work.tiles(owner):
                part = terms(work.keys(n, half, cols), here)
                for side in range(2):
                    if not masked:
                        add(side, pick(half == side, part, 0))
                    elif half == side:
                        add(side, part)
        for half in range(2):
            place = at_rows(works[0].query_slot(owner, half) * rows, rows)
            grads = (jnp.transpose(totals[half]) * SCALE).astype(target.dtype)
            for h in range(GROUP):
                target[place, h * HEAD : (h + 1) * HEAD] = grads[h * rows : (h + 1) * rows, :]


def sum_kernel(outer, *refs):
    terms, outs, total_ref = refs[:outer], refs[outer:-1], refs[-1]
    total = terms[0][...]
    for term_ref in terms[1:]:
        total = total + term_ref[...].astype(jnp.float32)
    total_ref[...] = total
    kvh = len(outs)
    rows = outs[0].shape[0]
    for e, out_ref in enumerate(outs):
        target = target_of(lax.axis_index("kvh"), e, kvh)
        out_ref[...] = total_ref[at_rows(target * rows, rows), :].astype(jnp.bfloat16)


def place_kernel(own_ref, received_ref, *refs):
    parts, (dq_out, key_out, value_out, dq_ref, sems) = refs[:-5], refs[-5:]
    kvh = len(parts)
    copies = []
    for e, part_ref in enumerate(parts):
        cols = at_rows(partner(lax.axis_index("kvh"), e, kvh) * HEAD, HEAD)
        copies.append(load(part_ref.at[:, pl.ds(0, HEAD)], key_out.at[:, cols], sems.at[2 * e]))
        copies.append(load(part_ref.at[:, pl.ds(HEAD, HEAD)], value_out.at[:, cols], sems.at[2 * e + 1]))
    dq_ref[...] = (own_ref[...] + received_ref[...].astype(jnp.float32)).astype(jnp.bfloat16)
    copies.append(load(dq_ref, dq_out, sems.at[2 * kvh]))
    wait_all(copies)


def per_device(queries, keys, values, d_out, slab_order):
    kvh = lax.axis_size("kvh")
    outer = lax.axis_size("outer")
    local_rows, query_width = queries.shape
    cache_rows = keys.shape[0]
    slab_rows = local_rows // 2
    columns = GROUP * slab_rows
    params = pltpu.CompilerParams(vmem_limit_bytes=(8 << 20) + (10 << 10) * outer * local_rows)
    beside = pl.CostEstimate(flops=2 * 10**10, bytes_accessed=10**6, transcendentals=0)
    vmem = pl.BlockSpec(memory_space=pltpu.VMEM)
    smem = pl.BlockSpec(memory_space=pltpu.SMEM)
    anywhere = pl.BlockSpec(memory_space=pl.ANY)
    shape = jax.ShapeDtypeStruct
    dma = pltpu.SemaphoreType.DMA
    low, full = jnp.bfloat16, jnp.float32

    def call(kernel, name, **arguments):
        return pl.pallas_call(kernel, compiler_params=params, name=name, **arguments)

    def shift(array, axis, by):
        size = lax.axis_size(axis)
        if by > 0:
            return lax.ppermute(array, axis, [(n, target_of(n, by, size)) for n in range(size)])
        return lax.ppermute(array, axis, [(n, partner(n, -by, size)) for n in range(size)])

    part = shape((cache_rows, 2 * HEAD), low)
    block = shape((local_rows, 2 * HEAD), low)
    parts = call(
        split_kernel,
        "split",
        out_shape=(part,) * kvh,
        in_specs=[vmem],
        out_specs=(vmem,) * kvh,
        scratch_shapes=[dma((2 * kvh,))],
    )(jnp.concatenate([keys, values], axis=0))
    own_qd = call(
        stack_kernel,
        "stack",
        out_shape=shape((2, 2, columns, HEAD), low),
        in_specs=[vmem, vmem, anywhere],
        out_specs=vmem,
        cost_estimate=beside,
    )(queries, d_out, parts[0])
    parts = [parts[0]] + [shift(parts[e], "kvh", e) for e in range(1, kvh)]
    other_qd = shift(own_qd, "pair", 1)
    own_block = call(
        join_kernel,
        "join",
        out_shape=block,
        in_specs=[anywhere] * kvh,
        out_specs=vmem,
        scratch_shapes=[dma((kvh,))],
        cost_estimate=beside,
    )(*parts)
    blocks = [own_block] + [shift(own_block, "outer", d) for d in range(1, outer)]

    far = outer // 2 + 1
    groups = [[0, *range(far, outer)], list(range(1, far))]
    all_stats = shape((12, columns), full)
    results = []
    for n, members in enumerate(groups):
        score_rows = shape((2, (2 * len(members) + 1) * slab_rows, columns), full)
        results.append(
            call(
                functools.partial(stats_kernel, outer, members),
                "stats",
                out_shape=(all_stats, score_rows, score_rows),
                in_specs=[smem] + [vmem] * (2 + len(members)) + [anywhere] * min(n, 1),
                out_specs=(vmem,) * 3,
                cost_estimate=beside if n + 1 < len(groups) else None,
            )(slab_order, own_qd, other_qd, *[blocks[d] for d in members], *[done[0] for done in results[-1:]])
        )
    stats, expon, grad_probs = zip(*results)
    mine = call(
        merge_kernel, "merge", out_shape=all_stats, in_specs=[vmem] * len(stats), out_specs=vmem
    )(*stats)
    theirs = shift(mine, "pair", 1)
    count = len(groups)
    grads = call(
        functools.partial(grads_kernel, outer, groups),
        "grads",
        out_shape=(shape(block.shape, full),)
        + (block,) * (outer - 1)
        + tuple(shape(scores.shape, low) for scores in expon),
        in_specs=[smem] + [vmem] * (3 + 3 * count),
        out_specs=(vmem,) * (outer + count),
    )(slab_order, own_qd, other_qd, *stats, theirs, *expon, *grad_probs)
    terms, score_grads = grads[:outer], grads[outer:]
    terms = [terms[0]] + [shift(terms[d], "outer", -d) for d in range(outer - 1, 0, -1)]
    own_grads, other_grads = call(
        functools.partial(query_kernel, outer, groups),
        "query_terms",
        out_shape=(shape(queries.shape, full), shape(queries.shape, low)),
        in_specs=[smem] + [vmem] * (outer + count),
        out_specs=(vmem, vmem),
        cost_estimate=beside,
    )(slab_order, *blocks, *score_grads)
    received_grads = shift(other_grads, "pair", 1)
    owned = call(
        functools.partial(sum_kernel, outer),
        "sum",
        out_shape=(part,) * kvh,
        in_specs=[vmem] * outer,
        out_specs=(vmem,) * kvh,
        scratch_shapes=[pltpu.VMEM(block.shape, full)],
        cost_estimate=beside,
    )(*terms)
    owned = [owned[0]] + [shift(owned[e], "kvh", e) for e in range(1, kvh)]
    return call(
        place_kernel,
        "place",
        out_shape=(shape(queries.shape, low), shape(keys.shape, low), shape(values.shape, low)),
        in_specs=[vmem, vmem] + [anywhere] * kvh,
        out_specs=(anywhere,) * 3,
        scratch_shapes=[pltpu.VMEM(queries.shape, low), dma((2 * kvh + 1,))],
    )(own_grads, received_grads, *owned)


def solution(mesh):
    kvh = mesh.shape["kvh"]
    pairs = mesh.shape["seq"] // 2
    paired = Mesh(mesh.devices.reshape(pairs, 2, kvh), ("outer", "pair", "kvh"))
    seq = ("outer", "pair")
    cache = P(("outer", "pair", "kvh"), None)
    placed = (P(seq, "kvh"), cache, cache, P(seq, "kvh"), P())
    return jax.shard_map(
        per_device,
        mesh=paired,
        in_specs=placed,
        out_specs=(P(seq, "kvh"), cache, cache),
        check_vma=False,
    )
```

time: 40.8 us -> 38.5 us (0.944)
  Pallas kernels: 7.9 us -> 6.23 us
    pallas_call x3 -> x2, Pallas kernels: 3.68 us -> 2.45 us  [per_device(): call(functools.partial(stats_kernel, outer, members), 'stats', out_shape=...]
    ppermute x15, starting transfers between devices: 19.4 us -> 19 us  [the longest x12 14.5 us: shift(): lax.ppermute(array, axis, [(n, target_of(n, by, size)) for n in range(siz...]
  transfers between devices with their start and end apart: 15 -> 15, of which waited for: 9 -> 8; matrix products, arithmetic and copies ran while one was open for 0% -> 0% of each run, Pallas kernels for 11% -> 7%
where the time goes in v8:
time: 38.5 us; the launch traced here: 38.3 us
  starting transfers between devices  19 us (49%)
  waiting for transfers between devices  10.6 us (28%)
  Pallas kernels  6.23 us (16%)
  local copies, waits for them, and re-layouts  0.93 us (2%)
  other arithmetic  0.82 us (2%)
  between operations  0.72 us (2%)
    ppermute x12, starting transfers between devices, shift(): lax.ppermute(array, axis, [(n, target_of(n, by, size)) for n in range(siz...  14.5 us
    ppermute x12, waiting for transfers between devices, shift(): lax.ppermute(array, axis, [(n, target_of(n, by, size)) for n in range(siz...  9.26 us
    ppermute x3, starting transfers between devices, shift(): lax.ppermute(array, axis, [(n, partner(n, -by, size)) for n in range(size)])  4.45 us
    pallas_call x2, Pallas kernels, per_device(): call(functools.partial(stats_kernel, outer, members), 'stats', out_shape=...  2.45 us
    pallas_call x1, Pallas kernels, per_device(): call(functools.partial(grads_kernel, outer, groups), 'grads', out_shape=(...  1.42 us
    ppermute x3, waiting for transfers between devices, shift(): lax.ppermute(array, axis, [(n, partner(n, -by, size)) for n in range(size)])  1.37 us
    pallas_call x1, Pallas kernels, per_device(): call(functools.partial(query_kernel, outer, groups), 'query_terms', out_s...  1.22 us
    unnamed x6, local copies, waits for them, and re-layouts  0.93 us
  transfers between devices with their start and end apart: 15, of which 8 were waited for; matrix products, arithmetic and copies ran while one was open for 0% of the time, Pallas kernels for 7%

profile of v8, /device:TPU:0, one launch (start us, length us, event | category | flops | bytes accessed | tf_op | source)
XLA Modules:
  0.0 38.3 jit_solution(6436038854878267101)
XLA Ops:
  0.6 0.0 copy-start.1
  0.6 0.8 %pad_maximum_fusion.cache_ref = bf16[64,512]{1,0:T(8,128)(2,1)S(1)} fusion(bf16[32,512]{1,0:T(8,128)(2,1)} %param.7, bf16[32,512]{1,0:T(8,128)(2,1)} %param.6), kind=kLoop, calls=%fused_computation | loop fusion | flops 131072 | bytes 131072 | tf_op jit(solution)/shard_map/concatenate | solution.py:368
  1.5 0.1 split.1
  1.6 0.5 %collective-permute-start = (bf16[32,256]{1,0:T(8,128)(2,1)S(1)}, bf16[32,256]{1,0:T(8,128)(2,1)S(1)}, u32[]{:S(2)}, u32[]{:S(2)}) collective-permute-start(bf16[32,256]{1,0:T(8,128)(2,1)S(1)} %get-tuple-element.26), channel_id=1, source_target_pairs={{0,1},{1,0},{2,3},{3,2},{4,5},{5,4},{6,7},{7,6},{8,9},{9,8},{10,11... | collective-permute-start | bytes 49160 | tf_op jit(solution)/shard_map/ppermute | solution.py:356
  2.1 2.6 %collective-permute-start.1 = (bf16[32,256]{1,0:T(8,128)(2,1)S(1)}, bf16[32,256]{1,0:T(8,128)(2,1)S(1)}, u32[]{:S(2)}, u32[]{:S(2)}) collective-permute-start(bf16[32,256]{1,0:T(8,128)(2,1)S(1)} %get-tuple-element.27), channel_id=1, source_target_pairs={{0,2},{1,3},{2,0},{3,1},{4,6},{5,7},{6,4},{7,5},{8,10},{9,11},{10,... | collective-permute-start | bytes 49160 | tf_op jit(solution)/shard_map/ppermute | solution.py:356
  4.7 0.1 collective-permute-start.2
  4.7 0.0 copy-done.1
  4.7 0.0 copy-start.2
  4.7 0.9 %copy-done.2 = bf16[128,640]{1,0:T(8,128)(2,1)S(1)} copy-done((bf16[128,640]{1,0:T(8,128)(2,1)S(1)}, bf16[128,640]{1,0:T(8,128)(2,1)}, u32[]{:S(2)}) %copy-start.2) | copy-done | bytes 163864
  5.6 0.1 stack.1.own_ref
  5.7 0.0 copy-start
  5.7 1.8 %collective-permute-start.6 = (bf16[2,2,320,128]{3,2,1,0:T(8,128)(2,1)S(1)}, bf16[2,2,320,128]{3,2,1,0:T(8,128)(2,1)S(1)}, u32[]{:S(2)}, u32[]{:S(2)}) collective-permute-start(bf16[2,2,320,128]{3,2,1,0:T(8,128)(2,1)S(1)} %stack.1.own_ref), channel_id=1, source_target_pairs={{0,4},{4,0},{1,5},{5,1},{2,6},{6,2},{3,7},{7,3},{8,12},{12,8},{9,1... | collective-permute-start | bytes 983048 | tf_op jit(solution)/shard_map/ppermute | solution.py:356
  7.5 0.0 collective-permute-done.refs_1_
  7.5 0.0 collective-permute-done.1.refs_2_
  7.5 0.3 collective-permute-done.2.refs_3_
  7.8 0.1 join.1.refs_0_
  7.9 3.7 %collective-permute-start.5 = (bf16[128,256]{1,0:T(8,128)(2,1)S(1)}, bf16[128,256]{1,0:T(8,128)(2,1)S(1)}, u32[]{:S(2)}, u32[]{:S(2)}) collective-permute-start(bf16[128,256]{1,0:T(8,128)(2,1)S(1)} %join.1.refs_0_), channel_id=1, source_target_pairs={{0,24},{8,16},{16,8},{24,0},{1,25},{9,17},{17,9},{25,1},{2,26},{10... | collective-permute-start | bytes 196616 | tf_op jit(solution)/shard_map/ppermute | solution.py:356
  11.6 0.0 collective-permute-start.4
  11.6 0.8 %collective-permute-start.3 = (bf16[128,256]{1,0:T(8,128)(2,1)S(1)}, bf16[128,256]{1,0:T(8,128)(2,1)S(1)}, u32[]{:S(2)}, u32[]{:S(2)}) collective-permute-start(bf16[128,256]{1,0:T(8,128)(2,1)S(1)} %join.1.refs_0_), channel_id=1, source_target_pairs={{0,8},{8,0},{16,24},{24,16},{1,9},{9,1},{17,25},{25,17},{2,10},{10... | collective-permute-start | bytes 196616 | tf_op jit(solution)/shard_map/ppermute | solution.py:356
  12.4 1.9 %collective-permute-done.5.refs_1_.refs_3_ = bf16[128,256]{1,0:T(8,128)(2,1)S(1)} collective-permute-done((bf16[128,256]{1,0:T(8,128)(2,1)S(1)}, bf16[128,256]{1,0:T(8,128)(2,1)S(1)}, u32[]{:S(2)}, u32[]{:S(2)}) %collective-permute-start.5) | collective-permute-done | bytes 65568 | tf_op jit(solution)/shard_map/ppermute | solution.py:356
  14.3 1.5 %collective-permute-done.6.other_ref = bf16[2,2,320,128]{3,2,1,0:T(8,128)(2,1)S(1)} collective-permute-done((bf16[2,2,320,128]{3,2,1,0:T(8,128)(2,1)S(1)}, bf16[2,2,320,128]{3,2,1,0:T(8,128)(2,1)S(1)}, u32[]{:S(2)}, u32[]{:S(2)}) %collective-permute-start.6) | collective-permute-done | bytes 327712 | tf_op jit(solution)/shard_map/ppermute | solution.py:356
  15.8 0.0 copy-done
  15.8 1.3 %stats.2 = (f32[12,320]{1,0:T(8,128)S(1)}, f32[2,320,320]{2,1,0:T(8,128)S(1)}, f32[2,320,320]{2,1,0:T(8,128)S(1)}) custom-call(s32[16]{0:T(128)S(1)} %copy-done, bf16[2,2,320,128]{3,2,1,0:T(8,128)(2,1)S(1)} %stack.1.own_ref, bf16[2,2,320,128]{3,2,1,0:T(8,128)(2,1)S(1)} %collective-permute-done.6.other_ref, bf16[128,256]{1,0:T(8,128)(2,1)S(1)} %join.1.refs_0_, ...), custom_call_target="tpu_custom_call" | custom-call | flops 20000000000 | bytes 1000000 | tf_op jit(solution)/shard_map/stats/pallas_call | solution.py:397
  17.0 0.4 %collective-permute-done.4.refs_1_.refs_2_ = bf16[128,256]{1,0:T(8,128)(2,1)S(1)} collective-permute-done((bf16[128,256]{1,0:T(8,128)(2,1)S(1)}, bf16[128,256]{1,0:T(8,128)(2,1)S(1)}, u32[]{:S(2)}, u32[]{:S(2)}) %collective-permute-start.4) | collective-permute-done | bytes 65568 | tf_op jit(solution)/shard_map/ppermute | solution.py:356
  17.5 0.0 collective-permute-done.3.refs_0_.refs_1_
  17.5 1.2 %stats.3 = (f32[12,320]{1,0:T(8,128)S(1)}, f32[2,320,320]{2,1,0:T(8,128)S(1)}, f32[2,320,320]{2,1,0:T(8,128)S(1)}) custom-call(s32[16]{0:T(128)S(1)} %copy-done, bf16[2,2,320,128]{3,2,1,0:T(8,128)(2,1)S(1)} %stack.1.own_ref, bf16[2,2,320,128]{3,2,1,0:T(8,128)(2,1)S(1)} %collective-permute-done.6.other_ref, ...), custom_call_target="tpu_custom_call" | custom-call | tf_op jit(solution)/shard_map/stats/pallas_call | solution.py:397
  18.7 1.6 %collective-permute-start.7 = (f32[12,320]{1,0:T(8,128)S(1)}, f32[12,320]{1,0:T(8,128)S(1)}, u32[]{:S(2)}, u32[]{:S(2)}) collective-permute-start(f32[12,320]{1,0:T(8,128)S(1)} %merge.1), channel_id=1, source_target_pairs={{0,4},{4,0},{1,5},{5,1},{2,6},{6,2},{3,7},{7,3},{8,12},{12,8},{9,1... | collective-permute-start | bytes 46088 | tf_op jit(solution)/shard_map/ppermute | solution.py:356
  20.3 2.3 %collective-permute-done.7.refs_2_ = f32[12,320]{1,0:T(8,128)S(1)} collective-permute-done((f32[12,320]{1,0:T(8,128)S(1)}, f32[12,320]{1,0:T(8,128)S(1)}, u32[]{:S(2)}, u32[]{:S(2)}) %collective-permute-start.7) | collective-permute-done | bytes 15392 | tf_op jit(solution)/shard_map/ppermute | solution.py:356
  22.6 1.4 %grads.1 = (f32[128,256]{1,0:T(8,128)S(1)}, bf16[128,256]{1,0:T(8,128)(2,1)S(1)}, bf16[128,256]{1,0:T(8,128)(2,1)S(1)}, bf16[128,256]{1,0:T(8,128)(2,1)S(1)}, bf...) custom-call(s32[16]{0:T(128)S(1)} %copy-done, bf16[2,2,320,128]{3,2,1,0:T(8,128)(2,1)S(1)} %stack.1.own_ref, ...), custom_call_target="tpu_custom_call" | custom-call | tf_op jit(solution)/shard_map/grads/pallas_call | solution.py:412
  24.0 3.5 %collective-permute-start.9 = (bf16[128,256]{1,0:T(8,128)(2,1)S(1)}, bf16[128,256]{1,0:T(8,128)(2,1)S(1)}, u32[]{:S(2)}, u32[]{:S(2)}) collective-permute-start(bf16[128,256]{1,0:T(8,128)(2,1)S(1)} %get-tuple-element.40), channel_id=1, source_target_pairs={{0,24},{8,16},{16,8},{24,0},{1,25},{9,17},{17,9},{25,1},{2,26},{10... | collective-permute-start | bytes 196616 | tf_op jit(solution)/shard_map/ppermute | solution.py:357
  27.5 0.0 collective-permute-start.10
  27.5 1.0 %collective-permute-start.11 = (bf16[128,256]{1,0:T(8,128)(2,1)S(1)}, bf16[128,256]{1,0:T(8,128)(2,1)S(1)}, u32[]{:S(2)}, u32[]{:S(2)}) collective-permute-start(bf16[128,256]{1,0:T(8,128)(2,1)S(1)} %get-tuple-element.42), channel_id=1, source_target_pairs={{0,8},{8,0},{16,24},{24,16},{1,9},{9,1},{17,25},{25,17},{2,10},{10... | collective-permute-start | bytes 196616 | tf_op jit(solution)/shard_map/ppermute | solution.py:357
  28.5 1.2 %query_terms.1 = (f32[128,640]{1,0:T(8,128)S(1)}, bf16[128,640]{1,0:T(8,128)(2,1)S(1)}) custom-call(s32[16]{0:T(128)S(1)} %copy-done, bf16[128,256]{1,0:T(8,128)(2,1)S(1)} %join.1.refs_0_, bf16[128,256]{1,0:T(8,128)(2,1)S(1)} %collective-permute-done.3.refs_0_.refs_1_, bf16[128,256]{1,0:T(8,128)(2,1)S(1)} %collective-permute-done.4.refs_1_.refs_2_, ...), custom_call_target="tpu_custom_call" | custom-call | flops 20000000000 | bytes 1000000 | tf_op jit(solution)/shard_map/query_terms/pallas_call | solution.py:423
  29.7 1.6 %collective-permute-start.8 = (bf16[128,640]{1,0:T(8,128)(2,1)S(1)}, bf16[128,640]{1,0:T(8,128)(2,1)S(1)}, u32[]{:S(2)}, u32[]{:S(2)}) collective-permute-start(bf16[128,640]{1,0:T(8,128)(2,1)S(1)} %get-tuple-element.38), channel_id=1, source_target_pairs={{0,4},{4,0},{1,5},{5,1},{2,6},{6,2},{3,7},{7,3},{8,12},{12,8},{9,1... | collective-permute-start | bytes 491528 | tf_op jit(solution)/shard_map/ppermute | solution.py:356
  31.3 0.0 collective-permute-done.9.refs_1_
  31.3 1.4 %collective-permute-done.10.refs_2_ = bf16[128,256]{1,0:T(8,128)(2,1)S(1)} collective-permute-done((bf16[128,256]{1,0:T(8,128)(2,1)S(1)}, bf16[128,256]{1,0:T(8,128)(2,1)S(1)}, u32[]{:S(2)}, u32[]{:S(2)}) %collective-permute-start.10) | collective-permute-done | bytes 65568 | tf_op jit(solution)/shard_map/ppermute | solution.py:357
  32.7 0.0 collective-permute-done.11.refs_3_
  32.7 0.1 collective-permute-start.12
  32.8 1.6 %collective-permute-start.13 = (bf16[32,256]{1,0:T(8,128)(2,1)S(1)}, bf16[32,256]{1,0:T(8,128)(2,1)S(1)}, u32[]{:S(2)}, u32[]{:S(2)}) collective-permute-start(bf16[32,256]{1,0:T(8,128)(2,1)S(1)} %get-tuple-element.45), channel_id=1, source_target_pairs={{0,2},{1,3},{2,0},{3,1},{4,6},{5,7},{6,4},{7,5},{8,10},{9,11},{10,... | collective-permute-start | bytes 49160 | tf_op jit(solution)/shard_map/ppermute | solution.py:356
  34.3 0.3 collective-permute-start.14
  34.7 0.0 collective-permute-done.12.refs_1_
  34.7 1.9 %collective-permute-done.13.refs_2_ = bf16[32,256]{1,0:T(8,128)(2,1)S(1)} collective-permute-done((bf16[32,256]{1,0:T(8,128)(2,1)S(1)}, bf16[32,256]{1,0:T(8,128)(2,1)S(1)}, u32[]{:S(2)}, u32[]{:S(2)}) %collective-permute-start.13) | collective-permute-done | bytes 16416 | tf_op jit(solution)/shard_map/ppermute | solution.py:356
  36.6 0.9 %collective-permute-done.14.refs_3_ = bf16[32,256]{1,0:T(8,128)(2,1)S(1)} collective-permute-done((bf16[32,256]{1,0:T(8,128)(2,1)S(1)}, bf16[32,256]{1,0:T(8,128)(2,1)S(1)}, u32[]{:S(2)}, u32[]{:S(2)}) %collective-permute-start.14) | collective-permute-done | bytes 16416 | tf_op jit(solution)/shard_map/ppermute | solution.py:356
  37.5 0.0 collective-permute-done.8.received_ref
  37.5 0.8 %place.1 = (bf16[128,640]{1,0:T(8,128)(2,1)}, bf16[32,512]{1,0:T(8,128)(2,1)}, bf16[32,512]{1,0:T(8,128)(2,1)}) custom-call(f32[128,640]{1,0:T(8,128)S(1)} %get-tuple-element.37.own_ref, bf16[128,640]{1,0:T(8,128)(2,1)S(1)} %collective-permute-done.8.received_ref, bf16[32,256]{1,0:T(8,128)(2,1)S(1)} %get-tuple-element.43.refs_0_, ...), custom_call_target="tpu_custom_call" | custom-call | tf_op jit(solution)/shard_map/place/pallas_call | solution.py:442
  (2 shorter events, 0.1 us)
Async XLA Ops:
  0.6 4.1 %copy-start.1 = (bf16[128,640]{1,0:T(8,128)(2,1)S(1)}, bf16[128,640]{1,0:T(8,128)(2,1)}, u32[]{:S(2)}) copy-start(bf16[128,640]{1,0:T(8,128)(2,1)} %q_ref.1) | copy-start | bytes 491524
  1.6 6.0 %collective-permute-start = (bf16[32,256]{1,0:T(8,128)(2,1)S(1)}, bf16[32,256]{1,0:T(8,128)(2,1)S(1)}, u32[]{:S(2)}, u32[]{:S(2)}) collective-permute-start(bf16[32,256]{1,0:T(8,128)(2,1)S(1)} %get-tuple-element.26), channel_id=1, source_target_pairs={{0,1},{1,0},{2,3},{3,2},{4,5},{5,4},{6,7},{7,6},{8,9},{9,8},{10,11... | collective-permute-start | bytes 49160 | tf_op jit(solution)/shard_map/ppermute | solution.py:356
  2.1 5.5 %collective-permute-start.1 = (bf16[32,256]{1,0:T(8,128)(2,1)S(1)}, bf16[32,256]{1,0:T(8,128)(2,1)S(1)}, u32[]{:S(2)}, u32[]{:S(2)}) collective-permute-start(bf16[32,256]{1,0:T(8,128)(2,1)S(1)} %get-tuple-element.27), channel_id=1, source_target_pairs={{0,2},{1,3},{2,0},{3,1},{4,6},{5,7},{6,4},{7,5},{8,10},{9,11},{10,... | collective-permute-start | bytes 49160 | tf_op jit(solution)/shard_map/ppermute | solution.py:356
  4.7 3.2 %collective-permute-start.2 = (bf16[32,256]{1,0:T(8,128)(2,1)S(1)}, bf16[32,256]{1,0:T(8,128)(2,1)S(1)}, u32[]{:S(2)}, u32[]{:S(2)}) collective-permute-start(bf16[32,256]{1,0:T(8,128)(2,1)S(1)} %get-tuple-element.28), channel_id=1, source_target_pairs={{0,3},{1,2},{2,1},{3,0},{4,7},{5,6},{6,5},{7,4},{8,11},{9,10},{10,... | collective-permute-start | bytes 49160 | tf_op jit(solution)/shard_map/ppermute | solution.py:356
  4.7 0.9 %copy-start.2 = (bf16[128,640]{1,0:T(8,128)(2,1)S(1)}, bf16[128,640]{1,0:T(8,128)(2,1)}, u32[]{:S(2)}) copy-start(bf16[128,640]{1,0:T(8,128)(2,1)} %do_ref.1) | copy-start | bytes 491524
  5.7 10.1 %copy-start = (s32[16]{0:T(128)S(1)}, s32[16]{0:T(128)}, u32[]{:S(2)}) copy-start(s32[16]{0:T(128)} %order_ref.7) | copy-start | bytes 196
  5.7 10.0 %collective-permute-start.6 = (bf16[2,2,320,128]{3,2,1,0:T(8,128)(2,1)S(1)}, bf16[2,2,320,128]{3,2,1,0:T(8,128)(2,1)S(1)}, u32[]{:S(2)}, u32[]{:S(2)}) collective-permute-start(bf16[2,2,320,128]{3,2,1,0:T(8,128)(2,1)S(1)} %stack.1.own_ref), channel_id=1, source_target_pairs={{0,4},{4,0},{1,5},{5,1},{2,6},{6,2},{3,7},{7,3},{8,12},{12,8},{9,1... | collective-permute-start | bytes 983048 | tf_op jit(solution)/shard_map/ppermute | solution.py:356
  7.9 6.4 %collective-permute-start.5 = (bf16[128,256]{1,0:T(8,128)(2,1)S(1)}, bf16[128,256]{1,0:T(8,128)(2,1)S(1)}, u32[]{:S(2)}, u32[]{:S(2)}) collective-permute-start(bf16[128,256]{1,0:T(8,128)(2,1)S(1)} %join.1.refs_0_), channel_id=1, source_target_pairs={{0,24},{8,16},{16,8},{24,0},{1,25},{9,17},{17,9},{25,1},{2,26},{10... | collective-permute-start | bytes 196616 | tf_op jit(solution)/shard_map/ppermute | solution.py:356
  11.6 5.9 %collective-permute-start.4 = (bf16[128,256]{1,0:T(8,128)(2,1)S(1)}, bf16[128,256]{1,0:T(8,128)(2,1)S(1)}, u32[]{:S(2)}, u32[]{:S(2)}) collective-permute-start(bf16[128,256]{1,0:T(8,128)(2,1)S(1)} %join.1.refs_0_), channel_id=1, source_target_pairs={{0,16},{8,24},{16,0},{24,8},{1,17},{9,25},{17,1},{25,9},{2,18},{10... | collective-permute-start | bytes 196616 | tf_op jit(solution)/shard_map/ppermute | solution.py:356
  11.6 5.9 %collective-permute-start.3 = (bf16[128,256]{1,0:T(8,128)(2,1)S(1)}, bf16[128,256]{1,0:T(8,128)(2,1)S(1)}, u32[]{:S(2)}, u32[]{:S(2)}) collective-permute-start(bf16[128,256]{1,0:T(8,128)(2,1)S(1)} %join.1.refs_0_), channel_id=1, source_target_pairs={{0,8},{8,0},{16,24},{24,16},{1,9},{9,1},{17,25},{25,17},{2,10},{10... | collective-permute-start | bytes 196616 | tf_op jit(solution)/shard_map/ppermute | solution.py:356
  18.7 3.9 %collective-permute-start.7 = (f32[12,320]{1,0:T(8,128)S(1)}, f32[12,320]{1,0:T(8,128)S(1)}, u32[]{:S(2)}, u32[]{:S(2)}) collective-permute-start(f32[12,320]{1,0:T(8,128)S(1)} %merge.1), channel_id=1, source_target_pairs={{0,4},{4,0},{1,5},{5,1},{2,6},{6,2},{3,7},{7,3},{8,12},{12,8},{9,1... | collective-permute-start | bytes 46088 | tf_op jit(solution)/shard_map/ppermute | solution.py:356
  24.0 7.3 %collective-permute-start.9 = (bf16[128,256]{1,0:T(8,128)(2,1)S(1)}, bf16[128,256]{1,0:T(8,128)(2,1)S(1)}, u32[]{:S(2)}, u32[]{:S(2)}) collective-permute-start(bf16[128,256]{1,0:T(8,128)(2,1)S(1)} %get-tuple-element.40), channel_id=1, source_target_pairs={{0,24},{8,16},{16,8},{24,0},{1,25},{9,17},{17,9},{25,1},{2,26},{10... | collective-permute-start | bytes 196616 | tf_op jit(solution)/shard_map/ppermute | solution.py:357
  27.5 5.2 %collective-permute-start.10 = (bf16[128,256]{1,0:T(8,128)(2,1)S(1)}, bf16[128,256]{1,0:T(8,128)(2,1)S(1)}, u32[]{:S(2)}, u32[]{:S(2)}) collective-permute-start(bf16[128,256]{1,0:T(8,128)(2,1)S(1)} %get-tuple-element.41), channel_id=1, source_target_pairs={{0,16},{8,24},{16,0},{24,8},{1,17},{9,25},{17,1},{25,9},{2,18},{10... | collective-permute-start | bytes 196616 | tf_op jit(solution)/shard_map/ppermute | solution.py:357
  27.5 5.2 %collective-permute-start.11 = (bf16[128,256]{1,0:T(8,128)(2,1)S(1)}, bf16[128,256]{1,0:T(8,128)(2,1)S(1)}, u32[]{:S(2)}, u32[]{:S(2)}) collective-permute-start(bf16[128,256]{1,0:T(8,128)(2,1)S(1)} %get-tuple-element.42), channel_id=1, source_target_pairs={{0,8},{8,0},{16,24},{24,16},{1,9},{9,1},{17,25},{25,17},{2,10},{10... | collective-permute-start | bytes 196616 | tf_op jit(solution)/shard_map/ppermute | solution.py:357
  29.7 7.8 %collective-permute-start.8 = (bf16[128,640]{1,0:T(8,128)(2,1)S(1)}, bf16[128,640]{1,0:T(8,128)(2,1)S(1)}, u32[]{:S(2)}, u32[]{:S(2)}) collective-permute-start(bf16[128,640]{1,0:T(8,128)(2,1)S(1)} %get-tuple-element.38), channel_id=1, source_target_pairs={{0,4},{4,0},{1,5},{5,1},{2,6},{6,2},{3,7},{7,3},{8,12},{12,8},{9,1... | collective-permute-start | bytes 491528 | tf_op jit(solution)/shard_map/ppermute | solution.py:356
  32.7 1.9 %collective-permute-start.12 = (bf16[32,256]{1,0:T(8,128)(2,1)S(1)}, bf16[32,256]{1,0:T(8,128)(2,1)S(1)}, u32[]{:S(2)}, u32[]{:S(2)}) collective-permute-start(bf16[32,256]{1,0:T(8,128)(2,1)S(1)} %get-tuple-element.44), channel_id=1, source_target_pairs={{0,1},{1,0},{2,3},{3,2},{4,5},{5,4},{6,7},{7,6},{8,9},{9,8},{10,11... | collective-permute-start | bytes 49160 | tf_op jit(solution)/shard_map/ppermute | solution.py:356
  32.8 3.8 %collective-permute-start.13 = (bf16[32,256]{1,0:T(8,128)(2,1)S(1)}, bf16[32,256]{1,0:T(8,128)(2,1)S(1)}, u32[]{:S(2)}, u32[]{:S(2)}) collective-permute-start(bf16[32,256]{1,0:T(8,128)(2,1)S(1)} %get-tuple-element.45), channel_id=1, source_target_pairs={{0,2},{1,3},{2,0},{3,1},{4,6},{5,7},{6,4},{7,5},{8,10},{9,11},{10,... | collective-permute-start | bytes 49160 | tf_op jit(solution)/shard_map/ppermute | solution.py:356
  34.3 3.2 %collective-permute-start.14 = (bf16[32,256]{1,0:T(8,128)(2,1)S(1)}, bf16[32,256]{1,0:T(8,128)(2,1)S(1)}, u32[]{:S(2)}, u32[]{:S(2)}) collective-permute-start(bf16[32,256]{1,0:T(8,128)(2,1)S(1)} %get-tuple-element.46), channel_id=1, source_target_pairs={{0,3},{1,2},{2,1},{3,0},{4,7},{5,6},{6,5},{7,4},{8,11},{9,10},{10,... | collective-permute-start | bytes 49160 | tf_op jit(solution)/shard_map/ppermute | solution.py:356

commit v9 on v8

--- a/solution.py
+++ b/solution.py
@@ -52,17 +52,15 @@
 
 
 class Work:
-    def __init__(self, order_ref, rows, outer, members, block_refs):
+    def __init__(self, table_ref, rows, members, block_refs):
         self.rows, self.members, self.block_refs = rows, members, block_refs
         self.low_rows = len(members) * rows
-        at, side = lax.axis_index("outer"), lax.axis_index("pair")
-
-        def pair_of(index):
-            first, second = order_ref[2 * index], order_ref[2 * index + 1]
-            return jnp.minimum(first, second), jnp.where(first < second, 0, 1)
-
-        self.owners = [pair_of(2 * at + side), pair_of(2 * at + 1 - side)]
-        self.pairs = [pair_of(2 * partner(at, d, outer) + side) for d in members]
+
+        def pair(at):
+            return jnp.max(table_ref[2 * at : 2 * at + 1, :]), jnp.max(table_ref[2 * at + 1 : 2 * at + 2, :])
+
+        self.pairs = [pair(d) for d in members]
+        self.owners = [pair(table_ref.shape[0] // 2 - 2), pair(table_ref.shape[0] // 2 - 1)]
 
     @staticmethod
     def slot(place, half):
@@ -106,17 +104,29 @@
     wait_all(copies)
 
 
-def stack_kernel(q_ref, do_ref, after_ref, out_ref):
-    rows = q_ref.shape[0] // 2
-    for n, source_ref in enumerate((q_ref, do_ref)):
+def table_kernel(outer, order_ref, after_ref, table_ref):
+    at, side = lax.axis_index("outer"), lax.axis_index("pair")
+    indices = [2 * partner(at, d, outer) + side for d in range(outer)]
+    indices += [2 * at + side, 2 * at + 1 - side]
+    for n, index in enumerate(indices):
+        first, second = order_ref[2 * index], order_ref[2 * index + 1]
+        row = table_ref.shape[1:]
+        table_ref[2 * n : 2 * n + 1, :] = jnp.full((1, *row), jnp.minimum(first, second), jnp.int32)
+        table_ref[2 * n + 1 : 2 * n + 2, :] = jnp.full((1, *row), jnp.where(first < second, 0, 1), jnp.int32)
+
+
+def stack_kernel(*refs):
+    sources, outs = refs[:4], refs[4:]
+    rows = sources[0].shape[0] // 2
+    for n, source_ref in enumerate(sources):
         for slot in range(2):
             for h in range(GROUP):
-                out_ref[n, slot, h * rows : (h + 1) * rows, :] = source_ref[
+                outs[n // 2][n % 2, slot, h * rows : (h + 1) * rows, :] = source_ref[
                     slot * rows : (slot + 1) * rows, h * HEAD : (h + 1) * HEAD
                 ]
 
 
-def join_kernel(*refs):
+def join_kernel(after_ref, *refs):
     parts, (out_ref, sems) = refs[:-2], refs[-2:]
     kvh = len(parts)
     rows = parts[0].shape[0]
@@ -127,10 +137,10 @@
     wait_all(copies)
 
 
-def stats_kernel(outer, members, order_ref, own_ref, other_ref, *refs):
+def stats_kernel(members, table_ref, own_ref, other_ref, *refs):
     block_refs, (out_ref, e_ref, dp_ref) = refs[: len(members)], refs[-3:]
     rows = block_refs[0].shape[0] // 2
-    work = Work(order_ref, rows, outer, members, block_refs)
+    work = Work(table_ref, rows, members, block_refs)
     low_part = pl.ds(0, work.low_rows)
     key_cols, value_cols = slice(0, HEAD), slice(HEAD, 2 * HEAD)
 
@@ -200,7 +210,7 @@
             out_ref[base + n : base + n + 1, :] = row
 
 
-def grads_kernel(outer, groups, order_ref, own_ref, other_ref, *refs):
+def grads_kernel(outer, groups, table_ref, own_ref, other_ref, *refs):
     count = len(groups)
     stats_refs, theirs_ref, refs = refs[:count], refs[count], refs[count + 1 :]
     e_refs, dp_refs, refs = refs[:count], refs[count : 2 * count], refs[2 * count :]
@@ -228,7 +238,7 @@
             weights[n].append(group_weights[n])
 
     for n, members in enumerate(groups):
-        work = Work(order_ref, rows, outer, members, None)
+        work = Work(table_ref, rows, members, None)
         terms = [[None] * len(members), [None] * len(members)]
 
         def add(half, at, pair):
@@ -269,13 +279,11 @@
                 term_ref[target, HEAD:] = of_values.astype(term_ref.dtype)
 
 
-def query_kernel(outer, groups, order_ref, *refs):
+def query_kernel(outer, groups, table_ref, *refs):
     count = len(groups)
     block_refs, gs_refs, (own_ref, other_ref) = refs[:outer], refs[outer : outer + count], refs[outer + count :]
     rows = own_ref.shape[0] // 2
-    works = [
-        Work(order_ref, rows, outer, members, [block_refs[d] for d in members]) for members in groups
-    ]
+    works = [Work(table_ref, rows, members, [block_refs[d] for d in members]) for members in groups]
     cols = slice(0, HEAD)
     for owner, target in ((0, own_ref), (1, other_ref)):
         totals = [None, None]
@@ -366,25 +374,32 @@
         out_specs=(vmem,) * kvh,
         scratch_shapes=[dma((2 * kvh,))],
     )(jnp.concatenate([keys, values], axis=0))
-    own_qd = call(
+    table = call(
+        functools.partial(table_kernel, outer),
+        "table",
+        out_shape=shape((2 * outer + 4, HEAD), jnp.int32),
+        in_specs=[smem, anywhere],
+        out_specs=vmem,
+        cost_estimate=beside,
+    )(slab_order, parts[0])
+    parts = [parts[0]] + [shift(parts[e], "kvh", e) for e in range(1, kvh)]
+    stack = shape((2, 2, columns, HEAD), low)
+    own_qd, other_qd = call(
         stack_kernel,
         "stack",
-        out_shape=shape((2, 2, columns, HEAD), low),
-        in_specs=[vmem, vmem, anywhere],
-        out_specs=vmem,
-        cost_estimate=beside,
-    )(queries, d_out, parts[0])
-    parts = [parts[0]] + [shift(parts[e], "kvh", e) for e in range(1, kvh)]
-    other_qd = shift(own_qd, "pair", 1)
+        out_shape=(stack, stack),
+        in_specs=[vmem] * 4,
+        out_specs=(vmem, vmem),
+    )(queries, d_out, shift(queries, "pair", 1), shift(d_out, "pair", 1))
     own_block = call(
         join_kernel,
         "join",
         out_shape=block,
-        in_specs=[anywhere] * kvh,
+        in_specs=[anywhere] * (1 + kvh),
         out_specs=vmem,
         scratch_shapes=[dma((kvh,))],
         cost_estimate=beside,
-    )(*parts)
+    )(table, *parts)
     blocks = [own_block] + [shift(own_block, "outer", d) for d in range(1, outer)]
 
     far = outer // 2 + 1
@@ -395,13 +410,13 @@
         score_rows = shape((2, (2 * len(members) + 1) * slab_rows, columns), full)
         results.append(
             call(
-                functools.partial(stats_kernel, outer, members),
+                functools.partial(stats_kernel, members),
                 "stats",
                 out_shape=(all_stats, score_rows, score_rows),
-                in_specs=[smem] + [vmem] * (2 + len(members)) + [anywhere] * min(n, 1),
+                in_specs=[vmem] * (3 + len(members)) + [anywhere] * min(n, 1),
                 out_specs=(vmem,) * 3,
                 cost_estimate=beside if n + 1 < len(groups) else None,
-            )(slab_order, own_qd, other_qd, *[blocks[d] for d in members], *[done[0] for done in results[-1:]])
+            )(table, own_qd, other_qd, *[blocks[d] for d in members], *[done[0] for done in results[-1:]])
         )
     stats, expon, grad_probs = zip(*results)
     mine = call(
@@ -415,19 +430,19 @@
         out_shape=(shape(block.shape, full),)
         + (block,) * (outer - 1)
         + tuple(shape(scores.shape, low) for scores in expon),
-        in_specs=[smem] + [vmem] * (3 + 3 * count),
+        in_specs=[vmem] * (4 + 3 * count),
         out_specs=(vmem,) * (outer + count),
-    )(slab_order, own_qd, other_qd, *stats, theirs, *expon, *grad_probs)
+    )(table, own_qd, other_qd, *stats, theirs, *expon, *grad_probs)
     terms, score_grads = grads[:outer], grads[outer:]
     terms = [terms[0]] + [shift(terms[d], "outer", -d) for d in range(outer - 1, 0, -1)]
     own_grads, other_grads = call(
         functools.partial(query_kernel, outer, groups),
         "query_terms",
         out_shape=(shape(queries.shape, full), shape(queries.shape, low)),
-        in_specs=[smem] + [vmem] * (outer + count),
+        in_specs=[vmem] * (1 + outer + count),
         out_specs=(vmem, vmem),
         cost_estimate=beside,
-    )(slab_order, *blocks, *score_grads)
+    )(table, *blocks, *score_grads)
     received_grads = shift(other_grads, "pair", 1)
     owned = call(
         functools.partial(sum_kernel, outer),

time: 38.5 us -> 36.8 us (0.956)
  local copies, waits for them, and re-layouts: 0.93 us -> 0.01 us
  Pallas kernels: 6.23 us -> 5.44 us
    unnamed x6, local copies, waits for them, and re-layouts: 0.93 us -> 0.01 us
    ppermute x3, waiting for transfers between devices: 1.37 us -> 0.93 us  [shift(): lax.ppermute(array, axis, [(n, partner(n, -by, size)) for n in range(size)])]
    pallas_call x1, Pallas kernels: 1.42 us -> 1.02 us  [per_device(): call(functools.partial(grads_kernel, outer, groups), 'grads', out_shape=(...]
    ppermute x12 -> x13, waiting for transfers between devices: 9.26 us -> 9.52 us  [shift(): lax.ppermute(array, axis, [(n, target_of(n, by, size)) for n in range(siz...]
    ppermute x12 -> x13, starting transfers between devices: 14.5 us -> 14.7 us  [shift(): lax.ppermute(array, axis, [(n, target_of(n, by, size)) for n in range(siz...]
    pallas_call x4 -> x5, Pallas kernels: 2.61 us -> 2.48 us  [the longest x2 1.7 us: per_device(): call(functools.partial(stats_kernel, members), 'stats', out_shape=(all_st...]
  transfers between devices with their start and end apart: 15 -> 16, of which waited for: 8 -> 7; matrix products, arithmetic and copies ran while one was open for 0% -> 0% of each run, Pallas kernels for 7% -> 7%
where the time goes in v9:
time: 36.8 us; the launch traced here: 36.7 us
  starting transfers between devices  19.2 us (52%)
  waiting for transfers between devices  10.5 us (29%)
  Pallas kernels  5.44 us (15%)
  other arithmetic  0.82 us (2%)
  between operations  0.75 us (2%)
    ppermute x13, starting transfers between devices, shift(): lax.ppermute(array, axis, [(n, target_of(n, by, size)) for n in range(siz...  14.7 us
    ppermute x13, waiting for transfers between devices, shift(): lax.ppermute(array, axis, [(n, target_of(n, by, size)) for n in range(siz...  9.52 us
    ppermute x3, starting transfers between devices, shift(): lax.ppermute(array, axis, [(n, partner(n, -by, size)) for n in range(size)])  4.45 us
    pallas_call x2, Pallas kernels, per_device(): call(functools.partial(stats_kernel, members), 'stats', out_shape=(all_st...  1.7 us
    pallas_call x1, Pallas kernels, per_device(): call(functools.partial(grads_kernel, outer, groups), 'grads', out_shape=(...  1.02 us
    pallas_call x1, Pallas kernels, per_device(): call(functools.partial(query_kernel, outer, groups), 'query_terms', out_s...  0.96 us
    ppermute x3, waiting for transfers between devices, shift(): lax.ppermute(array, axis, [(n, partner(n, -by, size)) for n in range(size)])  0.93 us
    concatenate x1, other arithmetic, per_device(): jnp.concatenate([keys, values], axis=0)  0.82 us
  transfers between devices with their start and end apart: 16, of which 7 were waited for; matrix products, arithmetic and copies ran while one was open for 0% of the time, Pallas kernels for 7%

profile of v9, /device:TPU:0, one launch (start us, length us, event | category | flops | bytes accessed | tf_op | source)
XLA Modules:
  0.0 36.7 jit_solution(6568305124403996847)
XLA Ops:
  0.6 0.0 copy-start
  0.6 0.8 %pad_maximum_fusion.cache_ref = bf16[64,512]{1,0:T(8,128)(2,1)S(1)} fusion(bf16[32,512]{1,0:T(8,128)(2,1)} %param.7, bf16[32,512]{1,0:T(8,128)(2,1)} %param.6), kind=kLoop, calls=%fused_computation | loop fusion | flops 131072 | bytes 131072 | tf_op jit(solution)/shard_map/concatenate | solution.py:376
  1.5 0.1 split.1
  1.6 0.5 %collective-permute-start = (bf16[32,256]{1,0:T(8,128)(2,1)S(1)}, bf16[32,256]{1,0:T(8,128)(2,1)S(1)}, u32[]{:S(2)}, u32[]{:S(2)}) collective-permute-start(bf16[32,256]{1,0:T(8,128)(2,1)S(1)} %get-tuple-element.28), channel_id=1, source_target_pairs={{0,1},{1,0},{2,3},{3,2},{4,5},{5,4},{6,7},{7,6},{8,9},{9,8},{10,11... | collective-permute-start | bytes 49160 | tf_op jit(solution)/shard_map/ppermute | solution.py:364
  2.1 2.6 %collective-permute-start.1 = (bf16[32,256]{1,0:T(8,128)(2,1)S(1)}, bf16[32,256]{1,0:T(8,128)(2,1)S(1)}, u32[]{:S(2)}, u32[]{:S(2)}) collective-permute-start(bf16[32,256]{1,0:T(8,128)(2,1)S(1)} %get-tuple-element.29), channel_id=1, source_target_pairs={{0,2},{1,3},{2,0},{3,1},{4,6},{5,7},{6,4},{7,5},{8,10},{9,11},{10,... | collective-permute-start | bytes 49160 | tf_op jit(solution)/shard_map/ppermute | solution.py:364
  4.7 0.0 copy-start.2
  4.7 0.1 collective-permute-start.2
  4.7 0.0 copy-done
  4.7 1.8 %collective-permute-start.6 = (bf16[128,640]{1,0:T(8,128)(2,1)S(1)}, bf16[128,640]{1,0:T(8,128)(2,1)S(1)}, u32[]{:S(2)}, u32[]{:S(2)}) collective-permute-start(bf16[128,640]{1,0:T(8,128)(2,1)S(1)} %copy-done), channel_id=1, source_target_pairs={{0,4},{4,0},{1,5},{5,1},{2,6},{6,2},{3,7},{7,3},{8,12},{12,8},{9,1... | collective-permute-start | bytes 491528 | tf_op jit(solution)/shard_map/ppermute | solution.py:364
  6.5 0.3 collective-permute-start.7
  6.8 0.0 copy-done.2
  6.8 0.6 %table.1.after_ref.table_ref = s32[12,128]{1,0:T(8,128)S(1)} custom-call(s32[16]{0:T(128)S(1)} %copy-done.2, bf16[32,256]{1,0:T(8,128)(2,1)S(1)} %get-tuple-element.27.after_ref.refs_0_), custom_call_target="tpu_custom_call" | custom-call | flops 20000000000 | bytes 1000000 | tf_op jit(solution)/shard_map/table/pallas_call | solution.py:377
  7.3 0.0 copy-start.1
  7.3 0.0 collective-permute-done.refs_1_
  7.4 0.0 collective-permute-done.1.refs_2_
  7.4 0.5 %collective-permute-done.2.refs_3_ = bf16[32,256]{1,0:T(8,128)(2,1)S(1)} collective-permute-done((bf16[32,256]{1,0:T(8,128)(2,1)S(1)}, bf16[32,256]{1,0:T(8,128)(2,1)S(1)}, u32[]{:S(2)}, u32[]{:S(2)}) %collective-permute-start.2) | collective-permute-done | bytes 16416 | tf_op jit(solution)/shard_map/ppermute | solution.py:364
  7.8 0.1 join.1.refs_0_
  7.9 3.7 %collective-permute-start.5 = (bf16[128,256]{1,0:T(8,128)(2,1)S(1)}, bf16[128,256]{1,0:T(8,128)(2,1)S(1)}, u32[]{:S(2)}, u32[]{:S(2)}) collective-permute-start(bf16[128,256]{1,0:T(8,128)(2,1)S(1)} %join.1.refs_0_), channel_id=1, source_target_pairs={{0,24},{8,16},{16,8},{24,0},{1,25},{9,17},{17,9},{25,1},{2,26},{10... | collective-permute-start | bytes 196616 | tf_op jit(solution)/shard_map/ppermute | solution.py:364
  11.6 0.0 collective-permute-start.4
  11.6 0.8 %collective-permute-start.3 = (bf16[128,256]{1,0:T(8,128)(2,1)S(1)}, bf16[128,256]{1,0:T(8,128)(2,1)S(1)}, u32[]{:S(2)}, u32[]{:S(2)}) collective-permute-start(bf16[128,256]{1,0:T(8,128)(2,1)S(1)} %join.1.refs_0_), channel_id=1, source_target_pairs={{0,8},{8,0},{16,24},{24,16},{1,9},{9,1},{17,25},{25,17},{2,10},{10... | collective-permute-start | bytes 196616 | tf_op jit(solution)/shard_map/ppermute | solution.py:364
  12.4 0.0 collective-permute-done.6.refs_2_
  12.4 2.3 %collective-permute-done.7.refs_3_ = bf16[128,640]{1,0:T(8,128)(2,1)S(1)} collective-permute-done((bf16[128,640]{1,0:T(8,128)(2,1)}, bf16[128,640]{1,0:T(8,128)(2,1)S(1)}, u32[]{:S(2)}, u32[]{:S(2)}) %collective-permute-start.7) | collective-permute-done | bytes 163872 | tf_op jit(solution)/shard_map/ppermute | solution.py:364
  14.7 0.0 copy-done.1
  14.7 0.1 stack.1
  14.8 0.0 collective-permute-done.5.refs_1_.refs_3_
  14.8 0.9 %stats.2 = (f32[12,320]{1,0:T(8,128)S(1)}, f32[2,320,320]{2,1,0:T(8,128)S(1)}, f32[2,320,320]{2,1,0:T(8,128)S(1)}) custom-call(s32[12,128]{1,0:T(8,128)S(1)} %table.1.after_ref.table_ref, bf16[2,2,320,128]{3,2,1,0:T(8,128)(2,1)S(1)} %get-tuple-element.31.own_ref, bf16[2,2,320,128]{3,2,1,0:T(8,128)(2,1)S(1)} %get-tuple-element.32.other_ref, ...), custom_call_target="tpu_custom_call" | custom-call | flops 20000000000 | bytes 1000000 | tf_op jit(solution)/shard_map/stats/pallas_call | solution.py:412
  15.7 1.8 %collective-permute-done.4.refs_1_.refs_2_ = bf16[128,256]{1,0:T(8,128)(2,1)S(1)} collective-permute-done((bf16[128,256]{1,0:T(8,128)(2,1)S(1)}, bf16[128,256]{1,0:T(8,128)(2,1)S(1)}, u32[]{:S(2)}, u32[]{:S(2)}) %collective-permute-start.4) | collective-permute-done | bytes 65568 | tf_op jit(solution)/shard_map/ppermute | solution.py:364
  17.5 0.0 collective-permute-done.3.refs_0_.refs_1_
  17.5 0.8 %stats.3 = (f32[12,320]{1,0:T(8,128)S(1)}, f32[2,320,320]{2,1,0:T(8,128)S(1)}, f32[2,320,320]{2,1,0:T(8,128)S(1)}) custom-call(s32[12,128]{1,0:T(8,128)S(1)} %table.1.after_ref.table_ref, bf16[2,2,320,128]{3,2,1,0:T(8,128)(2,1)S(1)} %get-tuple-element.31.own_ref, bf16[2,2,320,128]{3,2,1,0:T(8,128)(2,1)S(1)} %get-tuple-element.32.other_ref, ...), custom_call_target="tpu_custom_call" | custom-call | tf_op jit(solution)/shard_map/stats/pallas_call | solution.py:412
  18.3 1.6 %collective-permute-start.8 = (f32[12,320]{1,0:T(8,128)S(1)}, f32[12,320]{1,0:T(8,128)S(1)}, u32[]{:S(2)}, u32[]{:S(2)}) collective-permute-start(f32[12,320]{1,0:T(8,128)S(1)} %merge.1), channel_id=1, source_target_pairs={{0,4},{4,0},{1,5},{5,1},{2,6},{6,2},{3,7},{7,3},{8,12},{12,8},{9,1... | collective-permute-start | bytes 46088 | tf_op jit(solution)/shard_map/ppermute | solution.py:364
  19.9 2.3 %collective-permute-done.8.refs_2_ = f32[12,320]{1,0:T(8,128)S(1)} collective-permute-done((f32[12,320]{1,0:T(8,128)S(1)}, f32[12,320]{1,0:T(8,128)S(1)}, u32[]{:S(2)}, u32[]{:S(2)}) %collective-permute-start.8) | collective-permute-done | bytes 15392 | tf_op jit(solution)/shard_map/ppermute | solution.py:364
  22.2 1.0 %grads.1 = (f32[128,256]{1,0:T(8,128)S(1)}, bf16[128,256]{1,0:T(8,128)(2,1)S(1)}, bf16[128,256]{1,0:T(8,128)(2,1)S(1)}, bf16[128,256]{1,0:T(8,128)(2,1)S(1)}, bf...) custom-call(s32[12,128]{1,0:T(8,128)S(1)} %table.1.after_ref.table_ref, ...), custom_call_target="tpu_custom_call" | custom-call | tf_op jit(solution)/shard_map/grads/pallas_call | solution.py:427
  23.3 2.5 %collective-permute-start.10 = (bf16[128,256]{1,0:T(8,128)(2,1)S(1)}, bf16[128,256]{1,0:T(8,128)(2,1)S(1)}, u32[]{:S(2)}, u32[]{:S(2)}) collective-permute-start(bf16[128,256]{1,0:T(8,128)(2,1)S(1)} %get-tuple-element.44), channel_id=1, source_target_pairs={{0,24},{8,16},{16,8},{24,0},{1,25},{9,17},{17,9},{25,1},{2,26},{10... | collective-permute-start | bytes 196616 | tf_op jit(solution)/shard_map/ppermute | solution.py:365
  25.8 0.1 collective-permute-start.11
  25.9 1.8 %collective-permute-start.12 = (bf16[128,256]{1,0:T(8,128)(2,1)S(1)}, bf16[128,256]{1,0:T(8,128)(2,1)S(1)}, u32[]{:S(2)}, u32[]{:S(2)}) collective-permute-start(bf16[128,256]{1,0:T(8,128)(2,1)S(1)} %get-tuple-element.46), channel_id=1, source_target_pairs={{0,8},{8,0},{16,24},{24,16},{1,9},{9,1},{17,25},{25,17},{2,10},{10... | collective-permute-start | bytes 196616 | tf_op jit(solution)/shard_map/ppermute | solution.py:365
  27.7 1.0 %query_terms.1 = (f32[128,640]{1,0:T(8,128)S(1)}, bf16[128,640]{1,0:T(8,128)(2,1)S(1)}) custom-call(s32[12,128]{1,0:T(8,128)S(1)} %table.1.after_ref.table_ref, bf16[128,256]{1,0:T(8,128)(2,1)S(1)} %join.1.refs_0_, bf16[128,256]{1,0:T(8,128)(2,1)S(1)} %collective-permute-done.3.refs_0_.refs_1_, bf16[128,256]{1,0:T(8,128)(2,1)S(1)} %collective-permute-done.4.refs_1_.refs_2_, ...), custom_call_target="tpu_custom_call" | custom-call | flops 20000000000 | bytes 1000000 | tf_op jit(solution)/shard_map/query_terms/pallas_call | solution.py:438
  28.7 1.6 %collective-permute-start.9 = (bf16[128,640]{1,0:T(8,128)(2,1)S(1)}, bf16[128,640]{1,0:T(8,128)(2,1)S(1)}, u32[]{:S(2)}, u32[]{:S(2)}) collective-permute-start(bf16[128,640]{1,0:T(8,128)(2,1)S(1)} %get-tuple-element.42), channel_id=1, source_target_pairs={{0,4},{4,0},{1,5},{5,1},{2,6},{6,2},{3,7},{7,3},{8,12},{12,8},{9,1... | collective-permute-start | bytes 491528 | tf_op jit(solution)/shard_map/ppermute | solution.py:364
  30.3 0.0 collective-permute-done.10.refs_1_
  30.3 0.9 %collective-permute-done.11.refs_2_ = bf16[128,256]{1,0:T(8,128)(2,1)S(1)} collective-permute-done((bf16[128,256]{1,0:T(8,128)(2,1)S(1)}, bf16[128,256]{1,0:T(8,128)(2,1)S(1)}, u32[]{:S(2)}, u32[]{:S(2)}) %collective-permute-start.11) | collective-permute-done | bytes 65568 | tf_op jit(solution)/shard_map/ppermute | solution.py:365
  31.2 0.0 collective-permute-done.12.refs_3_
  31.3 0.1 collective-permute-start.13
  31.3 1.4 %collective-permute-start.14 = (bf16[32,256]{1,0:T(8,128)(2,1)S(1)}, bf16[32,256]{1,0:T(8,128)(2,1)S(1)}, u32[]{:S(2)}, u32[]{:S(2)}) collective-permute-start(bf16[32,256]{1,0:T(8,128)(2,1)S(1)} %get-tuple-element.49), channel_id=1, source_target_pairs={{0,2},{1,3},{2,0},{3,1},{4,6},{5,7},{6,4},{7,5},{8,10},{9,11},{10,... | collective-permute-start | bytes 49160 | tf_op jit(solution)/shard_map/ppermute | solution.py:364
  32.7 0.5 %collective-permute-start.15 = (bf16[32,256]{1,0:T(8,128)(2,1)S(1)}, bf16[32,256]{1,0:T(8,128)(2,1)S(1)}, u32[]{:S(2)}, u32[]{:S(2)}) collective-permute-start(bf16[32,256]{1,0:T(8,128)(2,1)S(1)} %get-tuple-element.50), channel_id=1, source_target_pairs={{0,3},{1,2},{2,1},{3,0},{4,7},{5,6},{6,5},{7,4},{8,11},{9,10},{10,... | collective-permute-start | bytes 49160 | tf_op jit(solution)/shard_map/ppermute | solution.py:364
  33.2 0.0 collective-permute-done.13.refs_1_
  33.2 1.9 %collective-permute-done.14.refs_2_ = bf16[32,256]{1,0:T(8,128)(2,1)S(1)} collective-permute-done((bf16[32,256]{1,0:T(8,128)(2,1)S(1)}, bf16[32,256]{1,0:T(8,128)(2,1)S(1)}, u32[]{:S(2)}, u32[]{:S(2)}) %collective-permute-start.14) | collective-permute-done | bytes 16416 | tf_op jit(solution)/shard_map/ppermute | solution.py:364
  35.1 0.7 %collective-permute-done.15.refs_3_ = bf16[32,256]{1,0:T(8,128)(2,1)S(1)} collective-permute-done((bf16[32,256]{1,0:T(8,128)(2,1)S(1)}, bf16[32,256]{1,0:T(8,128)(2,1)S(1)}, u32[]{:S(2)}, u32[]{:S(2)}) %collective-permute-start.15) | collective-permute-done | bytes 16416 | tf_op jit(solution)/shard_map/ppermute | solution.py:364
  35.9 0.0 collective-permute-done.9.received_ref
  35.9 0.8 %place.1 = (bf16[128,640]{1,0:T(8,128)(2,1)}, bf16[32,512]{1,0:T(8,128)(2,1)}, bf16[32,512]{1,0:T(8,128)(2,1)}) custom-call(f32[128,640]{1,0:T(8,128)S(1)} %get-tuple-element.41.own_ref, bf16[128,640]{1,0:T(8,128)(2,1)S(1)} %collective-permute-done.9.received_ref, bf16[32,256]{1,0:T(8,128)(2,1)S(1)} %get-tuple-element.47.refs_0_, ...), custom_call_target="tpu_custom_call" | custom-call | tf_op jit(solution)/shard_map/place/pallas_call | solution.py:457
  (2 shorter events, 0.1 us)
Async XLA Ops:
  0.6 4.1 %copy-start = (bf16[128,640]{1,0:T(8,128)(2,1)S(1)}, bf16[128,640]{1,0:T(8,128)(2,1)}, u32[]{:S(2)}) copy-start(bf16[128,640]{1,0:T(8,128)(2,1)} %refs_0_.1) | copy-start | bytes 491524
  1.6 5.8 %collective-permute-start = (bf16[32,256]{1,0:T(8,128)(2,1)S(1)}, bf16[32,256]{1,0:T(8,128)(2,1)S(1)}, u32[]{:S(2)}, u32[]{:S(2)}) collective-permute-start(bf16[32,256]{1,0:T(8,128)(2,1)S(1)} %get-tuple-element.28), channel_id=1, source_target_pairs={{0,1},{1,0},{2,3},{3,2},{4,5},{5,4},{6,7},{7,6},{8,9},{9,8},{10,11... | collective-permute-start | bytes 49160 | tf_op jit(solution)/shard_map/ppermute | solution.py:364
  2.1 5.3 %collective-permute-start.1 = (bf16[32,256]{1,0:T(8,128)(2,1)S(1)}, bf16[32,256]{1,0:T(8,128)(2,1)S(1)}, u32[]{:S(2)}, u32[]{:S(2)}) collective-permute-start(bf16[32,256]{1,0:T(8,128)(2,1)S(1)} %get-tuple-element.29), channel_id=1, source_target_pairs={{0,2},{1,3},{2,0},{3,1},{4,6},{5,7},{6,4},{7,5},{8,10},{9,11},{10,... | collective-permute-start | bytes 49160 | tf_op jit(solution)/shard_map/ppermute | solution.py:364
  4.7 2.1 %copy-start.2 = (s32[16]{0:T(128)S(1)}, s32[16]{0:T(128)}, u32[]{:S(2)}) copy-start(s32[16]{0:T(128)} %order_ref.1) | copy-start | bytes 196
  4.7 3.2 %collective-permute-start.2 = (bf16[32,256]{1,0:T(8,128)(2,1)S(1)}, bf16[32,256]{1,0:T(8,128)(2,1)S(1)}, u32[]{:S(2)}, u32[]{:S(2)}) collective-permute-start(bf16[32,256]{1,0:T(8,128)(2,1)S(1)} %get-tuple-element.30), channel_id=1, source_target_pairs={{0,3},{1,2},{2,1},{3,0},{4,7},{5,6},{6,5},{7,4},{8,11},{9,10},{10,... | collective-permute-start | bytes 49160 | tf_op jit(solution)/shard_map/ppermute | solution.py:364
  4.7 7.7 %collective-permute-start.6 = (bf16[128,640]{1,0:T(8,128)(2,1)S(1)}, bf16[128,640]{1,0:T(8,128)(2,1)S(1)}, u32[]{:S(2)}, u32[]{:S(2)}) collective-permute-start(bf16[128,640]{1,0:T(8,128)(2,1)S(1)} %copy-done), channel_id=1, source_target_pairs={{0,4},{4,0},{1,5},{5,1},{2,6},{6,2},{3,7},{7,3},{8,12},{12,8},{9,1... | collective-permute-start | bytes 491528 | tf_op jit(solution)/shard_map/ppermute | solution.py:364
  6.5 8.2 %collective-permute-start.7 = (bf16[128,640]{1,0:T(8,128)(2,1)}, bf16[128,640]{1,0:T(8,128)(2,1)S(1)}, u32[]{:S(2)}, u32[]{:S(2)}) collective-permute-start(bf16[128,640]{1,0:T(8,128)(2,1)} %refs_1_.1), channel_id=1, source_target_pairs={{0,4},{4,0},{1,5},{5,1},{2,6},{6,2},{3,7},{7,3},{8,12},{12,8},{9,1... | collective-permute-start | bytes 491528 | tf_op jit(solution)/shard_map/ppermute | solution.py:364
  7.3 7.4 %copy-start.1 = (bf16[128,640]{1,0:T(8,128)(2,1)S(1)}, bf16[128,640]{1,0:T(8,128)(2,1)}, u32[]{:S(2)}) copy-start(bf16[128,640]{1,0:T(8,128)(2,1)} %refs_1_.1) | copy-start | bytes 491524
  7.9 6.9 %collective-permute-start.5 = (bf16[128,256]{1,0:T(8,128)(2,1)S(1)}, bf16[128,256]{1,0:T(8,128)(2,1)S(1)}, u32[]{:S(2)}, u32[]{:S(2)}) collective-permute-start(bf16[128,256]{1,0:T(8,128)(2,1)S(1)} %join.1.refs_0_), channel_id=1, source_target_pairs={{0,24},{8,16},{16,8},{24,0},{1,25},{9,17},{17,9},{25,1},{2,26},{10... | collective-permute-start | bytes 196616 | tf_op jit(solution)/shard_map/ppermute | solution.py:364
  11.6 5.9 %collective-permute-start.4 = (bf16[128,256]{1,0:T(8,128)(2,1)S(1)}, bf16[128,256]{1,0:T(8,128)(2,1)S(1)}, u32[]{:S(2)}, u32[]{:S(2)}) collective-permute-start(bf16[128,256]{1,0:T(8,128)(2,1)S(1)} %join.1.refs_0_), channel_id=1, source_target_pairs={{0,16},{8,24},{16,0},{24,8},{1,17},{9,25},{17,1},{25,9},{2,18},{10... | collective-permute-start | bytes 196616 | tf_op jit(solution)/shard_map/ppermute | solution.py:364
  11.6 5.9 %collective-permute-start.3 = (bf16[128,256]{1,0:T(8,128)(2,1)S(1)}, bf16[128,256]{1,0:T(8,128)(2,1)S(1)}, u32[]{:S(2)}, u32[]{:S(2)}) collective-permute-start(bf16[128,256]{1,0:T(8,128)(2,1)S(1)} %join.1.refs_0_), channel_id=1, source_target_pairs={{0,8},{8,0},{16,24},{24,16},{1,9},{9,1},{17,25},{25,17},{2,10},{10... | collective-permute-start | bytes 196616 | tf_op jit(solution)/shard_map/ppermute | solution.py:364
  18.3 3.9 %collective-permute-start.8 = (f32[12,320]{1,0:T(8,128)S(1)}, f32[12,320]{1,0:T(8,128)S(1)}, u32[]{:S(2)}, u32[]{:S(2)}) collective-permute-start(f32[12,320]{1,0:T(8,128)S(1)} %merge.1), channel_id=1, source_target_pairs={{0,4},{4,0},{1,5},{5,1},{2,6},{6,2},{3,7},{7,3},{8,12},{12,8},{9,1... | collective-permute-start | bytes 46088 | tf_op jit(solution)/shard_map/ppermute | solution.py:364
  23.3 7.0 %collective-permute-start.10 = (bf16[128,256]{1,0:T(8,128)(2,1)S(1)}, bf16[128,256]{1,0:T(8,128)(2,1)S(1)}, u32[]{:S(2)}, u32[]{:S(2)}) collective-permute-start(bf16[128,256]{1,0:T(8,128)(2,1)S(1)} %get-tuple-element.44), channel_id=1, source_target_pairs={{0,24},{8,16},{16,8},{24,0},{1,25},{9,17},{17,9},{25,1},{2,26},{10... | collective-permute-start | bytes 196616 | tf_op jit(solution)/shard_map/ppermute | solution.py:365
  25.8 5.4 %collective-permute-start.11 = (bf16[128,256]{1,0:T(8,128)(2,1)S(1)}, bf16[128,256]{1,0:T(8,128)(2,1)S(1)}, u32[]{:S(2)}, u32[]{:S(2)}) collective-permute-start(bf16[128,256]{1,0:T(8,128)(2,1)S(1)} %get-tuple-element.45), channel_id=1, source_target_pairs={{0,16},{8,24},{16,0},{24,8},{1,17},{9,25},{17,1},{25,9},{2,18},{10... | collective-permute-start | bytes 196616 | tf_op jit(solution)/shard_map/ppermute | solution.py:365
  25.9 5.3 %collective-permute-start.12 = (bf16[128,256]{1,0:T(8,128)(2,1)S(1)}, bf16[128,256]{1,0:T(8,128)(2,1)S(1)}, u32[]{:S(2)}, u32[]{:S(2)}) collective-permute-start(bf16[128,256]{1,0:T(8,128)(2,1)S(1)} %get-tuple-element.46), channel_id=1, source_target_pairs={{0,8},{8,0},{16,24},{24,16},{1,9},{9,1},{17,25},{25,17},{2,10},{10... | collective-permute-start | bytes 196616 | tf_op jit(solution)/shard_map/ppermute | solution.py:365
  28.7 7.2 %collective-permute-start.9 = (bf16[128,640]{1,0:T(8,128)(2,1)S(1)}, bf16[128,640]{1,0:T(8,128)(2,1)S(1)}, u32[]{:S(2)}, u32[]{:S(2)}) collective-permute-start(bf16[128,640]{1,0:T(8,128)(2,1)S(1)} %get-tuple-element.42), channel_id=1, source_target_pairs={{0,4},{4,0},{1,5},{5,1},{2,6},{6,2},{3,7},{7,3},{8,12},{12,8},{9,1... | collective-permute-start | bytes 491528 | tf_op jit(solution)/shard_map/ppermute | solution.py:364
  31.3 1.9 %collective-permute-start.13 = (bf16[32,256]{1,0:T(8,128)(2,1)S(1)}, bf16[32,256]{1,0:T(8,128)(2,1)S(1)}, u32[]{:S(2)}, u32[]{:S(2)}) collective-permute-start(bf16[32,256]{1,0:T(8,128)(2,1)S(1)} %get-tuple-element.48), channel_id=1, source_target_pairs={{0,1},{1,0},{2,3},{3,2},{4,5},{5,4},{6,7},{7,6},{8,9},{9,8},{10,11... | collective-permute-start | bytes 49160 | tf_op jit(solution)/shard_map/ppermute | solution.py:364
  31.3 3.8 %collective-permute-start.14 = (bf16[32,256]{1,0:T(8,128)(2,1)S(1)}, bf16[32,256]{1,0:T(8,128)(2,1)S(1)}, u32[]{:S(2)}, u32[]{:S(2)}) collective-permute-start(bf16[32,256]{1,0:T(8,128)(2,1)S(1)} %get-tuple-element.49), channel_id=1, source_target_pairs={{0,2},{1,3},{2,0},{3,1},{4,6},{5,7},{6,4},{7,5},{8,10},{9,11},{10,... | collective-permute-start | bytes 49160 | tf_op jit(solution)/shard_map/ppermute | solution.py:364
  32.7 3.2 %collective-permute-start.15 = (bf16[32,256]{1,0:T(8,128)(2,1)S(1)}, bf16[32,256]{1,0:T(8,128)(2,1)S(1)}, u32[]{:S(2)}, u32[]{:S(2)}) collective-permute-start(bf16[32,256]{1,0:T(8,128)(2,1)S(1)} %get-tuple-element.50), channel_id=1, source_target_pairs={{0,3},{1,2},{2,1},{3,0},{4,7},{5,6},{6,5},{7,4},{8,11},{9,10},{10,... | collective-permute-start | bytes 49160 | tf_op jit(solution)/shard_map/ppermute | solution.py:364

commit v10 on v9

--- a/solution.py
+++ b/solution.py
@@ -126,7 +126,7 @@
                 ]
 
 
-def join_kernel(after_ref, *refs):
+def join_kernel(*refs):
     parts, (out_ref, sems) = refs[:-2], refs[-2:]
     kvh = len(parts)
     rows = parts[0].shape[0]
@@ -149,20 +149,40 @@
 
     tops = []
     for owner, qd_ref in enumerate((own_ref, other_ref)):
-        high = work.query_slot(owner, 1)
-        scores = products(work.low_keys(key_cols), qd_ref[0, high])
+        tiles = work.tiles(owner)
+        seen_by_low = [tile for tile in tiles if not (tile[3] and tile[1] == 1)]
+        seen_by_high = [tile for tile in tiles if not (tile[3] and tile[1] == 0)]
+
+        def both(kind, cols):
+            low_keys, high_keys = [
+                [work.keys(n, half, cols) for n, half, _, _ in found] for found in (seen_by_low, seen_by_high)
+            ]
+            low = products(jnp.concatenate(low_keys, axis=0), qd_ref[kind, work.query_slot(owner, 0)])
+            high = products(
+                jnp.concatenate([work.low_keys(cols), *high_keys], axis=0),
+                qd_ref[kind, work.query_slot(owner, 1)],
+            )
+            found = {}
+            for at, tile in enumerate(seen_by_low):
+                found[tile[2].start] = low[at * rows : (at + 1) * rows]
+            for at, (n, half, here, masked) in enumerate(seen_by_high):
+                mine = high[work.low_rows + at * rows : work.low_rows + (at + 1) * rows]
+                found[here.start] = mine if masked else lax.select(half == 0, found[here.start], mine)
+            return high[: work.low_rows], found
+
+        scores, tile_scores = both(0, key_cols)
         e_ref[owner, low_part, :] = scores
-        dp_ref[owner, low_part, :] = products(work.low_keys(value_cols), qd_ref[1, high])
+        low_grads, tile_grads = both(1, value_cols)
+        dp_ref[owner, low_part, :] = low_grads
         top = [jnp.full((1, scores.shape[1]), LOWEST, jnp.float32), jnp.max(scores, axis=0, keepdims=True)]
-        for n, half, here, masked in work.tiles(owner):
-            slot = work.query_slot(owner, half)
-            scores = products(work.keys(n, half, key_cols), qd_ref[0, slot])
+        for n, half, here, masked in tiles:
+            scores = tile_scores[here.start]
             if masked:
                 key = lax.broadcasted_iota(jnp.int32, scores.shape, 0)
                 query = lax.rem(lax.broadcasted_iota(jnp.int32, (1, scores.shape[1]), 1), rows)
                 scores = jnp.where(key <= query, scores, LOWEST)
             e_ref[owner, here, :] = scores
-            dp_ref[owner, here, :] = products(work.keys(n, half, value_cols), qd_ref[1, slot])
+            dp_ref[owner, here, :] = tile_grads[here.start]
             most = jnp.max(scores, axis=0, keepdims=True)
             for side in range(2):
                 seen = most if masked else pick(half == side, most, LOWEST)
@@ -214,7 +234,7 @@
     count = len(groups)
     stats_refs, theirs_ref, refs = refs[:count], refs[count], refs[count + 1 :]
     e_refs, dp_refs, refs = refs[:count], refs[count : 2 * count], refs[2 * count :]
-    term_refs, gs_refs = refs[:outer], refs[outer:]
+    term_refs, (high_ref, low_ref, p_high_ref, p_low_ref) = refs[:outer], refs[outer:]
     rows = term_refs[0].shape[0] // 2
     weights, deltas = [[] for _ in groups], []
     for owner in range(2):
@@ -237,78 +257,72 @@
         for n in range(count):
             weights[n].append(group_weights[n])
 
-    for n, members in enumerate(groups):
-        work = Work(table_ref, rows, members, None)
-        terms = [[None] * len(members), [None] * len(members)]
-
-        def add(half, at, pair):
-            old = terms[half][at]
-            terms[half][at] = pair if old is None else [one + more for one, more in zip(old, pair)]
-
-        for owner, qd_ref in enumerate((own_ref, other_ref)):
-
-            def gradients(here, slot, weight, delta):
+    works = [Work(table_ref, rows, members, None) for members in groups]
+    all_rows = outer * rows
+    totals = None
+    for owner, qd_ref in enumerate((own_ref, other_ref)):
+        delta = deltas[owner]
+        base = 0
+        for n, work in enumerate(works):
+
+            def gradients(here, weight, half, targets, target):
                 probs = e_refs[n][owner, here, :] * weight
-                grads = (probs * (dp_refs[n][owner, here, :] - delta)).astype(jnp.bfloat16)
-                gs_refs[n][owner, here, :] = grads
-                return [
-                    jnp.dot(grads, qd_ref[0, slot], preferred_element_type=jnp.float32),
-                    jnp.dot(probs.astype(jnp.bfloat16), qd_ref[1, slot], preferred_element_type=jnp.float32),
-                ]
-
-            weight, delta = weights[n][owner], deltas[owner]
+                grads = probs * (dp_refs[n][owner, here, :] - delta[half])
+                targets[0][owner, target, :] = grads.astype(jnp.bfloat16)
+                targets[1][owner, target, :] = probs.astype(jnp.bfloat16)
+
+            weight = weights[n][owner]
+            high_targets, low_targets = (high_ref, p_high_ref), (low_ref, p_low_ref)
             low_part = pl.ds(0, work.low_rows)
-            part = gradients(low_part, work.query_slot(owner, 1), weight[1], delta[1])
-            for at in range(len(members)):
-                add(0, at, [one[at * rows : (at + 1) * rows] for one in part])
+            gradients(low_part, weight[1], 1, high_targets, pl.ds(base, work.low_rows))
             for at, half, here, masked in work.tiles(owner):
-                slot = work.query_slot(owner, half)
-                if masked:
-                    add(half, at, gradients(here, slot, weight[half], delta[half]))
-                else:
-                    is_low = half == 0
-                    part = gradients(here, slot, lax.select(is_low, *weight), lax.select(is_low, *delta))
-                    for side in range(2):
-                        add(side, at, [pick(half == side, one, 0) for one in part])
-        for at, d in enumerate(members):
+                first = base + at * rows
+                if not masked or half == 0:
+                    seen = weight[0] if masked else pick(half == 0, weight[0], 0)
+                    gradients(here, seen, 0, low_targets, pl.ds(first, rows))
+                if not masked or half == 1:
+                    seen = weight[1] if masked else pick(half == 1, weight[1], 0)
+                    gradients(here, seen, 1, high_targets, pl.ds(all_rows + first, rows))
+            base += work.low_rows
+        slots = [works[0].query_slot(owner, half) for half in range(2)]
+        part = [
+            jnp.dot(target[owner], qd_ref[kind, slots[half]], preferred_element_type=jnp.float32)
+            for half, targets in enumerate(((low_ref, p_low_ref), (high_ref, p_high_ref)))
+            for kind, target in enumerate(targets)
+        ]
+        totals = part if totals is None else [one + more for one, more in zip(totals, part)]
+    low_keys, low_values, high_keys, high_values = totals
+    base = 0
+    for work in works:
+        for at, d in enumerate(work.members):
+            here, above = slice(base, base + rows), slice(all_rows + base, all_rows + base + rows)
             term_ref = term_refs[d]
-            for half in range(2):
+            for half, of_keys, of_values in (
+                (0, low_keys[here] + high_keys[here], low_values[here] + high_values[here]),
+                (1, high_keys[above], high_values[above]),
+            ):
                 target = work.key_rows(at, half)
-                of_keys, of_values = terms[half][at]
                 term_ref[target, :HEAD] = (of_keys * SCALE).astype(term_ref.dtype)
                 term_ref[target, HEAD:] = of_values.astype(term_ref.dtype)
+            base += rows
 
 
 def query_kernel(outer, groups, table_ref, *refs):
-    count = len(groups)
-    block_refs, gs_refs, (own_ref, other_ref) = refs[:outer], refs[outer : outer + count], refs[outer + count :]
+    block_refs, (high_ref, low_ref, own_ref, other_ref) = refs[:outer], refs[outer:]
     rows = own_ref.shape[0] // 2
-    works = [Work(table_ref, rows, members, [block_refs[d] for d in members]) for members in groups]
-    cols = slice(0, HEAD)
+    members = sum(groups, [])
+    work = Work(table_ref, rows, members, [block_refs[d] for d in members])
+    low_keys, high_keys = [
+        jnp.concatenate([work.keys(n, half, slice(0, HEAD)) for n in range(outer)], axis=0) for half in range(2)
+    ]
+    all_keys = jnp.concatenate([low_keys, high_keys], axis=0)
     for owner, target in ((0, own_ref), (1, other_ref)):
-        totals = [None, None]
-
-        def add(half, part):
-            totals[half] = part if totals[half] is None else totals[half] + part
-
-        for gs_ref, work in zip(gs_refs, works):
-
-            def terms(keys, here):
-                return lax.dot_general(
-                    keys, gs_ref[owner, here, :], COLS_DOT_COLS, preferred_element_type=jnp.float32
-                )
-
-            add(1, terms(work.low_keys(cols), pl.ds(0, work.low_rows)))
-            for n, half, here, masked in work.tiles(owner):
-                part = terms(work.keys(n, half, cols), here)
-                for side in range(2):
-                    if not masked:
-                        add(side, pick(half == side, part, 0))
-                    elif half == side:
-                        add(side, part)
-        for half in range(2):
-            place = at_rows(works[0].query_slot(owner, half) * rows, rows)
-            grads = (jnp.transpose(totals[half]) * SCALE).astype(target.dtype)
+        for half, keys, grads_ref in ((0, low_keys, low_ref), (1, all_keys, high_ref)):
+            total = lax.dot_general(
+                keys, grads_ref[owner], COLS_DOT_COLS, preferred_element_type=jnp.float32
+            )
+            place = at_rows(work.query_slot(owner, half) * rows, rows)
+            grads = (jnp.transpose(total) * SCALE).astype(target.dtype)
             for h in range(GROUP):
                 target[place, h * HEAD : (h + 1) * HEAD] = grads[h * rows : (h + 1) * rows, :]
 
@@ -346,7 +360,7 @@
     cache_rows = keys.shape[0]
     slab_rows = local_rows // 2
     columns = GROUP * slab_rows
-    params = pltpu.CompilerParams(vmem_limit_bytes=(8 << 20) + (10 << 10) * outer * local_rows)
+    params = pltpu.CompilerParams(vmem_limit_bytes=(8 << 20) + (13 << 10) * outer * local_rows)
     beside = pl.CostEstimate(flops=2 * 10**10, bytes_accessed=10**6, transcendentals=0)
     vmem = pl.BlockSpec(memory_space=pltpu.VMEM)
     smem = pl.BlockSpec(memory_space=pltpu.SMEM)
@@ -374,14 +388,6 @@
         out_specs=(vmem,) * kvh,
         scratch_shapes=[dma((2 * kvh,))],
     )(jnp.concatenate([keys, values], axis=0))
-    table = call(
-        functools.partial(table_kernel, outer),
-        "table",
-        out_shape=shape((2 * outer + 4, HEAD), jnp.int32),
-        in_specs=[smem, anywhere],
-        out_specs=vmem,
-        cost_estimate=beside,
-    )(slab_order, parts[0])
     parts = [parts[0]] + [shift(parts[e], "kvh", e) for e in range(1, kvh)]
     stack = shape((2, 2, columns, HEAD), low)
     own_qd, other_qd = call(
@@ -395,13 +401,20 @@
         join_kernel,
         "join",
         out_shape=block,
-        in_specs=[anywhere] * (1 + kvh),
+        in_specs=[anywhere] * kvh,
         out_specs=vmem,
         scratch_shapes=[dma((kvh,))],
         cost_estimate=beside,
-    )(table, *parts)
+    )(*parts)
     blocks = [own_block] + [shift(own_block, "outer", d) for d in range(1, outer)]
 
+    table = call(
+        functools.partial(table_kernel, outer),
+        "table",
+        out_shape=shape((2 * outer + 4, HEAD), jnp.int32),
+        in_specs=[smem, anywhere],
+        out_specs=vmem,
+    )(slab_order, blocks[outer - 1])
     far = outer // 2 + 1
     groups = [[0, *range(far, outer)], list(range(1, far))]
     all_stats = shape((12, columns), full)
@@ -424,14 +437,15 @@
     )(*stats)
     theirs = shift(mine, "pair", 1)
     count = len(groups)
+    high_rows = shape((2, 2 * outer * slab_rows, columns), low)
+    low_rows = shape((2, outer * slab_rows, columns), low)
     grads = call(
         functools.partial(grads_kernel, outer, groups),
         "grads",
-        out_shape=(shape(block.shape, full),)
-        + (block,) * (outer - 1)
-        + tuple(shape(scores.shape, low) for scores in expon),
+        out_shape=(shape(block.shape, full),) + (block,) * (outer - 1) + (high_rows, low_rows),
         in_specs=[vmem] * (4 + 3 * count),
-        out_specs=(vmem,) * (outer + count),
+        out_specs=(vmem,) * (outer + 2),
+        scratch_shapes=[pltpu.VMEM(high_rows.shape, low), pltpu.VMEM(low_rows.shape, low)],
     )(table, own_qd, other_qd, *stats, theirs, *expon, *grad_probs)
     terms, score_grads = grads[:outer], grads[outer:]
     terms = [terms[0]] + [shift(terms[d], "outer", -d) for d in range(outer - 1, 0, -1)]
@@ -439,7 +453,7 @@
         functools.partial(query_kernel, outer, groups),
         "query_terms",
         out_shape=(shape(queries.shape, full), shape(queries.shape, low)),
-        in_specs=[vmem] * (1 + outer + count),
+        in_specs=[vmem] * (3 + outer),
         out_specs=(vmem, vmem),
         cost_estimate=beside,
     )(table, *blocks, *score_grads)

time: 36.8 us -> 36.7 us (level)
  transfers between devices with their start and end apart: 16 -> 16, of which waited for: 7 -> 7; matrix products, arithmetic and copies ran while one was open for 0% -> 0% of each run, Pallas kernels for 7% -> 6%
where the time goes in v10:
time: 36.7 us; the launch traced here: 36.6 us
  starting transfers between devices  19.2 us (52%)
  waiting for transfers between devices  10.5 us (29%)
  Pallas kernels  5.29 us (14%)
  other arithmetic  0.82 us (2%)
  between operations  0.75 us (2%)
    ppermute x13, starting transfers between devices, shift(): lax.ppermute(array, axis, [(n, target_of(n, by, size)) for n in range(siz...  14.7 us
    ppermute x13, waiting for transfers between devices, shift(): lax.ppermute(array, axis, [(n, target_of(n, by, size)) for n in range(siz...  9.3 us
    ppermute x3, starting transfers between devices, shift(): lax.ppermute(array, axis, [(n, partner(n, -by, size)) for n in range(size)])  4.45 us
    pallas_call x2, Pallas kernels, per_device(): call(functools.partial(stats_kernel, members), 'stats', out_shape=(all_st...  1.61 us
    pallas_call x1, Pallas kernels, per_device(): call(functools.partial(grads_kernel, outer, groups), 'grads', out_shape=(...  1.21 us
    ppermute x3, waiting for transfers between devices, shift(): lax.ppermute(array, axis, [(n, partner(n, -by, size)) for n in range(size)])  1.2 us
    concatenate x1, other arithmetic, per_device(): jnp.concatenate([keys, values], axis=0)  0.82 us
    pallas_call x1, Pallas kernels, per_device(): call(place_kernel, 'place', out_shape=(shape(queries.shape, low), shape(k...  0.79 us
  transfers between devices with their start and end apart: 16, of which 7 were waited for; matrix products, arithmetic and copies ran while one was open for 0% of the time, Pallas kernels for 6%

profile of v10, /device:TPU:0, one launch (start us, length us, event | category | flops | bytes accessed | tf_op | source)
XLA Modules:
  0.0 36.6 jit_solution(2734153571781484733)
XLA Ops:
  0.6 0.0 copy-start
  0.6 0.8 %pad_maximum_fusion.cache_ref = bf16[64,512]{1,0:T(8,128)(2,1)S(1)} fusion(bf16[32,512]{1,0:T(8,128)(2,1)} %param.7, bf16[32,512]{1,0:T(8,128)(2,1)} %param.6), kind=kLoop, calls=%fused_computation | loop fusion | flops 131072 | bytes 131072 | tf_op jit(solution)/shard_map/concatenate | solution.py:390
  1.5 0.1 split.1
  1.6 0.5 %collective-permute-start = (bf16[32,256]{1,0:T(8,128)(2,1)S(1)}, bf16[32,256]{1,0:T(8,128)(2,1)S(1)}, u32[]{:S(2)}, u32[]{:S(2)}) collective-permute-start(bf16[32,256]{1,0:T(8,128)(2,1)S(1)} %get-tuple-element.28), channel_id=1, source_target_pairs={{0,1},{1,0},{2,3},{3,2},{4,5},{5,4},{6,7},{7,6},{8,9},{9,8},{10,11... | collective-permute-start | bytes 49160 | tf_op jit(solution)/shard_map/ppermute | solution.py:378
  2.1 2.6 %collective-permute-start.1 = (bf16[32,256]{1,0:T(8,128)(2,1)S(1)}, bf16[32,256]{1,0:T(8,128)(2,1)S(1)}, u32[]{:S(2)}, u32[]{:S(2)}) collective-permute-start(bf16[32,256]{1,0:T(8,128)(2,1)S(1)} %get-tuple-element.29), channel_id=1, source_target_pairs={{0,2},{1,3},{2,0},{3,1},{4,6},{5,7},{6,4},{7,5},{8,10},{9,11},{10,... | collective-permute-start | bytes 49160 | tf_op jit(solution)/shard_map/ppermute | solution.py:378
  4.7 0.1 collective-permute-start.2
  4.7 0.0 copy-done
  4.7 1.8 %collective-permute-start.6 = (bf16[128,640]{1,0:T(8,128)(2,1)S(1)}, bf16[128,640]{1,0:T(8,128)(2,1)S(1)}, u32[]{:S(2)}, u32[]{:S(2)}) collective-permute-start(bf16[128,640]{1,0:T(8,128)(2,1)S(1)} %copy-done), channel_id=1, source_target_pairs={{0,4},{4,0},{1,5},{5,1},{2,6},{6,2},{3,7},{7,3},{8,12},{12,8},{9,1... | collective-permute-start | bytes 491528 | tf_op jit(solution)/shard_map/ppermute | solution.py:378
  6.5 0.3 collective-permute-start.7
  6.8 0.0 collective-permute-done.refs_1_
  6.8 0.0 collective-permute-done.1.refs_2_
  6.8 1.1 %collective-permute-done.2.refs_3_ = bf16[32,256]{1,0:T(8,128)(2,1)S(1)} collective-permute-done((bf16[32,256]{1,0:T(8,128)(2,1)S(1)}, bf16[32,256]{1,0:T(8,128)(2,1)S(1)}, u32[]{:S(2)}, u32[]{:S(2)}) %collective-permute-start.2) | collective-permute-done | bytes 16416 | tf_op jit(solution)/shard_map/ppermute | solution.py:378
  7.8 0.0 copy-start.2
  7.8 0.0 copy-start.1
  7.8 0.1 join.1.refs_0_
  7.9 3.7 %collective-permute-start.3 = (bf16[128,256]{1,0:T(8,128)(2,1)S(1)}, bf16[128,256]{1,0:T(8,128)(2,1)S(1)}, u32[]{:S(2)}, u32[]{:S(2)}) collective-permute-start(bf16[128,256]{1,0:T(8,128)(2,1)S(1)} %join.1.refs_0_), channel_id=1, source_target_pairs={{0,24},{8,16},{16,8},{24,0},{1,25},{9,17},{17,9},{25,1},{2,26},{10... | collective-permute-start | bytes 196616 | tf_op jit(solution)/shard_map/ppermute | solution.py:378
  11.6 0.0 collective-permute-start.5
  11.6 0.8 %collective-permute-start.4 = (bf16[128,256]{1,0:T(8,128)(2,1)S(1)}, bf16[128,256]{1,0:T(8,128)(2,1)S(1)}, u32[]{:S(2)}, u32[]{:S(2)}) collective-permute-start(bf16[128,256]{1,0:T(8,128)(2,1)S(1)} %join.1.refs_0_), channel_id=1, source_target_pairs={{0,8},{8,0},{16,24},{24,16},{1,9},{9,1},{17,25},{25,17},{2,10},{10... | collective-permute-start | bytes 196616 | tf_op jit(solution)/shard_map/ppermute | solution.py:378
  12.4 1.9 %collective-permute-done.3.after_ref.refs_1_.refs_3_ = bf16[128,256]{1,0:T(8,128)(2,1)S(1)} collective-permute-done((bf16[128,256]{1,0:T(8,128)(2,1)S(1)}, bf16[128,256]{1,0:T(8,128)(2,1)S(1)}, u32[]{:S(2)}, u32[]{:S(2)}) %collective-permute-start.3) | collective-permute-done | bytes 65568 | tf_op jit(solution)/shard_map/ppermute | solution.py:378
  14.3 0.0 copy-done.2
  14.3 0.6 %table.1.table_ref = s32[12,128]{1,0:T(8,128)S(1)} custom-call(s32[16]{0:T(128)S(1)} %copy-done.2, bf16[128,256]{1,0:T(8,128)(2,1)S(1)} %collective-permute-done.3.after_ref.refs_1_.refs_3_), custom_call_target="tpu_custom_call" | custom-call | tf_op jit(solution)/shard_map/table/pallas_call | solution.py:411
  14.9 0.0 collective-permute-done.6.refs_2_
  14.9 0.0 collective-permute-done.7.refs_3_
  14.9 0.0 copy-done.1
  14.9 0.1 stack.1
  15.0 0.8 %stats.2 = (f32[12,320]{1,0:T(8,128)S(1)}, f32[2,320,320]{2,1,0:T(8,128)S(1)}, f32[2,320,320]{2,1,0:T(8,128)S(1)}) custom-call(s32[12,128]{1,0:T(8,128)S(1)} %table.1.table_ref, bf16[2,2,320,128]{3,2,1,0:T(8,128)(2,1)S(1)} %get-tuple-element.31.own_ref, bf16[2,2,320,128]{3,2,1,0:T(8,128)(2,1)S(1)} %get-tuple-element.32.other_ref, ...), custom_call_target="tpu_custom_call" | custom-call | flops 20000000000 | bytes 1000000 | tf_op jit(solution)/shard_map/stats/pallas_call | solution.py:425
  15.9 1.6 %collective-permute-done.5.refs_1_.refs_2_ = bf16[128,256]{1,0:T(8,128)(2,1)S(1)} collective-permute-done((bf16[128,256]{1,0:T(8,128)(2,1)S(1)}, bf16[128,256]{1,0:T(8,128)(2,1)S(1)}, u32[]{:S(2)}, u32[]{:S(2)}) %collective-permute-start.5) | collective-permute-done | bytes 65568 | tf_op jit(solution)/shard_map/ppermute | solution.py:378
  17.5 0.0 collective-permute-done.4.refs_0_.refs_1_
  17.5 0.8 %stats.3 = (f32[12,320]{1,0:T(8,128)S(1)}, f32[2,320,320]{2,1,0:T(8,128)S(1)}, f32[2,320,320]{2,1,0:T(8,128)S(1)}) custom-call(s32[12,128]{1,0:T(8,128)S(1)} %table.1.table_ref, bf16[2,2,320,128]{3,2,1,0:T(8,128)(2,1)S(1)} %get-tuple-element.31.own_ref, bf16[2,2,320,128]{3,2,1,0:T(8,128)(2,1)S(1)} %get-tuple-element.32.other_ref, ...), custom_call_target="tpu_custom_call" | custom-call | tf_op jit(solution)/shard_map/stats/pallas_call | solution.py:425
  18.4 1.6 %collective-permute-start.8 = (f32[12,320]{1,0:T(8,128)S(1)}, f32[12,320]{1,0:T(8,128)S(1)}, u32[]{:S(2)}, u32[]{:S(2)}) collective-permute-start(f32[12,320]{1,0:T(8,128)S(1)} %merge.1), channel_id=1, source_target_pairs={{0,4},{4,0},{1,5},{5,1},{2,6},{6,2},{3,7},{7,3},{8,12},{12,8},{9,1... | collective-permute-start | bytes 46088 | tf_op jit(solution)/shard_map/ppermute | solution.py:378
  19.9 2.3 %collective-permute-done.8.refs_2_ = f32[12,320]{1,0:T(8,128)S(1)} collective-permute-done((f32[12,320]{1,0:T(8,128)S(1)}, f32[12,320]{1,0:T(8,128)S(1)}, u32[]{:S(2)}, u32[]{:S(2)}) %collective-permute-start.8) | collective-permute-done | bytes 15392 | tf_op jit(solution)/shard_map/ppermute | solution.py:378
  22.2 1.2 %grads.1 = (f32[128,256]{1,0:T(8,128)S(1)}, bf16[128,256]{1,0:T(8,128)(2,1)S(1)}, bf16[128,256]{1,0:T(8,128)(2,1)S(1)}, bf16[128,256]{1,0:T(8,128)(2,1)S(1)}, bf...) custom-call(s32[12,128]{1,0:T(8,128)S(1)} %table.1.table_ref, ...), custom_call_target="tpu_custom_call" | custom-call | tf_op jit(solution)/shard_map/grads/pallas_call | solution.py:442
  23.5 2.5 %collective-permute-start.10 = (bf16[128,256]{1,0:T(8,128)(2,1)S(1)}, bf16[128,256]{1,0:T(8,128)(2,1)S(1)}, u32[]{:S(2)}, u32[]{:S(2)}) collective-permute-start(bf16[128,256]{1,0:T(8,128)(2,1)S(1)} %get-tuple-element.44), channel_id=1, source_target_pairs={{0,24},{8,16},{16,8},{24,0},{1,25},{9,17},{17,9},{25,1},{2,26},{10... | collective-permute-start | bytes 196616 | tf_op jit(solution)/shard_map/ppermute | solution.py:379
  26.0 0.1 collective-permute-start.11
  26.1 1.8 %collective-permute-start.12 = (bf16[128,256]{1,0:T(8,128)(2,1)S(1)}, bf16[128,256]{1,0:T(8,128)(2,1)S(1)}, u32[]{:S(2)}, u32[]{:S(2)}) collective-permute-start(bf16[128,256]{1,0:T(8,128)(2,1)S(1)} %get-tuple-element.46), channel_id=1, source_target_pairs={{0,8},{8,0},{16,24},{24,16},{1,9},{9,1},{17,25},{25,17},{2,10},{10... | collective-permute-start | bytes 196616 | tf_op jit(solution)/shard_map/ppermute | solution.py:379
  27.9 0.7 %query_terms.1 = (f32[128,640]{1,0:T(8,128)S(1)}, bf16[128,640]{1,0:T(8,128)(2,1)S(1)}) custom-call(s32[12,128]{1,0:T(8,128)S(1)} %table.1.table_ref, bf16[128,256]{1,0:T(8,128)(2,1)S(1)} %join.1.refs_0_, bf16[128,256]{1,0:T(8,128)(2,1)S(1)} %collective-permute-done.4.refs_0_.refs_1_, bf16[128,256]{1,0:T(8,128)(2,1)S(1)} %collective-permute-done.5.refs_1_.refs_2_, ...), custom_call_target="tpu_custom_call" | custom-call | flops 20000000000 | bytes 1000000 | tf_op jit(solution)/shard_map/query_terms/pallas_call | solution.py:452
  28.6 1.6 %collective-permute-start.9 = (bf16[128,640]{1,0:T(8,128)(2,1)S(1)}, bf16[128,640]{1,0:T(8,128)(2,1)S(1)}, u32[]{:S(2)}, u32[]{:S(2)}) collective-permute-start(bf16[128,640]{1,0:T(8,128)(2,1)S(1)} %get-tuple-element.42), channel_id=1, source_target_pairs={{0,4},{4,0},{1,5},{5,1},{2,6},{6,2},{3,7},{7,3},{8,12},{12,8},{9,1... | collective-permute-start | bytes 491528 | tf_op jit(solution)/shard_map/ppermute | solution.py:378
  30.2 0.0 collective-permute-done.10.refs_1_
  30.2 1.2 %collective-permute-done.11.refs_2_ = bf16[128,256]{1,0:T(8,128)(2,1)S(1)} collective-permute-done((bf16[128,256]{1,0:T(8,128)(2,1)S(1)}, bf16[128,256]{1,0:T(8,128)(2,1)S(1)}, u32[]{:S(2)}, u32[]{:S(2)}) %collective-permute-start.11) | collective-permute-done | bytes 65568 | tf_op jit(solution)/shard_map/ppermute | solution.py:379
  31.4 0.0 collective-permute-done.12.refs_3_
  31.4 0.1 collective-permute-start.13
  31.5 1.1 %collective-permute-start.14 = (bf16[32,256]{1,0:T(8,128)(2,1)S(1)}, bf16[32,256]{1,0:T(8,128)(2,1)S(1)}, u32[]{:S(2)}, u32[]{:S(2)}) collective-permute-start(bf16[32,256]{1,0:T(8,128)(2,1)S(1)} %get-tuple-element.49), channel_id=1, source_target_pairs={{0,2},{1,3},{2,0},{3,1},{4,6},{5,7},{6,4},{7,5},{8,10},{9,11},{10,... | collective-permute-start | bytes 49160 | tf_op jit(solution)/shard_map/ppermute | solution.py:378
  32.6 0.8 %collective-permute-start.15 = (bf16[32,256]{1,0:T(8,128)(2,1)S(1)}, bf16[32,256]{1,0:T(8,128)(2,1)S(1)}, u32[]{:S(2)}, u32[]{:S(2)}) collective-permute-start(bf16[32,256]{1,0:T(8,128)(2,1)S(1)} %get-tuple-element.50), channel_id=1, source_target_pairs={{0,3},{1,2},{2,1},{3,0},{4,7},{5,6},{6,5},{7,4},{8,11},{9,10},{10,... | collective-permute-start | bytes 49160 | tf_op jit(solution)/shard_map/ppermute | solution.py:378
  33.4 0.0 collective-permute-done.13.refs_1_
  33.4 1.9 %collective-permute-done.14.refs_2_ = bf16[32,256]{1,0:T(8,128)(2,1)S(1)} collective-permute-done((bf16[32,256]{1,0:T(8,128)(2,1)S(1)}, bf16[32,256]{1,0:T(8,128)(2,1)S(1)}, u32[]{:S(2)}, u32[]{:S(2)}) %collective-permute-start.14) | collective-permute-done | bytes 16416 | tf_op jit(solution)/shard_map/ppermute | solution.py:378
  35.3 0.4 %collective-permute-done.15.refs_3_ = bf16[32,256]{1,0:T(8,128)(2,1)S(1)} collective-permute-done((bf16[32,256]{1,0:T(8,128)(2,1)S(1)}, bf16[32,256]{1,0:T(8,128)(2,1)S(1)}, u32[]{:S(2)}, u32[]{:S(2)}) %collective-permute-start.15) | collective-permute-done | bytes 16416 | tf_op jit(solution)/shard_map/ppermute | solution.py:378
  35.8 0.0 collective-permute-done.9.received_ref
  35.8 0.8 %place.1 = (bf16[128,640]{1,0:T(8,128)(2,1)}, bf16[32,512]{1,0:T(8,128)(2,1)}, bf16[32,512]{1,0:T(8,128)(2,1)}) custom-call(f32[128,640]{1,0:T(8,128)S(1)} %get-tuple-element.41.own_ref, bf16[128,640]{1,0:T(8,128)(2,1)S(1)} %collective-permute-done.9.received_ref, bf16[32,256]{1,0:T(8,128)(2,1)S(1)} %get-tuple-element.47.refs_0_, ...), custom_call_target="tpu_custom_call" | custom-call | tf_op jit(solution)/shard_map/place/pallas_call | solution.py:471
  (2 shorter events, 0.1 us)
Async XLA Ops:
  0.6 4.1 %copy-start = (bf16[128,640]{1,0:T(8,128)(2,1)S(1)}, bf16[128,640]{1,0:T(8,128)(2,1)}, u32[]{:S(2)}) copy-start(bf16[128,640]{1,0:T(8,128)(2,1)} %refs_0_.1) | copy-start | bytes 491524
  1.6 5.2 %collective-permute-start = (bf16[32,256]{1,0:T(8,128)(2,1)S(1)}, bf16[32,256]{1,0:T(8,128)(2,1)S(1)}, u32[]{:S(2)}, u32[]{:S(2)}) collective-permute-start(bf16[32,256]{1,0:T(8,128)(2,1)S(1)} %get-tuple-element.28), channel_id=1, source_target_pairs={{0,1},{1,0},{2,3},{3,2},{4,5},{5,4},{6,7},{7,6},{8,9},{9,8},{10,11... | collective-permute-start | bytes 49160 | tf_op jit(solution)/shard_map/ppermute | solution.py:378
  2.1 4.7 %collective-permute-start.1 = (bf16[32,256]{1,0:T(8,128)(2,1)S(1)}, bf16[32,256]{1,0:T(8,128)(2,1)S(1)}, u32[]{:S(2)}, u32[]{:S(2)}) collective-permute-start(bf16[32,256]{1,0:T(8,128)(2,1)S(1)} %get-tuple-element.29), channel_id=1, source_target_pairs={{0,2},{1,3},{2,0},{3,1},{4,6},{5,7},{6,4},{7,5},{8,10},{9,11},{10,... | collective-permute-start | bytes 49160 | tf_op jit(solution)/shard_map/ppermute | solution.py:378
  4.7 3.2 %collective-permute-start.2 = (bf16[32,256]{1,0:T(8,128)(2,1)S(1)}, bf16[32,256]{1,0:T(8,128)(2,1)S(1)}, u32[]{:S(2)}, u32[]{:S(2)}) collective-permute-start(bf16[32,256]{1,0:T(8,128)(2,1)S(1)} %get-tuple-element.30), channel_id=1, source_target_pairs={{0,3},{1,2},{2,1},{3,0},{4,7},{5,6},{6,5},{7,4},{8,11},{9,10},{10,... | collective-permute-start | bytes 49160 | tf_op jit(solution)/shard_map/ppermute | solution.py:378
  4.7 10.2 %collective-permute-start.6 = (bf16[128,640]{1,0:T(8,128)(2,1)S(1)}, bf16[128,640]{1,0:T(8,128)(2,1)S(1)}, u32[]{:S(2)}, u32[]{:S(2)}) collective-permute-start(bf16[128,640]{1,0:T(8,128)(2,1)S(1)} %copy-done), channel_id=1, source_target_pairs={{0,4},{4,0},{1,5},{5,1},{2,6},{6,2},{3,7},{7,3},{8,12},{12,8},{9,1... | collective-permute-start | bytes 491528 | tf_op jit(solution)/shard_map/ppermute | solution.py:378
  6.5 8.4 %collective-permute-start.7 = (bf16[128,640]{1,0:T(8,128)(2,1)}, bf16[128,640]{1,0:T(8,128)(2,1)S(1)}, u32[]{:S(2)}, u32[]{:S(2)}) collective-permute-start(bf16[128,640]{1,0:T(8,128)(2,1)} %refs_1_.1), channel_id=1, source_target_pairs={{0,4},{4,0},{1,5},{5,1},{2,6},{6,2},{3,7},{7,3},{8,12},{12,8},{9,1... | collective-permute-start | bytes 491528 | tf_op jit(solution)/shard_map/ppermute | solution.py:378
  7.8 6.5 %copy-start.2 = (s32[16]{0:T(128)S(1)}, s32[16]{0:T(128)}, u32[]{:S(2)}) copy-start(s32[16]{0:T(128)} %order_ref.1) | copy-start | bytes 196
  7.8 7.1 %copy-start.1 = (bf16[128,640]{1,0:T(8,128)(2,1)S(1)}, bf16[128,640]{1,0:T(8,128)(2,1)}, u32[]{:S(2)}) copy-start(bf16[128,640]{1,0:T(8,128)(2,1)} %refs_1_.1) | copy-start | bytes 491524
  7.9 6.4 %collective-permute-start.3 = (bf16[128,256]{1,0:T(8,128)(2,1)S(1)}, bf16[128,256]{1,0:T(8,128)(2,1)S(1)}, u32[]{:S(2)}, u32[]{:S(2)}) collective-permute-start(bf16[128,256]{1,0:T(8,128)(2,1)S(1)} %join.1.refs_0_), channel_id=1, source_target_pairs={{0,24},{8,16},{16,8},{24,0},{1,25},{9,17},{17,9},{25,1},{2,26},{10... | collective-permute-start | bytes 196616 | tf_op jit(solution)/shard_map/ppermute | solution.py:378
  11.6 5.9 %collective-permute-start.5 = (bf16[128,256]{1,0:T(8,128)(2,1)S(1)}, bf16[128,256]{1,0:T(8,128)(2,1)S(1)}, u32[]{:S(2)}, u32[]{:S(2)}) collective-permute-start(bf16[128,256]{1,0:T(8,128)(2,1)S(1)} %join.1.refs_0_), channel_id=1, source_target_pairs={{0,16},{8,24},{16,0},{24,8},{1,17},{9,25},{17,1},{25,9},{2,18},{10... | collective-permute-start | bytes 196616 | tf_op jit(solution)/shard_map/ppermute | solution.py:378
  11.6 5.9 %collective-permute-start.4 = (bf16[128,256]{1,0:T(8,128)(2,1)S(1)}, bf16[128,256]{1,0:T(8,128)(2,1)S(1)}, u32[]{:S(2)}, u32[]{:S(2)}) collective-permute-start(bf16[128,256]{1,0:T(8,128)(2,1)S(1)} %join.1.refs_0_), channel_id=1, source_target_pairs={{0,8},{8,0},{16,24},{24,16},{1,9},{9,1},{17,25},{25,17},{2,10},{10... | collective-permute-start | bytes 196616 | tf_op jit(solution)/shard_map/ppermute | solution.py:378
  18.4 3.9 %collective-permute-start.8 = (f32[12,320]{1,0:T(8,128)S(1)}, f32[12,320]{1,0:T(8,128)S(1)}, u32[]{:S(2)}, u32[]{:S(2)}) collective-permute-start(f32[12,320]{1,0:T(8,128)S(1)} %merge.1), channel_id=1, source_target_pairs={{0,4},{4,0},{1,5},{5,1},{2,6},{6,2},{3,7},{7,3},{8,12},{12,8},{9,1... | collective-permute-start | bytes 46088 | tf_op jit(solution)/shard_map/ppermute | solution.py:378
  23.5 6.7 %collective-permute-start.10 = (bf16[128,256]{1,0:T(8,128)(2,1)S(1)}, bf16[128,256]{1,0:T(8,128)(2,1)S(1)}, u32[]{:S(2)}, u32[]{:S(2)}) collective-permute-start(bf16[128,256]{1,0:T(8,128)(2,1)S(1)} %get-tuple-element.44), channel_id=1, source_target_pairs={{0,24},{8,16},{16,8},{24,0},{1,25},{9,17},{17,9},{25,1},{2,26},{10... | collective-permute-start | bytes 196616 | tf_op jit(solution)/shard_map/ppermute | solution.py:379
  26.0 5.4 %collective-permute-start.11 = (bf16[128,256]{1,0:T(8,128)(2,1)S(1)}, bf16[128,256]{1,0:T(8,128)(2,1)S(1)}, u32[]{:S(2)}, u32[]{:S(2)}) collective-permute-start(bf16[128,256]{1,0:T(8,128)(2,1)S(1)} %get-tuple-element.45), channel_id=1, source_target_pairs={{0,16},{8,24},{16,0},{24,8},{1,17},{9,25},{17,1},{25,9},{2,18},{10... | collective-permute-start | bytes 196616 | tf_op jit(solution)/shard_map/ppermute | solution.py:379
  26.1 5.3 %collective-permute-start.12 = (bf16[128,256]{1,0:T(8,128)(2,1)S(1)}, bf16[128,256]{1,0:T(8,128)(2,1)S(1)}, u32[]{:S(2)}, u32[]{:S(2)}) collective-permute-start(bf16[128,256]{1,0:T(8,128)(2,1)S(1)} %get-tuple-element.46), channel_id=1, source_target_pairs={{0,8},{8,0},{16,24},{24,16},{1,9},{9,1},{17,25},{25,17},{2,10},{10... | collective-permute-start | bytes 196616 | tf_op jit(solution)/shard_map/ppermute | solution.py:379
  28.6 7.2 %collective-permute-start.9 = (bf16[128,640]{1,0:T(8,128)(2,1)S(1)}, bf16[128,640]{1,0:T(8,128)(2,1)S(1)}, u32[]{:S(2)}, u32[]{:S(2)}) collective-permute-start(bf16[128,640]{1,0:T(8,128)(2,1)S(1)} %get-tuple-element.42), channel_id=1, source_target_pairs={{0,4},{4,0},{1,5},{5,1},{2,6},{6,2},{3,7},{7,3},{8,12},{12,8},{9,1... | collective-permute-start | bytes 491528 | tf_op jit(solution)/shard_map/ppermute | solution.py:378
  31.4 1.9 %collective-permute-start.13 = (bf16[32,256]{1,0:T(8,128)(2,1)S(1)}, bf16[32,256]{1,0:T(8,128)(2,1)S(1)}, u32[]{:S(2)}, u32[]{:S(2)}) collective-permute-start(bf16[32,256]{1,0:T(8,128)(2,1)S(1)} %get-tuple-element.48), channel_id=1, source_target_pairs={{0,1},{1,0},{2,3},{3,2},{4,5},{5,4},{6,7},{7,6},{8,9},{9,8},{10,11... | collective-permute-start | bytes 49160 | tf_op jit(solution)/shard_map/ppermute | solution.py:378
  31.5 3.8 %collective-permute-start.14 = (bf16[32,256]{1,0:T(8,128)(2,1)S(1)}, bf16[32,256]{1,0:T(8,128)(2,1)S(1)}, u32[]{:S(2)}, u32[]{:S(2)}) collective-permute-start(bf16[32,256]{1,0:T(8,128)(2,1)S(1)} %get-tuple-element.49), channel_id=1, source_target_pairs={{0,2},{1,3},{2,0},{3,1},{4,6},{5,7},{6,4},{7,5},{8,10},{9,11},{10,... | collective-permute-start | bytes 49160 | tf_op jit(solution)/shard_map/ppermute | solution.py:378
  32.6 3.2 %collective-permute-start.15 = (bf16[32,256]{1,0:T(8,128)(2,1)S(1)}, bf16[32,256]{1,0:T(8,128)(2,1)S(1)}, u32[]{:S(2)}, u32[]{:S(2)}) collective-permute-start(bf16[32,256]{1,0:T(8,128)(2,1)S(1)} %get-tuple-element.50), channel_id=1, source_target_pairs={{0,3},{1,2},{2,1},{3,0},{4,7},{5,6},{6,5},{7,4},{8,11},{9,10},{10,... | collective-permute-start | bytes 49160 | tf_op jit(solution)/shard_map/ppermute | solution.py:378

commit v11 on v9

--- a/solution.py
+++ b/solution.py
@@ -126,12 +126,12 @@
                 ]
 
 
-def join_kernel(after_ref, *refs):
+def join_kernel(order, *refs):
     parts, (out_ref, sems) = refs[:-2], refs[-2:]
     kvh = len(parts)
     rows = parts[0].shape[0]
     copies = []
-    for e, part_ref in enumerate(parts):
+    for e, part_ref in zip(order, parts):
         source = partner(lax.axis_index("kvh"), e, kvh)
         copies.append(load(part_ref, out_ref.at[at_rows(source * rows, rows)], sems.at[e]))
     wait_all(copies)
@@ -279,38 +279,37 @@
                 term_ref[target, HEAD:] = of_values.astype(term_ref.dtype)
 
 
-def query_kernel(outer, groups, table_ref, *refs):
+def query_kernel(outer, groups, owner, table_ref, *refs):
     count = len(groups)
-    block_refs, gs_refs, (own_ref, other_ref) = refs[:outer], refs[outer : outer + count], refs[outer + count :]
-    rows = own_ref.shape[0] // 2
+    block_refs, gs_refs, out_ref = refs[:outer], refs[outer : outer + count], refs[-1]
+    rows = out_ref.shape[0] // 2
     works = [Work(table_ref, rows, members, [block_refs[d] for d in members]) for members in groups]
     cols = slice(0, HEAD)
-    for owner, target in ((0, own_ref), (1, other_ref)):
-        totals = [None, None]
-
-        def add(half, part):
-            totals[half] = part if totals[half] is None else totals[half] + part
-
-        for gs_ref, work in zip(gs_refs, works):
-
-            def terms(keys, here):
-                return lax.dot_general(
-                    keys, gs_ref[owner, here, :], COLS_DOT_COLS, preferred_element_type=jnp.float32
-                )
-
-            add(1, terms(work.low_keys(cols), pl.ds(0, work.low_rows)))
-            for n, half, here, masked in work.tiles(owner):
-                part = terms(work.keys(n, half, cols), here)
-                for side in range(2):
-                    if not masked:
-                        add(side, pick(half == side, part, 0))
-                    elif half == side:
-                        add(side, part)
-        for half in range(2):
-            place = at_rows(works[0].query_slot(owner, half) * rows, rows)
-            grads = (jnp.transpose(totals[half]) * SCALE).astype(target.dtype)
-            for h in range(GROUP):
-                target[place, h * HEAD : (h + 1) * HEAD] = grads[h * rows : (h + 1) * rows, :]
+    totals = [None, None]
+
+    def add(half, part):
+        totals[half] = part if totals[half] is None else totals[half] + part
+
+    for gs_ref, work in zip(gs_refs, works):
+
+        def terms(keys, here):
+            return lax.dot_general(
+                keys, gs_ref[owner, here, :], COLS_DOT_COLS, preferred_element_type=jnp.float32
+            )
+
+        add(1, terms(work.low_keys(cols), pl.ds(0, work.low_rows)))
+        for n, half, here, masked in work.tiles(owner):
+            part = terms(work.keys(n, half, cols), here)
+            for side in range(2):
+                if not masked:
+                    add(side, pick(half == side, part, 0))
+                elif half == side:
+                    add(side, part)
+    for half in range(2):
+        place = at_rows(works[0].query_slot(owner, half) * rows, rows)
+        grads = (jnp.transpose(totals[half]) * SCALE).astype(out_ref.dtype)
+        for h in range(GROUP):
+            out_ref[place, h * HEAD : (h + 1) * HEAD] = grads[h * rows : (h + 1) * rows, :]
 
 
 def sum_kernel(outer, *refs):
@@ -326,11 +325,11 @@
         out_ref[...] = total_ref[at_rows(target * rows, rows), :].astype(jnp.bfloat16)
 
 
-def place_kernel(own_ref, received_ref, *refs):
+def place_kernel(order, own_ref, received_ref, *refs):
     parts, (dq_out, key_out, value_out, dq_ref, sems) = refs[:-5], refs[-5:]
     kvh = len(parts)
     copies = []
-    for e, part_ref in enumerate(parts):
+    for e, part_ref in zip(order, parts):
         cols = at_rows(partner(lax.axis_index("kvh"), e, kvh) * HEAD, HEAD)
         copies.append(load(part_ref.at[:, pl.ds(0, HEAD)], key_out.at[:, cols], sems.at[2 * e]))
         copies.append(load(part_ref.at[:, pl.ds(HEAD, HEAD)], value_out.at[:, cols], sems.at[2 * e + 1]))
@@ -364,6 +363,11 @@
             return lax.ppermute(array, axis, [(n, target_of(n, by, size)) for n in range(size)])
         return lax.ppermute(array, axis, [(n, partner(n, -by, size)) for n in range(size)])
 
+    order = (0, *range(2, kvh), *range(1, min(kvh, 2)))
+
+    def exchange(parts):
+        return [shift(parts[e], "kvh", e) if e > 0 else parts[e] for e in order]
+
     part = shape((cache_rows, 2 * HEAD), low)
     block = shape((local_rows, 2 * HEAD), low)
     parts = call(
@@ -374,15 +378,7 @@
         out_specs=(vmem,) * kvh,
         scratch_shapes=[dma((2 * kvh,))],
     )(jnp.concatenate([keys, values], axis=0))
-    table = call(
-        functools.partial(table_kernel, outer),
-        "table",
-        out_shape=shape((2 * outer + 4, HEAD), jnp.int32),
-        in_specs=[smem, anywhere],
-        out_specs=vmem,
-        cost_estimate=beside,
-    )(slab_order, parts[0])
-    parts = [parts[0]] + [shift(parts[e], "kvh", e) for e in range(1, kvh)]
+    parts = exchange(parts)
     stack = shape((2, 2, columns, HEAD), low)
     own_qd, other_qd = call(
         stack_kernel,
@@ -392,16 +388,23 @@
         out_specs=(vmem, vmem),
     )(queries, d_out, shift(queries, "pair", 1), shift(d_out, "pair", 1))
     own_block = call(
-        join_kernel,
+        functools.partial(join_kernel, order),
         "join",
         out_shape=block,
-        in_specs=[anywhere] * (1 + kvh),
+        in_specs=[anywhere] * kvh,
         out_specs=vmem,
         scratch_shapes=[dma((kvh,))],
         cost_estimate=beside,
-    )(table, *parts)
+    )(*parts)
     blocks = [own_block] + [shift(own_block, "outer", d) for d in range(1, outer)]
 
+    table = call(
+        functools.partial(table_kernel, outer),
+        "table",
+        out_shape=shape((2 * outer + 4, HEAD), jnp.int32),
+        in_specs=[smem, anywhere],
+        out_specs=vmem,
+    )(slab_order, blocks[outer - 1])
     far = outer // 2 + 1
     groups = [[0, *range(far, outer)], list(range(1, far))]
     all_stats = shape((12, columns), full)
@@ -435,15 +438,19 @@
     )(table, own_qd, other_qd, *stats, theirs, *expon, *grad_probs)
     terms, score_grads = grads[:outer], grads[outer:]
     terms = [terms[0]] + [shift(terms[d], "outer", -d) for d in range(outer - 1, 0, -1)]
-    own_grads, other_grads = call(
-        functools.partial(query_kernel, outer, groups),
-        "query_terms",
-        out_shape=(shape(queries.shape, full), shape(queries.shape, low)),
-        in_specs=[vmem] * (1 + outer + count),
-        out_specs=(vmem, vmem),
-        cost_estimate=beside,
-    )(table, *blocks, *score_grads)
+    def query_terms(owner, kind, *after):
+        return call(
+            functools.partial(query_kernel, outer, groups, owner),
+            "query_terms",
+            out_shape=shape(queries.shape, kind),
+            in_specs=[vmem] * (1 + outer + count) + [anywhere] * len(after),
+            out_specs=vmem,
+            cost_estimate=beside,
+        )(table, *blocks, *score_grads, *after)
+
+    other_grads = query_terms(1, low)
     received_grads = shift(other_grads, "pair", 1)
+    own_grads = query_terms(0, full, other_grads)
     owned = call(
         functools.partial(sum_kernel, outer),
         "sum",
@@ -453,9 +460,9 @@
         scratch_shapes=[pltpu.VMEM(block.shape, full)],
         cost_estimate=beside,
     )(*terms)
-    owned = [owned[0]] + [shift(owned[e], "kvh", e) for e in range(1, kvh)]
+    owned = exchange(owned)
     return call(
-        place_kernel,
+        functools.partial(place_kernel, order),
         "place",
         out_shape=(shape(queries.shape, low), shape(keys.shape, low), shape(values.shape, low)),
         in_specs=[vmem, vmem] + [anywhere] * kvh,

time: 36.8 us -> 36.3 us (0.986)
  waiting for transfers between devices: 10.5 us -> 9.14 us
  Pallas kernels: 5.44 us -> 5.91 us
    ppermute x13, waiting for transfers between devices: 9.52 us -> 7.53 us  [shift(): lax.ppermute(array, axis, [(n, target_of(n, by, size)) for n in range(siz...]
    ppermute x3, waiting for transfers between devices: 0.93 us -> 1.61 us  [shift(): lax.ppermute(array, axis, [(n, partner(n, -by, size)) for n in range(size)])]
    pallas_call x3 -> x4, Pallas kernels: 1.84 us -> 2.31 us  [the longest x2 1.39 us: query_terms(): call(functools.partial(query_kernel, outer, groups, owner), 'query_terms'...]
  transfers between devices with their start and end apart: 16 -> 16, of which waited for: 7 -> 8; matrix products, arithmetic and copies ran while one was open for 0% -> 0% of each run, Pallas kernels for 7% -> 9%
where the time goes in v11:
time: 36.3 us; the launch traced here: 36.1 us
  starting transfers between devices  19.5 us (54%)
  waiting for transfers between devices  9.14 us (25%)
  Pallas kernels  5.91 us (16%)
  other arithmetic  0.82 us (2%)
  between operations  0.74 us (2%)
    ppermute x13, starting transfers between devices, shift(): lax.ppermute(array, axis, [(n, target_of(n, by, size)) for n in range(siz...  15.1 us
    ppermute x13, waiting for transfers between devices, shift(): lax.ppermute(array, axis, [(n, target_of(n, by, size)) for n in range(siz...  7.53 us
    ppermute x3, starting transfers between devices, shift(): lax.ppermute(array, axis, [(n, partner(n, -by, size)) for n in range(size)])  4.45 us
    pallas_call x2, Pallas kernels, per_device(): call(functools.partial(stats_kernel, members), 'stats', out_shape=(all_st...  1.69 us
    ppermute x3, waiting for transfers between devices, shift(): lax.ppermute(array, axis, [(n, partner(n, -by, size)) for n in range(size)])  1.61 us
    pallas_call x2, Pallas kernels, query_terms(): call(functools.partial(query_kernel, outer, groups, owner), 'query_terms'...  1.39 us
    pallas_call x1, Pallas kernels, per_device(): call(functools.partial(grads_kernel, outer, groups), 'grads', out_shape=(...  1.03 us
    concatenate x1, other arithmetic, per_device(): jnp.concatenate([keys, values], axis=0)  0.82 us
  transfers between devices with their start and end apart: 16, of which 8 were waited for; matrix products, arithmetic and copies ran while one was open for 0% of the time, Pallas kernels for 9%

profile of v11, /device:TPU:0, one launch (start us, length us, event | category | flops | bytes accessed | tf_op | source)
XLA Modules:
  0.0 36.1 jit_solution(12916745637684983383)
XLA Ops:
  0.6 0.0 copy-start
  0.6 0.8 %pad_maximum_fusion.cache_ref = bf16[64,512]{1,0:T(8,128)(2,1)S(1)} fusion(bf16[32,512]{1,0:T(8,128)(2,1)} %param.7, bf16[32,512]{1,0:T(8,128)(2,1)} %param.6), kind=kLoop, calls=%fused_computation | loop fusion | flops 131072 | bytes 131072 | tf_op jit(solution)/shard_map/concatenate | solution.py:380
  1.5 0.1 split.1
  1.6 3.0 %collective-permute-start = (bf16[32,256]{1,0:T(8,128)(2,1)S(1)}, bf16[32,256]{1,0:T(8,128)(2,1)S(1)}, u32[]{:S(2)}, u32[]{:S(2)}) collective-permute-start(bf16[32,256]{1,0:T(8,128)(2,1)S(1)} %get-tuple-element.26), channel_id=1, source_target_pairs={{0,2},{1,3},{2,0},{3,1},{4,6},{5,7},{6,4},{7,5},{8,10},{9,11},{10,... | collective-permute-start | bytes 49160 | tf_op jit(solution)/shard_map/ppermute | solution.py:363
  4.6 0.0 collective-permute-start.1
  4.6 0.2 collective-permute-start.2
  4.8 0.0 copy-done
  4.8 2.0 %collective-permute-start.6 = (bf16[128,640]{1,0:T(8,128)(2,1)S(1)}, bf16[128,640]{1,0:T(8,128)(2,1)S(1)}, u32[]{:S(2)}, u32[]{:S(2)}) collective-permute-start(bf16[128,640]{1,0:T(8,128)(2,1)S(1)} %copy-done), channel_id=1, source_target_pairs={{0,4},{4,0},{1,5},{5,1},{2,6},{6,2},{3,7},{7,3},{8,12},{12,8},{9,1... | collective-permute-start | bytes 491528 | tf_op jit(solution)/shard_map/ppermute | solution.py:363
  6.7 0.1 collective-permute-start.7
  6.8 0.0 collective-permute-done.refs_1_
  6.8 0.9 %collective-permute-done.1.refs_2_ = bf16[32,256]{1,0:T(8,128)(2,1)S(1)} collective-permute-done((bf16[32,256]{1,0:T(8,128)(2,1)S(1)}, bf16[32,256]{1,0:T(8,128)(2,1)S(1)}, u32[]{:S(2)}, u32[]{:S(2)}) %collective-permute-start.1) | collective-permute-done | bytes 16416 | tf_op jit(solution)/shard_map/ppermute | solution.py:363
  7.7 0.0 collective-permute-done.2.refs_3_
  7.7 0.0 copy-start.2
  7.7 0.0 copy-start.1
  7.7 0.1 join.1.refs_0_
  7.9 3.7 %collective-permute-start.3 = (bf16[128,256]{1,0:T(8,128)(2,1)S(1)}, bf16[128,256]{1,0:T(8,128)(2,1)S(1)}, u32[]{:S(2)}, u32[]{:S(2)}) collective-permute-start(bf16[128,256]{1,0:T(8,128)(2,1)S(1)} %join.1.refs_0_), channel_id=1, source_target_pairs={{0,24},{8,16},{16,8},{24,0},{1,25},{9,17},{17,9},{25,1},{2,26},{10... | collective-permute-start | bytes 196616 | tf_op jit(solution)/shard_map/ppermute | solution.py:363
  11.6 0.0 collective-permute-start.5
  11.6 0.8 %collective-permute-start.4 = (bf16[128,256]{1,0:T(8,128)(2,1)S(1)}, bf16[128,256]{1,0:T(8,128)(2,1)S(1)}, u32[]{:S(2)}, u32[]{:S(2)}) collective-permute-start(bf16[128,256]{1,0:T(8,128)(2,1)S(1)} %join.1.refs_0_), channel_id=1, source_target_pairs={{0,8},{8,0},{16,24},{24,16},{1,9},{9,1},{17,25},{25,17},{2,10},{10... | collective-permute-start | bytes 196616 | tf_op jit(solution)/shard_map/ppermute | solution.py:363
  12.3 2.5 %collective-permute-done.3.after_ref.refs_1_.refs_3_ = bf16[128,256]{1,0:T(8,128)(2,1)S(1)} collective-permute-done((bf16[128,256]{1,0:T(8,128)(2,1)S(1)}, bf16[128,256]{1,0:T(8,128)(2,1)S(1)}, u32[]{:S(2)}, u32[]{:S(2)}) %collective-permute-start.3) | collective-permute-done | bytes 65568 | tf_op jit(solution)/shard_map/ppermute | solution.py:363
  14.8 0.0 copy-done.2
  14.8 0.6 %table.1.table_ref = s32[12,128]{1,0:T(8,128)S(1)} custom-call(s32[16]{0:T(128)S(1)} %copy-done.2, bf16[128,256]{1,0:T(8,128)(2,1)S(1)} %collective-permute-done.3.after_ref.refs_1_.refs_3_), custom_call_target="tpu_custom_call" | custom-call | tf_op jit(solution)/shard_map/table/pallas_call | solution.py:401
  15.4 0.0 collective-permute-done.6.refs_2_
  15.4 0.0 collective-permute-done.7.refs_3_
  15.4 0.0 copy-done.1
  15.4 0.1 stack.1
  15.6 0.9 %stats.2 = (f32[12,320]{1,0:T(8,128)S(1)}, f32[2,320,320]{2,1,0:T(8,128)S(1)}, f32[2,320,320]{2,1,0:T(8,128)S(1)}) custom-call(s32[12,128]{1,0:T(8,128)S(1)} %table.1.table_ref, bf16[2,2,320,128]{3,2,1,0:T(8,128)(2,1)S(1)} %get-tuple-element.29.own_ref, bf16[2,2,320,128]{3,2,1,0:T(8,128)(2,1)S(1)} %get-tuple-element.30.other_ref, ...), custom_call_target="tpu_custom_call" | custom-call | flops 20000000000 | bytes 1000000 | tf_op jit(solution)/shard_map/stats/pallas_call | solution.py:415
  16.5 0.5 %collective-permute-done.5.refs_1_.refs_2_ = bf16[128,256]{1,0:T(8,128)(2,1)S(1)} collective-permute-done((bf16[128,256]{1,0:T(8,128)(2,1)S(1)}, bf16[128,256]{1,0:T(8,128)(2,1)S(1)}, u32[]{:S(2)}, u32[]{:S(2)}) %collective-permute-start.5) | collective-permute-done | bytes 65568 | tf_op jit(solution)/shard_map/ppermute | solution.py:363
  16.9 0.1 collective-permute-done.4.refs_0_.refs_1_
  17.0 0.8 %stats.3 = (f32[12,320]{1,0:T(8,128)S(1)}, f32[2,320,320]{2,1,0:T(8,128)S(1)}, f32[2,320,320]{2,1,0:T(8,128)S(1)}) custom-call(s32[12,128]{1,0:T(8,128)S(1)} %table.1.table_ref, bf16[2,2,320,128]{3,2,1,0:T(8,128)(2,1)S(1)} %get-tuple-element.29.own_ref, bf16[2,2,320,128]{3,2,1,0:T(8,128)(2,1)S(1)} %get-tuple-element.30.other_ref, ...), custom_call_target="tpu_custom_call" | custom-call | tf_op jit(solution)/shard_map/stats/pallas_call | solution.py:415
  17.8 1.6 %collective-permute-start.8 = (f32[12,320]{1,0:T(8,128)S(1)}, f32[12,320]{1,0:T(8,128)S(1)}, u32[]{:S(2)}, u32[]{:S(2)}) collective-permute-start(f32[12,320]{1,0:T(8,128)S(1)} %merge.1), channel_id=1, source_target_pairs={{0,4},{4,0},{1,5},{5,1},{2,6},{6,2},{3,7},{7,3},{8,12},{12,8},{9,1... | collective-permute-start | bytes 46088 | tf_op jit(solution)/shard_map/ppermute | solution.py:363
  19.4 2.3 %collective-permute-done.8.refs_2_ = f32[12,320]{1,0:T(8,128)S(1)} collective-permute-done((f32[12,320]{1,0:T(8,128)S(1)}, f32[12,320]{1,0:T(8,128)S(1)}, u32[]{:S(2)}, u32[]{:S(2)}) %collective-permute-start.8) | collective-permute-done | bytes 15392 | tf_op jit(solution)/shard_map/ppermute | solution.py:363
  21.7 1.0 %grads.1 = (f32[128,256]{1,0:T(8,128)S(1)}, bf16[128,256]{1,0:T(8,128)(2,1)S(1)}, bf16[128,256]{1,0:T(8,128)(2,1)S(1)}, bf16[128,256]{1,0:T(8,128)(2,1)S(1)}, bf...) custom-call(s32[12,128]{1,0:T(8,128)S(1)} %table.1.table_ref, ...), custom_call_target="tpu_custom_call" | custom-call | tf_op jit(solution)/shard_map/grads/pallas_call | solution.py:430
  22.8 3.2 %collective-permute-start.10 = (bf16[128,256]{1,0:T(8,128)(2,1)S(1)}, bf16[128,256]{1,0:T(8,128)(2,1)S(1)}, u32[]{:S(2)}, u32[]{:S(2)}) collective-permute-start(bf16[128,256]{1,0:T(8,128)(2,1)S(1)} %get-tuple-element.40), channel_id=1, source_target_pairs={{0,24},{8,16},{16,8},{24,0},{1,25},{9,17},{17,9},{25,1},{2,26},{10... | collective-permute-start | bytes 196616 | tf_op jit(solution)/shard_map/ppermute | solution.py:364
  26.0 0.0 collective-permute-start.11
  26.0 1.3 %collective-permute-start.12 = (bf16[128,256]{1,0:T(8,128)(2,1)S(1)}, bf16[128,256]{1,0:T(8,128)(2,1)S(1)}, u32[]{:S(2)}, u32[]{:S(2)}) collective-permute-start(bf16[128,256]{1,0:T(8,128)(2,1)S(1)} %get-tuple-element.42), channel_id=1, source_target_pairs={{0,8},{8,0},{16,24},{24,16},{1,9},{9,1},{17,25},{25,17},{2,10},{10... | collective-permute-start | bytes 196616 | tf_op jit(solution)/shard_map/ppermute | solution.py:364
  27.2 0.7 %query_terms.2.refs_6_ = bf16[128,640]{1,0:T(8,128)(2,1)S(1)} custom-call(s32[12,128]{1,0:T(8,128)S(1)} %table.1.table_ref, bf16[128,256]{1,0:T(8,128)(2,1)S(1)} %join.1.refs_0_, bf16[128,256]{1,0:T(8,128)(2,1)S(1)} %collective-permute-done.4.refs_0_.refs_1_, bf16[128,256]{1,0:T(8,128)(2,1)S(1)} %collective-permute-done.5.refs_1_.refs_2_, ...), custom_call_target="tpu_custom_call" | custom-call | flops 20000000000 | bytes 1000000 | tf_op jit(solution)/shard_map/query_terms/pallas_call | solution.py:442
  27.9 1.6 %collective-permute-start.9 = (bf16[128,640]{1,0:T(8,128)(2,1)S(1)}, bf16[128,640]{1,0:T(8,128)(2,1)S(1)}, u32[]{:S(2)}, u32[]{:S(2)}) collective-permute-start(bf16[128,640]{1,0:T(8,128)(2,1)S(1)} %query_terms.2.refs_6_), channel_id=1, source_target_pairs={{0,4},{4,0},{1,5},{5,1},{2,6},{6,2},{3,7},{7,3},{8,12},{12,8},{9,1... | collective-permute-start | bytes 491528 | tf_op jit(solution)/shard_map/ppermute | solution.py:363
  29.5 0.0 collective-permute-done.10.refs_1_
  29.5 1.6 %collective-permute-done.11.refs_2_ = bf16[128,256]{1,0:T(8,128)(2,1)S(1)} collective-permute-done((bf16[128,256]{1,0:T(8,128)(2,1)S(1)}, bf16[128,256]{1,0:T(8,128)(2,1)S(1)}, u32[]{:S(2)}, u32[]{:S(2)}) %collective-permute-start.11) | collective-permute-done | bytes 65568 | tf_op jit(solution)/shard_map/ppermute | solution.py:364
  31.1 0.0 collective-permute-done.12.refs_3_
  31.2 1.0 %collective-permute-start.13 = (bf16[32,256]{1,0:T(8,128)(2,1)S(1)}, bf16[32,256]{1,0:T(8,128)(2,1)S(1)}, u32[]{:S(2)}, u32[]{:S(2)}) collective-permute-start(bf16[32,256]{1,0:T(8,128)(2,1)S(1)} %get-tuple-element.44), channel_id=1, source_target_pairs={{0,2},{1,3},{2,0},{3,1},{4,6},{5,7},{6,4},{7,5},{8,10},{9,11},{10,... | collective-permute-start | bytes 49160 | tf_op jit(solution)/shard_map/ppermute | solution.py:363
  32.2 0.0 collective-permute-start.14
  32.2 1.2 %collective-permute-start.15 = (bf16[32,256]{1,0:T(8,128)(2,1)S(1)}, bf16[32,256]{1,0:T(8,128)(2,1)S(1)}, u32[]{:S(2)}, u32[]{:S(2)}) collective-permute-start(bf16[32,256]{1,0:T(8,128)(2,1)S(1)} %get-tuple-element.46), channel_id=1, source_target_pairs={{0,1},{1,0},{2,3},{3,2},{4,5},{5,4},{6,7},{7,6},{8,9},{9,8},{10,11... | collective-permute-start | bytes 49160 | tf_op jit(solution)/shard_map/ppermute | solution.py:363
  33.4 0.7 %query_terms.3.own_ref = f32[128,640]{1,0:T(8,128)S(1)} custom-call(s32[12,128]{1,0:T(8,128)S(1)} %table.1.table_ref, bf16[128,256]{1,0:T(8,128)(2,1)S(1)} %join.1.refs_0_, bf16[128,256]{1,0:T(8,128)(2,1)S(1)} %collective-permute-done.4.refs_0_.refs_1_, bf16[128,256]{1,0:T(8,128)(2,1)S(1)} %collective-permute-done.5.refs_1_.refs_2_, ...), custom_call_target="tpu_custom_call" | custom-call | flops 20000000000 | bytes 1000000 | tf_op jit(solution)/shard_map/query_terms/pallas_call | solution.py:442
  34.1 0.9 %collective-permute-done.13.refs_1_ = bf16[32,256]{1,0:T(8,128)(2,1)S(1)} collective-permute-done((bf16[32,256]{1,0:T(8,128)(2,1)S(1)}, bf16[32,256]{1,0:T(8,128)(2,1)S(1)}, u32[]{:S(2)}, u32[]{:S(2)}) %collective-permute-start.13) | collective-permute-done | bytes 16416 | tf_op jit(solution)/shard_map/ppermute | solution.py:363
  35.0 0.4 collective-permute-done.14.refs_2_
  35.3 0.0 collective-permute-done.15.refs_3_
  35.3 0.0 collective-permute-done.9.received_ref
  35.3 0.8 %place.1 = (bf16[128,640]{1,0:T(8,128)(2,1)}, bf16[32,512]{1,0:T(8,128)(2,1)}, bf16[32,512]{1,0:T(8,128)(2,1)}) custom-call(f32[128,640]{1,0:T(8,128)S(1)} %query_terms.3.own_ref, bf16[128,640]{1,0:T(8,128)(2,1)S(1)} %collective-permute-done.9.received_ref, bf16[32,256]{1,0:T(8,128)(2,1)S(1)} %get-tuple-element.43.refs_0_, ...), custom_call_target="tpu_custom_call" | custom-call | tf_op jit(solution)/shard_map/place/pallas_call | solution.py:464
  (2 shorter events, 0.1 us)
Async XLA Ops:
  0.6 4.1 %copy-start = (bf16[128,640]{1,0:T(8,128)(2,1)S(1)}, bf16[128,640]{1,0:T(8,128)(2,1)}, u32[]{:S(2)}) copy-start(bf16[128,640]{1,0:T(8,128)(2,1)} %refs_0_.1) | copy-start | bytes 491524
  1.6 5.2 %collective-permute-start = (bf16[32,256]{1,0:T(8,128)(2,1)S(1)}, bf16[32,256]{1,0:T(8,128)(2,1)S(1)}, u32[]{:S(2)}, u32[]{:S(2)}) collective-permute-start(bf16[32,256]{1,0:T(8,128)(2,1)S(1)} %get-tuple-element.26), channel_id=1, source_target_pairs={{0,2},{1,3},{2,0},{3,1},{4,6},{5,7},{6,4},{7,5},{8,10},{9,11},{10,... | collective-permute-start | bytes 49160 | tf_op jit(solution)/shard_map/ppermute | solution.py:363
  4.6 3.2 %collective-permute-start.1 = (bf16[32,256]{1,0:T(8,128)(2,1)S(1)}, bf16[32,256]{1,0:T(8,128)(2,1)S(1)}, u32[]{:S(2)}, u32[]{:S(2)}) collective-permute-start(bf16[32,256]{1,0:T(8,128)(2,1)S(1)} %get-tuple-element.27), channel_id=1, source_target_pairs={{0,3},{1,2},{2,1},{3,0},{4,7},{5,6},{6,5},{7,4},{8,11},{9,10},{10,... | collective-permute-start | bytes 49160 | tf_op jit(solution)/shard_map/ppermute | solution.py:363
  4.6 3.2 %collective-permute-start.2 = (bf16[32,256]{1,0:T(8,128)(2,1)S(1)}, bf16[32,256]{1,0:T(8,128)(2,1)S(1)}, u32[]{:S(2)}, u32[]{:S(2)}) collective-permute-start(bf16[32,256]{1,0:T(8,128)(2,1)S(1)} %get-tuple-element.28), channel_id=1, source_target_pairs={{0,1},{1,0},{2,3},{3,2},{4,5},{5,4},{6,7},{7,6},{8,9},{9,8},{10,11... | collective-permute-start | bytes 49160 | tf_op jit(solution)/shard_map/ppermute | solution.py:363
  4.8 10.6 %collective-permute-start.6 = (bf16[128,640]{1,0:T(8,128)(2,1)S(1)}, bf16[128,640]{1,0:T(8,128)(2,1)S(1)}, u32[]{:S(2)}, u32[]{:S(2)}) collective-permute-start(bf16[128,640]{1,0:T(8,128)(2,1)S(1)} %copy-done), channel_id=1, source_target_pairs={{0,4},{4,0},{1,5},{5,1},{2,6},{6,2},{3,7},{7,3},{8,12},{12,8},{9,1... | collective-permute-start | bytes 491528 | tf_op jit(solution)/shard_map/ppermute | solution.py:363
  6.7 8.7 %collective-permute-start.7 = (bf16[128,640]{1,0:T(8,128)(2,1)}, bf16[128,640]{1,0:T(8,128)(2,1)S(1)}, u32[]{:S(2)}, u32[]{:S(2)}) collective-permute-start(bf16[128,640]{1,0:T(8,128)(2,1)} %refs_1_.1), channel_id=1, source_target_pairs={{0,4},{4,0},{1,5},{5,1},{2,6},{6,2},{3,7},{7,3},{8,12},{12,8},{9,1... | collective-permute-start | bytes 491528 | tf_op jit(solution)/shard_map/ppermute | solution.py:363
  7.7 7.1 %copy-start.2 = (s32[16]{0:T(128)S(1)}, s32[16]{0:T(128)}, u32[]{:S(2)}) copy-start(s32[16]{0:T(128)} %order_ref.1) | copy-start | bytes 196
  7.7 7.7 %copy-start.1 = (bf16[128,640]{1,0:T(8,128)(2,1)S(1)}, bf16[128,640]{1,0:T(8,128)(2,1)}, u32[]{:S(2)}) copy-start(bf16[128,640]{1,0:T(8,128)(2,1)} %refs_1_.1) | copy-start | bytes 491524
  7.9 6.9 %collective-permute-start.3 = (bf16[128,256]{1,0:T(8,128)(2,1)S(1)}, bf16[128,256]{1,0:T(8,128)(2,1)S(1)}, u32[]{:S(2)}, u32[]{:S(2)}) collective-permute-start(bf16[128,256]{1,0:T(8,128)(2,1)S(1)} %join.1.refs_0_), channel_id=1, source_target_pairs={{0,24},{8,16},{16,8},{24,0},{1,25},{9,17},{17,9},{25,1},{2,26},{10... | collective-permute-start | bytes 196616 | tf_op jit(solution)/shard_map/ppermute | solution.py:363
  11.6 5.4 %collective-permute-start.5 = (bf16[128,256]{1,0:T(8,128)(2,1)S(1)}, bf16[128,256]{1,0:T(8,128)(2,1)S(1)}, u32[]{:S(2)}, u32[]{:S(2)}) collective-permute-start(bf16[128,256]{1,0:T(8,128)(2,1)S(1)} %join.1.refs_0_), channel_id=1, source_target_pairs={{0,16},{8,24},{16,0},{24,8},{1,17},{9,25},{17,1},{25,9},{2,18},{10... | collective-permute-start | bytes 196616 | tf_op jit(solution)/shard_map/ppermute | solution.py:363
  11.6 5.4 %collective-permute-start.4 = (bf16[128,256]{1,0:T(8,128)(2,1)S(1)}, bf16[128,256]{1,0:T(8,128)(2,1)S(1)}, u32[]{:S(2)}, u32[]{:S(2)}) collective-permute-start(bf16[128,256]{1,0:T(8,128)(2,1)S(1)} %join.1.refs_0_), channel_id=1, source_target_pairs={{0,8},{8,0},{16,24},{24,16},{1,9},{9,1},{17,25},{25,17},{2,10},{10... | collective-permute-start | bytes 196616 | tf_op jit(solution)/shard_map/ppermute | solution.py:363
  17.8 3.9 %collective-permute-start.8 = (f32[12,320]{1,0:T(8,128)S(1)}, f32[12,320]{1,0:T(8,128)S(1)}, u32[]{:S(2)}, u32[]{:S(2)}) collective-permute-start(f32[12,320]{1,0:T(8,128)S(1)} %merge.1), channel_id=1, source_target_pairs={{0,4},{4,0},{1,5},{5,1},{2,6},{6,2},{3,7},{7,3},{8,12},{12,8},{9,1... | collective-permute-start | bytes 46088 | tf_op jit(solution)/shard_map/ppermute | solution.py:363
  22.8 6.7 %collective-permute-start.10 = (bf16[128,256]{1,0:T(8,128)(2,1)S(1)}, bf16[128,256]{1,0:T(8,128)(2,1)S(1)}, u32[]{:S(2)}, u32[]{:S(2)}) collective-permute-start(bf16[128,256]{1,0:T(8,128)(2,1)S(1)} %get-tuple-element.40), channel_id=1, source_target_pairs={{0,24},{8,16},{16,8},{24,0},{1,25},{9,17},{17,9},{25,1},{2,26},{10... | collective-permute-start | bytes 196616 | tf_op jit(solution)/shard_map/ppermute | solution.py:364
  26.0 5.2 %collective-permute-start.11 = (bf16[128,256]{1,0:T(8,128)(2,1)S(1)}, bf16[128,256]{1,0:T(8,128)(2,1)S(1)}, u32[]{:S(2)}, u32[]{:S(2)}) collective-permute-start(bf16[128,256]{1,0:T(8,128)(2,1)S(1)} %get-tuple-element.41), channel_id=1, source_target_pairs={{0,16},{8,24},{16,0},{24,8},{1,17},{9,25},{17,1},{25,9},{2,18},{10... | collective-permute-start | bytes 196616 | tf_op jit(solution)/shard_map/ppermute | solution.py:364
  26.0 5.2 %collective-permute-start.12 = (bf16[128,256]{1,0:T(8,128)(2,1)S(1)}, bf16[128,256]{1,0:T(8,128)(2,1)S(1)}, u32[]{:S(2)}, u32[]{:S(2)}) collective-permute-start(bf16[128,256]{1,0:T(8,128)(2,1)S(1)} %get-tuple-element.42), channel_id=1, source_target_pairs={{0,8},{8,0},{16,24},{24,16},{1,9},{9,1},{17,25},{25,17},{2,10},{10... | collective-permute-start | bytes 196616 | tf_op jit(solution)/shard_map/ppermute | solution.py:364
  27.9 7.4 %collective-permute-start.9 = (bf16[128,640]{1,0:T(8,128)(2,1)S(1)}, bf16[128,640]{1,0:T(8,128)(2,1)S(1)}, u32[]{:S(2)}, u32[]{:S(2)}) collective-permute-start(bf16[128,640]{1,0:T(8,128)(2,1)S(1)} %query_terms.2.refs_6_), channel_id=1, source_target_pairs={{0,4},{4,0},{1,5},{5,1},{2,6},{6,2},{3,7},{7,3},{8,12},{12,8},{9,1... | collective-permute-start | bytes 491528 | tf_op jit(solution)/shard_map/ppermute | solution.py:363
  31.2 3.8 %collective-permute-start.13 = (bf16[32,256]{1,0:T(8,128)(2,1)S(1)}, bf16[32,256]{1,0:T(8,128)(2,1)S(1)}, u32[]{:S(2)}, u32[]{:S(2)}) collective-permute-start(bf16[32,256]{1,0:T(8,128)(2,1)S(1)} %get-tuple-element.44), channel_id=1, source_target_pairs={{0,2},{1,3},{2,0},{3,1},{4,6},{5,7},{6,4},{7,5},{8,10},{9,11},{10,... | collective-permute-start | bytes 49160 | tf_op jit(solution)/shard_map/ppermute | solution.py:363
  32.2 3.2 %collective-permute-start.14 = (bf16[32,256]{1,0:T(8,128)(2,1)S(1)}, bf16[32,256]{1,0:T(8,128)(2,1)S(1)}, u32[]{:S(2)}, u32[]{:S(2)}) collective-permute-start(bf16[32,256]{1,0:T(8,128)(2,1)S(1)} %get-tuple-element.45), channel_id=1, source_target_pairs={{0,3},{1,2},{2,1},{3,0},{4,7},{5,6},{6,5},{7,4},{8,11},{9,10},{10,... | collective-permute-start | bytes 49160 | tf_op jit(solution)/shard_map/ppermute | solution.py:363
  32.2 3.2 %collective-permute-start.15 = (bf16[32,256]{1,0:T(8,128)(2,1)S(1)}, bf16[32,256]{1,0:T(8,128)(2,1)S(1)}, u32[]{:S(2)}, u32[]{:S(2)}) collective-permute-start(bf16[32,256]{1,0:T(8,128)(2,1)S(1)} %get-tuple-element.46), channel_id=1, source_target_pairs={{0,1},{1,0},{2,3},{3,2},{4,5},{5,4},{6,7},{7,6},{8,9},{9,8},{10,11... | collective-permute-start | bytes 49160 | tf_op jit(solution)/shard_map/ppermute | solution.py:363

commit v12 on v11

--- a/solution.py
+++ b/solution.py
@@ -380,13 +380,14 @@
     )(jnp.concatenate([keys, values], axis=0))
     parts = exchange(parts)
     stack = shape((2, 2, columns, HEAD), low)
+    queries2 = shift(queries, "pair", 1)
     own_qd, other_qd = call(
         stack_kernel,
         "stack",
         out_shape=(stack, stack),
         in_specs=[vmem] * 4,
         out_specs=(vmem, vmem),
-    )(queries, d_out, shift(queries, "pair", 1), shift(d_out, "pair", 1))
+    )(queries, d_out, queries2, shift(d_out, "pair", 1))
     own_block = call(
         functools.partial(join_kernel, order),
         "join",
@@ -404,9 +405,8 @@
         out_shape=shape((2 * outer + 4, HEAD), jnp.int32),
         in_specs=[smem, anywhere],
         out_specs=vmem,
-    )(slab_order, blocks[outer - 1])
-    far = outer // 2 + 1
-    groups = [[0, *range(far, outer)], list(range(1, far))]
+    )(slab_order, queries2)
+    groups = [[0, *range(outer - 1, 0, -1)]]
     all_stats = shape((12, columns), full)
     results = []
     for n, members in enumerate(groups):
@@ -422,9 +422,11 @@
             )(table, own_qd, other_qd, *[blocks[d] for d in members], *[done[0] for done in results[-1:]])
         )
     stats, expon, grad_probs = zip(*results)
-    mine = call(
-        merge_kernel, "merge", out_shape=all_stats, in_specs=[vmem] * len(stats), out_specs=vmem
-    )(*stats)
+    mine = stats[0]
+    if len(stats) > 1:
+        mine = call(
+            merge_kernel, "merge", out_shape=all_stats, in_specs=[vmem] * len(stats), out_specs=vmem
+        )(*stats)
     theirs = shift(mine, "pair", 1)
     count = len(groups)
     grads = call(

time: 36.3 us -> 36.7 us (1.011)
  waiting for transfers between devices: 9.14 us -> 9.96 us
    ppermute x13, waiting for transfers between devices: 7.53 us -> 8.86 us  [shift(): lax.ppermute(array, axis, [(n, target_of(n, by, size)) for n in range(siz...]
    ppermute x3, waiting for transfers between devices: 1.61 us -> 1.1 us  [shift(): lax.ppermute(array, axis, [(n, partner(n, -by, size)) for n in range(size)])]
    pallas_call x2 -> x1, Pallas kernels: 1.69 us -> 1.42 us  [per_device(): call(functools.partial(stats_kernel, members), 'stats', out_shape=(all_st...]
  transfers between devices with their start and end apart: 16 -> 16, of which waited for: 8 -> 8; matrix products, arithmetic and copies ran while one was open for 0% -> 0% of each run, Pallas kernels for 9% -> 6%
where the time goes in v12:
time: 36.7 us; the launch traced here: 36.5 us
  starting transfers between devices  19.5 us (53%)
  waiting for transfers between devices  9.96 us (27%)
  Pallas kernels  5.56 us (15%)
  other arithmetic  0.78 us (2%)
  between operations  0.71 us (2%)
    ppermute x13, starting transfers between devices, shift(): lax.ppermute(array, axis, [(n, target_of(n, by, size)) for n in range(siz...  15 us
    ppermute x13, waiting for transfers between devices, shift(): lax.ppermute(array, axis, [(n, target_of(n, by, size)) for n in range(siz...  8.86 us
    ppermute x3, starting transfers between devices, shift(): lax.ppermute(array, axis, [(n, partner(n, -by, size)) for n in range(size)])  4.45 us
    pallas_call x1, Pallas kernels, per_device(): call(functools.partial(stats_kernel, members), 'stats', out_shape=(all_st...  1.42 us
    pallas_call x2, Pallas kernels, query_terms(): call(functools.partial(query_kernel, outer, groups, owner), 'query_terms'...  1.39 us
    ppermute x3, waiting for transfers between devices, shift(): lax.ppermute(array, axis, [(n, partner(n, -by, size)) for n in range(size)])  1.1 us
    pallas_call x1, Pallas kernels, per_device(): call(functools.partial(grads_kernel, outer, groups), 'grads', out_shape=(...  0.99 us
    pallas_call x1, Pallas kernels, per_device(): call(functools.partial(place_kernel, order), 'place', out_shape=(shape(qu...  0.79 us
  transfers between devices with their start and end apart: 16, of which 8 were waited for; matrix products, arithmetic and copies ran while one was open for 0% of the time, Pallas kernels for 6%

profile of v12, /device:TPU:0, one launch (start us, length us, event | category | flops | bytes accessed | tf_op | source)
XLA Modules:
  0.0 36.5 jit_solution(7263949071835151547)
XLA Ops:
  0.6 0.8 %pad_maximum_fusion.cache_ref = bf16[64,512]{1,0:T(8,128)(2,1)S(1)} fusion(bf16[32,512]{1,0:T(8,128)(2,1)} %param.7, bf16[32,512]{1,0:T(8,128)(2,1)} %param.6), kind=kLoop, calls=%fused_computation | loop fusion | flops 131072 | bytes 131072 | tf_op jit(solution)/shard_map/concatenate | solution.py:380
  1.4 0.1 split.1
  1.5 3.0 %collective-permute-start.1 = (bf16[32,256]{1,0:T(8,128)(2,1)S(1)}, bf16[32,256]{1,0:T(8,128)(2,1)S(1)}, u32[]{:S(2)}, u32[]{:S(2)}) collective-permute-start(bf16[32,256]{1,0:T(8,128)(2,1)S(1)} %get-tuple-element.22), channel_id=1, source_target_pairs={{0,2},{1,3},{2,0},{3,1},{4,6},{5,7},{6,4},{7,5},{8,10},{9,11},{10,... | collective-permute-start | bytes 49160 | tf_op jit(solution)/shard_map/ppermute | solution.py:363
  4.5 0.0 collective-permute-start.2
  4.5 0.2 collective-permute-start.3
  4.7 2.0 %collective-permute-start = (bf16[128,640]{1,0:T(8,128)(2,1)}, bf16[128,640]{1,0:T(8,128)(2,1)S(1)}, u32[]{:S(2)}, u32[]{:S(2)}) collective-permute-start(bf16[128,640]{1,0:T(8,128)(2,1)} %refs_0_.1), channel_id=1, source_target_pairs={{0,4},{4,0},{1,5},{5,1},{2,6},{6,2},{3,7},{7,3},{8,12},{12,8},{9,1... | collective-permute-start | bytes 491528 | tf_op jit(solution)/shard_map/ppermute | solution.py:363
  6.7 0.1 collective-permute-start.7
  6.8 0.0 collective-permute-done.1.refs_1_
  6.8 0.9 %collective-permute-done.2.refs_2_ = bf16[32,256]{1,0:T(8,128)(2,1)S(1)} collective-permute-done((bf16[32,256]{1,0:T(8,128)(2,1)S(1)}, bf16[32,256]{1,0:T(8,128)(2,1)S(1)}, u32[]{:S(2)}, u32[]{:S(2)}) %collective-permute-start.2) | collective-permute-done | bytes 16416 | tf_op jit(solution)/shard_map/ppermute | solution.py:363
  7.7 0.0 collective-permute-done.3.refs_3_
  7.7 0.0 copy-start.2
  7.7 0.0 copy-start
  7.7 0.0 copy-start.1
  7.7 0.1 join.1.refs_0_
  7.9 3.7 %collective-permute-start.6 = (bf16[128,256]{1,0:T(8,128)(2,1)S(1)}, bf16[128,256]{1,0:T(8,128)(2,1)S(1)}, u32[]{:S(2)}, u32[]{:S(2)}) collective-permute-start(bf16[128,256]{1,0:T(8,128)(2,1)S(1)} %join.1.refs_0_), channel_id=1, source_target_pairs={{0,24},{8,16},{16,8},{24,0},{1,25},{9,17},{17,9},{25,1},{2,26},{10... | collective-permute-start | bytes 196616 | tf_op jit(solution)/shard_map/ppermute | solution.py:363
  11.5 0.0 collective-permute-start.5
  11.5 0.8 %collective-permute-start.4 = (bf16[128,256]{1,0:T(8,128)(2,1)S(1)}, bf16[128,256]{1,0:T(8,128)(2,1)S(1)}, u32[]{:S(2)}, u32[]{:S(2)}) collective-permute-start(bf16[128,256]{1,0:T(8,128)(2,1)S(1)} %join.1.refs_0_), channel_id=1, source_target_pairs={{0,8},{8,0},{16,24},{24,16},{1,9},{9,1},{17,25},{25,17},{2,10},{10... | collective-permute-start | bytes 196616 | tf_op jit(solution)/shard_map/ppermute | solution.py:363
  12.3 0.0 collective-permute-done.after_ref.refs_2_
  12.3 0.0 copy-done.2
  12.3 0.6 %table.1.table_ref = s32[12,128]{1,0:T(8,128)S(1)} custom-call(s32[16]{0:T(128)S(1)} %copy-done.2, bf16[128,640]{1,0:T(8,128)(2,1)S(1)} %collective-permute-done.after_ref.refs_2_), custom_call_target="tpu_custom_call" | custom-call | tf_op jit(solution)/shard_map/table/pallas_call | solution.py:402
  12.9 2.0 %collective-permute-done.7.refs_3_ = bf16[128,640]{1,0:T(8,128)(2,1)S(1)} collective-permute-done((bf16[128,640]{1,0:T(8,128)(2,1)}, bf16[128,640]{1,0:T(8,128)(2,1)S(1)}, u32[]{:S(2)}, u32[]{:S(2)}) %collective-permute-start.7) | collective-permute-done | bytes 163872 | tf_op jit(solution)/shard_map/ppermute | solution.py:363
  14.9 0.0 copy-done
  14.9 0.0 copy-done.1
  14.9 0.1 stack.1
  15.0 0.0 collective-permute-done.6.refs_1_.refs_3_
  15.0 1.9 %collective-permute-done.5.refs_2_ = bf16[128,256]{1,0:T(8,128)(2,1)S(1)} collective-permute-done((bf16[128,256]{1,0:T(8,128)(2,1)S(1)}, bf16[128,256]{1,0:T(8,128)(2,1)S(1)}, u32[]{:S(2)}, u32[]{:S(2)}) %collective-permute-start.5) | collective-permute-done | bytes 65568 | tf_op jit(solution)/shard_map/ppermute | solution.py:363
  16.9 0.1 collective-permute-done.4.refs_3_.refs_1_
  17.0 1.4 %stats.1 = (f32[12,320]{1,0:T(8,128)S(1)}, f32[2,576,320]{2,1,0:T(8,128)S(1)}, f32[2,576,320]{2,1,0:T(8,128)S(1)}) custom-call(s32[12,128]{1,0:T(8,128)S(1)} %table.1.table_ref, bf16[2,2,320,128]{3,2,1,0:T(8,128)(2,1)S(1)} %get-tuple-element.25.own_ref, bf16[2,2,320,128]{3,2,1,0:T(8,128)(2,1)S(1)} %get-tuple-element.26.other_ref, ...), custom_call_target="tpu_custom_call" | custom-call | tf_op jit(solution)/shard_map/stats/pallas_call | solution.py:415
  18.4 1.6 %collective-permute-start.8 = (f32[12,320]{1,0:T(8,128)S(1)}, f32[12,320]{1,0:T(8,128)S(1)}, u32[]{:S(2)}, u32[]{:S(2)}) collective-permute-start(f32[12,320]{1,0:T(8,128)S(1)} %get-tuple-element.27.refs_0_), channel_id=1, source_target_pairs={{0,4},{4,0},{1,5},{5,1},{2,6},{6,2},{3,7},{7,3},{8,12},{12,8},{9,1... | collective-permute-start | bytes 46088 | tf_op jit(solution)/shard_map/ppermute | solution.py:363
  20.0 2.3 %collective-permute-done.8.refs_1_ = f32[12,320]{1,0:T(8,128)S(1)} collective-permute-done((f32[12,320]{1,0:T(8,128)S(1)}, f32[12,320]{1,0:T(8,128)S(1)}, u32[]{:S(2)}, u32[]{:S(2)}) %collective-permute-start.8) | collective-permute-done | bytes 15392 | tf_op jit(solution)/shard_map/ppermute | solution.py:363
  22.3 1.0 %grads.1 = (f32[128,256]{1,0:T(8,128)S(1)}, bf16[128,256]{1,0:T(8,128)(2,1)S(1)}, bf16[128,256]{1,0:T(8,128)(2,1)S(1)}, bf16[128,256]{1,0:T(8,128)(2,1)S(1)}, bf16[2,576,320]{2,1,0:T(8,128)(2,1)S(1)}) custom-call(s32[12,128]{1,0:T(8,128)S(1)} %table.1.table_ref, bf16[2,2,320,128]{3,2,1,0:T(8,128)(2,1)S(1)} %get-tuple-element.25.own_ref, ...), custom_call_target="tpu_custom_call" | custom-call | tf_op jit(solution)/shard_map/grads/pallas_call | solution.py:432
  23.3 2.7 %collective-permute-start.10 = (bf16[128,256]{1,0:T(8,128)(2,1)S(1)}, bf16[128,256]{1,0:T(8,128)(2,1)S(1)}, u32[]{:S(2)}, u32[]{:S(2)}) collective-permute-start(bf16[128,256]{1,0:T(8,128)(2,1)S(1)} %get-tuple-element.32), channel_id=1, source_target_pairs={{0,24},{8,16},{16,8},{24,0},{1,25},{9,17},{17,9},{25,1},{2,26},{10... | collective-permute-start | bytes 196616 | tf_op jit(solution)/shard_map/ppermute | solution.py:364
  25.9 0.0 collective-permute-start.11
  25.9 1.8 %collective-permute-start.12 = (bf16[128,256]{1,0:T(8,128)(2,1)S(1)}, bf16[128,256]{1,0:T(8,128)(2,1)S(1)}, u32[]{:S(2)}, u32[]{:S(2)}) collective-permute-start(bf16[128,256]{1,0:T(8,128)(2,1)S(1)} %get-tuple-element.34), channel_id=1, source_target_pairs={{0,8},{8,0},{16,24},{24,16},{1,9},{9,1},{17,25},{25,17},{2,10},{10... | collective-permute-start | bytes 196616 | tf_op jit(solution)/shard_map/ppermute | solution.py:364
  27.7 0.7 %query_terms.2.refs_5_ = bf16[128,640]{1,0:T(8,128)(2,1)S(1)} custom-call(s32[12,128]{1,0:T(8,128)S(1)} %table.1.table_ref, bf16[128,256]{1,0:T(8,128)(2,1)S(1)} %join.1.refs_0_, bf16[128,256]{1,0:T(8,128)(2,1)S(1)} %collective-permute-done.4.refs_3_.refs_1_, bf16[128,256]{1,0:T(8,128)(2,1)S(1)} %collective-permute-done.5.refs_2_, ...), custom_call_target="tpu_custom_call" | custom-call | flops 20000000000 | bytes 1000000 | tf_op jit(solution)/shard_map/query_terms/pallas_call | solution.py:444
  28.4 1.6 %collective-permute-start.9 = (bf16[128,640]{1,0:T(8,128)(2,1)S(1)}, bf16[128,640]{1,0:T(8,128)(2,1)S(1)}, u32[]{:S(2)}, u32[]{:S(2)}) collective-permute-start(bf16[128,640]{1,0:T(8,128)(2,1)S(1)} %query_terms.2.refs_5_), channel_id=1, source_target_pairs={{0,4},{4,0},{1,5},{5,1},{2,6},{6,2},{3,7},{7,3},{8,12},{12,8},{9,1... | collective-permute-start | bytes 491528 | tf_op jit(solution)/shard_map/ppermute | solution.py:363
  30.0 0.0 collective-permute-done.10.refs_1_
  30.0 1.1 %collective-permute-done.11.refs_2_ = bf16[128,256]{1,0:T(8,128)(2,1)S(1)} collective-permute-done((bf16[128,256]{1,0:T(8,128)(2,1)S(1)}, bf16[128,256]{1,0:T(8,128)(2,1)S(1)}, u32[]{:S(2)}, u32[]{:S(2)}) %collective-permute-start.11) | collective-permute-done | bytes 65568 | tf_op jit(solution)/shard_map/ppermute | solution.py:364
  31.1 0.0 collective-permute-done.12.refs_3_
  31.2 1.4 %collective-permute-start.13 = (bf16[32,256]{1,0:T(8,128)(2,1)S(1)}, bf16[32,256]{1,0:T(8,128)(2,1)S(1)}, u32[]{:S(2)}, u32[]{:S(2)}) collective-permute-start(bf16[32,256]{1,0:T(8,128)(2,1)S(1)} %get-tuple-element.36), channel_id=1, source_target_pairs={{0,2},{1,3},{2,0},{3,1},{4,6},{5,7},{6,4},{7,5},{8,10},{9,11},{10,... | collective-permute-start | bytes 49160 | tf_op jit(solution)/shard_map/ppermute | solution.py:363
  32.6 0.0 collective-permute-start.14
  32.6 0.8 %collective-permute-start.15 = (bf16[32,256]{1,0:T(8,128)(2,1)S(1)}, bf16[32,256]{1,0:T(8,128)(2,1)S(1)}, u32[]{:S(2)}, u32[]{:S(2)}) collective-permute-start(bf16[32,256]{1,0:T(8,128)(2,1)S(1)} %get-tuple-element.38), channel_id=1, source_target_pairs={{0,1},{1,0},{2,3},{3,2},{4,5},{5,4},{6,7},{7,6},{8,9},{9,8},{10,11... | collective-permute-start | bytes 49160 | tf_op jit(solution)/shard_map/ppermute | solution.py:363
  33.4 0.7 %query_terms.3.own_ref = f32[128,640]{1,0:T(8,128)S(1)} custom-call(s32[12,128]{1,0:T(8,128)S(1)} %table.1.table_ref, bf16[128,256]{1,0:T(8,128)(2,1)S(1)} %join.1.refs_0_, bf16[128,256]{1,0:T(8,128)(2,1)S(1)} %collective-permute-done.4.refs_3_.refs_1_, bf16[128,256]{1,0:T(8,128)(2,1)S(1)} %collective-permute-done.5.refs_2_, ...), custom_call_target="tpu_custom_call" | custom-call | flops 20000000000 | bytes 1000000 | tf_op jit(solution)/shard_map/query_terms/pallas_call | solution.py:444
  34.1 0.9 %collective-permute-done.13.refs_1_ = bf16[32,256]{1,0:T(8,128)(2,1)S(1)} collective-permute-done((bf16[32,256]{1,0:T(8,128)(2,1)S(1)}, bf16[32,256]{1,0:T(8,128)(2,1)S(1)}, u32[]{:S(2)}, u32[]{:S(2)}) %collective-permute-start.13) | collective-permute-done | bytes 16416 | tf_op jit(solution)/shard_map/ppermute | solution.py:363
  35.0 0.8 %collective-permute-done.14.refs_2_ = bf16[32,256]{1,0:T(8,128)(2,1)S(1)} collective-permute-done((bf16[32,256]{1,0:T(8,128)(2,1)S(1)}, bf16[32,256]{1,0:T(8,128)(2,1)S(1)}, u32[]{:S(2)}, u32[]{:S(2)}) %collective-permute-start.14) | collective-permute-done | bytes 16416 | tf_op jit(solution)/shard_map/ppermute | solution.py:363
  35.7 0.0 collective-permute-done.15.refs_3_
  35.7 0.0 collective-permute-done.9.received_ref
  35.7 0.8 %place.1 = (bf16[128,640]{1,0:T(8,128)(2,1)}, bf16[32,512]{1,0:T(8,128)(2,1)}, bf16[32,512]{1,0:T(8,128)(2,1)}) custom-call(f32[128,640]{1,0:T(8,128)S(1)} %query_terms.3.own_ref, bf16[128,640]{1,0:T(8,128)(2,1)S(1)} %collective-permute-done.9.received_ref, bf16[32,256]{1,0:T(8,128)(2,1)S(1)} %get-tuple-element.35.refs_0_, ...), custom_call_target="tpu_custom_call" | custom-call | tf_op jit(solution)/shard_map/place/pallas_call | solution.py:466
  (1 shorter events, 0.0 us)
Async XLA Ops:
  1.5 5.2 %collective-permute-start.1 = (bf16[32,256]{1,0:T(8,128)(2,1)S(1)}, bf16[32,256]{1,0:T(8,128)(2,1)S(1)}, u32[]{:S(2)}, u32[]{:S(2)}) collective-permute-start(bf16[32,256]{1,0:T(8,128)(2,1)S(1)} %get-tuple-element.22), channel_id=1, source_target_pairs={{0,2},{1,3},{2,0},{3,1},{4,6},{5,7},{6,4},{7,5},{8,10},{9,11},{10,... | collective-permute-start | bytes 49160 | tf_op jit(solution)/shard_map/ppermute | solution.py:363
  4.5 3.2 %collective-permute-start.2 = (bf16[32,256]{1,0:T(8,128)(2,1)S(1)}, bf16[32,256]{1,0:T(8,128)(2,1)S(1)}, u32[]{:S(2)}, u32[]{:S(2)}) collective-permute-start(bf16[32,256]{1,0:T(8,128)(2,1)S(1)} %get-tuple-element.23), channel_id=1, source_target_pairs={{0,3},{1,2},{2,1},{3,0},{4,7},{5,6},{6,5},{7,4},{8,11},{9,10},{10,... | collective-permute-start | bytes 49160 | tf_op jit(solution)/shard_map/ppermute | solution.py:363
  4.5 3.2 %collective-permute-start.3 = (bf16[32,256]{1,0:T(8,128)(2,1)S(1)}, bf16[32,256]{1,0:T(8,128)(2,1)S(1)}, u32[]{:S(2)}, u32[]{:S(2)}) collective-permute-start(bf16[32,256]{1,0:T(8,128)(2,1)S(1)} %get-tuple-element.24), channel_id=1, source_target_pairs={{0,1},{1,0},{2,3},{3,2},{4,5},{5,4},{6,7},{7,6},{8,9},{9,8},{10,11... | collective-permute-start | bytes 49160 | tf_op jit(solution)/shard_map/ppermute | solution.py:363
  4.7 7.6 %collective-permute-start = (bf16[128,640]{1,0:T(8,128)(2,1)}, bf16[128,640]{1,0:T(8,128)(2,1)S(1)}, u32[]{:S(2)}, u32[]{:S(2)}) collective-permute-start(bf16[128,640]{1,0:T(8,128)(2,1)} %refs_0_.1), channel_id=1, source_target_pairs={{0,4},{4,0},{1,5},{5,1},{2,6},{6,2},{3,7},{7,3},{8,12},{12,8},{9,1... | collective-permute-start | bytes 491528 | tf_op jit(solution)/shard_map/ppermute | solution.py:363
  6.7 8.2 %collective-permute-start.7 = (bf16[128,640]{1,0:T(8,128)(2,1)}, bf16[128,640]{1,0:T(8,128)(2,1)S(1)}, u32[]{:S(2)}, u32[]{:S(2)}) collective-permute-start(bf16[128,640]{1,0:T(8,128)(2,1)} %refs_1_.1), channel_id=1, source_target_pairs={{0,4},{4,0},{1,5},{5,1},{2,6},{6,2},{3,7},{7,3},{8,12},{12,8},{9,1... | collective-permute-start | bytes 491528 | tf_op jit(solution)/shard_map/ppermute | solution.py:363
  7.7 4.6 %copy-start.2 = (s32[16]{0:T(128)S(1)}, s32[16]{0:T(128)}, u32[]{:S(2)}) copy-start(s32[16]{0:T(128)} %order_ref.1) | copy-start | bytes 196
  7.7 7.2 %copy-start = (bf16[128,640]{1,0:T(8,128)(2,1)S(1)}, bf16[128,640]{1,0:T(8,128)(2,1)}, u32[]{:S(2)}) copy-start(bf16[128,640]{1,0:T(8,128)(2,1)} %refs_0_.1) | copy-start | bytes 491524
  7.7 7.2 %copy-start.1 = (bf16[128,640]{1,0:T(8,128)(2,1)S(1)}, bf16[128,640]{1,0:T(8,128)(2,1)}, u32[]{:S(2)}) copy-start(bf16[128,640]{1,0:T(8,128)(2,1)} %refs_1_.1) | copy-start | bytes 491524
  7.9 7.1 %collective-permute-start.6 = (bf16[128,256]{1,0:T(8,128)(2,1)S(1)}, bf16[128,256]{1,0:T(8,128)(2,1)S(1)}, u32[]{:S(2)}, u32[]{:S(2)}) collective-permute-start(bf16[128,256]{1,0:T(8,128)(2,1)S(1)} %join.1.refs_0_), channel_id=1, source_target_pairs={{0,24},{8,16},{16,8},{24,0},{1,25},{9,17},{17,9},{25,1},{2,26},{10... | collective-permute-start | bytes 196616 | tf_op jit(solution)/shard_map/ppermute | solution.py:363
  11.5 5.4 %collective-permute-start.5 = (bf16[128,256]{1,0:T(8,128)(2,1)S(1)}, bf16[128,256]{1,0:T(8,128)(2,1)S(1)}, u32[]{:S(2)}, u32[]{:S(2)}) collective-permute-start(bf16[128,256]{1,0:T(8,128)(2,1)S(1)} %join.1.refs_0_), channel_id=1, source_target_pairs={{0,16},{8,24},{16,0},{24,8},{1,17},{9,25},{17,1},{25,9},{2,18},{10... | collective-permute-start | bytes 196616 | tf_op jit(solution)/shard_map/ppermute | solution.py:363
  11.5 5.4 %collective-permute-start.4 = (bf16[128,256]{1,0:T(8,128)(2,1)S(1)}, bf16[128,256]{1,0:T(8,128)(2,1)S(1)}, u32[]{:S(2)}, u32[]{:S(2)}) collective-permute-start(bf16[128,256]{1,0:T(8,128)(2,1)S(1)} %join.1.refs_0_), channel_id=1, source_target_pairs={{0,8},{8,0},{16,24},{24,16},{1,9},{9,1},{17,25},{25,17},{2,10},{10... | collective-permute-start | bytes 196616 | tf_op jit(solution)/shard_map/ppermute | solution.py:363
  18.4 3.9 %collective-permute-start.8 = (f32[12,320]{1,0:T(8,128)S(1)}, f32[12,320]{1,0:T(8,128)S(1)}, u32[]{:S(2)}, u32[]{:S(2)}) collective-permute-start(f32[12,320]{1,0:T(8,128)S(1)} %get-tuple-element.27.refs_0_), channel_id=1, source_target_pairs={{0,4},{4,0},{1,5},{5,1},{2,6},{6,2},{3,7},{7,3},{8,12},{12,8},{9,1... | collective-permute-start | bytes 46088 | tf_op jit(solution)/shard_map/ppermute | solution.py:363
  23.3 6.7 %collective-permute-start.10 = (bf16[128,256]{1,0:T(8,128)(2,1)S(1)}, bf16[128,256]{1,0:T(8,128)(2,1)S(1)}, u32[]{:S(2)}, u32[]{:S(2)}) collective-permute-start(bf16[128,256]{1,0:T(8,128)(2,1)S(1)} %get-tuple-element.32), channel_id=1, source_target_pairs={{0,24},{8,16},{16,8},{24,0},{1,25},{9,17},{17,9},{25,1},{2,26},{10... | collective-permute-start | bytes 196616 | tf_op jit(solution)/shard_map/ppermute | solution.py:364
  25.9 5.2 %collective-permute-start.11 = (bf16[128,256]{1,0:T(8,128)(2,1)S(1)}, bf16[128,256]{1,0:T(8,128)(2,1)S(1)}, u32[]{:S(2)}, u32[]{:S(2)}) collective-permute-start(bf16[128,256]{1,0:T(8,128)(2,1)S(1)} %get-tuple-element.33), channel_id=1, source_target_pairs={{0,16},{8,24},{16,0},{24,8},{1,17},{9,25},{17,1},{25,9},{2,18},{10... | collective-permute-start | bytes 196616 | tf_op jit(solution)/shard_map/ppermute | solution.py:364
  25.9 5.2 %collective-permute-start.12 = (bf16[128,256]{1,0:T(8,128)(2,1)S(1)}, bf16[128,256]{1,0:T(8,128)(2,1)S(1)}, u32[]{:S(2)}, u32[]{:S(2)}) collective-permute-start(bf16[128,256]{1,0:T(8,128)(2,1)S(1)} %get-tuple-element.34), channel_id=1, source_target_pairs={{0,8},{8,0},{16,24},{24,16},{1,9},{9,1},{17,25},{25,17},{2,10},{10... | collective-permute-start | bytes 196616 | tf_op jit(solution)/shard_map/ppermute | solution.py:364
  28.4 7.3 %collective-permute-start.9 = (bf16[128,640]{1,0:T(8,128)(2,1)S(1)}, bf16[128,640]{1,0:T(8,128)(2,1)S(1)}, u32[]{:S(2)}, u32[]{:S(2)}) collective-permute-start(bf16[128,640]{1,0:T(8,128)(2,1)S(1)} %query_terms.2.refs_5_), channel_id=1, source_target_pairs={{0,4},{4,0},{1,5},{5,1},{2,6},{6,2},{3,7},{7,3},{8,12},{12,8},{9,1... | collective-permute-start | bytes 491528 | tf_op jit(solution)/shard_map/ppermute | solution.py:363
  31.2 3.8 %collective-permute-start.13 = (bf16[32,256]{1,0:T(8,128)(2,1)S(1)}, bf16[32,256]{1,0:T(8,128)(2,1)S(1)}, u32[]{:S(2)}, u32[]{:S(2)}) collective-permute-start(bf16[32,256]{1,0:T(8,128)(2,1)S(1)} %get-tuple-element.36), channel_id=1, source_target_pairs={{0,2},{1,3},{2,0},{3,1},{4,6},{5,7},{6,4},{7,5},{8,10},{9,11},{10,... | collective-permute-start | bytes 49160 | tf_op jit(solution)/shard_map/ppermute | solution.py:363
  32.6 3.2 %collective-permute-start.14 = (bf16[32,256]{1,0:T(8,128)(2,1)S(1)}, bf16[32,256]{1,0:T(8,128)(2,1)S(1)}, u32[]{:S(2)}, u32[]{:S(2)}) collective-permute-start(bf16[32,256]{1,0:T(8,128)(2,1)S(1)} %get-tuple-element.37), channel_id=1, source_target_pairs={{0,3},{1,2},{2,1},{3,0},{4,7},{5,6},{6,5},{7,4},{8,11},{9,10},{10,... | collective-permute-start | bytes 49160 | tf_op jit(solution)/shard_map/ppermute | solution.py:363
  32.6 3.2 %collective-permute-start.15 = (bf16[32,256]{1,0:T(8,128)(2,1)S(1)}, bf16[32,256]{1,0:T(8,128)(2,1)S(1)}, u32[]{:S(2)}, u32[]{:S(2)}) collective-permute-start(bf16[32,256]{1,0:T(8,128)(2,1)S(1)} %get-tuple-element.38), channel_id=1, source_target_pairs={{0,1},{1,0},{2,3},{3,2},{4,5},{5,4},{6,7},{7,6},{8,9},{9,8},{10,11... | collective-permute-start | bytes 49160 | tf_op jit(solution)/shard_map/ppermute | solution.py:363

commit v13 on v12

--- a/solution.py
+++ b/solution.py
@@ -406,7 +406,8 @@
         in_specs=[smem, anywhere],
         out_specs=vmem,
     )(slab_order, queries2)
-    groups = [[0, *range(outer - 1, 0, -1)]]
+    far = outer // 2 + 1
+    groups = [[0, *range(far, outer)], list(range(far - 1, 0, -1))]
     all_stats = shape((12, columns), full)
     results = []
     for n, members in enumerate(groups):

time: 36.7 us -> 36.3 us (0.989)
  waiting for transfers between devices: 9.96 us -> 9.15 us
    ppermute x13, waiting for transfers between devices: 8.86 us -> 8.05 us  [shift(): lax.ppermute(array, axis, [(n, target_of(n, by, size)) for n in range(siz...]
    pallas_call x1 -> x2, Pallas kernels: 1.42 us -> 1.69 us  [per_device(): call(functools.partial(stats_kernel, members), 'stats', out_shape=(all_st...]
  transfers between devices with their start and end apart: 16 -> 16, of which waited for: 8 -> 8; matrix products, arithmetic and copies ran while one was open for 0% -> 0% of each run, Pallas kernels for 6% -> 9%
where the time goes in v13:
time: 36.3 us; the launch traced here: 36.1 us
  starting transfers between devices  19.5 us (54%)
  waiting for transfers between devices  9.15 us (25%)
  Pallas kernels  5.89 us (16%)
  other arithmetic  0.82 us (2%)
  between operations  0.73 us (2%)
    ppermute x13, starting transfers between devices, shift(): lax.ppermute(array, axis, [(n, target_of(n, by, size)) for n in range(siz...  15.1 us
    ppermute x13, waiting for transfers between devices, shift(): lax.ppermute(array, axis, [(n, target_of(n, by, size)) for n in range(siz...  8.05 us
    ppermute x3, starting transfers between devices, shift(): lax.ppermute(array, axis, [(n, partner(n, -by, size)) for n in range(size)])  4.45 us
    pallas_call x2, Pallas kernels, per_device(): call(functools.partial(stats_kernel, members), 'stats', out_shape=(all_st...  1.69 us
    pallas_call x2, Pallas kernels, query_terms(): call(functools.partial(query_kernel, outer, groups, owner), 'query_terms'...  1.39 us
    ppermute x3, waiting for transfers between devices, shift(): lax.ppermute(array, axis, [(n, partner(n, -by, size)) for n in range(size)])  1.09 us
    pallas_call x1, Pallas kernels, per_device(): call(functools.partial(grads_kernel, outer, groups), 'grads', out_shape=(...  1.03 us
    concatenate x1, other arithmetic, per_device(): jnp.concatenate([keys, values], axis=0)  0.82 us
  transfers between devices with their start and end apart: 16, of which 8 were waited for; matrix products, arithmetic and copies ran while one was open for 0% of the time, Pallas kernels for 9%

profile of v13, /device:TPU:0, one launch (start us, length us, event | category | flops | bytes accessed | tf_op | source)
XLA Modules:
  0.0 36.1 jit_solution(8702278598709277462)
XLA Ops:
  0.6 0.0 copy-start
  0.6 0.8 %pad_maximum_fusion.cache_ref = bf16[64,512]{1,0:T(8,128)(2,1)S(1)} fusion(bf16[32,512]{1,0:T(8,128)(2,1)} %param.7, bf16[32,512]{1,0:T(8,128)(2,1)} %param.6), kind=kLoop, calls=%fused_computation | loop fusion | flops 131072 | bytes 131072 | tf_op jit(solution)/shard_map/concatenate | solution.py:380
  1.5 0.1 split.1
  1.6 3.0 %collective-permute-start.1 = (bf16[32,256]{1,0:T(8,128)(2,1)S(1)}, bf16[32,256]{1,0:T(8,128)(2,1)S(1)}, u32[]{:S(2)}, u32[]{:S(2)}) collective-permute-start(bf16[32,256]{1,0:T(8,128)(2,1)S(1)} %get-tuple-element.26), channel_id=1, source_target_pairs={{0,2},{1,3},{2,0},{3,1},{4,6},{5,7},{6,4},{7,5},{8,10},{9,11},{10,... | collective-permute-start | bytes 49160 | tf_op jit(solution)/shard_map/ppermute | solution.py:363
  4.6 0.0 collective-permute-start.2
  4.6 0.2 collective-permute-start.3
  4.8 0.0 copy-done
  4.8 2.0 %collective-permute-start = (bf16[128,640]{1,0:T(8,128)(2,1)S(1)}, bf16[128,640]{1,0:T(8,128)(2,1)S(1)}, u32[]{:S(2)}, u32[]{:S(2)}) collective-permute-start(bf16[128,640]{1,0:T(8,128)(2,1)S(1)} %copy-done), channel_id=1, source_target_pairs={{0,4},{4,0},{1,5},{5,1},{2,6},{6,2},{3,7},{7,3},{8,12},{12,8},{9,1... | collective-permute-start | bytes 491528 | tf_op jit(solution)/shard_map/ppermute | solution.py:363
  6.7 0.1 collective-permute-start.7
  6.8 0.0 collective-permute-done.1.refs_1_
  6.8 0.9 %collective-permute-done.2.refs_2_ = bf16[32,256]{1,0:T(8,128)(2,1)S(1)} collective-permute-done((bf16[32,256]{1,0:T(8,128)(2,1)S(1)}, bf16[32,256]{1,0:T(8,128)(2,1)S(1)}, u32[]{:S(2)}, u32[]{:S(2)}) %collective-permute-start.2) | collective-permute-done | bytes 16416 | tf_op jit(solution)/shard_map/ppermute | solution.py:363
  7.7 0.0 collective-permute-done.3.refs_3_
  7.7 0.0 copy-start.2
  7.7 0.1 join.1.refs_0_
  7.9 0.0 copy-start.1
  7.9 3.7 %collective-permute-start.6 = (bf16[128,256]{1,0:T(8,128)(2,1)S(1)}, bf16[128,256]{1,0:T(8,128)(2,1)S(1)}, u32[]{:S(2)}, u32[]{:S(2)}) collective-permute-start(bf16[128,256]{1,0:T(8,128)(2,1)S(1)} %join.1.refs_0_), channel_id=1, source_target_pairs={{0,24},{8,16},{16,8},{24,0},{1,25},{9,17},{17,9},{25,1},{2,26},{10... | collective-permute-start | bytes 196616 | tf_op jit(solution)/shard_map/ppermute | solution.py:363
  11.6 0.0 collective-permute-start.5
  11.6 0.8 %collective-permute-start.4 = (bf16[128,256]{1,0:T(8,128)(2,1)S(1)}, bf16[128,256]{1,0:T(8,128)(2,1)S(1)}, u32[]{:S(2)}, u32[]{:S(2)}) collective-permute-start(bf16[128,256]{1,0:T(8,128)(2,1)S(1)} %join.1.refs_0_), channel_id=1, source_target_pairs={{0,8},{8,0},{16,24},{24,16},{1,9},{9,1},{17,25},{25,17},{2,10},{10... | collective-permute-start | bytes 196616 | tf_op jit(solution)/shard_map/ppermute | solution.py:363
  12.3 0.0 collective-permute-done.after_ref.refs_2_
  12.3 0.0 copy-done.2
  12.3 0.6 %table.1.table_ref = s32[12,128]{1,0:T(8,128)S(1)} custom-call(s32[16]{0:T(128)S(1)} %copy-done.2, bf16[128,640]{1,0:T(8,128)(2,1)S(1)} %collective-permute-done.after_ref.refs_2_), custom_call_target="tpu_custom_call" | custom-call | tf_op jit(solution)/shard_map/table/pallas_call | solution.py:402
  12.9 1.8 %collective-permute-done.7.refs_3_ = bf16[128,640]{1,0:T(8,128)(2,1)S(1)} collective-permute-done((bf16[128,640]{1,0:T(8,128)(2,1)}, bf16[128,640]{1,0:T(8,128)(2,1)S(1)}, u32[]{:S(2)}, u32[]{:S(2)}) %collective-permute-start.7) | collective-permute-done | bytes 163872 | tf_op jit(solution)/shard_map/ppermute | solution.py:363
  14.7 0.0 copy-done.1
  14.7 0.1 stack.1
  14.8 0.0 collective-permute-done.6.refs_1_.refs_3_
  14.8 0.9 %stats.2 = (f32[12,320]{1,0:T(8,128)S(1)}, f32[2,320,320]{2,1,0:T(8,128)S(1)}, f32[2,320,320]{2,1,0:T(8,128)S(1)}) custom-call(s32[12,128]{1,0:T(8,128)S(1)} %table.1.table_ref, bf16[2,2,320,128]{3,2,1,0:T(8,128)(2,1)S(1)} %get-tuple-element.29.own_ref, bf16[2,2,320,128]{3,2,1,0:T(8,128)(2,1)S(1)} %get-tuple-element.30.other_ref, ...), custom_call_target="tpu_custom_call" | custom-call | flops 20000000000 | bytes 1000000 | tf_op jit(solution)/shard_map/stats/pallas_call | solution.py:416
  15.7 1.2 %collective-permute-done.5.refs_0_.refs_2_ = bf16[128,256]{1,0:T(8,128)(2,1)S(1)} collective-permute-done((bf16[128,256]{1,0:T(8,128)(2,1)S(1)}, bf16[128,256]{1,0:T(8,128)(2,1)S(1)}, u32[]{:S(2)}, u32[]{:S(2)}) %collective-permute-start.5) | collective-permute-done | bytes 65568 | tf_op jit(solution)/shard_map/ppermute | solution.py:363
  16.9 0.1 collective-permute-done.4.refs_1_
  17.0 0.8 %stats.3 = (f32[12,320]{1,0:T(8,128)S(1)}, f32[2,320,320]{2,1,0:T(8,128)S(1)}, f32[2,320,320]{2,1,0:T(8,128)S(1)}) custom-call(s32[12,128]{1,0:T(8,128)S(1)} %table.1.table_ref, bf16[2,2,320,128]{3,2,1,0:T(8,128)(2,1)S(1)} %get-tuple-element.29.own_ref, bf16[2,2,320,128]{3,2,1,0:T(8,128)(2,1)S(1)} %get-tuple-element.30.other_ref, ...), custom_call_target="tpu_custom_call" | custom-call | tf_op jit(solution)/shard_map/stats/pallas_call | solution.py:416
  17.8 1.6 %collective-permute-start.8 = (f32[12,320]{1,0:T(8,128)S(1)}, f32[12,320]{1,0:T(8,128)S(1)}, u32[]{:S(2)}, u32[]{:S(2)}) collective-permute-start(f32[12,320]{1,0:T(8,128)S(1)} %merge.1), channel_id=1, source_target_pairs={{0,4},{4,0},{1,5},{5,1},{2,6},{6,2},{3,7},{7,3},{8,12},{12,8},{9,1... | collective-permute-start | bytes 46088 | tf_op jit(solution)/shard_map/ppermute | solution.py:363
  19.4 2.3 %collective-permute-done.8.refs_2_ = f32[12,320]{1,0:T(8,128)S(1)} collective-permute-done((f32[12,320]{1,0:T(8,128)S(1)}, f32[12,320]{1,0:T(8,128)S(1)}, u32[]{:S(2)}, u32[]{:S(2)}) %collective-permute-start.8) | collective-permute-done | bytes 15392 | tf_op jit(solution)/shard_map/ppermute | solution.py:363
  21.7 1.0 %grads.1 = (f32[128,256]{1,0:T(8,128)S(1)}, bf16[128,256]{1,0:T(8,128)(2,1)S(1)}, bf16[128,256]{1,0:T(8,128)(2,1)S(1)}, bf16[128,256]{1,0:T(8,128)(2,1)S(1)}, bf...) custom-call(s32[12,128]{1,0:T(8,128)S(1)} %table.1.table_ref, ...), custom_call_target="tpu_custom_call" | custom-call | tf_op jit(solution)/shard_map/grads/pallas_call | solution.py:433
  22.8 2.7 %collective-permute-start.10 = (bf16[128,256]{1,0:T(8,128)(2,1)S(1)}, bf16[128,256]{1,0:T(8,128)(2,1)S(1)}, u32[]{:S(2)}, u32[]{:S(2)}) collective-permute-start(bf16[128,256]{1,0:T(8,128)(2,1)S(1)} %get-tuple-element.40), channel_id=1, source_target_pairs={{0,24},{8,16},{16,8},{24,0},{1,25},{9,17},{17,9},{25,1},{2,26},{10... | collective-permute-start | bytes 196616 | tf_op jit(solution)/shard_map/ppermute | solution.py:364
  25.4 0.0 collective-permute-start.11
  25.4 1.8 %collective-permute-start.12 = (bf16[128,256]{1,0:T(8,128)(2,1)S(1)}, bf16[128,256]{1,0:T(8,128)(2,1)S(1)}, u32[]{:S(2)}, u32[]{:S(2)}) collective-permute-start(bf16[128,256]{1,0:T(8,128)(2,1)S(1)} %get-tuple-element.42), channel_id=1, source_target_pairs={{0,8},{8,0},{16,24},{24,16},{1,9},{9,1},{17,25},{25,17},{2,10},{10... | collective-permute-start | bytes 196616 | tf_op jit(solution)/shard_map/ppermute | solution.py:364
  27.2 0.7 %query_terms.2.refs_6_ = bf16[128,640]{1,0:T(8,128)(2,1)S(1)} custom-call(s32[12,128]{1,0:T(8,128)S(1)} %table.1.table_ref, bf16[128,256]{1,0:T(8,128)(2,1)S(1)} %join.1.refs_0_, bf16[128,256]{1,0:T(8,128)(2,1)S(1)} %collective-permute-done.4.refs_1_, bf16[128,256]{1,0:T(8,128)(2,1)S(1)} %collective-permute-done.5.refs_0_.refs_2_, ...), custom_call_target="tpu_custom_call" | custom-call | flops 20000000000 | bytes 1000000 | tf_op jit(solution)/shard_map/query_terms/pallas_call | solution.py:445
  27.9 1.6 %collective-permute-start.9 = (bf16[128,640]{1,0:T(8,128)(2,1)S(1)}, bf16[128,640]{1,0:T(8,128)(2,1)S(1)}, u32[]{:S(2)}, u32[]{:S(2)}) collective-permute-start(bf16[128,640]{1,0:T(8,128)(2,1)S(1)} %query_terms.2.refs_6_), channel_id=1, source_target_pairs={{0,4},{4,0},{1,5},{5,1},{2,6},{6,2},{3,7},{7,3},{8,12},{12,8},{9,1... | collective-permute-start | bytes 491528 | tf_op jit(solution)/shard_map/ppermute | solution.py:363
  29.5 0.0 collective-permute-done.10.refs_1_
  29.5 1.1 %collective-permute-done.11.refs_2_ = bf16[128,256]{1,0:T(8,128)(2,1)S(1)} collective-permute-done((bf16[128,256]{1,0:T(8,128)(2,1)S(1)}, bf16[128,256]{1,0:T(8,128)(2,1)S(1)}, u32[]{:S(2)}, u32[]{:S(2)}) %collective-permute-start.11) | collective-permute-done | bytes 65568 | tf_op jit(solution)/shard_map/ppermute | solution.py:364
  30.6 0.0 collective-permute-done.12.refs_3_
  30.7 1.5 %collective-permute-start.13 = (bf16[32,256]{1,0:T(8,128)(2,1)S(1)}, bf16[32,256]{1,0:T(8,128)(2,1)S(1)}, u32[]{:S(2)}, u32[]{:S(2)}) collective-permute-start(bf16[32,256]{1,0:T(8,128)(2,1)S(1)} %get-tuple-element.44), channel_id=1, source_target_pairs={{0,2},{1,3},{2,0},{3,1},{4,6},{5,7},{6,4},{7,5},{8,10},{9,11},{10,... | collective-permute-start | bytes 49160 | tf_op jit(solution)/shard_map/ppermute | solution.py:363
  32.2 0.0 collective-permute-start.14
  32.2 0.7 %collective-permute-start.15 = (bf16[32,256]{1,0:T(8,128)(2,1)S(1)}, bf16[32,256]{1,0:T(8,128)(2,1)S(1)}, u32[]{:S(2)}, u32[]{:S(2)}) collective-permute-start(bf16[32,256]{1,0:T(8,128)(2,1)S(1)} %get-tuple-element.46), channel_id=1, source_target_pairs={{0,1},{1,0},{2,3},{3,2},{4,5},{5,4},{6,7},{7,6},{8,9},{9,8},{10,11... | collective-permute-start | bytes 49160 | tf_op jit(solution)/shard_map/ppermute | solution.py:363
  32.9 0.7 %query_terms.3.own_ref = f32[128,640]{1,0:T(8,128)S(1)} custom-call(s32[12,128]{1,0:T(8,128)S(1)} %table.1.table_ref, bf16[128,256]{1,0:T(8,128)(2,1)S(1)} %join.1.refs_0_, bf16[128,256]{1,0:T(8,128)(2,1)S(1)} %collective-permute-done.4.refs_1_, bf16[128,256]{1,0:T(8,128)(2,1)S(1)} %collective-permute-done.5.refs_0_.refs_2_, ...), custom_call_target="tpu_custom_call" | custom-call | flops 20000000000 | bytes 1000000 | tf_op jit(solution)/shard_map/query_terms/pallas_call | solution.py:445
  33.6 0.9 %collective-permute-done.13.refs_1_ = bf16[32,256]{1,0:T(8,128)(2,1)S(1)} collective-permute-done((bf16[32,256]{1,0:T(8,128)(2,1)S(1)}, bf16[32,256]{1,0:T(8,128)(2,1)S(1)}, u32[]{:S(2)}, u32[]{:S(2)}) %collective-permute-start.13) | collective-permute-done | bytes 16416 | tf_op jit(solution)/shard_map/ppermute | solution.py:363
  34.5 0.9 %collective-permute-done.14.refs_2_ = bf16[32,256]{1,0:T(8,128)(2,1)S(1)} collective-permute-done((bf16[32,256]{1,0:T(8,128)(2,1)S(1)}, bf16[32,256]{1,0:T(8,128)(2,1)S(1)}, u32[]{:S(2)}, u32[]{:S(2)}) %collective-permute-start.14) | collective-permute-done | bytes 16416 | tf_op jit(solution)/shard_map/ppermute | solution.py:363
  35.3 0.0 collective-permute-done.15.refs_3_
  35.3 0.0 collective-permute-done.9.received_ref
  35.3 0.8 %place.1 = (bf16[128,640]{1,0:T(8,128)(2,1)}, bf16[32,512]{1,0:T(8,128)(2,1)}, bf16[32,512]{1,0:T(8,128)(2,1)}) custom-call(f32[128,640]{1,0:T(8,128)S(1)} %query_terms.3.own_ref, bf16[128,640]{1,0:T(8,128)(2,1)S(1)} %collective-permute-done.9.received_ref, bf16[32,256]{1,0:T(8,128)(2,1)S(1)} %get-tuple-element.43.refs_0_, ...), custom_call_target="tpu_custom_call" | custom-call | tf_op jit(solution)/shard_map/place/pallas_call | solution.py:467
  (2 shorter events, 0.1 us)
Async XLA Ops:
  0.6 4.1 %copy-start = (bf16[128,640]{1,0:T(8,128)(2,1)S(1)}, bf16[128,640]{1,0:T(8,128)(2,1)}, u32[]{:S(2)}) copy-start(bf16[128,640]{1,0:T(8,128)(2,1)} %refs_0_.1) | copy-start | bytes 491524
  1.6 5.2 %collective-permute-start.1 = (bf16[32,256]{1,0:T(8,128)(2,1)S(1)}, bf16[32,256]{1,0:T(8,128)(2,1)S(1)}, u32[]{:S(2)}, u32[]{:S(2)}) collective-permute-start(bf16[32,256]{1,0:T(8,128)(2,1)S(1)} %get-tuple-element.26), channel_id=1, source_target_pairs={{0,2},{1,3},{2,0},{3,1},{4,6},{5,7},{6,4},{7,5},{8,10},{9,11},{10,... | collective-permute-start | bytes 49160 | tf_op jit(solution)/shard_map/ppermute | solution.py:363
  4.6 3.2 %collective-permute-start.2 = (bf16[32,256]{1,0:T(8,128)(2,1)S(1)}, bf16[32,256]{1,0:T(8,128)(2,1)S(1)}, u32[]{:S(2)}, u32[]{:S(2)}) collective-permute-start(bf16[32,256]{1,0:T(8,128)(2,1)S(1)} %get-tuple-element.27), channel_id=1, source_target_pairs={{0,3},{1,2},{2,1},{3,0},{4,7},{5,6},{6,5},{7,4},{8,11},{9,10},{10,... | collective-permute-start | bytes 49160 | tf_op jit(solution)/shard_map/ppermute | solution.py:363
  4.6 3.2 %collective-permute-start.3 = (bf16[32,256]{1,0:T(8,128)(2,1)S(1)}, bf16[32,256]{1,0:T(8,128)(2,1)S(1)}, u32[]{:S(2)}, u32[]{:S(2)}) collective-permute-start(bf16[32,256]{1,0:T(8,128)(2,1)S(1)} %get-tuple-element.28), channel_id=1, source_target_pairs={{0,1},{1,0},{2,3},{3,2},{4,5},{5,4},{6,7},{7,6},{8,9},{9,8},{10,11... | collective-permute-start | bytes 49160 | tf_op jit(solution)/shard_map/ppermute | solution.py:363
  4.8 7.6 %collective-permute-start = (bf16[128,640]{1,0:T(8,128)(2,1)S(1)}, bf16[128,640]{1,0:T(8,128)(2,1)S(1)}, u32[]{:S(2)}, u32[]{:S(2)}) collective-permute-start(bf16[128,640]{1,0:T(8,128)(2,1)S(1)} %copy-done), channel_id=1, source_target_pairs={{0,4},{4,0},{1,5},{5,1},{2,6},{6,2},{3,7},{7,3},{8,12},{12,8},{9,1... | collective-permute-start | bytes 491528 | tf_op jit(solution)/shard_map/ppermute | solution.py:363
  6.7 8.0 %collective-permute-start.7 = (bf16[128,640]{1,0:T(8,128)(2,1)}, bf16[128,640]{1,0:T(8,128)(2,1)S(1)}, u32[]{:S(2)}, u32[]{:S(2)}) collective-permute-start(bf16[128,640]{1,0:T(8,128)(2,1)} %refs_1_.1), channel_id=1, source_target_pairs={{0,4},{4,0},{1,5},{5,1},{2,6},{6,2},{3,7},{7,3},{8,12},{12,8},{9,1... | collective-permute-start | bytes 491528 | tf_op jit(solution)/shard_map/ppermute | solution.py:363
  7.7 4.6 %copy-start.2 = (s32[16]{0:T(128)S(1)}, s32[16]{0:T(128)}, u32[]{:S(2)}) copy-start(s32[16]{0:T(128)} %order_ref.1) | copy-start | bytes 196
  7.9 6.8 %copy-start.1 = (bf16[128,640]{1,0:T(8,128)(2,1)S(1)}, bf16[128,640]{1,0:T(8,128)(2,1)}, u32[]{:S(2)}) copy-start(bf16[128,640]{1,0:T(8,128)(2,1)} %refs_1_.1) | copy-start | bytes 491524
  7.9 6.9 %collective-permute-start.6 = (bf16[128,256]{1,0:T(8,128)(2,1)S(1)}, bf16[128,256]{1,0:T(8,128)(2,1)S(1)}, u32[]{:S(2)}, u32[]{:S(2)}) collective-permute-start(bf16[128,256]{1,0:T(8,128)(2,1)S(1)} %join.1.refs_0_), channel_id=1, source_target_pairs={{0,24},{8,16},{16,8},{24,0},{1,25},{9,17},{17,9},{25,1},{2,26},{10... | collective-permute-start | bytes 196616 | tf_op jit(solution)/shard_map/ppermute | solution.py:363
  11.6 5.4 %collective-permute-start.5 = (bf16[128,256]{1,0:T(8,128)(2,1)S(1)}, bf16[128,256]{1,0:T(8,128)(2,1)S(1)}, u32[]{:S(2)}, u32[]{:S(2)}) collective-permute-start(bf16[128,256]{1,0:T(8,128)(2,1)S(1)} %join.1.refs_0_), channel_id=1, source_target_pairs={{0,16},{8,24},{16,0},{24,8},{1,17},{9,25},{17,1},{25,9},{2,18},{10... | collective-permute-start | bytes 196616 | tf_op jit(solution)/shard_map/ppermute | solution.py:363
  11.6 5.4 %collective-permute-start.4 = (bf16[128,256]{1,0:T(8,128)(2,1)S(1)}, bf16[128,256]{1,0:T(8,128)(2,1)S(1)}, u32[]{:S(2)}, u32[]{:S(2)}) collective-permute-start(bf16[128,256]{1,0:T(8,128)(2,1)S(1)} %join.1.refs_0_), channel_id=1, source_target_pairs={{0,8},{8,0},{16,24},{24,16},{1,9},{9,1},{17,25},{25,17},{2,10},{10... | collective-permute-start | bytes 196616 | tf_op jit(solution)/shard_map/ppermute | solution.py:363
  17.8 3.9 %collective-permute-start.8 = (f32[12,320]{1,0:T(8,128)S(1)}, f32[12,320]{1,0:T(8,128)S(1)}, u32[]{:S(2)}, u32[]{:S(2)}) collective-permute-start(f32[12,320]{1,0:T(8,128)S(1)} %merge.1), channel_id=1, source_target_pairs={{0,4},{4,0},{1,5},{5,1},{2,6},{6,2},{3,7},{7,3},{8,12},{12,8},{9,1... | collective-permute-start | bytes 46088 | tf_op jit(solution)/shard_map/ppermute | solution.py:363
  22.8 6.7 %collective-permute-start.10 = (bf16[128,256]{1,0:T(8,128)(2,1)S(1)}, bf16[128,256]{1,0:T(8,128)(2,1)S(1)}, u32[]{:S(2)}, u32[]{:S(2)}) collective-permute-start(bf16[128,256]{1,0:T(8,128)(2,1)S(1)} %get-tuple-element.40), channel_id=1, source_target_pairs={{0,24},{8,16},{16,8},{24,0},{1,25},{9,17},{17,9},{25,1},{2,26},{10... | collective-permute-start | bytes 196616 | tf_op jit(solution)/shard_map/ppermute | solution.py:364
  25.4 5.2 %collective-permute-start.11 = (bf16[128,256]{1,0:T(8,128)(2,1)S(1)}, bf16[128,256]{1,0:T(8,128)(2,1)S(1)}, u32[]{:S(2)}, u32[]{:S(2)}) collective-permute-start(bf16[128,256]{1,0:T(8,128)(2,1)S(1)} %get-tuple-element.41), channel_id=1, source_target_pairs={{0,16},{8,24},{16,0},{24,8},{1,17},{9,25},{17,1},{25,9},{2,18},{10... | collective-permute-start | bytes 196616 | tf_op jit(solution)/shard_map/ppermute | solution.py:364
  25.4 5.2 %collective-permute-start.12 = (bf16[128,256]{1,0:T(8,128)(2,1)S(1)}, bf16[128,256]{1,0:T(8,128)(2,1)S(1)}, u32[]{:S(2)}, u32[]{:S(2)}) collective-permute-start(bf16[128,256]{1,0:T(8,128)(2,1)S(1)} %get-tuple-element.42), channel_id=1, source_target_pairs={{0,8},{8,0},{16,24},{24,16},{1,9},{9,1},{17,25},{25,17},{2,10},{10... | collective-permute-start | bytes 196616 | tf_op jit(solution)/shard_map/ppermute | solution.py:364
  27.9 7.4 %collective-permute-start.9 = (bf16[128,640]{1,0:T(8,128)(2,1)S(1)}, bf16[128,640]{1,0:T(8,128)(2,1)S(1)}, u32[]{:S(2)}, u32[]{:S(2)}) collective-permute-start(bf16[128,640]{1,0:T(8,128)(2,1)S(1)} %query_terms.2.refs_6_), channel_id=1, source_target_pairs={{0,4},{4,0},{1,5},{5,1},{2,6},{6,2},{3,7},{7,3},{8,12},{12,8},{9,1... | collective-permute-start | bytes 491528 | tf_op jit(solution)/shard_map/ppermute | solution.py:363
  30.7 3.8 %collective-permute-start.13 = (bf16[32,256]{1,0:T(8,128)(2,1)S(1)}, bf16[32,256]{1,0:T(8,128)(2,1)S(1)}, u32[]{:S(2)}, u32[]{:S(2)}) collective-permute-start(bf16[32,256]{1,0:T(8,128)(2,1)S(1)} %get-tuple-element.44), channel_id=1, source_target_pairs={{0,2},{1,3},{2,0},{3,1},{4,6},{5,7},{6,4},{7,5},{8,10},{9,11},{10,... | collective-permute-start | bytes 49160 | tf_op jit(solution)/shard_map/ppermute | solution.py:363
  32.2 3.2 %collective-permute-start.14 = (bf16[32,256]{1,0:T(8,128)(2,1)S(1)}, bf16[32,256]{1,0:T(8,128)(2,1)S(1)}, u32[]{:S(2)}, u32[]{:S(2)}) collective-permute-start(bf16[32,256]{1,0:T(8,128)(2,1)S(1)} %get-tuple-element.45), channel_id=1, source_target_pairs={{0,3},{1,2},{2,1},{3,0},{4,7},{5,6},{6,5},{7,4},{8,11},{9,10},{10,... | collective-permute-start | bytes 49160 | tf_op jit(solution)/shard_map/ppermute | solution.py:363
  32.2 3.2 %collective-permute-start.15 = (bf16[32,256]{1,0:T(8,128)(2,1)S(1)}, bf16[32,256]{1,0:T(8,128)(2,1)S(1)}, u32[]{:S(2)}, u32[]{:S(2)}) collective-permute-start(bf16[32,256]{1,0:T(8,128)(2,1)S(1)} %get-tuple-element.46), channel_id=1, source_target_pairs={{0,1},{1,0},{2,3},{3,2},{4,5},{5,4},{6,7},{7,6},{8,9},{9,8},{10,11... | collective-permute-start | bytes 49160 | tf_op jit(solution)/shard_map/ppermute | solution.py:363

commit v14 on v13

--- a/solution.py
+++ b/solution.py
@@ -381,13 +381,6 @@
     parts = exchange(parts)
     stack = shape((2, 2, columns, HEAD), low)
     queries2 = shift(queries, "pair", 1)
-    own_qd, other_qd = call(
-        stack_kernel,
-        "stack",
-        out_shape=(stack, stack),
-        in_specs=[vmem] * 4,
-        out_specs=(vmem, vmem),
-    )(queries, d_out, queries2, shift(d_out, "pair", 1))
     own_block = call(
         functools.partial(join_kernel, order),
         "join",
@@ -397,6 +390,14 @@
         scratch_shapes=[dma((kvh,))],
         cost_estimate=beside,
     )(*parts)
+    late_d_out, own_block = lax.optimization_barrier((d_out, own_block))
+    own_qd, other_qd = call(
+        stack_kernel,
+        "stack",
+        out_shape=(stack, stack),
+        in_specs=[vmem] * 4,
+        out_specs=(vmem, vmem),
+    )(queries, d_out, queries2, shift(late_d_out, "pair", 1))
     blocks = [own_block] + [shift(own_block, "outer", d) for d in range(1, outer)]
 
     table = call(

time: 36.3 us -> 38.2 us (1.052)
  waiting for transfers between devices: 9.15 us -> 10.9 us
  local copies, waits for them, and re-layouts: 0.01 us -> 0.78 us
  starting transfers between devices: 19.5 us -> 18.9 us
    ppermute x3, waiting for transfers between devices: 1.09 us -> 2.14 us  [shift(): lax.ppermute(array, axis, [(n, partner(n, -by, size)) for n in range(size)])]
    unnamed x6, local copies, waits for them, and re-layouts: 0.01 us -> 0.78 us
    ppermute x13, waiting for transfers between devices: 8.05 us -> 8.75 us  [shift(): lax.ppermute(array, axis, [(n, target_of(n, by, size)) for n in range(siz...]
    ppermute x13, starting transfers between devices: 15.1 us -> 14.4 us  [shift(): lax.ppermute(array, axis, [(n, target_of(n, by, size)) for n in range(siz...]
  transfers between devices with their start and end apart: 16 -> 16, of which waited for: 8 -> 8; matrix products, arithmetic and copies ran while one was open for 0% -> 0% of each run, Pallas kernels for 9% -> 8%
where the time goes in v14:
time: 38.2 us; the launch traced here: 38 us
  starting transfers between devices  18.9 us (49%)
  waiting for transfers between devices  10.9 us (29%)
  Pallas kernels  5.91 us (15%)
  other arithmetic  0.82 us (2%)
  local copies, waits for them, and re-layouts  0.78 us (2%)
  between operations  0.73 us (2%)
    ppermute x13, starting transfers between devices, shift(): lax.ppermute(array, axis, [(n, target_of(n, by, size)) for n in range(siz...  14.4 us
    ppermute x13, waiting for transfers between devices, shift(): lax.ppermute(array, axis, [(n, target_of(n, by, size)) for n in range(siz...  8.75 us
    ppermute x3, starting transfers between devices, shift(): lax.ppermute(array, axis, [(n, partner(n, -by, size)) for n in range(size)])  4.45 us
    ppermute x3, waiting for transfers between devices, shift(): lax.ppermute(array, axis, [(n, partner(n, -by, size)) for n in range(size)])  2.14 us
    pallas_call x2, Pallas kernels, per_device(): call(functools.partial(stats_kernel, members), 'stats', out_shape=(all_st...  1.69 us
    pallas_call x2, Pallas kernels, query_terms(): call(functools.partial(query_kernel, outer, groups, owner), 'query_terms'...  1.39 us
    pallas_call x1, Pallas kernels, per_device(): call(functools.partial(grads_kernel, outer, groups), 'grads', out_shape=(...  1.03 us
    concatenate x1, other arithmetic, per_device(): jnp.concatenate([keys, values], axis=0)  0.82 us
  transfers between devices with their start and end apart: 16, of which 8 were waited for; matrix products, arithmetic and copies ran while one was open for 0% of the time, Pallas kernels for 8%

profile of v14, /device:TPU:0, one launch (start us, length us, event | category | flops | bytes accessed | tf_op | source)
XLA Modules:
  0.0 38.0 jit_solution(15428729768313362804)
XLA Ops:
  0.6 0.0 copy-start
  0.6 0.8 %pad_maximum_fusion.cache_ref = bf16[64,512]{1,0:T(8,128)(2,1)S(1)} fusion(bf16[32,512]{1,0:T(8,128)(2,1)} %param.7, bf16[32,512]{1,0:T(8,128)(2,1)} %param.6), kind=kLoop, calls=%fused_computation | loop fusion | flops 131072 | bytes 131072 | tf_op jit(solution)/shard_map/concatenate | solution.py:380
  1.5 0.1 split.1
  1.6 3.0 %collective-permute-start.1 = (bf16[32,256]{1,0:T(8,128)(2,1)S(1)}, bf16[32,256]{1,0:T(8,128)(2,1)S(1)}, u32[]{:S(2)}, u32[]{:S(2)}) collective-permute-start(bf16[32,256]{1,0:T(8,128)(2,1)S(1)} %get-tuple-element.28), channel_id=1, source_target_pairs={{0,2},{1,3},{2,0},{3,1},{4,6},{5,7},{6,4},{7,5},{8,10},{9,11},{10,... | collective-permute-start | bytes 49160 | tf_op jit(solution)/shard_map/ppermute | solution.py:363
  4.6 0.0 collective-permute-start.2
  4.6 0.2 collective-permute-start.3
  4.8 0.0 copy-done
  4.8 2.0 %collective-permute-start = (bf16[128,640]{1,0:T(8,128)(2,1)S(1)}, bf16[128,640]{1,0:T(8,128)(2,1)S(1)}, u32[]{:S(2)}, u32[]{:S(2)}) collective-permute-start(bf16[128,640]{1,0:T(8,128)(2,1)S(1)} %copy-done), channel_id=1, source_target_pairs={{0,4},{4,0},{1,5},{5,1},{2,6},{6,2},{3,7},{7,3},{8,12},{12,8},{9,1... | collective-permute-start | bytes 491528 | tf_op jit(solution)/shard_map/ppermute | solution.py:363
  6.7 0.0 collective-permute-done.1.refs_1_
  6.8 1.0 %collective-permute-done.2.refs_2_ = bf16[32,256]{1,0:T(8,128)(2,1)S(1)} collective-permute-done((bf16[32,256]{1,0:T(8,128)(2,1)S(1)}, bf16[32,256]{1,0:T(8,128)(2,1)S(1)}, u32[]{:S(2)}, u32[]{:S(2)}) %collective-permute-start.2) | collective-permute-done | bytes 16416 | tf_op jit(solution)/shard_map/ppermute | solution.py:363
  7.7 0.0 collective-permute-done.3.refs_3_
  7.7 0.0 copy-start.1
  7.7 0.0 copy-start.2
  7.7 0.1 join.1.refs_0_
  7.9 0.8 %copy-done.1 = bf16[128,640]{1,0:T(8,128)(2,1)S(1)} copy-done((bf16[128,640]{1,0:T(8,128)(2,1)S(1)}, bf16[128,640]{1,0:T(8,128)(2,1)}, u32[]{:S(2)}) %copy-start.1) | copy-done | bytes 163864
  8.7 1.5 %collective-permute-start.7 = (bf16[128,640]{1,0:T(8,128)(2,1)S(1)}, bf16[128,640]{1,0:T(8,128)(2,1)S(1)}, u32[]{:S(2)}, u32[]{:S(2)}) collective-permute-start(bf16[128,640]{1,0:T(8,128)(2,1)S(1)} %copy-done.1), channel_id=1, source_target_pairs={{0,4},{4,0},{1,5},{5,1},{2,6},{6,2},{3,7},{7,3},{8,12},{12,8},{9,1... | collective-permute-start | bytes 491528 | tf_op jit(solution)/shard_map/ppermute | solution.py:363
  10.2 3.6 %collective-permute-start.6 = (bf16[128,256]{1,0:T(8,128)(2,1)S(1)}, bf16[128,256]{1,0:T(8,128)(2,1)S(1)}, u32[]{:S(2)}, u32[]{:S(2)}) collective-permute-start(bf16[128,256]{1,0:T(8,128)(2,1)S(1)} %join.1.refs_0_), channel_id=1, source_target_pairs={{0,24},{8,16},{16,8},{24,0},{1,25},{9,17},{17,9},{25,1},{2,26},{10... | collective-permute-start | bytes 196616 | tf_op jit(solution)/shard_map/ppermute | solution.py:363
  13.8 0.0 collective-permute-start.5
  13.8 0.8 %collective-permute-start.4 = (bf16[128,256]{1,0:T(8,128)(2,1)S(1)}, bf16[128,256]{1,0:T(8,128)(2,1)S(1)}, u32[]{:S(2)}, u32[]{:S(2)}) collective-permute-start(bf16[128,256]{1,0:T(8,128)(2,1)S(1)} %join.1.refs_0_), channel_id=1, source_target_pairs={{0,8},{8,0},{16,24},{24,16},{1,9},{9,1},{17,25},{25,17},{2,10},{10... | collective-permute-start | bytes 196616 | tf_op jit(solution)/shard_map/ppermute | solution.py:363
  14.6 0.0 collective-permute-done.after_ref.refs_2_
  14.6 0.0 copy-done.2
  14.6 0.6 %table.1.table_ref = s32[12,128]{1,0:T(8,128)S(1)} custom-call(s32[16]{0:T(128)S(1)} %copy-done.2, bf16[128,640]{1,0:T(8,128)(2,1)S(1)} %collective-permute-done.after_ref.refs_2_), custom_call_target="tpu_custom_call" | custom-call | tf_op jit(solution)/shard_map/table/pallas_call | solution.py:403
  15.2 0.0 collective-permute-done.7.refs_3_
  15.2 0.1 stack.1
  15.3 1.5 %collective-permute-done.6.refs_1_.refs_3_ = bf16[128,256]{1,0:T(8,128)(2,1)S(1)} collective-permute-done((bf16[128,256]{1,0:T(8,128)(2,1)S(1)}, bf16[128,256]{1,0:T(8,128)(2,1)S(1)}, u32[]{:S(2)}, u32[]{:S(2)}) %collective-permute-start.6) | collective-permute-done | bytes 65568 | tf_op jit(solution)/shard_map/ppermute | solution.py:363
  16.8 0.9 %stats.2 = (f32[12,320]{1,0:T(8,128)S(1)}, f32[2,320,320]{2,1,0:T(8,128)S(1)}, f32[2,320,320]{2,1,0:T(8,128)S(1)}) custom-call(s32[12,128]{1,0:T(8,128)S(1)} %table.1.table_ref, bf16[2,2,320,128]{3,2,1,0:T(8,128)(2,1)S(1)} %get-tuple-element.33.own_ref, bf16[2,2,320,128]{3,2,1,0:T(8,128)(2,1)S(1)} %get-tuple-element.34.other_ref, ...), custom_call_target="tpu_custom_call" | custom-call | flops 20000000000 | bytes 1000000 | tf_op jit(solution)/shard_map/stats/pallas_call | solution.py:417
  17.7 1.4 %collective-permute-done.5.refs_0_.refs_2_ = bf16[128,256]{1,0:T(8,128)(2,1)S(1)} collective-permute-done((bf16[128,256]{1,0:T(8,128)(2,1)S(1)}, bf16[128,256]{1,0:T(8,128)(2,1)S(1)}, u32[]{:S(2)}, u32[]{:S(2)}) %collective-permute-start.5) | collective-permute-done | bytes 65568 | tf_op jit(solution)/shard_map/ppermute | solution.py:363
  19.0 0.0 collective-permute-done.4.refs_1_
  19.0 0.8 %stats.3 = (f32[12,320]{1,0:T(8,128)S(1)}, f32[2,320,320]{2,1,0:T(8,128)S(1)}, f32[2,320,320]{2,1,0:T(8,128)S(1)}) custom-call(s32[12,128]{1,0:T(8,128)S(1)} %table.1.table_ref, bf16[2,2,320,128]{3,2,1,0:T(8,128)(2,1)S(1)} %get-tuple-element.33.own_ref, bf16[2,2,320,128]{3,2,1,0:T(8,128)(2,1)S(1)} %get-tuple-element.34.other_ref, ...), custom_call_target="tpu_custom_call" | custom-call | tf_op jit(solution)/shard_map/stats/pallas_call | solution.py:417
  19.9 0.6 %collective-permute-start.8 = (f32[12,320]{1,0:T(8,128)S(1)}, f32[12,320]{1,0:T(8,128)S(1)}, u32[]{:S(2)}, u32[]{:S(2)}) collective-permute-start(f32[12,320]{1,0:T(8,128)S(1)} %merge.1), channel_id=1, source_target_pairs={{0,4},{4,0},{1,5},{5,1},{2,6},{6,2},{3,7},{7,3},{8,12},{12,8},{9,1... | collective-permute-start | bytes 46088 | tf_op jit(solution)/shard_map/ppermute | solution.py:363
  20.5 3.3 %collective-permute-done.8.refs_2_ = f32[12,320]{1,0:T(8,128)S(1)} collective-permute-done((f32[12,320]{1,0:T(8,128)S(1)}, f32[12,320]{1,0:T(8,128)S(1)}, u32[]{:S(2)}, u32[]{:S(2)}) %collective-permute-start.8) | collective-permute-done | bytes 15392 | tf_op jit(solution)/shard_map/ppermute | solution.py:363
  23.8 1.0 %grads.1 = (f32[128,256]{1,0:T(8,128)S(1)}, bf16[128,256]{1,0:T(8,128)(2,1)S(1)}, bf16[128,256]{1,0:T(8,128)(2,1)S(1)}, bf16[128,256]{1,0:T(8,128)(2,1)S(1)}, bf...) custom-call(s32[12,128]{1,0:T(8,128)S(1)} %table.1.table_ref, ...), custom_call_target="tpu_custom_call" | custom-call | tf_op jit(solution)/shard_map/grads/pallas_call | solution.py:434
  24.8 2.5 %collective-permute-start.10 = (bf16[128,256]{1,0:T(8,128)(2,1)S(1)}, bf16[128,256]{1,0:T(8,128)(2,1)S(1)}, u32[]{:S(2)}, u32[]{:S(2)}) collective-permute-start(bf16[128,256]{1,0:T(8,128)(2,1)S(1)} %get-tuple-element.44), channel_id=1, source_target_pairs={{0,24},{8,16},{16,8},{24,0},{1,25},{9,17},{17,9},{25,1},{2,26},{10... | collective-permute-start | bytes 196616 | tf_op jit(solution)/shard_map/ppermute | solution.py:364
  27.3 0.0 collective-permute-start.11
  27.3 1.9 %collective-permute-start.12 = (bf16[128,256]{1,0:T(8,128)(2,1)S(1)}, bf16[128,256]{1,0:T(8,128)(2,1)S(1)}, u32[]{:S(2)}, u32[]{:S(2)}) collective-permute-start(bf16[128,256]{1,0:T(8,128)(2,1)S(1)} %get-tuple-element.46), channel_id=1, source_target_pairs={{0,8},{8,0},{16,24},{24,16},{1,9},{9,1},{17,25},{25,17},{2,10},{10... | collective-permute-start | bytes 196616 | tf_op jit(solution)/shard_map/ppermute | solution.py:364
  29.3 0.7 %query_terms.2.refs_6_ = bf16[128,640]{1,0:T(8,128)(2,1)S(1)} custom-call(s32[12,128]{1,0:T(8,128)S(1)} %table.1.table_ref, bf16[128,256]{1,0:T(8,128)(2,1)S(1)} %join.1.refs_0_, bf16[128,256]{1,0:T(8,128)(2,1)S(1)} %collective-permute-done.4.refs_1_, bf16[128,256]{1,0:T(8,128)(2,1)S(1)} %collective-permute-done.5.refs_0_.refs_2_, ...), custom_call_target="tpu_custom_call" | custom-call | flops 20000000000 | bytes 1000000 | tf_op jit(solution)/shard_map/query_terms/pallas_call | solution.py:446
  30.0 0.6 %collective-permute-start.9 = (bf16[128,640]{1,0:T(8,128)(2,1)S(1)}, bf16[128,640]{1,0:T(8,128)(2,1)S(1)}, u32[]{:S(2)}, u32[]{:S(2)}) collective-permute-start(bf16[128,640]{1,0:T(8,128)(2,1)S(1)} %query_terms.2.refs_6_), channel_id=1, source_target_pairs={{0,4},{4,0},{1,5},{5,1},{2,6},{6,2},{3,7},{7,3},{8,12},{12,8},{9,1... | collective-permute-start | bytes 491528 | tf_op jit(solution)/shard_map/ppermute | solution.py:363
  30.5 0.4 %collective-permute-done.10.refs_1_ = bf16[128,256]{1,0:T(8,128)(2,1)S(1)} collective-permute-done((bf16[128,256]{1,0:T(8,128)(2,1)S(1)}, bf16[128,256]{1,0:T(8,128)(2,1)S(1)}, u32[]{:S(2)}, u32[]{:S(2)}) %collective-permute-start.10) | collective-permute-done | bytes 65568 | tf_op jit(solution)/shard_map/ppermute | solution.py:364
  31.0 1.7 %collective-permute-done.11.refs_2_ = bf16[128,256]{1,0:T(8,128)(2,1)S(1)} collective-permute-done((bf16[128,256]{1,0:T(8,128)(2,1)S(1)}, bf16[128,256]{1,0:T(8,128)(2,1)S(1)}, u32[]{:S(2)}, u32[]{:S(2)}) %collective-permute-start.11) | collective-permute-done | bytes 65568 | tf_op jit(solution)/shard_map/ppermute | solution.py:364
  32.7 0.0 collective-permute-done.12.refs_3_
  32.7 1.3 %collective-permute-start.13 = (bf16[32,256]{1,0:T(8,128)(2,1)S(1)}, bf16[32,256]{1,0:T(8,128)(2,1)S(1)}, u32[]{:S(2)}, u32[]{:S(2)}) collective-permute-start(bf16[32,256]{1,0:T(8,128)(2,1)S(1)} %get-tuple-element.48), channel_id=1, source_target_pairs={{0,2},{1,3},{2,0},{3,1},{4,6},{5,7},{6,4},{7,5},{8,10},{9,11},{10,... | collective-permute-start | bytes 49160 | tf_op jit(solution)/shard_map/ppermute | solution.py:363
  34.1 0.0 collective-permute-start.14
  34.1 0.9 %collective-permute-start.15 = (bf16[32,256]{1,0:T(8,128)(2,1)S(1)}, bf16[32,256]{1,0:T(8,128)(2,1)S(1)}, u32[]{:S(2)}, u32[]{:S(2)}) collective-permute-start(bf16[32,256]{1,0:T(8,128)(2,1)S(1)} %get-tuple-element.50), channel_id=1, source_target_pairs={{0,1},{1,0},{2,3},{3,2},{4,5},{5,4},{6,7},{7,6},{8,9},{9,8},{10,11... | collective-permute-start | bytes 49160 | tf_op jit(solution)/shard_map/ppermute | solution.py:363
  34.9 0.7 %query_terms.3.own_ref = f32[128,640]{1,0:T(8,128)S(1)} custom-call(s32[12,128]{1,0:T(8,128)S(1)} %table.1.table_ref, bf16[128,256]{1,0:T(8,128)(2,1)S(1)} %join.1.refs_0_, bf16[128,256]{1,0:T(8,128)(2,1)S(1)} %collective-permute-done.4.refs_1_, bf16[128,256]{1,0:T(8,128)(2,1)S(1)} %collective-permute-done.5.refs_0_.refs_2_, ...), custom_call_target="tpu_custom_call" | custom-call | flops 20000000000 | bytes 1000000 | tf_op jit(solution)/shard_map/query_terms/pallas_call | solution.py:446
  35.6 0.9 %collective-permute-done.13.refs_1_ = bf16[32,256]{1,0:T(8,128)(2,1)S(1)} collective-permute-done((bf16[32,256]{1,0:T(8,128)(2,1)S(1)}, bf16[32,256]{1,0:T(8,128)(2,1)S(1)}, u32[]{:S(2)}, u32[]{:S(2)}) %collective-permute-start.13) | collective-permute-done | bytes 16416 | tf_op jit(solution)/shard_map/ppermute | solution.py:363
  36.5 0.7 %collective-permute-done.14.refs_2_ = bf16[32,256]{1,0:T(8,128)(2,1)S(1)} collective-permute-done((bf16[32,256]{1,0:T(8,128)(2,1)S(1)}, bf16[32,256]{1,0:T(8,128)(2,1)S(1)}, u32[]{:S(2)}, u32[]{:S(2)}) %collective-permute-start.14) | collective-permute-done | bytes 16416 | tf_op jit(solution)/shard_map/ppermute | solution.py:363
  37.2 0.0 collective-permute-done.15.refs_3_
  37.2 0.0 collective-permute-done.9.received_ref
  37.2 0.8 %place.1 = (bf16[128,640]{1,0:T(8,128)(2,1)}, bf16[32,512]{1,0:T(8,128)(2,1)}, bf16[32,512]{1,0:T(8,128)(2,1)}) custom-call(f32[128,640]{1,0:T(8,128)S(1)} %query_terms.3.own_ref, bf16[128,640]{1,0:T(8,128)(2,1)S(1)} %collective-permute-done.9.received_ref, bf16[32,256]{1,0:T(8,128)(2,1)S(1)} %get-tuple-element.47.refs_0_, ...), custom_call_target="tpu_custom_call" | custom-call | tf_op jit(solution)/shard_map/place/pallas_call | solution.py:468
  (2 shorter events, 0.1 us)
Async XLA Ops:
  0.6 4.1 %copy-start = (bf16[128,640]{1,0:T(8,128)(2,1)S(1)}, bf16[128,640]{1,0:T(8,128)(2,1)}, u32[]{:S(2)}) copy-start(bf16[128,640]{1,0:T(8,128)(2,1)} %refs_0_.1) | copy-start | bytes 491524
  1.6 5.2 %collective-permute-start.1 = (bf16[32,256]{1,0:T(8,128)(2,1)S(1)}, bf16[32,256]{1,0:T(8,128)(2,1)S(1)}, u32[]{:S(2)}, u32[]{:S(2)}) collective-permute-start(bf16[32,256]{1,0:T(8,128)(2,1)S(1)} %get-tuple-element.28), channel_id=1, source_target_pairs={{0,2},{1,3},{2,0},{3,1},{4,6},{5,7},{6,4},{7,5},{8,10},{9,11},{10,... | collective-permute-start | bytes 49160 | tf_op jit(solution)/shard_map/ppermute | solution.py:363
  4.6 3.2 %collective-permute-start.2 = (bf16[32,256]{1,0:T(8,128)(2,1)S(1)}, bf16[32,256]{1,0:T(8,128)(2,1)S(1)}, u32[]{:S(2)}, u32[]{:S(2)}) collective-permute-start(bf16[32,256]{1,0:T(8,128)(2,1)S(1)} %get-tuple-element.29), channel_id=1, source_target_pairs={{0,3},{1,2},{2,1},{3,0},{4,7},{5,6},{6,5},{7,4},{8,11},{9,10},{10,... | collective-permute-start | bytes 49160 | tf_op jit(solution)/shard_map/ppermute | solution.py:363
  4.6 3.2 %collective-permute-start.3 = (bf16[32,256]{1,0:T(8,128)(2,1)S(1)}, bf16[32,256]{1,0:T(8,128)(2,1)S(1)}, u32[]{:S(2)}, u32[]{:S(2)}) collective-permute-start(bf16[32,256]{1,0:T(8,128)(2,1)S(1)} %get-tuple-element.30), channel_id=1, source_target_pairs={{0,1},{1,0},{2,3},{3,2},{4,5},{5,4},{6,7},{7,6},{8,9},{9,8},{10,11... | collective-permute-start | bytes 49160 | tf_op jit(solution)/shard_map/ppermute | solution.py:363
  4.8 9.8 %collective-permute-start = (bf16[128,640]{1,0:T(8,128)(2,1)S(1)}, bf16[128,640]{1,0:T(8,128)(2,1)S(1)}, u32[]{:S(2)}, u32[]{:S(2)}) collective-permute-start(bf16[128,640]{1,0:T(8,128)(2,1)S(1)} %copy-done), channel_id=1, source_target_pairs={{0,4},{4,0},{1,5},{5,1},{2,6},{6,2},{3,7},{7,3},{8,12},{12,8},{9,1... | collective-permute-start | bytes 491528 | tf_op jit(solution)/shard_map/ppermute | solution.py:363
  7.7 0.9 %copy-start.1 = (bf16[128,640]{1,0:T(8,128)(2,1)S(1)}, bf16[128,640]{1,0:T(8,128)(2,1)}, u32[]{:S(2)}) copy-start(bf16[128,640]{1,0:T(8,128)(2,1)} %refs_1_.1) | copy-start | bytes 491524
  7.7 6.8 %copy-start.2 = (s32[16]{0:T(128)S(1)}, s32[16]{0:T(128)}, u32[]{:S(2)}) copy-start(s32[16]{0:T(128)} %order_ref.1) | copy-start | bytes 196
  8.7 6.5 %collective-permute-start.7 = (bf16[128,640]{1,0:T(8,128)(2,1)S(1)}, bf16[128,640]{1,0:T(8,128)(2,1)S(1)}, u32[]{:S(2)}, u32[]{:S(2)}) collective-permute-start(bf16[128,640]{1,0:T(8,128)(2,1)S(1)} %copy-done.1), channel_id=1, source_target_pairs={{0,4},{4,0},{1,5},{5,1},{2,6},{6,2},{3,7},{7,3},{8,12},{12,8},{9,1... | collective-permute-start | bytes 491528 | tf_op jit(solution)/shard_map/ppermute | solution.py:363
  10.2 6.6 %collective-permute-start.6 = (bf16[128,256]{1,0:T(8,128)(2,1)S(1)}, bf16[128,256]{1,0:T(8,128)(2,1)S(1)}, u32[]{:S(2)}, u32[]{:S(2)}) collective-permute-start(bf16[128,256]{1,0:T(8,128)(2,1)S(1)} %join.1.refs_0_), channel_id=1, source_target_pairs={{0,24},{8,16},{16,8},{24,0},{1,25},{9,17},{17,9},{25,1},{2,26},{10... | collective-permute-start | bytes 196616 | tf_op jit(solution)/shard_map/ppermute | solution.py:363
  13.8 5.2 %collective-permute-start.5 = (bf16[128,256]{1,0:T(8,128)(2,1)S(1)}, bf16[128,256]{1,0:T(8,128)(2,1)S(1)}, u32[]{:S(2)}, u32[]{:S(2)}) collective-permute-start(bf16[128,256]{1,0:T(8,128)(2,1)S(1)} %join.1.refs_0_), channel_id=1, source_target_pairs={{0,16},{8,24},{16,0},{24,8},{1,17},{9,25},{17,1},{25,9},{2,18},{10... | collective-permute-start | bytes 196616 | tf_op jit(solution)/shard_map/ppermute | solution.py:363
  13.8 5.2 %collective-permute-start.4 = (bf16[128,256]{1,0:T(8,128)(2,1)S(1)}, bf16[128,256]{1,0:T(8,128)(2,1)S(1)}, u32[]{:S(2)}, u32[]{:S(2)}) collective-permute-start(bf16[128,256]{1,0:T(8,128)(2,1)S(1)} %join.1.refs_0_), channel_id=1, source_target_pairs={{0,8},{8,0},{16,24},{24,16},{1,9},{9,1},{17,25},{25,17},{2,10},{10... | collective-permute-start | bytes 196616 | tf_op jit(solution)/shard_map/ppermute | solution.py:363
  19.9 3.9 %collective-permute-start.8 = (f32[12,320]{1,0:T(8,128)S(1)}, f32[12,320]{1,0:T(8,128)S(1)}, u32[]{:S(2)}, u32[]{:S(2)}) collective-permute-start(f32[12,320]{1,0:T(8,128)S(1)} %merge.1), channel_id=1, source_target_pairs={{0,4},{4,0},{1,5},{5,1},{2,6},{6,2},{3,7},{7,3},{8,12},{12,8},{9,1... | collective-permute-start | bytes 46088 | tf_op jit(solution)/shard_map/ppermute | solution.py:363
  24.8 6.1 %collective-permute-start.10 = (bf16[128,256]{1,0:T(8,128)(2,1)S(1)}, bf16[128,256]{1,0:T(8,128)(2,1)S(1)}, u32[]{:S(2)}, u32[]{:S(2)}) collective-permute-start(bf16[128,256]{1,0:T(8,128)(2,1)S(1)} %get-tuple-element.44), channel_id=1, source_target_pairs={{0,24},{8,16},{16,8},{24,0},{1,25},{9,17},{17,9},{25,1},{2,26},{10... | collective-permute-start | bytes 196616 | tf_op jit(solution)/shard_map/ppermute | solution.py:364
  27.3 5.4 %collective-permute-start.11 = (bf16[128,256]{1,0:T(8,128)(2,1)S(1)}, bf16[128,256]{1,0:T(8,128)(2,1)S(1)}, u32[]{:S(2)}, u32[]{:S(2)}) collective-permute-start(bf16[128,256]{1,0:T(8,128)(2,1)S(1)} %get-tuple-element.45), channel_id=1, source_target_pairs={{0,16},{8,24},{16,0},{24,8},{1,17},{9,25},{17,1},{25,9},{2,18},{10... | collective-permute-start | bytes 196616 | tf_op jit(solution)/shard_map/ppermute | solution.py:364
  27.3 5.4 %collective-permute-start.12 = (bf16[128,256]{1,0:T(8,128)(2,1)S(1)}, bf16[128,256]{1,0:T(8,128)(2,1)S(1)}, u32[]{:S(2)}, u32[]{:S(2)}) collective-permute-start(bf16[128,256]{1,0:T(8,128)(2,1)S(1)} %get-tuple-element.46), channel_id=1, source_target_pairs={{0,8},{8,0},{16,24},{24,16},{1,9},{9,1},{17,25},{25,17},{2,10},{10... | collective-permute-start | bytes 196616 | tf_op jit(solution)/shard_map/ppermute | solution.py:364
  30.0 7.3 %collective-permute-start.9 = (bf16[128,640]{1,0:T(8,128)(2,1)S(1)}, bf16[128,640]{1,0:T(8,128)(2,1)S(1)}, u32[]{:S(2)}, u32[]{:S(2)}) collective-permute-start(bf16[128,640]{1,0:T(8,128)(2,1)S(1)} %query_terms.2.refs_6_), channel_id=1, source_target_pairs={{0,4},{4,0},{1,5},{5,1},{2,6},{6,2},{3,7},{7,3},{8,12},{12,8},{9,1... | collective-permute-start | bytes 491528 | tf_op jit(solution)/shard_map/ppermute | solution.py:363
  32.7 3.8 %collective-permute-start.13 = (bf16[32,256]{1,0:T(8,128)(2,1)S(1)}, bf16[32,256]{1,0:T(8,128)(2,1)S(1)}, u32[]{:S(2)}, u32[]{:S(2)}) collective-permute-start(bf16[32,256]{1,0:T(8,128)(2,1)S(1)} %get-tuple-element.48), channel_id=1, source_target_pairs={{0,2},{1,3},{2,0},{3,1},{4,6},{5,7},{6,4},{7,5},{8,10},{9,11},{10,... | collective-permute-start | bytes 49160 | tf_op jit(solution)/shard_map/ppermute | solution.py:363
  34.1 3.2 %collective-permute-start.14 = (bf16[32,256]{1,0:T(8,128)(2,1)S(1)}, bf16[32,256]{1,0:T(8,128)(2,1)S(1)}, u32[]{:S(2)}, u32[]{:S(2)}) collective-permute-start(bf16[32,256]{1,0:T(8,128)(2,1)S(1)} %get-tuple-element.49), channel_id=1, source_target_pairs={{0,3},{1,2},{2,1},{3,0},{4,7},{5,6},{6,5},{7,4},{8,11},{9,10},{10,... | collective-permute-start | bytes 49160 | tf_op jit(solution)/shard_map/ppermute | solution.py:363
  34.1 3.2 %collective-permute-start.15 = (bf16[32,256]{1,0:T(8,128)(2,1)S(1)}, bf16[32,256]{1,0:T(8,128)(2,1)S(1)}, u32[]{:S(2)}, u32[]{:S(2)}) collective-permute-start(bf16[32,256]{1,0:T(8,128)(2,1)S(1)} %get-tuple-element.50), channel_id=1, source_target_pairs={{0,1},{1,0},{2,3},{3,2},{4,5},{5,4},{6,7},{7,6},{8,9},{9,8},{10,11... | collective-permute-start | bytes 49160 | tf_op jit(solution)/shard_map/ppermute | solution.py:363
